TPU v7x, 512 devices: a whole 4x4x16 slice. The times are simulated.
512 devices in a mesh: dp: 32 (over x, z_lo), mp: 16 (over y, z_hi, core).
Axes of the slice: x: 4, y: 4, z: 16 (z_hi: 2, z_lo: 8; z = z_hi * 8 + z_lo), core: 2. Of those that a mesh axis runs over, the one named last changes fastest.
Arguments:
- tokens: bfloat16 [8192, 4096], P('dp', 'mp'), may hold values from -1200 to 1200
- norm_gain: bfloat16 [4096], P('mp'), may hold values from 0.099609375 to 1.8984375
- w_inner: bfloat16 [4096, 12288], P('dp', 'mp'), may hold values from -0.09375 to 0.09375
- w_outer: bfloat16 [12288, 4096], P('mp', 'dp'), may hold values from -0.109375 to 0.109375
Outputs:
- mlp_out: bfloat16 [8192, 4096], P('dp', 'mp')
All inputs are finite; a program needn't handle non-finite values.
Results may differ from a plain program's by a relative error of at most 0.017.
Values may be sent and summed in bfloat16 or wider, within the bound.
No kernel may reach another device: no remote copies, remote signals or barrier semaphores. Data moves between devices by JAX's collectives and lax.ppermute only.
A program may use at most 64 MiB of HBM per device.

v0:
```python
import jax
import jax.numpy as jnp
from jax import lax
from jax.sharding import PartitionSpec as P

epsilon = 1e-06


def gelu_exact(values):
    return 0.5 * values * (1.0 + lax.erf(values * 0.7071067811865476))


def per_device(tokens, norm_gain, w_inner, w_outer):
    gathered, full_gain = (
        lax.all_gather(tokens, "mp", axis=1, tiled=True),
        lax.all_gather(norm_gain, "mp", axis=0, tiled=True),
    )
    values = gathered.astype(jnp.float32)
    center = jnp.mean(values, axis=1, keepdims=True)
    spread = jnp.mean(jnp.square(values - center), axis=1, keepdims=True)
    normed = (
        (values - center) * lax.rsqrt(spread + epsilon) * full_gain.astype(jnp.float32)
    ).astype(jnp.bfloat16)
    inner_full, outer_full = (
        lax.all_gather(w_inner, "dp", axis=0, tiled=True),
        lax.all_gather(w_outer, "dp", axis=1, tiled=True),
    )
    hidden_pre = jnp.dot(normed, inner_full, preferred_element_type=jnp.float32)
    activated = gelu_exact(hidden_pre).astype(jnp.bfloat16)
    partial_value = jnp.dot(activated, outer_full, preferred_element_type=jnp.float32)
    return lax.psum_scatter(
        partial_value.astype(jnp.bfloat16), "mp", scatter_dimension=1, tiled=True
    )


def solution(mesh):
    in_specs = (P("dp", "mp"), P("mp"), P("dp", "mp"), P("mp", "dp"))
    out_specs = P("dp", "mp")
    return jax.shard_map(
        per_device, mesh=mesh, in_specs=in_specs, out_specs=out_specs, check_vma=False
    )
```

profile of v0, /device:TPU:1, one launch (start us, length us, event | category | flops | bytes accessed | tf_op | source)
XLA Modules:
  0.0 713.2 jit_solution(8334902931922558268)
XLA Ops:
  6.5 0.0 all-gather.5.cloned.1.call-start
  6.5 0.7 all-gather.5.cloned.1.call-update
  7.3 0.0 all-gather.7.cloned.1.call-start
  7.3 0.7 all-gather.7.cloned.1.call-update
  8.0 0.0 all-gather.9.cloned.1.call-start
  8.1 0.7 all-gather.9.cloned.1.call-update
  8.7 0.0 reduce-scatter.2.cloned.1.call-start
  8.8 0.7 reshape.13
  9.4 51.1 %all-gather = bf16[16,1,256]{2,1,0:T(2,128)(2,1)S(1)} all-gather(bf16[1,1,256]{2,1,0:T(2,128)(2,1)S(1)} %reshape.13), channel_id=1, replica_groups=mesh['dp'=32,'mp'=16] {'mp'}, dimensions={0}, use_global_device_ids=true | all-gather | bytes 8704 | tf_op jit(solution)/shard_map/all_gather | solution.py:16
  60.5 45.9 %all-gather.5.cloned.1.call-done = bf16[256,4096]{1,0:T(8,128)(2,1)} async-done(((bf16[256,256]{1,0:T(8,128)(2,1)}), bf16[256,4096]{1,0:T(8,128)(2,1)}) %all-gather.5.cloned.1.call-update) | async-done | bytes 2097168 | tf_op jit(solution)/shard_map/all_gather | solution.py:15
  106.5 0.0 copy-start
  106.5 2.1 convert_reduce_fusion
  108.6 2.3 fusion.2
  110.9 216.3 %all-gather.7.cloned.1.call-done = bf16[4096,768]{1,0:T(8,128)(2,1)} async-done(((bf16[128,768]{1,0:T(8,128)(2,1)}), bf16[4096,768]{1,0:T(8,128)(2,1)}) %all-gather.7.cloned.1.call-update) | async-done | bytes 6291472 | tf_op jit(solution)/shard_map/all_gather | solution.py:25
  327.1 237.7 %all-gather.9.cloned.1.call-done = bf16[768,4096]{1,0:T(8,128)(2,1)} async-done(((bf16[768,128]{1,0:T(8,128)(2,1)}), bf16[768,4096]{1,0:T(8,128)(2,1)}) %all-gather.9.cloned.1.call-update) | async-done | bytes 6291472 | tf_op jit(solution)/shard_map/all_gather | solution.py:26
  564.8 0.0 copy-done
  564.8 10.6 %convolution_convert_fusion = bf16[256,4096]{1,0:T(8,128)(2,1)} fusion(bf16[768,4096]{1,0:T(8,128)(2,1)} %all-gather.9.cloned.1.call-done, bf16[4096,768]{1,0:T(8,128)(2,1)} %all-gather.7.cloned.1.call-done, bf16[256,4096]{1,0:T(8,128)(2,1)S(1)} %copy-done, f32[4096]{0:T(1024)S(1)} %bitcast.3, f32[256]{0:T(256)S(1)} %add_rsqrt_fusion, ...), kind=kOutput, calls=%fused_computation.2 | convolution fusion | flops 3228499968 | bytes 16795648 | tf_op jit(solution)/shard_map/dot_general | solution.py:30
  575.4 0.0 reduce-scatter.2.cloned.1.call-update
  575.5 131.2 %reduce-scatter.2.cloned.1.call-done = bf16[256,256]{1,0:T(8,128)(2,1)} async-done(((bf16[256,4096]{1,0:T(8,128)(2,1)}), bf16[256,256]{1,0:T(8,128)(2,1)}) %reduce-scatter.2.cloned.1.call-update) | async-done | bytes 131088 | tf_op jit(solution)/shard_map/reduce_scatter | solution.py:31
  (3 shorter events, 0.0 us)
Async XLA Ops:
  6.5 99.9 %all-gather.5.cloned.1.call-start = ((), (), s32[]{:S(2)}) async-start(), calls=%async_computation.1 | async-start | bytes 2228224 | tf_op jit(solution)/shard_map/all_gather | solution.py:15
  7.3 319.9 %all-gather.7.cloned.1.call-start = ((), (), s32[]{:S(2)}) async-start(), calls=%async_computation.2 | async-start | bytes 6488064 | tf_op jit(solution)/shard_map/all_gather | solution.py:25
  8.0 556.8 %all-gather.9.cloned.1.call-start = ((), (), s32[]{:S(2)}) async-start(), calls=%async_computation.3 | async-start | bytes 6488064 | tf_op jit(solution)/shard_map/all_gather | solution.py:26
  8.7 698.0 %reduce-scatter.2.cloned.1.call-start = ((), (), s32[]{:S(2)}) async-start(), calls=%async_computation.4 | async-start | bytes 2228224 | tf_op jit(solution)/shard_map/reduce_scatter | solution.py:31
  106.5 458.4 %copy-start = (bf16[256,4096]{1,0:T(8,128)(2,1)S(1)}, bf16[256,4096]{1,0:T(8,128)(2,1)}, u32[]{:S(2)}) copy-start(bf16[256,4096]{1,0:T(8,128)(2,1)} %all-gather.5.cloned.1.call-done) | copy-start | bytes 6291460
Sparse Core Ops, SparseCore 0:
  10.5 95.9 all-gather.4
  108.5 218.5 all-gather.6
  329.2 235.6 all-gather.8
  575.6 131.0 reduce-scatter.1
where the time goes:
time: 714 us; the launch traced here: 713 us
  waiting for transfers between devices  633 us (89%)
  blocking collectives  51.1 us (7%)
  between operations  13.1 us (2%)
  matrix products  10.6 us (1%)
    all_gather x1, waiting for transfers between devices, per_device(): lax.all_gather(w_outer, 'dp', axis=1, tiled=True)  238 us
    all_gather x1, waiting for transfers between devices, per_device(): lax.all_gather(w_inner, 'dp', axis=0, tiled=True)  216 us
    reduce_scatter x1, waiting for transfers between devices, per_device(): lax.psum_scatter(partial_value.astype(jnp.bfloat16), 'mp', scatter_dimens...  131 us
    all_gather x1, blocking collectives, per_device(): lax.all_gather(norm_gain, 'mp', axis=0, tiled=True)  51.1 us
    all_gather x1, waiting for transfers between devices, per_device(): lax.all_gather(tokens, 'mp', axis=1, tiled=True)  45.9 us
  transfers between devices with their start and end apart: 4, of which 4 were waited for; matrix products, arithmetic and copies ran while one was open for 1% of the time, Pallas kernels for 0%

commit v1 on v0

v1 whole, which is shorter than its diff:
```python
import jax
import jax.numpy as jnp
import numpy as np
from jax import lax
from jax.experimental import pallas as pl
from jax.experimental.pallas import tpu as pltpu
from jax.sharding import Mesh, PartitionSpec as P

epsilon = 1e-06
AXES = ("x", "zt", "zq", "y", "zh", "c")
SIZES = (4, 2, 4, 4, 2, 2)
SIZE = dict(zip(AXES, SIZES))
GAIN_ROWS = 16


def gelu_exact(values):
    return 0.5 * values * (1.0 + lax.erf(values * 0.7071067811865476))


def send(value, axes, k):
    count = int(np.prod([SIZE[a] for a in axes]))
    return lax.ppermute(value, axes, [(i, i ^ k) for i in range(count)])


def after(value, *others):
    return lax.optimization_barrier((value, *others))[0]


def swap_halves(first, second):
    both = [(a, b) for a in (0, 1) for b in (0, 1)]
    straight = lax.ppermute(first, ("zt", "c"), [(2 * a + b, 2 * b + a) for a, b in both])
    crossed = lax.ppermute(second, ("zt", "c"), [(2 * a + b, 2 * b + 1 - a) for a, b in both])
    return straight, crossed


def coordinates():
    return {a: lax.axis_index(a) for a in AXES}


def hidden_kernel(place, mine, other, w0, w1, w2, w3, act):
    x, zq, y, zh, c = (place[i] for i in range(5))
    cores = (mine, other)
    rows = act.shape[1]
    width = mine.shape[3]
    count = 2 * mine.shape[0] * 2 * width
    for a in range(2):
        blocks = [(ref, i, 2 * a + j) for ref in cores for i in range(4) for j in range(2)]
        total = jnp.zeros((rows, width), jnp.float32)
        for ref, i, j in blocks:
            total += ref[i, j, :rows, :].astype(jnp.float32)
        center = jnp.sum(total, axis=1, keepdims=True) * (1.0 / count)
        total = jnp.zeros((rows, width), jnp.float32)
        for ref, i, j in blocks:
            total += jnp.square(ref[i, j, :rows, :].astype(jnp.float32) - center)
        spread = jnp.sum(total, axis=1, keepdims=True) * (1.0 / count)
        scale = lax.rsqrt(spread + epsilon)
        acc = jnp.zeros((rows, act.shape[2]), jnp.float32)
        for k, weights in enumerate((w0, w1, w2, w3)):
            i = x ^ k ^ y
            for s in range(2):
                j = 2 * a + (zh ^ c ^ s)
                for ck, ref in enumerate(cores):
                    first = 2 * (c ^ ck)
                    block = jnp.concatenate(
                        [weights[first ^ zq, s], weights[(first + 1) ^ zq, s]], axis=0
                    )
                    gain = ref[i, j, rows : rows + GAIN_ROWS, :].astype(jnp.float32)[0:1]
                    values = ref[i, j, :rows, :].astype(jnp.float32)
                    normed = ((values - center) * scale * gain).astype(jnp.bfloat16)
                    acc += jnp.dot(normed, block, preferred_element_type=jnp.float32)
        act[a] = gelu_exact(acc).astype(act.dtype)


def out_kernel(place, act, w0, w1, w2, w3, mine, other):
    x, zq, y, zh, c = (place[i] for i in range(5))
    for ck, ref in ((1, other), (0, mine)):
        first = 2 * (c ^ ck)
        for k, weights in enumerate((w0, w1, w2, w3)):
            i = x ^ k ^ y
            for s in range(2):
                block = jnp.concatenate(
                    [weights[first ^ zq, s], weights[(first + 1) ^ zq, s]], axis=1
                )
                for a in range(2):
                    ref[i, 2 * a + (zh ^ c ^ s)] = jnp.dot(
                        act[a], block, preferred_element_type=jnp.float32
                    ).astype(ref.dtype)


def call(kernel, out_shape, flops, *operands):
    vmem = pl.BlockSpec(memory_space=pltpu.VMEM)
    size = sum(o.size * o.dtype.itemsize for o in operands)
    return pl.pallas_call(
        kernel,
        out_shape=out_shape,
        in_specs=[pl.BlockSpec(memory_space=pltpu.SMEM)] + [vmem] * (len(operands) - 1),
        out_specs=jax.tree.map(lambda _: vmem, out_shape),
        compiler_params=pltpu.CompilerParams(vmem_limit_bytes=40 * 1024 * 1024),
        cost_estimate=pl.CostEstimate(flops=flops, bytes_accessed=size, transcendentals=0),
    )(*operands)


def per_device(tokens, norm_gain, w_inner, w_outer):
    at = coordinates()
    zt = at["zt"]
    rows, cols = tokens.shape
    d_dev, f_dev = w_inner.shape
    half = f_dev // 2
    place = jnp.stack([at[a] for a in ("x", "zq", "y", "zh", "c")]).astype(jnp.int32)

    def weight_half(which, axis, array):
        return lax.dynamic_slice_in_dim(array, which * half, half, axis)

    swapped = swap_halves(weight_half(zt, 1, w_inner), weight_half(1 - zt, 1, w_inner))
    inner = jnp.stack(swapped)
    inner = jnp.stack([inner] + [send(inner, ("zq",), k) for k in (1, 2, 3)])

    both = jnp.concatenate([tokens, jnp.broadcast_to(norm_gain[None], (GAIN_ROWS, cols))], axis=0)
    both = after(both, *swapped)
    both = jnp.stack([both] + [send(both, ("zt", "zh"), k) for k in (1, 2, 3)])

    inner_all = [inner] + [send(inner, ("x",), k) for k in (1, 2, 3)]

    outer = jnp.stack(
        swap_halves(*(weight_half(h, 0, after(w_outer, inner)) for h in (zt, 1 - zt)))
    )
    outer = jnp.stack([outer] + [send(outer, ("zq",), k) for k in (1, 2, 3)])

    both = after(both, inner)
    both = jnp.stack([both] + [send(both, ("y",), k) for k in (1, 2, 3)])
    other = send(both, ("c",), 1)
    outer_all = [outer] + [send(after(outer, inner_all[k]), ("x",), k) for k in (1, 2, 3)]

    flops = 2 * 2 * rows * half * 16 * cols
    act = call(
        hidden_kernel,
        jax.ShapeDtypeStruct((2, rows, half), jnp.bfloat16),
        flops, place, both, other, *inner_all,
    )
    shape = jax.ShapeDtypeStruct((4, 4, rows, cols), jnp.bfloat16)
    mine, other = call(out_kernel, (shape, shape), flops, place, act, *outer_all)

    total = mine.astype(jnp.float32) + send(other, ("c",), 1).astype(jnp.float32)
    sent = total.astype(jnp.bfloat16)
    total = total[0] + sum(send(sent[k], ("y",), k).astype(jnp.float32) for k in (1, 2, 3))
    sent = total.astype(jnp.bfloat16)
    total = total[0] + sum(send(sent[k], ("zt", "zh"), k).astype(jnp.float32) for k in (1, 2, 3))
    return total.astype(jnp.bfloat16)


def solution(mesh):
    fine = Mesh(np.asarray(mesh.devices).reshape(SIZES), AXES)
    dp, mp = ("x", "zt", "zq"), ("y", "zh", "c")
    in_specs = (P(dp, mp), P(mp), P(dp, mp), P(mp, dp))
    return jax.shard_map(
        per_device, mesh=fine, in_specs=in_specs, out_specs=P(dp, mp), check_vma=False
    )
```

time: 714 us -> 283 us (0.40)
  waiting for transfers between devices: 633 us -> 127 us
  starting transfers between devices: 0.12 us -> 128 us
  blocking collectives: 51.1 us -> 0 us
  between operations: 13.1 us -> 0.45 us
  matrix products: 10.6 us -> 0 us
  Pallas kernels: 0 us -> 10.5 us
  local copies, waits for them, and re-layouts: 0.66 us -> 7.96 us
    all_gather x3 -> x0, waiting for transfers between devices: 500 us -> none  [the longest x1 238 us: per_device(): lax.all_gather(w_outer, 'dp', axis=1, tiled=True)]
    reduce_scatter x1 -> x0, waiting for transfers between devices: 131 us -> none  [per_device(): lax.psum_scatter(partial_value.astype(jnp.bfloat16), 'mp', scatter_dimens...]
    ppermute x0 -> x30, starting transfers between devices: none -> 128 us  [the longest x26 106 us: send(): return lax.ppermute(value, axes, [(i, i ^ k) for i in range(count)])]
    ppermute x0 -> x30, waiting for transfers between devices: none -> 127 us  [the longest x26 127 us: send(): return lax.ppermute(value, axes, [(i, i ^ k) for i in range(count)])]
    all_gather x1 -> x0, blocking collectives: 51.1 us -> none  [per_device(): lax.all_gather(norm_gain, 'mp', axis=0, tiled=True)]
    dot_general x1 -> x0, matrix products: 10.6 us -> none  [per_device(): jnp.dot(activated, outer_full, preferred_element_type=jnp.float32)]
    pallas_call x0 -> x2, Pallas kernels: none -> 10.5 us  [call(): pl.pallas_call(kernel, out_shape=out_shape, in_specs=[pl.BlockSpec(memory...]
  transfers between devices with their start and end apart: 4 -> 30, of which waited for: 4 -> 15; matrix products, arithmetic and copies ran while one was open for 1% -> 1% of each run, Pallas kernels for 0% -> 2%
where the time goes in v1:
time: 283 us; the launch traced here: 278 us
  starting transfers between devices  128 us (45%)
  waiting for transfers between devices  127 us (45%)
  Pallas kernels  10.5 us (4%)
  local copies, waits for them, and re-layouts  7.96 us (3%)
  other arithmetic  4.1 us (1%)
    ppermute x26, waiting for transfers between devices, send(): return lax.ppermute(value, axes, [(i, i ^ k) for i in range(count)])  127 us
    ppermute x26, starting transfers between devices, send(): return lax.ppermute(value, axes, [(i, i ^ k) for i in range(count)])  106 us
    ppermute x2, starting transfers between devices, swap_halves(): lax.ppermute(first, ('zt', 'c'), [(2 * a + b, 2 * b + a) for a, b in both])  12.8 us
    pallas_call x2, Pallas kernels, call(): pl.pallas_call(kernel, out_shape=out_shape, in_specs=[pl.BlockSpec(memory...  10.5 us
    ppermute x2, starting transfers between devices, swap_halves(): lax.ppermute(second, ('zt', 'c'), [(2 * a + b, 2 * b + 1 - a) for a, b in...  8.68 us
    unnamed x14, local copies, waits for them, and re-layouts  6.1 us
  transfers between devices with their start and end apart: 30, of which 15 were waited for; matrix products, arithmetic and copies ran while one was open for 1% of the time, Pallas kernels for 2%

profile of v1, /device:TPU:1, one launch (start us, length us, event | category | flops | bytes accessed | tf_op | source)
XLA Modules:
  0.0 277.7 jit_solution(9548842359408875227)
XLA Ops:
  1.0 10.2 %collective-permute-start = (bf16[128,384]{1,0:T(8,128)(2,1)S(1)}, bf16[128,384]{1,0:T(8,128)(2,1)S(1)}, u32[]{:S(2)}, u32[]{:S(2)}) collective-permute-start(bf16[128,384]{1,0:T(8,128)(2,1)S(1)} %get-tuple-element.38), channel_id=1, source_target_pairs={{0,0},{1,64},{64,1},{65,65},{2,2},{3,66},{66,3},{67,67},{4,4},{5,6... | collective-permute-start | bytes 294920 | tf_op jit(solution)/shard_map/ppermute | solution.py:31
  14.7 11.5 %collective-permute-start.4 = (bf16[272,256]{1,0:T(8,128)(2,1)S(1)}, bf16[272,256]{1,0:T(8,128)(2,1)S(1)}, u32[]{:S(2)}, u32[]{:S(2)}) collective-permute-start(bf16[272,256]{1,0:T(8,128)(2,1)S(1)} %pad_maximum_fusion.6), channel_id=1, source_target_pairs={{0,66},{2,64},{64,2},{66,0},{1,67},{3,65},{65,3},{67,1},{4,70},{6,... | collective-permute-start | bytes 417800 | tf_op jit(solution)/shard_map/ppermute | solution.py:22
  26.2 9.4 %collective-permute-start.3 = (bf16[272,256]{1,0:T(8,128)(2,1)S(1)}, bf16[272,256]{1,0:T(8,128)(2,1)S(1)}, u32[]{:S(2)}, u32[]{:S(2)}) collective-permute-start(bf16[272,256]{1,0:T(8,128)(2,1)S(1)} %pad_maximum_fusion.6), channel_id=1, source_target_pairs={{0,64},{2,66},{64,0},{66,2},{1,65},{3,67},{65,1},{67,3},{4,68},{6,... | collective-permute-start | bytes 417800 | tf_op jit(solution)/shard_map/ppermute | solution.py:22
  37.6 6.5 %collective-permute-start.7 = (bf16[2,128,384]{2,1,0:T(8,128)(2,1)S(1)}, bf16[2,128,384]{2,1,0:T(8,128)(2,1)S(1)}, u32[]{:S(2)}, u32[]{:S(2)}) collective-permute-start(bf16[2,128,384]{2,1,0:T(8,128)(2,1)S(1)} %get-tuple-element.36), channel_id=1, source_target_pairs={{0,48},{16,32},{32,16},{48,0},{1,49},{17,33},{33,17},{49,1},{2,50}... | collective-permute-start | bytes 589832 | tf_op jit(solution)/shard_map/ppermute | solution.py:22
  48.2 6.9 %collective-permute-done.2 = bf16[272,256]{1,0:T(8,128)(2,1)S(1)} collective-permute-done((bf16[272,256]{1,0:T(8,128)(2,1)S(1)}, bf16[272,256]{1,0:T(8,128)(2,1)S(1)}, u32[]{:S(2)}, u32[]{:S(2)}) %collective-permute-start.2) | collective-permute-done | bytes 139296 | tf_op jit(solution)/shard_map/ppermute | solution.py:22
  55.2 3.7 %collective-permute-done.7 = bf16[2,128,384]{2,1,0:T(8,128)(2,1)S(1)} collective-permute-done((bf16[2,128,384]{2,1,0:T(8,128)(2,1)S(1)}, bf16[2,128,384]{2,1,0:T(8,128)(2,1)S(1)}, u32[]{:S(2)}, u32[]{:S(2)}) %collective-permute-start.7) | collective-permute-done | bytes 196640 | tf_op jit(solution)/shard_map/ppermute | solution.py:22
  58.9 14.7 %collective-permute-done.6 = bf16[2,128,384]{2,1,0:T(8,128)(2,1)S(1)} collective-permute-done((bf16[2,128,384]{2,1,0:T(8,128)(2,1)S(1)}, bf16[2,128,384]{2,1,0:T(8,128)(2,1)S(1)}, u32[]{:S(2)}, u32[]{:S(2)}) %collective-permute-start.6) | collective-permute-done | bytes 196640 | tf_op jit(solution)/shard_map/ppermute | solution.py:22
  73.8 4.6 %collective-permute-start.10 = (bf16[4,272,256]{2,1,0:T(8,128)(2,1)S(1)}, bf16[4,272,256]{2,1,0:T(8,128)(2,1)S(1)}, u32[]{:S(2)}, u32[]{:S(2)}) collective-permute-start(bf16[4,272,256]{2,1,0:T(8,128)(2,1)S(1)} %pad_maximum_fusion.3), channel_id=1, source_target_pairs={{0,12},{4,8},{8,4},{12,0},{1,13},{5,9},{9,5},{13,1},{2,14},{6,10},... | collective-permute-start | bytes 1671176 | tf_op jit(solution)/shard_map/ppermute | solution.py:22
  82.8 19.9 %collective-permute-done.10 = bf16[4,272,256]{2,1,0:T(8,128)(2,1)S(1)} collective-permute-done((bf16[4,272,256]{2,1,0:T(8,128)(2,1)S(1)}, bf16[4,272,256]{2,1,0:T(8,128)(2,1)S(1)}, u32[]{:S(2)}, u32[]{:S(2)}) %collective-permute-start.10) | collective-permute-done | bytes 557088 | tf_op jit(solution)/shard_map/ppermute | solution.py:22
  105.2 3.4 %collective-permute-start.11 = (bf16[4,4,272,256]{3,2,1,0:T(8,128)(2,1)S(1)}, bf16[4,4,272,256]{3,2,1,0:T(8,128)(2,1)}, u32[]{:S(2)}, u32[]{:S(2)}) collective-permute-start(bf16[4,4,272,256]{3,2,1,0:T(8,128)(2,1)S(1)} %pad_maximum_fusion.mine), channel_id=1, source_target_pairs={{0,1},{1,0},{2,3},{3,2},{4,5},{5,4},{6,7},{7,6},{8,9},{9,8},{10,11... | collective-permute-start | bytes 6684680 | tf_op jit(solution)/shard_map/ppermute | solution.py:22
  108.7 6.8 %collective-permute-start.16 = (bf16[384,128]{1,0:T(8,128)(2,1)S(1)}, bf16[384,128]{1,0:T(8,128)(2,1)S(1)}, u32[]{:S(2)}, u32[]{:S(2)}) collective-permute-start(bf16[384,128]{1,0:T(8,128)(2,1)S(1)} %get-tuple-element.34), channel_id=1, source_target_pairs={{0,1},{1,65},{64,0},{65,64},{2,3},{3,67},{66,2},{67,66},{4,5},{5,6... | collective-permute-start | bytes 294920 | tf_op jit(solution)/shard_map/ppermute | solution.py:32
  118.1 3.1 %collective-permute-start.12 = (bf16[4,2,128,384]{3,2,1,0:T(8,128)(2,1)S(1)}, bf16[4,2,128,384]{3,2,1,0:T(8,128)(2,1)S(1)}, u32[]{:S(2)}, u32[]{:S(2)}) collective-permute-start(bf16[4,2,128,384]{3,2,1,0:T(8,128)(2,1)S(1)} %pad_maximum_fusion.1.w0), channel_id=1, source_target_pairs={{0,128},{128,0},{256,384},{384,256},{1,129},{129,1},{257,385},{385... | collective-permute-start | bytes 2359304 | tf_op jit(solution)/shard_map/ppermute | solution.py:22
  121.2 4.4 %collective-permute-start.13 = (bf16[4,2,128,384]{3,2,1,0:T(8,128)(2,1)S(1)}, bf16[4,2,128,384]{3,2,1,0:T(8,128)(2,1)S(1)}, u32[]{:S(2)}, u32[]{:S(2)}) collective-permute-start(bf16[4,2,128,384]{3,2,1,0:T(8,128)(2,1)S(1)} %pad_maximum_fusion.1.w0), channel_id=1, source_target_pairs={{0,256},{128,384},{256,0},{384,128},{1,257},{129,385},{257,1},{385... | collective-permute-start | bytes 2359304 | tf_op jit(solution)/shard_map/ppermute | solution.py:22
  127.7 6.2 %collective-permute-start.19 = (bf16[2,384,128]{2,1,0:T(8,128)(2,1)S(1)}, bf16[2,384,128]{2,1,0:T(8,128)(2,1)S(1)}, u32[]{:S(2)}, u32[]{:S(2)}) collective-permute-start(bf16[2,384,128]{2,1,0:T(8,128)(2,1)S(1)} %get-tuple-element.32), channel_id=1, source_target_pairs={{0,48},{16,32},{32,16},{48,0},{1,49},{17,33},{33,17},{49,1},{2,50}... | collective-permute-start | bytes 589832 | tf_op jit(solution)/shard_map/ppermute | solution.py:22
  133.9 3.4 %collective-permute-done.19 = bf16[2,384,128]{2,1,0:T(8,128)(2,1)S(1)} collective-permute-done((bf16[2,384,128]{2,1,0:T(8,128)(2,1)S(1)}, bf16[2,384,128]{2,1,0:T(8,128)(2,1)S(1)}, u32[]{:S(2)}, u32[]{:S(2)}) %collective-permute-start.19) | collective-permute-done | bytes 196640 | tf_op jit(solution)/shard_map/ppermute | solution.py:22
  137.3 4.4 %collective-permute-start.18 = (bf16[2,384,128]{2,1,0:T(8,128)(2,1)S(1)}, bf16[2,384,128]{2,1,0:T(8,128)(2,1)S(1)}, u32[]{:S(2)}, u32[]{:S(2)}) collective-permute-start(bf16[2,384,128]{2,1,0:T(8,128)(2,1)S(1)} %get-tuple-element.32), channel_id=1, source_target_pairs={{0,32},{16,48},{32,0},{48,16},{1,33},{17,49},{33,1},{49,17},{2,34}... | collective-permute-start | bytes 589832 | tf_op jit(solution)/shard_map/ppermute | solution.py:22
  141.7 6.8 %collective-permute-done.18 = bf16[2,384,128]{2,1,0:T(8,128)(2,1)S(1)} collective-permute-done((bf16[2,384,128]{2,1,0:T(8,128)(2,1)S(1)}, bf16[2,384,128]{2,1,0:T(8,128)(2,1)S(1)}, u32[]{:S(2)}, u32[]{:S(2)}) %collective-permute-start.18) | collective-permute-done | bytes 196640 | tf_op jit(solution)/shard_map/ppermute | solution.py:22
  150.4 6.3 %collective-permute-done.17 = bf16[2,384,128]{2,1,0:T(8,128)(2,1)S(1)} collective-permute-done((bf16[2,384,128]{2,1,0:T(8,128)(2,1)S(1)}, bf16[2,384,128]{2,1,0:T(8,128)(2,1)S(1)}, u32[]{:S(2)}, u32[]{:S(2)}) %collective-permute-start.17) | collective-permute-done | bytes 196640 | tf_op jit(solution)/shard_map/ppermute | solution.py:22
  161.6 2.8 %collective-permute-start.21 = (bf16[4,2,384,128]{3,2,1,0:T(8,128)(2,1)}, bf16[4,2,384,128]{3,2,1,0:T(8,128)(2,1)}, u32[]{:S(2)}, u32[]{:S(2)}) collective-permute-start(bf16[4,2,384,128]{3,2,1,0:T(8,128)(2,1)} %pad_maximum_fusion.2.w0), channel_id=1, source_target_pairs={{0,256},{128,384},{256,0},{384,128},{1,257},{129,385},{257,1},{385... | collective-permute-start | bytes 2359304 | tf_op jit(solution)/shard_map/ppermute | solution.py:22
  165.4 4.6 %collective-permute-start.22 = (bf16[4,2,384,128]{3,2,1,0:T(8,128)(2,1)}, bf16[4,2,384,128]{3,2,1,0:T(8,128)(2,1)}, u32[]{:S(2)}, u32[]{:S(2)}) collective-permute-start(bf16[4,2,384,128]{3,2,1,0:T(8,128)(2,1)} %pad_maximum_fusion.2.w0), channel_id=1, source_target_pairs={{0,384},{128,256},{256,128},{384,0},{1,385},{129,257},{257,129},{3... | collective-permute-start | bytes 2359304 | tf_op jit(solution)/shard_map/ppermute | solution.py:22
  173.5 6.3 %shard_map.46.act = bf16[2,256,384]{2,1,0:T(8,128)(2,1)S(1)} custom-call(s32[5]{0:T(128)S(1)} %stack.101.place, bf16[4,4,272,256]{3,2,1,0:T(8,128)(2,1)S(1)} %pad_maximum_fusion.mine, bf16[4,4,272,256]{3,2,1,0:T(8,128)(2,1)} %collective-permute-done.11.other, bf16[4,2,128,384]{3,2,1,0:T(8,128)(2,1)S(1)} %pad_maximum_fusion.1.w0, ...), custom_call_target="tpu_custom_call" | custom-call | flops 1610612736 | bytes 7602196 | tf_op jit(solution)/shard_map/pallas_call | solution.py:93
  179.8 14.7 %collective-permute-done.21.w2 = bf16[4,2,384,128]{3,2,1,0:T(8,128)(2,1)} collective-permute-done((bf16[4,2,384,128]{3,2,1,0:T(8,128)(2,1)}, bf16[4,2,384,128]{3,2,1,0:T(8,128)(2,1)}, u32[]{:S(2)}, u32[]{:S(2)}) %collective-permute-start.21) | collective-permute-done | bytes 786464 | tf_op jit(solution)/shard_map/ppermute | solution.py:22
  194.4 9.7 %collective-permute-done.22.w3 = bf16[4,2,384,128]{3,2,1,0:T(8,128)(2,1)} collective-permute-done((bf16[4,2,384,128]{3,2,1,0:T(8,128)(2,1)}, bf16[4,2,384,128]{3,2,1,0:T(8,128)(2,1)}, u32[]{:S(2)}, u32[]{:S(2)}) %collective-permute-start.22) | collective-permute-done | bytes 786464 | tf_op jit(solution)/shard_map/ppermute | solution.py:22
  204.1 4.2 %shard_map.47 = (bf16[4,4,256,256]{3,2,1,0:T(8,128)(2,1)S(1)}, bf16[4,4,256,256]{3,2,1,0:T(8,128)(2,1)S(1)}) custom-call(s32[5]{0:T(128)S(1)} %stack.101.place, bf16[2,256,384]{2,1,0:T(8,128)(2,1)S(1)} %shard_map.46.act, bf16[4,2,384,128]{3,2,1,0:T(8,128)(2,1)} %pad_maximum_fusion.2.w0, bf16[4,2,384,128]{3,2,1,0:T(8,128)(2,1)} %collective-permute-done.20.w1, ...), custom_call_target="tpu_custom_call" | custom-call | flops 1610612736 | bytes 3538964 | tf_op jit(solution)/shard_map/pallas_call | solution.py:93
  208.4 3.4 %collective-permute-start.23 = (bf16[4,4,256,256]{3,2,1,0:T(8,128)(2,1)S(1)}, bf16[4,4,256,256]{3,2,1,0:T(8,128)(2,1)S(1)}, u32[]{:S(2)}, u32[]{:S(2)}) collective-permute-start(bf16[4,4,256,256]{3,2,1,0:T(8,128)(2,1)S(1)} %get-tuple-element.20), channel_id=1, source_target_pairs={{0,1},{1,0},{2,3},{3,2},{4,5},{5,4},{6,7},{7,6},{8,9},{9,8},{10,11... | collective-permute-start | bytes 6291464 | tf_op jit(solution)/shard_map/ppermute | solution.py:22
  211.8 3.8 %collective-permute-done.23 = bf16[4,4,256,256]{3,2,1,0:T(8,128)(2,1)S(1)} collective-permute-done((bf16[4,4,256,256]{3,2,1,0:T(8,128)(2,1)S(1)}, bf16[4,4,256,256]{3,2,1,0:T(8,128)(2,1)S(1)}, u32[]{:S(2)}, u32[]{:S(2)}) %collective-permute-start.23) | collective-permute-done | bytes 2097184 | tf_op jit(solution)/shard_map/ppermute | solution.py:22
  216.4 4.6 %collective-permute-start.26 = (bf16[4,256,256]{2,1,0:T(8,128)(2,1)S(1)}, bf16[4,256,256]{2,1,0:T(8,128)(2,1)S(1)}, u32[]{:S(2)}, u32[]{:S(2)}) collective-permute-start(bf16[4,256,256]{2,1,0:T(8,128)(2,1)S(1)} %get-tuple-element.26), channel_id=1, source_target_pairs={{0,12},{4,8},{8,4},{12,0},{1,13},{5,9},{9,5},{13,1},{2,14},{6,10},... | collective-permute-start | bytes 1572872 | tf_op jit(solution)/shard_map/ppermute | solution.py:22
  225.4 18.5 %collective-permute-done.26 = bf16[4,256,256]{2,1,0:T(8,128)(2,1)S(1)} collective-permute-done((bf16[4,256,256]{2,1,0:T(8,128)(2,1)S(1)}, bf16[4,256,256]{2,1,0:T(8,128)(2,1)S(1)}, u32[]{:S(2)}, u32[]{:S(2)}) %collective-permute-start.26) | collective-permute-done | bytes 524320 | tf_op jit(solution)/shard_map/ppermute | solution.py:22
  248.3 7.7 %collective-permute-start.28 = (bf16[256,256]{1,0:T(8,128)(2,1)S(1)}, bf16[256,256]{1,0:T(8,128)(2,1)S(1)}, u32[]{:S(2)}, u32[]{:S(2)}) collective-permute-start(bf16[256,256]{1,0:T(8,128)(2,1)S(1)} %get-tuple-element.30), channel_id=1, source_target_pairs={{0,64},{2,66},{64,0},{66,2},{1,65},{3,67},{65,1},{67,3},{4,68},{6,... | collective-permute-start | bytes 393224 | tf_op jit(solution)/shard_map/ppermute | solution.py:22
  256.0 6.6 %collective-permute-start.27 = (bf16[256,256]{1,0:T(8,128)(2,1)S(1)}, bf16[256,256]{1,0:T(8,128)(2,1)S(1)}, u32[]{:S(2)}, u32[]{:S(2)}) collective-permute-start(bf16[256,256]{1,0:T(8,128)(2,1)S(1)} %get-tuple-element.28), channel_id=1, source_target_pairs={{0,2},{2,0},{64,66},{66,64},{1,3},{3,1},{65,67},{67,65},{4,6},{6,4... | collective-permute-start | bytes 393224 | tf_op jit(solution)/shard_map/ppermute | solution.py:22
  262.6 3.6 %collective-permute-done.28 = bf16[256,256]{1,0:T(8,128)(2,1)S(1)} collective-permute-done((bf16[256,256]{1,0:T(8,128)(2,1)S(1)}, bf16[256,256]{1,0:T(8,128)(2,1)S(1)}, u32[]{:S(2)}, u32[]{:S(2)}) %collective-permute-start.28) | collective-permute-done | bytes 131104 | tf_op jit(solution)/shard_map/ppermute | solution.py:22
  266.3 10.7 %collective-permute-done.27 = bf16[256,256]{1,0:T(8,128)(2,1)S(1)} collective-permute-done((bf16[256,256]{1,0:T(8,128)(2,1)S(1)}, bf16[256,256]{1,0:T(8,128)(2,1)S(1)}, u32[]{:S(2)}, u32[]{:S(2)}) %collective-permute-start.27) | collective-permute-done | bytes 131104 | tf_op jit(solution)/shard_map/ppermute | solution.py:22
  (60 shorter events, 44.1 us)
Async XLA Ops:
  1.0 13.7 %collective-permute-start = (bf16[128,384]{1,0:T(8,128)(2,1)S(1)}, bf16[128,384]{1,0:T(8,128)(2,1)S(1)}, u32[]{:S(2)}, u32[]{:S(2)}) collective-permute-start(bf16[128,384]{1,0:T(8,128)(2,1)S(1)} %get-tuple-element.38), channel_id=1, source_target_pairs={{0,0},{1,64},{64,1},{65,65},{2,2},{3,66},{66,3},{67,67},{4,4},{5,6... | collective-permute-start | bytes 294920 | tf_op jit(solution)/shard_map/ppermute | solution.py:31
  11.2 3.5 %collective-permute-start.1 = (bf16[128,384]{1,0:T(8,128)(2,1)S(1)}, bf16[128,384]{1,0:T(8,128)(2,1)S(1)}, u32[]{:S(2)}, u32[]{:S(2)}) collective-permute-start(bf16[128,384]{1,0:T(8,128)(2,1)S(1)} %get-tuple-element.37), channel_id=1, source_target_pairs={{0,1},{1,65},{64,0},{65,64},{2,3},{3,67},{66,2},{67,66},{4,5},{5,6... | collective-permute-start | bytes 294920 | tf_op jit(solution)/shard_map/ppermute | solution.py:32
  14.7 31.3 %collective-permute-start.4 = (bf16[272,256]{1,0:T(8,128)(2,1)S(1)}, bf16[272,256]{1,0:T(8,128)(2,1)S(1)}, u32[]{:S(2)}, u32[]{:S(2)}) collective-permute-start(bf16[272,256]{1,0:T(8,128)(2,1)S(1)} %pad_maximum_fusion.6), channel_id=1, source_target_pairs={{0,66},{2,64},{64,2},{66,0},{1,67},{3,65},{65,3},{67,1},{4,70},{6,... | collective-permute-start | bytes 417800 | tf_op jit(solution)/shard_map/ppermute | solution.py:22
  26.2 22.0 %collective-permute-start.3 = (bf16[272,256]{1,0:T(8,128)(2,1)S(1)}, bf16[272,256]{1,0:T(8,128)(2,1)S(1)}, u32[]{:S(2)}, u32[]{:S(2)}) collective-permute-start(bf16[272,256]{1,0:T(8,128)(2,1)S(1)} %pad_maximum_fusion.6), channel_id=1, source_target_pairs={{0,64},{2,66},{64,0},{66,2},{1,65},{3,67},{65,1},{67,3},{4,68},{6,... | collective-permute-start | bytes 417800 | tf_op jit(solution)/shard_map/ppermute | solution.py:22
  35.6 19.5 %collective-permute-start.2 = (bf16[272,256]{1,0:T(8,128)(2,1)S(1)}, bf16[272,256]{1,0:T(8,128)(2,1)S(1)}, u32[]{:S(2)}, u32[]{:S(2)}) collective-permute-start(bf16[272,256]{1,0:T(8,128)(2,1)S(1)} %pad_maximum_fusion.6), channel_id=1, source_target_pairs={{0,2},{2,0},{64,66},{66,64},{1,3},{3,1},{65,67},{67,65},{4,6},{6,4... | collective-permute-start | bytes 417800 | tf_op jit(solution)/shard_map/ppermute | solution.py:22
  37.6 21.3 %collective-permute-start.7 = (bf16[2,128,384]{2,1,0:T(8,128)(2,1)S(1)}, bf16[2,128,384]{2,1,0:T(8,128)(2,1)S(1)}, u32[]{:S(2)}, u32[]{:S(2)}) collective-permute-start(bf16[2,128,384]{2,1,0:T(8,128)(2,1)S(1)} %get-tuple-element.36), channel_id=1, source_target_pairs={{0,48},{16,32},{32,16},{48,0},{1,49},{17,33},{33,17},{49,1},{2,50}... | collective-permute-start | bytes 589832 | tf_op jit(solution)/shard_map/ppermute | solution.py:22
  44.1 29.5 %collective-permute-start.6 = (bf16[2,128,384]{2,1,0:T(8,128)(2,1)S(1)}, bf16[2,128,384]{2,1,0:T(8,128)(2,1)S(1)}, u32[]{:S(2)}, u32[]{:S(2)}) collective-permute-start(bf16[2,128,384]{2,1,0:T(8,128)(2,1)S(1)} %get-tuple-element.36), channel_id=1, source_target_pairs={{0,32},{16,48},{32,0},{48,16},{1,33},{17,49},{33,1},{49,17},{2,34}... | collective-permute-start | bytes 589832 | tf_op jit(solution)/shard_map/ppermute | solution.py:22
  46.1 27.6 %collective-permute-start.5 = (bf16[2,128,384]{2,1,0:T(8,128)(2,1)S(1)}, bf16[2,128,384]{2,1,0:T(8,128)(2,1)S(1)}, u32[]{:S(2)}, u32[]{:S(2)}) collective-permute-start(bf16[2,128,384]{2,1,0:T(8,128)(2,1)S(1)} %get-tuple-element.36), channel_id=1, source_target_pairs={{0,16},{16,0},{32,48},{48,32},{1,17},{17,1},{33,49},{49,33},{2,18}... | collective-permute-start | bytes 589832 | tf_op jit(solution)/shard_map/ppermute | solution.py:22
  73.8 28.9 %collective-permute-start.10 = (bf16[4,272,256]{2,1,0:T(8,128)(2,1)S(1)}, bf16[4,272,256]{2,1,0:T(8,128)(2,1)S(1)}, u32[]{:S(2)}, u32[]{:S(2)}) collective-permute-start(bf16[4,272,256]{2,1,0:T(8,128)(2,1)S(1)} %pad_maximum_fusion.3), channel_id=1, source_target_pairs={{0,12},{4,8},{8,4},{12,0},{1,13},{5,9},{9,5},{13,1},{2,14},{6,10},... | collective-permute-start | bytes 1671176 | tf_op jit(solution)/shard_map/ppermute | solution.py:22
  78.4 24.3 %collective-permute-start.9 = (bf16[4,272,256]{2,1,0:T(8,128)(2,1)S(1)}, bf16[4,272,256]{2,1,0:T(8,128)(2,1)S(1)}, u32[]{:S(2)}, u32[]{:S(2)}) collective-permute-start(bf16[4,272,256]{2,1,0:T(8,128)(2,1)S(1)} %pad_maximum_fusion.3), channel_id=1, source_target_pairs={{0,8},{4,12},{8,0},{12,4},{1,9},{5,13},{9,1},{13,5},{2,10},{6,14},... | collective-permute-start | bytes 1671176 | tf_op jit(solution)/shard_map/ppermute | solution.py:22
  80.7 24.3 %collective-permute-start.8 = (bf16[4,272,256]{2,1,0:T(8,128)(2,1)S(1)}, bf16[4,272,256]{2,1,0:T(8,128)(2,1)S(1)}, u32[]{:S(2)}, u32[]{:S(2)}) collective-permute-start(bf16[4,272,256]{2,1,0:T(8,128)(2,1)S(1)} %pad_maximum_fusion.3), channel_id=1, source_target_pairs={{0,4},{4,0},{8,12},{12,8},{1,5},{5,1},{9,13},{13,9},{2,6},{6,2},{1... | collective-permute-start | bytes 1671176 | tf_op jit(solution)/shard_map/ppermute | solution.py:22
  105.0 3.7 %copy-start.6 = (bf16[768,128]{1,0:T(8,128)(2,1)S(1)}, bf16[768,128]{1,0:T(8,128)(2,1)}, u32[]{:S(2)}) copy-start(bf16[768,128]{1,0:T(8,128)(2,1)} %param.7) | copy-start | bytes 589828
  105.2 64.9 %collective-permute-start.11 = (bf16[4,4,272,256]{3,2,1,0:T(8,128)(2,1)S(1)}, bf16[4,4,272,256]{3,2,1,0:T(8,128)(2,1)}, u32[]{:S(2)}, u32[]{:S(2)}) collective-permute-start(bf16[4,4,272,256]{3,2,1,0:T(8,128)(2,1)S(1)} %pad_maximum_fusion.mine), channel_id=1, source_target_pairs={{0,1},{1,0},{2,3},{3,2},{4,5},{5,4},{6,7},{7,6},{8,9},{9,8},{10,11... | collective-permute-start | bytes 6684680 | tf_op jit(solution)/shard_map/ppermute | solution.py:22
  108.7 16.9 %collective-permute-start.16 = (bf16[384,128]{1,0:T(8,128)(2,1)S(1)}, bf16[384,128]{1,0:T(8,128)(2,1)S(1)}, u32[]{:S(2)}, u32[]{:S(2)}) collective-permute-start(bf16[384,128]{1,0:T(8,128)(2,1)S(1)} %get-tuple-element.34), channel_id=1, source_target_pairs={{0,1},{1,65},{64,0},{65,64},{2,3},{3,67},{66,2},{67,66},{4,5},{5,6... | collective-permute-start | bytes 294920 | tf_op jit(solution)/shard_map/ppermute | solution.py:32
  115.5 12.2 %collective-permute-start.15 = (bf16[384,128]{1,0:T(8,128)(2,1)S(1)}, bf16[384,128]{1,0:T(8,128)(2,1)S(1)}, u32[]{:S(2)}, u32[]{:S(2)}) collective-permute-start(bf16[384,128]{1,0:T(8,128)(2,1)S(1)} %get-tuple-element.33), channel_id=1, source_target_pairs={{0,0},{1,64},{64,1},{65,65},{2,2},{3,66},{66,3},{67,67},{4,4},{5,6... | collective-permute-start | bytes 294920 | tf_op jit(solution)/shard_map/ppermute | solution.py:31
  118.1 39.6 %collective-permute-start.12 = (bf16[4,2,128,384]{3,2,1,0:T(8,128)(2,1)S(1)}, bf16[4,2,128,384]{3,2,1,0:T(8,128)(2,1)S(1)}, u32[]{:S(2)}, u32[]{:S(2)}) collective-permute-start(bf16[4,2,128,384]{3,2,1,0:T(8,128)(2,1)S(1)} %pad_maximum_fusion.1.w0), channel_id=1, source_target_pairs={{0,128},{128,0},{256,384},{384,256},{1,129},{129,1},{257,385},{385... | collective-permute-start | bytes 2359304 | tf_op jit(solution)/shard_map/ppermute | solution.py:22
  121.2 39.5 %collective-permute-start.13 = (bf16[4,2,128,384]{3,2,1,0:T(8,128)(2,1)S(1)}, bf16[4,2,128,384]{3,2,1,0:T(8,128)(2,1)S(1)}, u32[]{:S(2)}, u32[]{:S(2)}) collective-permute-start(bf16[4,2,128,384]{3,2,1,0:T(8,128)(2,1)S(1)} %pad_maximum_fusion.1.w0), channel_id=1, source_target_pairs={{0,256},{128,384},{256,0},{384,128},{1,257},{129,385},{257,1},{385... | collective-permute-start | bytes 2359304 | tf_op jit(solution)/shard_map/ppermute | solution.py:22
  125.6 38.9 %collective-permute-start.14 = (bf16[4,2,128,384]{3,2,1,0:T(8,128)(2,1)S(1)}, bf16[4,2,128,384]{3,2,1,0:T(8,128)(2,1)S(1)}, u32[]{:S(2)}, u32[]{:S(2)}) collective-permute-start(bf16[4,2,128,384]{3,2,1,0:T(8,128)(2,1)S(1)} %pad_maximum_fusion.1.w0), channel_id=1, source_target_pairs={{0,384},{128,256},{256,128},{384,0},{1,385},{129,257},{257,129},{3... | collective-permute-start | bytes 2359304 | tf_op jit(solution)/shard_map/ppermute | solution.py:22
  127.7 9.6 %collective-permute-start.19 = (bf16[2,384,128]{2,1,0:T(8,128)(2,1)S(1)}, bf16[2,384,128]{2,1,0:T(8,128)(2,1)S(1)}, u32[]{:S(2)}, u32[]{:S(2)}) collective-permute-start(bf16[2,384,128]{2,1,0:T(8,128)(2,1)S(1)} %get-tuple-element.32), channel_id=1, source_target_pairs={{0,48},{16,32},{32,16},{48,0},{1,49},{17,33},{33,17},{49,1},{2,50}... | collective-permute-start | bytes 589832 | tf_op jit(solution)/shard_map/ppermute | solution.py:22
  137.3 11.2 %collective-permute-start.18 = (bf16[2,384,128]{2,1,0:T(8,128)(2,1)S(1)}, bf16[2,384,128]{2,1,0:T(8,128)(2,1)S(1)}, u32[]{:S(2)}, u32[]{:S(2)}) collective-permute-start(bf16[2,384,128]{2,1,0:T(8,128)(2,1)S(1)} %get-tuple-element.32), channel_id=1, source_target_pairs={{0,32},{16,48},{32,0},{48,16},{1,33},{17,49},{33,1},{49,17},{2,34}... | collective-permute-start | bytes 589832 | tf_op jit(solution)/shard_map/ppermute | solution.py:22
  148.5 8.2 %collective-permute-start.17 = (bf16[2,384,128]{2,1,0:T(8,128)(2,1)S(1)}, bf16[2,384,128]{2,1,0:T(8,128)(2,1)S(1)}, u32[]{:S(2)}, u32[]{:S(2)}) collective-permute-start(bf16[2,384,128]{2,1,0:T(8,128)(2,1)S(1)} %get-tuple-element.32), channel_id=1, source_target_pairs={{0,16},{16,0},{32,48},{48,32},{1,17},{17,1},{33,49},{49,33},{2,18}... | collective-permute-start | bytes 589832 | tf_op jit(solution)/shard_map/ppermute | solution.py:22
  158.6 21.2 %collective-permute-start.20 = (bf16[4,2,384,128]{3,2,1,0:T(8,128)(2,1)}, bf16[4,2,384,128]{3,2,1,0:T(8,128)(2,1)}, u32[]{:S(2)}, u32[]{:S(2)}) collective-permute-start(bf16[4,2,384,128]{3,2,1,0:T(8,128)(2,1)} %pad_maximum_fusion.2.w0), channel_id=1, source_target_pairs={{0,128},{128,0},{256,384},{384,256},{1,129},{129,1},{257,385},{385... | collective-permute-start | bytes 2359304 | tf_op jit(solution)/shard_map/ppermute | solution.py:22
  161.6 32.8 %collective-permute-start.21 = (bf16[4,2,384,128]{3,2,1,0:T(8,128)(2,1)}, bf16[4,2,384,128]{3,2,1,0:T(8,128)(2,1)}, u32[]{:S(2)}, u32[]{:S(2)}) collective-permute-start(bf16[4,2,384,128]{3,2,1,0:T(8,128)(2,1)} %pad_maximum_fusion.2.w0), channel_id=1, source_target_pairs={{0,256},{128,384},{256,0},{384,128},{1,257},{129,385},{257,1},{385... | collective-permute-start | bytes 2359304 | tf_op jit(solution)/shard_map/ppermute | solution.py:22
  165.4 38.7 %collective-permute-start.22 = (bf16[4,2,384,128]{3,2,1,0:T(8,128)(2,1)}, bf16[4,2,384,128]{3,2,1,0:T(8,128)(2,1)}, u32[]{:S(2)}, u32[]{:S(2)}) collective-permute-start(bf16[4,2,384,128]{3,2,1,0:T(8,128)(2,1)} %pad_maximum_fusion.2.w0), channel_id=1, source_target_pairs={{0,384},{128,256},{256,128},{384,0},{1,385},{129,257},{257,129},{3... | collective-permute-start | bytes 2359304 | tf_op jit(solution)/shard_map/ppermute | solution.py:22
  170.1 1.1 copy-start.1
  208.4 7.2 %collective-permute-start.23 = (bf16[4,4,256,256]{3,2,1,0:T(8,128)(2,1)S(1)}, bf16[4,4,256,256]{3,2,1,0:T(8,128)(2,1)S(1)}, u32[]{:S(2)}, u32[]{:S(2)}) collective-permute-start(bf16[4,4,256,256]{3,2,1,0:T(8,128)(2,1)S(1)} %get-tuple-element.20), channel_id=1, source_target_pairs={{0,1},{1,0},{2,3},{3,2},{4,5},{5,4},{6,7},{7,6},{8,9},{9,8},{10,11... | collective-permute-start | bytes 6291464 | tf_op jit(solution)/shard_map/ppermute | solution.py:22
  216.4 27.5 %collective-permute-start.26 = (bf16[4,256,256]{2,1,0:T(8,128)(2,1)S(1)}, bf16[4,256,256]{2,1,0:T(8,128)(2,1)S(1)}, u32[]{:S(2)}, u32[]{:S(2)}) collective-permute-start(bf16[4,256,256]{2,1,0:T(8,128)(2,1)S(1)} %get-tuple-element.26), channel_id=1, source_target_pairs={{0,12},{4,8},{8,4},{12,0},{1,13},{5,9},{9,5},{13,1},{2,14},{6,10},... | collective-permute-start | bytes 1572872 | tf_op jit(solution)/shard_map/ppermute | solution.py:22
  221.0 22.9 %collective-permute-start.25 = (bf16[4,256,256]{2,1,0:T(8,128)(2,1)S(1)}, bf16[4,256,256]{2,1,0:T(8,128)(2,1)S(1)}, u32[]{:S(2)}, u32[]{:S(2)}) collective-permute-start(bf16[4,256,256]{2,1,0:T(8,128)(2,1)S(1)} %get-tuple-element.27), channel_id=1, source_target_pairs={{0,8},{4,12},{8,0},{12,4},{1,9},{5,13},{9,1},{13,5},{2,10},{6,14},... | collective-permute-start | bytes 1572872 | tf_op jit(solution)/shard_map/ppermute | solution.py:22
  223.2 22.9 %collective-permute-start.24 = (bf16[4,256,256]{2,1,0:T(8,128)(2,1)S(1)}, bf16[4,256,256]{2,1,0:T(8,128)(2,1)S(1)}, u32[]{:S(2)}, u32[]{:S(2)}) collective-permute-start(bf16[4,256,256]{2,1,0:T(8,128)(2,1)S(1)} %get-tuple-element.25), channel_id=1, source_target_pairs={{0,4},{4,0},{8,12},{12,8},{1,5},{5,1},{9,13},{13,9},{2,6},{6,2},{1... | collective-permute-start | bytes 1572872 | tf_op jit(solution)/shard_map/ppermute | solution.py:22
  246.4 16.2 %collective-permute-start.29 = (bf16[256,256]{1,0:T(8,128)(2,1)S(1)}, bf16[256,256]{1,0:T(8,128)(2,1)S(1)}, u32[]{:S(2)}, u32[]{:S(2)}) collective-permute-start(bf16[256,256]{1,0:T(8,128)(2,1)S(1)} %get-tuple-element.29), channel_id=1, source_target_pairs={{0,66},{2,64},{64,2},{66,0},{1,67},{3,65},{65,3},{67,1},{4,70},{6,... | collective-permute-start | bytes 393224 | tf_op jit(solution)/shard_map/ppermute | solution.py:22
  248.3 17.9 %collective-permute-start.28 = (bf16[256,256]{1,0:T(8,128)(2,1)S(1)}, bf16[256,256]{1,0:T(8,128)(2,1)S(1)}, u32[]{:S(2)}, u32[]{:S(2)}) collective-permute-start(bf16[256,256]{1,0:T(8,128)(2,1)S(1)} %get-tuple-element.30), channel_id=1, source_target_pairs={{0,64},{2,66},{64,0},{66,2},{1,65},{3,67},{65,1},{67,3},{4,68},{6,... | collective-permute-start | bytes 393224 | tf_op jit(solution)/shard_map/ppermute | solution.py:22
  256.0 20.9 %collective-permute-start.27 = (bf16[256,256]{1,0:T(8,128)(2,1)S(1)}, bf16[256,256]{1,0:T(8,128)(2,1)S(1)}, u32[]{:S(2)}, u32[]{:S(2)}) collective-permute-start(bf16[256,256]{1,0:T(8,128)(2,1)S(1)} %get-tuple-element.28), channel_id=1, source_target_pairs={{0,2},{2,0},{64,66},{66,64},{1,3},{3,1},{65,67},{67,65},{4,6},{6,4... | collective-permute-start | bytes 393224 | tf_op jit(solution)/shard_map/ppermute | solution.py:22
  (5 other events, 5.0 us)

commit v2 on v1

--- a/solution.py
+++ b/solution.py
@@ -1,3 +1,5 @@
+import functools
+
 import jax
 import jax.numpy as jnp
 import numpy as np
@@ -33,16 +35,25 @@
     return straight, crossed
 
 
+def from_neighbours(value, axis):
+    return [send(value, (axis,), k) for k in (1, 3)]
+
+
+def from_far(one, three, axis, split):
+    return send(three[:split], (axis,), 1), send(one[split:], (axis,), 3)
+
+
 def coordinates():
     return {a: lax.axis_index(a) for a in AXES}
 
 
-def hidden_kernel(place, mine, other, w0, w1, w2, w3, act):
+def hidden_kernel(place, mine, other, w0, w1, w2a, w2b, w3, act):
     x, zq, y, zh, c = (place[i] for i in range(5))
     cores = (mine, other)
     rows = act.shape[1]
     width = mine.shape[3]
     count = 2 * mine.shape[0] * 2 * width
+    slots = [[w.at[s] for s in range(2)] for w in (w0, w1)] + [[w2a, w2b]] + [[w3.at[s] for s in range(2)]]
     for a in range(2):
         blocks = [(ref, i, 2 * a + j) for ref in cores for i in range(4) for j in range(2)]
         total = jnp.zeros((rows, width), jnp.float32)
@@ -55,14 +66,15 @@
         spread = jnp.sum(total, axis=1, keepdims=True) * (1.0 / count)
         scale = lax.rsqrt(spread + epsilon)
         acc = jnp.zeros((rows, act.shape[2]), jnp.float32)
-        for k, weights in enumerate((w0, w1, w2, w3)):
+        for k in range(4):
             i = x ^ k ^ y
             for s in range(2):
+                weights = slots[k][s]
                 j = 2 * a + (zh ^ c ^ s)
                 for ck, ref in enumerate(cores):
                     first = 2 * (c ^ ck)
                     block = jnp.concatenate(
-                        [weights[first ^ zq, s], weights[(first + 1) ^ zq, s]], axis=0
+                        [weights[first ^ zq], weights[(first + 1) ^ zq]], axis=0
                     )
                     gain = ref[i, j, rows : rows + GAIN_ROWS, :].astype(jnp.float32)[0:1]
                     values = ref[i, j, :rows, :].astype(jnp.float32)
@@ -71,20 +83,20 @@
         act[a] = gelu_exact(acc).astype(act.dtype)
 
 
-def out_kernel(place, act, w0, w1, w2, w3, mine, other):
+def out_kernel(a, place, act, w0, w1, w2a, w2b, w3, mine, other):
     x, zq, y, zh, c = (place[i] for i in range(5))
+    slots = [[w.at[s] for s in range(2)] for w in (w0, w1)] + [[w2a, w2b]] + [[w3.at[s] for s in range(2)]]
     for ck, ref in ((1, other), (0, mine)):
         first = 2 * (c ^ ck)
-        for k, weights in enumerate((w0, w1, w2, w3)):
-            i = x ^ k ^ y
+        for k in range(4):
             for s in range(2):
+                weights = slots[k][s]
                 block = jnp.concatenate(
-                    [weights[first ^ zq, s], weights[(first + 1) ^ zq, s]], axis=1
+                    [weights[first ^ zq], weights[(first + 1) ^ zq]], axis=1
                 )
-                for a in range(2):
-                    ref[i, 2 * a + (zh ^ c ^ s)] = jnp.dot(
-                        act[a], block, preferred_element_type=jnp.float32
-                    ).astype(ref.dtype)
+                ref[x ^ k ^ y, zh ^ c ^ s] = jnp.dot(
+                    act[a], block, preferred_element_type=jnp.float32
+                ).astype(ref.dtype)
 
 
 def call(kernel, out_shape, flops, *operands):
@@ -112,39 +124,54 @@
         return lax.dynamic_slice_in_dim(array, which * half, half, axis)
 
     swapped = swap_halves(weight_half(zt, 1, w_inner), weight_half(1 - zt, 1, w_inner))
-    inner = jnp.stack(swapped)
-    inner = jnp.stack([inner] + [send(inner, ("zq",), k) for k in (1, 2, 3)])
+    both = jnp.concatenate([tokens, jnp.broadcast_to(norm_gain[None], (GAIN_ROWS, cols))], axis=0)
+    near = [send(both, ("zt", "zh"), k) for k in (2, 3)]
 
-    both = jnp.concatenate([tokens, jnp.broadcast_to(norm_gain[None], (GAIN_ROWS, cols))], axis=0)
-    both = after(both, *swapped)
-    both = jnp.stack([both] + [send(both, ("zt", "zh"), k) for k in (1, 2, 3)])
+    inner = after(jnp.stack(swapped), *near)
+    inner = jnp.stack([inner] + [send(inner, ("zq",), k) for k in (1, 2, 3)], axis=1)
 
-    inner_all = [inner] + [send(inner, ("x",), k) for k in (1, 2, 3)]
+    in1, in3 = from_neighbours(inner, "x")
+    far = send(after(both, inner), ("zt", "zh"), 1)
+    swapped = swap_halves(*(weight_half(h, 0, after(w_outer, inner)) for h in (zt, 1 - zt)))
 
-    outer = jnp.stack(
-        swap_halves(*(weight_half(h, 0, after(w_outer, inner)) for h in (zt, 1 - zt)))
-    )
-    outer = jnp.stack([outer] + [send(outer, ("zq",), k) for k in (1, 2, 3)])
+    in2a, in2b = from_far(after(in1, far, *swapped), after(in3, far, *swapped), "x", 1)
+    both = after(jnp.stack([both, far] + near), in1, in3, *swapped)
+    y1, y3 = from_neighbours(both, "y")
+    outer = after(jnp.stack(swapped), in1, in3, far)
+    second = send(outer, ("zq",), 2)
 
-    both = after(both, inner)
-    both = jnp.stack([both] + [send(both, ("y",), k) for k in (1, 2, 3)])
-    other = send(both, ("c",), 1)
-    outer_all = [outer] + [send(after(outer, inner_all[k]), ("x",), k) for k in (1, 2, 3)]
+    y2a, y2b = from_far(after(y1, in2a, in2b, second), after(y3, in2a, in2b, second), "y", 2)
+    pair = send(after(jnp.stack([outer, second], axis=1), in2a, in2b, y1, y3), ("zq",), 1)
+    outer = jnp.stack([outer, pair[:, 0], second, pair[:, 1]], axis=1)
+
+    both = jnp.stack([both, y1, jnp.concatenate([y2a, y2b], axis=0), y3])
+    out1, out3 = from_neighbours(after(outer, y2a, y2b), "x")
+    other = send(after(both, pair), ("c",), 1)
+
+    out2a, out2b = from_far(after(out1, other), out3, "x", 1)
 
     flops = 2 * 2 * rows * half * 16 * cols
     act = call(
         hidden_kernel,
         jax.ShapeDtypeStruct((2, rows, half), jnp.bfloat16),
-        flops, place, both, other, *inner_all,
+        flops, place, both, other, inner, in1, in2a[0], in2b[0], in3,
     )
-    shape = jax.ShapeDtypeStruct((4, 4, rows, cols), jnp.bfloat16)
-    mine, other = call(out_kernel, (shape, shape), flops, place, act, *outer_all)
-
-    total = mine.astype(jnp.float32) + send(other, ("c",), 1).astype(jnp.float32)
-    sent = total.astype(jnp.bfloat16)
-    total = total[0] + sum(send(sent[k], ("y",), k).astype(jnp.float32) for k in (1, 2, 3))
-    sent = total.astype(jnp.bfloat16)
-    total = total[0] + sum(send(sent[k], ("zt", "zh"), k).astype(jnp.float32) for k in (1, 2, 3))
+    shape = jax.ShapeDtypeStruct((4, 2, rows, cols), jnp.bfloat16)
+    outer_all = (outer, out1, out2a[0], out2b[0], out3)
+    parts = []
+    for a in (1, 0):
+        mine, other = call(
+            functools.partial(out_kernel, a), (shape, shape), flops // 2, place, act, *outer_all
+        )
+        total = mine.astype(jnp.float32) + send(other, ("c",), 1).astype(jnp.float32)
+        sent = total.astype(jnp.bfloat16)
+        total = total[0] + sum(send(sent[k], ("y",), k).astype(jnp.float32) for k in (1, 2, 3))
+        parts.append((total, total.astype(jnp.bfloat16)))
+    (_, away), (total, stay) = parts
+    total = total[0] + sum(
+        send(piece, ("zt", "zh"), k).astype(jnp.float32)
+        for k, piece in ((2, away[0]), (3, away[1]), (1, stay[1]))
+    )
     return total.astype(jnp.bfloat16)
 
 

time: 283 us -> 250 us (0.88); the launches traced: 278 us -> 248 us
  waiting for transfers between devices: 127 us -> 91.3 us
  local copies, waits for them, and re-layouts: 7.96 us -> 12.2 us
  starting transfers between devices: 128 us -> 131 us
    ppermute x26 -> x32, waiting for transfers between devices: 127 us -> 84.8 us  [send(): return lax.ppermute(value, axes, [(i, i ^ k) for i in range(count)])]
    ppermute x2, waiting for transfers between devices: 0.01 us -> 6.5 us  [swap_halves(): lax.ppermute(first, ('zt', 'c'), [(2 * a + b, 2 * b + a) for a, b in both])]
    ppermute x2, starting transfers between devices: 8.68 us -> 11.6 us  [swap_halves(): lax.ppermute(second, ('zt', 'c'), [(2 * a + b, 2 * b + 1 - a) for a, b in...]
    unnamed x14 -> x34, local copies, waits for them, and re-layouts: 6.1 us -> 8.46 us
    ppermute x26 -> x32, starting transfers between devices: 106 us -> 108 us  [send(): return lax.ppermute(value, axes, [(i, i ^ k) for i in range(count)])]
    pallas_call x2 -> x3, Pallas kernels: 10.5 us -> 9.87 us  [call(): pl.pallas_call(kernel, out_shape=out_shape, in_specs=[pl.BlockSpec(memory...]
  transfers between devices with their start and end apart: 30 -> 36, of which waited for: 15 -> 14; matrix products, arithmetic and copies ran while one was open for 1% -> 2% of each run, Pallas kernels for 2% -> 3%
where the time goes in v2:
time: 250 us; the launch traced here: 248 us
  starting transfers between devices  131 us (52%)
  waiting for transfers between devices  91.3 us (37%)
  local copies, waits for them, and re-layouts  12.2 us (5%)
  Pallas kernels  9.87 us (4%)
  other arithmetic  3.19 us (1%)
    ppermute x32, starting transfers between devices, send(): return lax.ppermute(value, axes, [(i, i ^ k) for i in range(count)])  108 us
    ppermute x32, waiting for transfers between devices, send(): return lax.ppermute(value, axes, [(i, i ^ k) for i in range(count)])  84.8 us
    ppermute x2, starting transfers between devices, swap_halves(): lax.ppermute(first, ('zt', 'c'), [(2 * a + b, 2 * b + a) for a, b in both])  11.9 us
    ppermute x2, starting transfers between devices, swap_halves(): lax.ppermute(second, ('zt', 'c'), [(2 * a + b, 2 * b + 1 - a) for a, b in...  11.6 us
    pallas_call x3, Pallas kernels, call(): pl.pallas_call(kernel, out_shape=out_shape, in_specs=[pl.BlockSpec(memory...  9.87 us
    unnamed x34, local copies, waits for them, and re-layouts  8.46 us
    ppermute x2, waiting for transfers between devices, swap_halves(): lax.ppermute(first, ('zt', 'c'), [(2 * a + b, 2 * b + a) for a, b in both])  6.5 us
  transfers between devices with their start and end apart: 36, of which 14 were waited for; matrix products, arithmetic and copies ran while one was open for 2% of the time, Pallas kernels for 3%

profile of v2, /device:TPU:1, one launch (start us, length us, event | category | flops | bytes accessed | tf_op | source)
XLA Modules:
  0.0 248.4 jit_solution(6281786599007587513)
XLA Ops:
  1.0 9.6 %collective-permute-start.1 = (bf16[128,384]{1,0:T(8,128)(2,1)S(1)}, bf16[128,384]{1,0:T(8,128)(2,1)S(1)}, u32[]{:S(2)}, u32[]{:S(2)}) collective-permute-start(bf16[128,384]{1,0:T(8,128)(2,1)S(1)} %get-tuple-element.56), channel_id=1, source_target_pairs={{0,1},{1,65},{64,0},{65,64},{2,3},{3,67},{66,2},{67,66},{4,5},{5,6... | collective-permute-start | bytes 294920 | tf_op jit(solution)/shard_map/ppermute | solution.py:34
  10.7 6.6 %collective-permute-start = (bf16[128,384]{1,0:T(8,128)(2,1)S(1)}, bf16[128,384]{1,0:T(8,128)(2,1)S(1)}, u32[]{:S(2)}, u32[]{:S(2)}) collective-permute-start(bf16[128,384]{1,0:T(8,128)(2,1)S(1)} %get-tuple-element.55), channel_id=1, source_target_pairs={{0,0},{1,64},{64,1},{65,65},{2,2},{3,66},{66,3},{67,67},{4,4},{5,6... | collective-permute-start | bytes 294920 | tf_op jit(solution)/shard_map/ppermute | solution.py:33
  20.8 10.3 %collective-permute-start.2 = (bf16[272,256]{1,0:T(8,128)(2,1)S(1)}, bf16[272,256]{1,0:T(8,128)(2,1)S(1)}, u32[]{:S(2)}, u32[]{:S(2)}) collective-permute-start(bf16[272,256]{1,0:T(8,128)(2,1)S(1)} %get-tuple-element.23), channel_id=1, source_target_pairs={{0,64},{2,66},{64,0},{66,2},{1,65},{3,67},{65,1},{67,3},{4,68},{6,... | collective-permute-start | bytes 417800 | tf_op jit(solution)/shard_map/ppermute | solution.py:24
  31.2 4.3 %collective-permute-done.3 = bf16[272,256]{1,0:T(8,128)(2,1)S(1)} collective-permute-done((bf16[272,256]{1,0:T(8,128)(2,1)S(1)}, bf16[272,256]{1,0:T(8,128)(2,1)S(1)}, u32[]{:S(2)}, u32[]{:S(2)}) %collective-permute-start.3) | collective-permute-done | bytes 139296 | tf_op jit(solution)/shard_map/ppermute | solution.py:24
  35.5 7.7 %collective-permute-done.2 = bf16[272,256]{1,0:T(8,128)(2,1)S(1)} collective-permute-done((bf16[272,256]{1,0:T(8,128)(2,1)S(1)}, bf16[272,256]{1,0:T(8,128)(2,1)S(1)}, u32[]{:S(2)}, u32[]{:S(2)}) %collective-permute-start.2) | collective-permute-done | bytes 139296 | tf_op jit(solution)/shard_map/ppermute | solution.py:24
  47.7 4.7 %collective-permute-start.4 = (bf16[2,128,384]{2,1,0:T(8,128)(2,1)S(1)}, bf16[2,128,384]{2,1,0:T(8,128)(2,1)S(1)}, u32[]{:S(2)}, u32[]{:S(2)}) collective-permute-start(bf16[2,128,384]{2,1,0:T(8,128)(2,1)S(1)} %pad_maximum_fusion.5), channel_id=1, source_target_pairs={{0,16},{16,0},{32,48},{48,32},{1,17},{17,1},{33,49},{49,33},{2,18}... | collective-permute-start | bytes 589832 | tf_op jit(solution)/shard_map/ppermute | solution.py:24
  52.5 10.5 %collective-permute-done.5 = bf16[2,128,384]{2,1,0:T(8,128)(2,1)S(1)} collective-permute-done((bf16[2,128,384]{2,1,0:T(8,128)(2,1)S(1)}, bf16[2,128,384]{2,1,0:T(8,128)(2,1)S(1)}, u32[]{:S(2)}, u32[]{:S(2)}) %collective-permute-start.5) | collective-permute-done | bytes 196640 | tf_op jit(solution)/shard_map/ppermute | solution.py:24
  65.9 3.7 %collective-permute-start.9 = (bf16[2,4,128,384]{3,2,1,0:T(8,128)(2,1)S(1)}, bf16[2,4,128,384]{3,2,1,0:T(8,128)(2,1)S(1)}, u32[]{:S(2)}, u32[]{:S(2)}) collective-permute-start(bf16[2,4,128,384]{3,2,1,0:T(8,128)(2,1)S(1)} %pad_maximum_fusion.1.w0), channel_id=1, source_target_pairs={{0,384},{128,256},{256,128},{384,0},{1,385},{129,257},{257,129},{3... | collective-permute-start | bytes 2359304 | tf_op jit(solution)/shard_map/ppermute | solution.py:24
  69.6 5.6 %collective-permute-start.7 = (bf16[272,256]{1,0:T(8,128)(2,1)S(1)}, bf16[272,256]{1,0:T(8,128)(2,1)S(1)}, u32[]{:S(2)}, u32[]{:S(2)}) collective-permute-start(bf16[272,256]{1,0:T(8,128)(2,1)S(1)} %get-tuple-element.23), channel_id=1, source_target_pairs={{0,2},{2,0},{64,66},{66,64},{1,3},{3,1},{65,67},{67,65},{4,6},{6,4... | collective-permute-start | bytes 417800 | tf_op jit(solution)/shard_map/ppermute | solution.py:24
  75.3 5.3 %collective-permute-start.10 = (bf16[384,128]{1,0:T(8,128)(2,1)S(1)}, bf16[384,128]{1,0:T(8,128)(2,1)S(1)}, u32[]{:S(2)}, u32[]{:S(2)}) collective-permute-start(bf16[384,128]{1,0:T(8,128)(2,1)S(1)} %get-tuple-element.54), channel_id=1, source_target_pairs={{0,0},{1,64},{64,1},{65,65},{2,2},{3,66},{66,3},{67,67},{4,4},{5,6... | collective-permute-start | bytes 294920 | tf_op jit(solution)/shard_map/ppermute | solution.py:33
  82.5 9.4 %collective-permute-done.7 = bf16[272,256]{1,0:T(8,128)(2,1)S(1)} collective-permute-done((bf16[272,256]{1,0:T(8,128)(2,1)S(1)}, bf16[272,256]{1,0:T(8,128)(2,1)S(1)}, u32[]{:S(2)}, u32[]{:S(2)}) %collective-permute-start.7) | collective-permute-done | bytes 139296 | tf_op jit(solution)/shard_map/ppermute | solution.py:24
  91.9 6.5 %collective-permute-done.10 = bf16[384,128]{1,0:T(8,128)(2,1)S(1)} collective-permute-done((bf16[384,128]{1,0:T(8,128)(2,1)S(1)}, bf16[384,128]{1,0:T(8,128)(2,1)S(1)}, u32[]{:S(2)}, u32[]{:S(2)}) %collective-permute-start.10) | collective-permute-done | bytes 98336 | tf_op jit(solution)/shard_map/ppermute | solution.py:33
  98.5 3.2 %collective-permute-start.12 = (bf16[4,272,256]{2,1,0:T(8,128)(2,1)S(1)}, bf16[4,272,256]{2,1,0:T(8,128)(2,1)S(1)}, u32[]{:S(2)}, u32[]{:S(2)}) collective-permute-start(bf16[4,272,256]{2,1,0:T(8,128)(2,1)S(1)} %pad_maximum_fusion.3), channel_id=1, source_target_pairs={{0,4},{4,0},{8,12},{12,8},{1,5},{5,1},{9,13},{13,9},{2,6},{6,2},{1... | collective-permute-start | bytes 1671176 | tf_op jit(solution)/shard_map/ppermute | solution.py:24
  101.7 3.8 %collective-permute-start.13 = (bf16[4,272,256]{2,1,0:T(8,128)(2,1)S(1)}, bf16[4,272,256]{2,1,0:T(8,128)(2,1)S(1)}, u32[]{:S(2)}, u32[]{:S(2)}) collective-permute-start(bf16[4,272,256]{2,1,0:T(8,128)(2,1)S(1)} %pad_maximum_fusion.3), channel_id=1, source_target_pairs={{0,12},{4,8},{8,4},{12,0},{1,13},{5,9},{9,5},{13,1},{2,14},{6,10},... | collective-permute-start | bytes 1671176 | tf_op jit(solution)/shard_map/ppermute | solution.py:24
  112.5 8.6 %collective-permute-done.16 = bf16[2,384,128]{2,1,0:T(8,128)(2,1)S(1)} collective-permute-done((bf16[2,384,128]{2,1,0:T(8,128)(2,1)S(1)}, bf16[2,384,128]{2,1,0:T(8,128)(2,1)S(1)}, u32[]{:S(2)}, u32[]{:S(2)}) %collective-permute-start.16) | collective-permute-done | bytes 196640 | tf_op jit(solution)/shard_map/ppermute | solution.py:24
  132.3 4.1 %collective-permute-done.19 = bf16[2,2,384,128]{3,2,1,0:T(8,128)(2,1)S(1)} collective-permute-done((bf16[2,2,384,128]{3,2,1,0:T(8,128)(2,1)S(1)}, bf16[2,2,384,128]{3,2,1,0:T(8,128)(2,1)S(1)}, u32[]{:S(2)}, u32[]{:S(2)}) %collective-permute-start.19) | collective-permute-done | bytes 393248 | tf_op jit(solution)/shard_map/ppermute | solution.py:24
  136.4 4.9 %collective-permute-start.20 = (bf16[4,4,272,256]{3,2,1,0:T(8,128)(2,1)S(1)}, bf16[4,4,272,256]{3,2,1,0:T(8,128)(2,1)S(1)}, u32[]{:S(2)}, u32[]{:S(2)}) collective-permute-start(bf16[4,4,272,256]{3,2,1,0:T(8,128)(2,1)S(1)} %pad_maximum_fusion.mine), channel_id=1, source_target_pairs={{0,1},{1,0},{2,3},{3,2},{4,5},{5,4},{6,7},{7,6},{8,9},{9,8},{10,11... | collective-permute-start | bytes 6684680 | tf_op jit(solution)/shard_map/ppermute | solution.py:24
  141.4 3.8 %collective-permute-start.22 = (bf16[2,4,384,128]{3,2,1,0:T(8,128)(2,1)S(1)}, bf16[2,4,384,128]{3,2,1,0:T(8,128)(2,1)S(1)}, u32[]{:S(2)}, u32[]{:S(2)}) collective-permute-start(bf16[2,4,384,128]{3,2,1,0:T(8,128)(2,1)S(1)} %pad_maximum_fusion.2.w0), channel_id=1, source_target_pairs={{0,384},{128,256},{256,128},{384,0},{1,385},{129,257},{257,129},{3... | collective-permute-start | bytes 2359304 | tf_op jit(solution)/shard_map/ppermute | solution.py:24
  147.1 16.5 %collective-permute-done.22.w3 = bf16[2,4,384,128]{3,2,1,0:T(8,128)(2,1)S(1)} collective-permute-done((bf16[2,4,384,128]{3,2,1,0:T(8,128)(2,1)S(1)}, bf16[2,4,384,128]{3,2,1,0:T(8,128)(2,1)S(1)}, u32[]{:S(2)}, u32[]{:S(2)}) %collective-permute-start.22) | collective-permute-done | bytes 786464 | tf_op jit(solution)/shard_map/ppermute | solution.py:24
  168.7 3.8 %collective-permute-start.24 = (bf16[1,4,384,128]{3,2,1,0:T(8,128)(2,1)}, bf16[1,4,384,128]{3,2,1,0:T(8,128)(2,1)}, u32[]{:S(2)}, u32[]{:S(2)}) collective-permute-start(bf16[1,4,384,128]{3,2,1,0:T(8,128)(2,1)} %slice.67), channel_id=1, source_target_pairs={{0,384},{128,256},{256,128},{384,0},{1,385},{129,257},{257,129},{3... | collective-permute-start | bytes 1179656 | tf_op jit(solution)/shard_map/ppermute | solution.py:24
  179.6 5.3 %shard_map.46.act = bf16[2,256,384]{2,1,0:T(8,128)(2,1)S(1)} custom-call(s32[5]{0:T(128)S(1)} %stack.100.place, bf16[4,4,272,256]{3,2,1,0:T(8,128)(2,1)S(1)} %pad_maximum_fusion.mine, bf16[4,4,272,256]{3,2,1,0:T(8,128)(2,1)S(1)} %copy-done.7, bf16[2,4,128,384]{3,2,1,0:T(8,128)(2,1)S(1)} %copy-done.5, bf16[2,4,128,384]{3,2,1,0:T(8,128)(2,1)S(1)} %copy-done.9, ...), custom_call_target="tpu_custom_call" | custom-call | flops 1610612736 | bytes 7602196 | tf_op jit(solution)/shard_map/pallas_call | solution.py:105
  187.2 3.0 %collective-permute-start.25 = (bf16[4,2,256,256]{3,2,1,0:T(8,128)(2,1)S(1)}, bf16[4,2,256,256]{3,2,1,0:T(8,128)(2,1)S(1)}, u32[]{:S(2)}, u32[]{:S(2)}) collective-permute-start(bf16[4,2,256,256]{3,2,1,0:T(8,128)(2,1)S(1)} %get-tuple-element.36), channel_id=1, source_target_pairs={{0,1},{1,0},{2,3},{3,2},{4,5},{5,4},{6,7},{7,6},{8,9},{9,8},{10,11... | collective-permute-start | bytes 3145736 | tf_op jit(solution)/shard_map/ppermute | solution.py:24
  194.8 3.8 %collective-permute-start.28 = (bf16[2,256,256]{2,1,0:T(8,128)(2,1)S(1)}, bf16[2,256,256]{2,1,0:T(8,128)(2,1)S(1)}, u32[]{:S(2)}, u32[]{:S(2)}) collective-permute-start(bf16[2,256,256]{2,1,0:T(8,128)(2,1)S(1)} %get-tuple-element.47), channel_id=1, source_target_pairs={{0,12},{4,8},{8,4},{12,0},{1,13},{5,9},{9,5},{13,1},{2,14},{6,10},... | collective-permute-start | bytes 786440 | tf_op jit(solution)/shard_map/ppermute | solution.py:24
  198.6 3.3 %collective-permute-start.27 = (bf16[2,256,256]{2,1,0:T(8,128)(2,1)S(1)}, bf16[2,256,256]{2,1,0:T(8,128)(2,1)S(1)}, u32[]{:S(2)}, u32[]{:S(2)}) collective-permute-start(bf16[2,256,256]{2,1,0:T(8,128)(2,1)S(1)} %get-tuple-element.48), channel_id=1, source_target_pairs={{0,8},{4,12},{8,0},{12,4},{1,9},{5,13},{9,1},{13,5},{2,10},{6,14},... | collective-permute-start | bytes 786440 | tf_op jit(solution)/shard_map/ppermute | solution.py:24
  204.2 3.8 %collective-permute-start.32 = (bf16[2,256,256]{2,1,0:T(8,128)(2,1)S(1)}, bf16[2,256,256]{2,1,0:T(8,128)(2,1)S(1)}, u32[]{:S(2)}, u32[]{:S(2)}) collective-permute-start(bf16[2,256,256]{2,1,0:T(8,128)(2,1)S(1)} %get-tuple-element.44), channel_id=1, source_target_pairs={{0,12},{4,8},{8,4},{12,0},{1,13},{5,9},{9,5},{13,1},{2,14},{6,10},... | collective-permute-start | bytes 786440 | tf_op jit(solution)/shard_map/ppermute | solution.py:24
  208.0 3.2 %collective-permute-start.31 = (bf16[2,256,256]{2,1,0:T(8,128)(2,1)S(1)}, bf16[2,256,256]{2,1,0:T(8,128)(2,1)S(1)}, u32[]{:S(2)}, u32[]{:S(2)}) collective-permute-start(bf16[2,256,256]{2,1,0:T(8,128)(2,1)S(1)} %get-tuple-element.45), channel_id=1, source_target_pairs={{0,8},{4,12},{8,0},{12,4},{1,9},{5,13},{9,1},{13,5},{2,10},{6,14},... | collective-permute-start | bytes 786440 | tf_op jit(solution)/shard_map/ppermute | solution.py:24
  213.4 6.2 %collective-permute-start.35 = (bf16[256,256]{1,0:T(8,128)(2,1)S(1)}, bf16[256,256]{1,0:T(8,128)(2,1)S(1)}, u32[]{:S(2)}, u32[]{:S(2)}) collective-permute-start(bf16[256,256]{1,0:T(8,128)(2,1)S(1)} %fusion.5), channel_id=1, source_target_pairs={{0,2},{2,0},{64,66},{66,64},{1,3},{3,1},{65,67},{67,65},{4,6},{6,4... | collective-permute-start | bytes 393224 | tf_op jit(solution)/shard_map/ppermute | solution.py:24
  221.4 3.1 %collective-permute-done.30 = bf16[2,256,256]{2,1,0:T(8,128)(2,1)S(1)} collective-permute-done((bf16[2,256,256]{2,1,0:T(8,128)(2,1)S(1)}, bf16[2,256,256]{2,1,0:T(8,128)(2,1)S(1)}, u32[]{:S(2)}, u32[]{:S(2)}) %collective-permute-start.30) | collective-permute-done | bytes 262176 | tf_op jit(solution)/shard_map/ppermute | solution.py:24
  224.6 3.6 %collective-permute-start.34 = (bf16[256,256]{1,0:T(8,128)(2,1)S(1)}, bf16[256,256]{1,0:T(8,128)(2,1)S(1)}, u32[]{:S(2)}, u32[]{:S(2)}) collective-permute-start(bf16[256,256]{1,0:T(8,128)(2,1)S(1)} %get-tuple-element.52), channel_id=1, source_target_pairs={{0,66},{2,64},{64,2},{66,0},{1,67},{3,65},{65,3},{67,1},{4,70},{6,... | collective-permute-start | bytes 393224 | tf_op jit(solution)/shard_map/ppermute | solution.py:24
  228.3 4.8 %collective-permute-start.33 = (bf16[256,256]{1,0:T(8,128)(2,1)S(1)}, bf16[256,256]{1,0:T(8,128)(2,1)S(1)}, u32[]{:S(2)}, u32[]{:S(2)}) collective-permute-start(bf16[256,256]{1,0:T(8,128)(2,1)S(1)} %get-tuple-element.51), channel_id=1, source_target_pairs={{0,64},{2,66},{64,0},{66,2},{1,65},{3,67},{65,1},{67,3},{4,68},{6,... | collective-permute-start | bytes 393224 | tf_op jit(solution)/shard_map/ppermute | solution.py:24
  233.1 11.1 %collective-permute-done.34 = bf16[256,256]{1,0:T(8,128)(2,1)S(1)} collective-permute-done((bf16[256,256]{1,0:T(8,128)(2,1)S(1)}, bf16[256,256]{1,0:T(8,128)(2,1)S(1)}, u32[]{:S(2)}, u32[]{:S(2)}) %collective-permute-start.34) | collective-permute-done | bytes 131104 | tf_op jit(solution)/shard_map/ppermute | solution.py:24
  244.2 3.6 %collective-permute-done.33 = bf16[256,256]{1,0:T(8,128)(2,1)S(1)} collective-permute-done((bf16[256,256]{1,0:T(8,128)(2,1)S(1)}, bf16[256,256]{1,0:T(8,128)(2,1)S(1)}, u32[]{:S(2)}, u32[]{:S(2)}) %collective-permute-start.33) | collective-permute-done | bytes 131104 | tf_op jit(solution)/shard_map/ppermute | solution.py:24
  (106 shorter events, 60.0 us)
Async XLA Ops:
  1.0 30.1 %collective-permute-start.1 = (bf16[128,384]{1,0:T(8,128)(2,1)S(1)}, bf16[128,384]{1,0:T(8,128)(2,1)S(1)}, u32[]{:S(2)}, u32[]{:S(2)}) collective-permute-start(bf16[128,384]{1,0:T(8,128)(2,1)S(1)} %get-tuple-element.56), channel_id=1, source_target_pairs={{0,1},{1,65},{64,0},{65,64},{2,3},{3,67},{66,2},{67,66},{4,5},{5,6... | collective-permute-start | bytes 294920 | tf_op jit(solution)/shard_map/ppermute | solution.py:34
  10.7 20.5 %collective-permute-start = (bf16[128,384]{1,0:T(8,128)(2,1)S(1)}, bf16[128,384]{1,0:T(8,128)(2,1)S(1)}, u32[]{:S(2)}, u32[]{:S(2)}) collective-permute-start(bf16[128,384]{1,0:T(8,128)(2,1)S(1)} %get-tuple-element.55), channel_id=1, source_target_pairs={{0,0},{1,64},{64,1},{65,65},{2,2},{3,66},{66,3},{67,67},{4,4},{5,6... | collective-permute-start | bytes 294920 | tf_op jit(solution)/shard_map/ppermute | solution.py:33
  18.8 16.6 %collective-permute-start.3 = (bf16[272,256]{1,0:T(8,128)(2,1)S(1)}, bf16[272,256]{1,0:T(8,128)(2,1)S(1)}, u32[]{:S(2)}, u32[]{:S(2)}) collective-permute-start(bf16[272,256]{1,0:T(8,128)(2,1)S(1)} %get-tuple-element.23), channel_id=1, source_target_pairs={{0,66},{2,64},{64,2},{66,0},{1,67},{3,65},{65,3},{67,1},{4,70},{6,... | collective-permute-start | bytes 417800 | tf_op jit(solution)/shard_map/ppermute | solution.py:24
  20.8 22.4 %collective-permute-start.2 = (bf16[272,256]{1,0:T(8,128)(2,1)S(1)}, bf16[272,256]{1,0:T(8,128)(2,1)S(1)}, u32[]{:S(2)}, u32[]{:S(2)}) collective-permute-start(bf16[272,256]{1,0:T(8,128)(2,1)S(1)} %get-tuple-element.23), channel_id=1, source_target_pairs={{0,64},{2,66},{64,0},{66,2},{1,65},{3,67},{65,1},{67,3},{4,68},{6,... | collective-permute-start | bytes 417800 | tf_op jit(solution)/shard_map/ppermute | solution.py:24
  45.1 17.9 %collective-permute-start.5 = (bf16[2,128,384]{2,1,0:T(8,128)(2,1)S(1)}, bf16[2,128,384]{2,1,0:T(8,128)(2,1)S(1)}, u32[]{:S(2)}, u32[]{:S(2)}) collective-permute-start(bf16[2,128,384]{2,1,0:T(8,128)(2,1)S(1)} %pad_maximum_fusion.5), channel_id=1, source_target_pairs={{0,32},{16,48},{32,0},{48,16},{1,33},{17,49},{33,1},{49,17},{2,34}... | collective-permute-start | bytes 589832 | tf_op jit(solution)/shard_map/ppermute | solution.py:24
  47.7 15.2 %collective-permute-start.4 = (bf16[2,128,384]{2,1,0:T(8,128)(2,1)S(1)}, bf16[2,128,384]{2,1,0:T(8,128)(2,1)S(1)}, u32[]{:S(2)}, u32[]{:S(2)}) collective-permute-start(bf16[2,128,384]{2,1,0:T(8,128)(2,1)S(1)} %pad_maximum_fusion.5), channel_id=1, source_target_pairs={{0,16},{16,0},{32,48},{48,32},{1,17},{17,1},{33,49},{49,33},{2,18}... | collective-permute-start | bytes 589832 | tf_op jit(solution)/shard_map/ppermute | solution.py:24
  63.1 35.3 %collective-permute-start.8 = (bf16[2,4,128,384]{3,2,1,0:T(8,128)(2,1)S(1)}, bf16[2,4,128,384]{3,2,1,0:T(8,128)(2,1)S(1)}, u32[]{:S(2)}, u32[]{:S(2)}) collective-permute-start(bf16[2,4,128,384]{3,2,1,0:T(8,128)(2,1)S(1)} %pad_maximum_fusion.1.w0), channel_id=1, source_target_pairs={{0,128},{128,0},{256,384},{384,256},{1,129},{129,1},{257,385},{385... | collective-permute-start | bytes 2359304 | tf_op jit(solution)/shard_map/ppermute | solution.py:24
  65.9 32.6 %collective-permute-start.9 = (bf16[2,4,128,384]{3,2,1,0:T(8,128)(2,1)S(1)}, bf16[2,4,128,384]{3,2,1,0:T(8,128)(2,1)S(1)}, u32[]{:S(2)}, u32[]{:S(2)}) collective-permute-start(bf16[2,4,128,384]{3,2,1,0:T(8,128)(2,1)S(1)} %pad_maximum_fusion.1.w0), channel_id=1, source_target_pairs={{0,384},{128,256},{256,128},{384,0},{1,385},{129,257},{257,129},{3... | collective-permute-start | bytes 2359304 | tf_op jit(solution)/shard_map/ppermute | solution.py:24
  69.6 22.3 %collective-permute-start.7 = (bf16[272,256]{1,0:T(8,128)(2,1)S(1)}, bf16[272,256]{1,0:T(8,128)(2,1)S(1)}, u32[]{:S(2)}, u32[]{:S(2)}) collective-permute-start(bf16[272,256]{1,0:T(8,128)(2,1)S(1)} %get-tuple-element.23), channel_id=1, source_target_pairs={{0,2},{2,0},{64,66},{66,64},{1,3},{3,1},{65,67},{67,65},{4,6},{6,4... | collective-permute-start | bytes 417800 | tf_op jit(solution)/shard_map/ppermute | solution.py:24
  75.3 23.2 %collective-permute-start.10 = (bf16[384,128]{1,0:T(8,128)(2,1)S(1)}, bf16[384,128]{1,0:T(8,128)(2,1)S(1)}, u32[]{:S(2)}, u32[]{:S(2)}) collective-permute-start(bf16[384,128]{1,0:T(8,128)(2,1)S(1)} %get-tuple-element.54), channel_id=1, source_target_pairs={{0,0},{1,64},{64,1},{65,65},{2,2},{3,66},{66,3},{67,67},{4,4},{5,6... | collective-permute-start | bytes 294920 | tf_op jit(solution)/shard_map/ppermute | solution.py:33
  80.6 17.9 %collective-permute-start.11 = (bf16[384,128]{1,0:T(8,128)(2,1)S(1)}, bf16[384,128]{1,0:T(8,128)(2,1)S(1)}, u32[]{:S(2)}, u32[]{:S(2)}) collective-permute-start(bf16[384,128]{1,0:T(8,128)(2,1)S(1)} %get-tuple-element.53), channel_id=1, source_target_pairs={{0,1},{1,65},{64,0},{65,64},{2,3},{3,67},{66,2},{67,66},{4,5},{5,6... | collective-permute-start | bytes 294920 | tf_op jit(solution)/shard_map/ppermute | solution.py:34
  98.5 22.7 %collective-permute-start.12 = (bf16[4,272,256]{2,1,0:T(8,128)(2,1)S(1)}, bf16[4,272,256]{2,1,0:T(8,128)(2,1)S(1)}, u32[]{:S(2)}, u32[]{:S(2)}) collective-permute-start(bf16[4,272,256]{2,1,0:T(8,128)(2,1)S(1)} %pad_maximum_fusion.3), channel_id=1, source_target_pairs={{0,4},{4,0},{8,12},{12,8},{1,5},{5,1},{9,13},{13,9},{2,6},{6,2},{1... | collective-permute-start | bytes 1671176 | tf_op jit(solution)/shard_map/ppermute | solution.py:24
  101.7 22.2 %collective-permute-start.13 = (bf16[4,272,256]{2,1,0:T(8,128)(2,1)S(1)}, bf16[4,272,256]{2,1,0:T(8,128)(2,1)S(1)}, u32[]{:S(2)}, u32[]{:S(2)}) collective-permute-start(bf16[4,272,256]{2,1,0:T(8,128)(2,1)S(1)} %pad_maximum_fusion.3), channel_id=1, source_target_pairs={{0,12},{4,8},{8,4},{12,0},{1,13},{5,9},{9,5},{13,1},{2,14},{6,10},... | collective-permute-start | bytes 1671176 | tf_op jit(solution)/shard_map/ppermute | solution.py:24
  105.5 15.6 %collective-permute-start.14 = (bf16[1,4,128,384]{3,2,1,0:T(8,128)(2,1)S(1)}, bf16[1,4,128,384]{3,2,1,0:T(8,128)(2,1)S(1)}, u32[]{:S(2)}, u32[]{:S(2)}) collective-permute-start(bf16[1,4,128,384]{3,2,1,0:T(8,128)(2,1)S(1)} %slice.60), channel_id=1, source_target_pairs={{0,128},{128,0},{256,384},{384,256},{1,129},{129,1},{257,385},{385... | collective-permute-start | bytes 1179656 | tf_op jit(solution)/shard_map/ppermute | solution.py:24
  107.8 13.3 %collective-permute-start.15 = (bf16[1,4,128,384]{3,2,1,0:T(8,128)(2,1)S(1)}, bf16[1,4,128,384]{3,2,1,0:T(8,128)(2,1)S(1)}, u32[]{:S(2)}, u32[]{:S(2)}) collective-permute-start(bf16[1,4,128,384]{3,2,1,0:T(8,128)(2,1)S(1)} %slice.61), channel_id=1, source_target_pairs={{0,384},{128,256},{256,128},{384,0},{1,385},{129,257},{257,129},{3... | collective-permute-start | bytes 1179656 | tf_op jit(solution)/shard_map/ppermute | solution.py:24
  110.6 10.5 %collective-permute-start.16 = (bf16[2,384,128]{2,1,0:T(8,128)(2,1)S(1)}, bf16[2,384,128]{2,1,0:T(8,128)(2,1)S(1)}, u32[]{:S(2)}, u32[]{:S(2)}) collective-permute-start(bf16[2,384,128]{2,1,0:T(8,128)(2,1)S(1)} %pad_maximum_fusion.6), channel_id=1, source_target_pairs={{0,32},{16,48},{32,0},{48,16},{1,33},{17,49},{33,1},{49,17},{2,34}... | collective-permute-start | bytes 589832 | tf_op jit(solution)/shard_map/ppermute | solution.py:24
  125.9 10.5 %collective-permute-start.19 = (bf16[2,2,384,128]{3,2,1,0:T(8,128)(2,1)S(1)}, bf16[2,2,384,128]{3,2,1,0:T(8,128)(2,1)S(1)}, u32[]{:S(2)}, u32[]{:S(2)}) collective-permute-start(bf16[2,2,384,128]{3,2,1,0:T(8,128)(2,1)S(1)} %pad_maximum_fusion.4), channel_id=1, source_target_pairs={{0,16},{16,0},{32,48},{48,32},{1,17},{17,1},{33,49},{49,33},{2,18}... | collective-permute-start | bytes 1179656 | tf_op jit(solution)/shard_map/ppermute | solution.py:24
  136.4 30.1 %collective-permute-start.20 = (bf16[4,4,272,256]{3,2,1,0:T(8,128)(2,1)S(1)}, bf16[4,4,272,256]{3,2,1,0:T(8,128)(2,1)S(1)}, u32[]{:S(2)}, u32[]{:S(2)}) collective-permute-start(bf16[4,4,272,256]{3,2,1,0:T(8,128)(2,1)S(1)} %pad_maximum_fusion.mine), channel_id=1, source_target_pairs={{0,1},{1,0},{2,3},{3,2},{4,5},{5,4},{6,7},{7,6},{8,9},{9,8},{10,11... | collective-permute-start | bytes 6684680 | tf_op jit(solution)/shard_map/ppermute | solution.py:24
  141.4 22.3 %collective-permute-start.22 = (bf16[2,4,384,128]{3,2,1,0:T(8,128)(2,1)S(1)}, bf16[2,4,384,128]{3,2,1,0:T(8,128)(2,1)S(1)}, u32[]{:S(2)}, u32[]{:S(2)}) collective-permute-start(bf16[2,4,384,128]{3,2,1,0:T(8,128)(2,1)S(1)} %pad_maximum_fusion.2.w0), channel_id=1, source_target_pairs={{0,384},{128,256},{256,128},{384,0},{1,385},{129,257},{257,129},{3... | collective-permute-start | bytes 2359304 | tf_op jit(solution)/shard_map/ppermute | solution.py:24
  145.2 21.2 %collective-permute-start.21 = (bf16[2,4,384,128]{3,2,1,0:T(8,128)(2,1)S(1)}, bf16[2,4,384,128]{3,2,1,0:T(8,128)(2,1)S(1)}, u32[]{:S(2)}, u32[]{:S(2)}) collective-permute-start(bf16[2,4,384,128]{3,2,1,0:T(8,128)(2,1)S(1)} %pad_maximum_fusion.2.w0), channel_id=1, source_target_pairs={{0,128},{128,0},{256,384},{384,256},{1,129},{129,1},{257,385},{385... | collective-permute-start | bytes 2359304 | tf_op jit(solution)/shard_map/ppermute | solution.py:24
  164.5 20.4 %collective-permute-start.23 = (bf16[1,4,384,128]{3,2,1,0:T(8,128)(2,1)}, bf16[1,4,384,128]{3,2,1,0:T(8,128)(2,1)S(1)}, u32[]{:S(2)}, u32[]{:S(2)}) collective-permute-start(bf16[1,4,384,128]{3,2,1,0:T(8,128)(2,1)} %slice.82), channel_id=1, source_target_pairs={{0,128},{128,0},{256,384},{384,256},{1,129},{129,1},{257,385},{385... | collective-permute-start | bytes 1179656 | tf_op jit(solution)/shard_map/ppermute | solution.py:24
  168.7 16.2 %collective-permute-start.24 = (bf16[1,4,384,128]{3,2,1,0:T(8,128)(2,1)}, bf16[1,4,384,128]{3,2,1,0:T(8,128)(2,1)}, u32[]{:S(2)}, u32[]{:S(2)}) collective-permute-start(bf16[1,4,384,128]{3,2,1,0:T(8,128)(2,1)} %slice.67), channel_id=1, source_target_pairs={{0,384},{128,256},{256,128},{384,0},{1,385},{129,257},{257,129},{3... | collective-permute-start | bytes 1179656 | tf_op jit(solution)/shard_map/ppermute | solution.py:24
  192.5 11.3 %collective-permute-start.29 = (bf16[4,2,256,256]{3,2,1,0:T(8,128)(2,1)S(1)}, bf16[4,2,256,256]{3,2,1,0:T(8,128)(2,1)S(1)}, u32[]{:S(2)}, u32[]{:S(2)}) collective-permute-start(bf16[4,2,256,256]{3,2,1,0:T(8,128)(2,1)S(1)} %get-tuple-element.38), channel_id=1, source_target_pairs={{0,1},{1,0},{2,3},{3,2},{4,5},{5,4},{6,7},{7,6},{8,9},{9,8},{10,11... | collective-permute-start | bytes 3145736 | tf_op jit(solution)/shard_map/ppermute | solution.py:24
  194.8 16.4 %collective-permute-start.28 = (bf16[2,256,256]{2,1,0:T(8,128)(2,1)S(1)}, bf16[2,256,256]{2,1,0:T(8,128)(2,1)S(1)}, u32[]{:S(2)}, u32[]{:S(2)}) collective-permute-start(bf16[2,256,256]{2,1,0:T(8,128)(2,1)S(1)} %get-tuple-element.47), channel_id=1, source_target_pairs={{0,12},{4,8},{8,4},{12,0},{1,13},{5,9},{9,5},{13,1},{2,14},{6,10},... | collective-permute-start | bytes 786440 | tf_op jit(solution)/shard_map/ppermute | solution.py:24
  198.6 14.6 %collective-permute-start.27 = (bf16[2,256,256]{2,1,0:T(8,128)(2,1)S(1)}, bf16[2,256,256]{2,1,0:T(8,128)(2,1)S(1)}, u32[]{:S(2)}, u32[]{:S(2)}) collective-permute-start(bf16[2,256,256]{2,1,0:T(8,128)(2,1)S(1)} %get-tuple-element.48), channel_id=1, source_target_pairs={{0,8},{4,12},{8,0},{12,4},{1,9},{5,13},{9,1},{13,5},{2,10},{6,14},... | collective-permute-start | bytes 786440 | tf_op jit(solution)/shard_map/ppermute | solution.py:24
  201.9 11.3 %collective-permute-start.26 = (bf16[2,256,256]{2,1,0:T(8,128)(2,1)S(1)}, bf16[2,256,256]{2,1,0:T(8,128)(2,1)S(1)}, u32[]{:S(2)}, u32[]{:S(2)}) collective-permute-start(bf16[2,256,256]{2,1,0:T(8,128)(2,1)S(1)} %get-tuple-element.46), channel_id=1, source_target_pairs={{0,4},{4,0},{8,12},{12,8},{1,5},{5,1},{9,13},{13,9},{2,6},{6,2},{1... | collective-permute-start | bytes 786440 | tf_op jit(solution)/shard_map/ppermute | solution.py:24
  204.2 17.2 %collective-permute-start.32 = (bf16[2,256,256]{2,1,0:T(8,128)(2,1)S(1)}, bf16[2,256,256]{2,1,0:T(8,128)(2,1)S(1)}, u32[]{:S(2)}, u32[]{:S(2)}) collective-permute-start(bf16[2,256,256]{2,1,0:T(8,128)(2,1)S(1)} %get-tuple-element.44), channel_id=1, source_target_pairs={{0,12},{4,8},{8,4},{12,0},{1,13},{5,9},{9,5},{13,1},{2,14},{6,10},... | collective-permute-start | bytes 786440 | tf_op jit(solution)/shard_map/ppermute | solution.py:24
  208.0 13.4 %collective-permute-start.31 = (bf16[2,256,256]{2,1,0:T(8,128)(2,1)S(1)}, bf16[2,256,256]{2,1,0:T(8,128)(2,1)S(1)}, u32[]{:S(2)}, u32[]{:S(2)}) collective-permute-start(bf16[2,256,256]{2,1,0:T(8,128)(2,1)S(1)} %get-tuple-element.45), channel_id=1, source_target_pairs={{0,8},{4,12},{8,0},{12,4},{1,9},{5,13},{9,1},{13,5},{2,10},{6,14},... | collective-permute-start | bytes 786440 | tf_op jit(solution)/shard_map/ppermute | solution.py:24
  211.3 13.2 %collective-permute-start.30 = (bf16[2,256,256]{2,1,0:T(8,128)(2,1)S(1)}, bf16[2,256,256]{2,1,0:T(8,128)(2,1)S(1)}, u32[]{:S(2)}, u32[]{:S(2)}) collective-permute-start(bf16[2,256,256]{2,1,0:T(8,128)(2,1)S(1)} %get-tuple-element.43), channel_id=1, source_target_pairs={{0,4},{4,0},{8,12},{12,8},{1,5},{5,1},{9,13},{13,9},{2,6},{6,2},{1... | collective-permute-start | bytes 786440 | tf_op jit(solution)/shard_map/ppermute | solution.py:24
  213.4 19.7 %collective-permute-start.35 = (bf16[256,256]{1,0:T(8,128)(2,1)S(1)}, bf16[256,256]{1,0:T(8,128)(2,1)S(1)}, u32[]{:S(2)}, u32[]{:S(2)}) collective-permute-start(bf16[256,256]{1,0:T(8,128)(2,1)S(1)} %fusion.5), channel_id=1, source_target_pairs={{0,2},{2,0},{64,66},{66,64},{1,3},{3,1},{65,67},{67,65},{4,6},{6,4... | collective-permute-start | bytes 393224 | tf_op jit(solution)/shard_map/ppermute | solution.py:24
  224.6 19.5 %collective-permute-start.34 = (bf16[256,256]{1,0:T(8,128)(2,1)S(1)}, bf16[256,256]{1,0:T(8,128)(2,1)S(1)}, u32[]{:S(2)}, u32[]{:S(2)}) collective-permute-start(bf16[256,256]{1,0:T(8,128)(2,1)S(1)} %get-tuple-element.52), channel_id=1, source_target_pairs={{0,66},{2,64},{64,2},{66,0},{1,67},{3,65},{65,3},{67,1},{4,70},{6,... | collective-permute-start | bytes 393224 | tf_op jit(solution)/shard_map/ppermute | solution.py:24
  228.3 19.4 %collective-permute-start.33 = (bf16[256,256]{1,0:T(8,128)(2,1)S(1)}, bf16[256,256]{1,0:T(8,128)(2,1)S(1)}, u32[]{:S(2)}, u32[]{:S(2)}) collective-permute-start(bf16[256,256]{1,0:T(8,128)(2,1)S(1)} %get-tuple-element.51), channel_id=1, source_target_pairs={{0,64},{2,66},{64,0},{66,2},{1,65},{3,67},{65,1},{67,3},{4,68},{6,... | collective-permute-start | bytes 393224 | tf_op jit(solution)/shard_map/ppermute | solution.py:24
  (21 other events, 270.8 us)

commit v3 on v2

--- a/solution.py
+++ b/solution.py
@@ -48,36 +48,35 @@
 
 
 def hidden_kernel(place, mine, other, w0, w1, w2a, w2b, w3, act):
-    x, zq, y, zh, c = (place[i] for i in range(5))
+    x, zq, zt, c = (place[i] for i in (0, 1, 5, 4))
     cores = (mine, other)
     rows = act.shape[1]
-    width = mine.shape[3]
-    count = 2 * mine.shape[0] * 2 * width
+    width = mine.shape[2]
+    count = mine.shape[0] * width
     slots = [[w.at[s] for s in range(2)] for w in (w0, w1)] + [[w2a, w2b]] + [[w3.at[s] for s in range(2)]]
     for a in range(2):
-        blocks = [(ref, i, 2 * a + j) for ref in cores for i in range(4) for j in range(2)]
+        blocks = [(ref, 8 * (zt ^ a) + i) for ref in cores for i in range(8)]
         total = jnp.zeros((rows, width), jnp.float32)
-        for ref, i, j in blocks:
-            total += ref[i, j, :rows, :].astype(jnp.float32)
+        for ref, i in blocks:
+            total += ref[i, :rows, :].astype(jnp.float32)
         center = jnp.sum(total, axis=1, keepdims=True) * (1.0 / count)
         total = jnp.zeros((rows, width), jnp.float32)
-        for ref, i, j in blocks:
-            total += jnp.square(ref[i, j, :rows, :].astype(jnp.float32) - center)
+        for ref, i in blocks:
+            total += jnp.square(ref[i, :rows, :].astype(jnp.float32) - center)
         spread = jnp.sum(total, axis=1, keepdims=True) * (1.0 / count)
         scale = lax.rsqrt(spread + epsilon)
         acc = jnp.zeros((rows, act.shape[2]), jnp.float32)
         for k in range(4):
-            i = x ^ k ^ y
             for s in range(2):
                 weights = slots[k][s]
-                j = 2 * a + (zh ^ c ^ s)
+                i = 8 * (zt ^ a) + 2 * (x ^ k) + (c ^ s)
                 for ck, ref in enumerate(cores):
                     first = 2 * (c ^ ck)
                     block = jnp.concatenate(
                         [weights[first ^ zq], weights[(first + 1) ^ zq]], axis=0
                     )
-                    gain = ref[i, j, rows : rows + GAIN_ROWS, :].astype(jnp.float32)[0:1]
-                    values = ref[i, j, :rows, :].astype(jnp.float32)
+                    gain = ref[i, rows : rows + GAIN_ROWS, :].astype(jnp.float32)[0:1]
+                    values = ref[i, :rows, :].astype(jnp.float32)
                     normed = ((values - center) * scale * gain).astype(jnp.bfloat16)
                     acc += jnp.dot(normed, block, preferred_element_type=jnp.float32)
         act[a] = gelu_exact(acc).astype(act.dtype)
@@ -118,37 +117,31 @@
     rows, cols = tokens.shape
     d_dev, f_dev = w_inner.shape
     half = f_dev // 2
-    place = jnp.stack([at[a] for a in ("x", "zq", "y", "zh", "c")]).astype(jnp.int32)
+    place = jnp.stack([at[a] for a in ("x", "zq", "y", "zh", "c", "zt")]).astype(jnp.int32)
 
     def weight_half(which, axis, array):
         return lax.dynamic_slice_in_dim(array, which * half, half, axis)
 
-    swapped = swap_halves(weight_half(zt, 1, w_inner), weight_half(1 - zt, 1, w_inner))
     both = jnp.concatenate([tokens, jnp.broadcast_to(norm_gain[None], (GAIN_ROWS, cols))], axis=0)
-    near = [send(both, ("zt", "zh"), k) for k in (2, 3)]
+    both = lax.all_gather(both, ("zt", "y", "zh"))
 
-    inner = after(jnp.stack(swapped), *near)
-    inner = jnp.stack([inner] + [send(inner, ("zq",), k) for k in (1, 2, 3)], axis=1)
+    in_swapped = swap_halves(weight_half(zt, 1, w_inner), weight_half(1 - zt, 1, w_inner))
+    out_swapped = swap_halves(weight_half(zt, 0, w_outer), weight_half(1 - zt, 0, w_outer))
+
+    inner = jnp.stack(in_swapped)
+    others = [send(inner, ("zq",), k) for k in (2, 3)]
+    others = [send(after(inner, *out_swapped), ("zq",), 1)] + others
+    inner = jnp.stack([inner] + others, axis=1)
 
     in1, in3 = from_neighbours(inner, "x")
-    far = send(after(both, inner), ("zt", "zh"), 1)
-    swapped = swap_halves(*(weight_half(h, 0, after(w_outer, inner)) for h in (zt, 1 - zt)))
+    outer = after(jnp.stack(out_swapped), inner)
+    outer = jnp.stack([outer] + [send(outer, ("zq",), k) for k in (1, 2, 3)], axis=1)
 
-    in2a, in2b = from_far(after(in1, far, *swapped), after(in3, far, *swapped), "x", 1)
-    both = after(jnp.stack([both, far] + near), in1, in3, *swapped)
-    y1, y3 = from_neighbours(both, "y")
-    outer = after(jnp.stack(swapped), in1, in3, far)
-    second = send(outer, ("zq",), 2)
+    in2a, in2b = from_far(after(in1, outer), after(in3, outer), "x", 1)
+    out1, out3 = from_neighbours(after(outer, in1, in3), "x")
+    other = send(after(both, out1, out3), ("c",), 1)
 
-    y2a, y2b = from_far(after(y1, in2a, in2b, second), after(y3, in2a, in2b, second), "y", 2)
-    pair = send(after(jnp.stack([outer, second], axis=1), in2a, in2b, y1, y3), ("zq",), 1)
-    outer = jnp.stack([outer, pair[:, 0], second, pair[:, 1]], axis=1)
-
-    both = jnp.stack([both, y1, jnp.concatenate([y2a, y2b], axis=0), y3])
-    out1, out3 = from_neighbours(after(outer, y2a, y2b), "x")
-    other = send(after(both, pair), ("c",), 1)
-
-    out2a, out2b = from_far(after(out1, other), out3, "x", 1)
+    out2a, out2b = from_far(after(out1, in2a, in2b), out3, "x", 1)
 
     flops = 2 * 2 * rows * half * 16 * cols
     act = call(
@@ -167,6 +160,7 @@
         sent = total.astype(jnp.bfloat16)
         total = total[0] + sum(send(sent[k], ("y",), k).astype(jnp.float32) for k in (1, 2, 3))
         parts.append((total, total.astype(jnp.bfloat16)))
+        act = after(act, other)
     (_, away), (total, stay) = parts
     total = total[0] + sum(
         send(piece, ("zt", "zh"), k).astype(jnp.float32)

time: 250 us -> 391 us (1.56)
  waiting for transfers between devices: 91.3 us -> 180 us
  starting transfers between devices: 131 us -> 165 us
  between operations: 0.74 us -> 13.9 us
    all_gather x0 -> x1, waiting for transfers between devices: none -> 68.7 us  [per_device(): both = lax.all_gather(both, ('zt', 'y', 'zh'))]
    ppermute x32 -> x26, starting transfers between devices: 108 us -> 144 us  [send(): return lax.ppermute(value, axes, [(i, i ^ k) for i in range(count)])]
    ppermute x32 -> x26, waiting for transfers between devices: 84.8 us -> 102 us  [send(): return lax.ppermute(value, axes, [(i, i ^ k) for i in range(count)])]
    unnamed x34 -> x18, local copies, waits for them, and re-layouts: 8.46 us -> 7.48 us
  transfers between devices with their start and end apart: 36 -> 31, of which waited for: 14 -> 12; matrix products, arithmetic and copies ran while one was open for 2% -> 2% of each run, Pallas kernels for 3% -> 2%
where the time goes in v3:
time: 391 us; the launch traced here: 387 us
  waiting for transfers between devices  180 us (46%)
  starting transfers between devices  165 us (42%)
  local copies, waits for them, and re-layouts  13.9 us (4%)
  between operations  13.9 us (4%)
  Pallas kernels  10.7 us (3%)
    ppermute x26, starting transfers between devices, send(): return lax.ppermute(value, axes, [(i, i ^ k) for i in range(count)])  144 us
    ppermute x26, waiting for transfers between devices, send(): return lax.ppermute(value, axes, [(i, i ^ k) for i in range(count)])  102 us
    all_gather x1, waiting for transfers between devices, per_device(): both = lax.all_gather(both, ('zt', 'y', 'zh'))  68.7 us
    ppermute x2, starting transfers between devices, swap_halves(): lax.ppermute(second, ('zt', 'c'), [(2 * a + b, 2 * b + 1 - a) for a, b in...  11.6 us
    pallas_call x3, Pallas kernels, call(): pl.pallas_call(kernel, out_shape=out_shape, in_specs=[pl.BlockSpec(memory...  10.7 us
    ppermute x2, starting transfers between devices, swap_halves(): lax.ppermute(first, ('zt', 'c'), [(2 * a + b, 2 * b + a) for a, b in both])  9.47 us
    ppermute x2, waiting for transfers between devices, swap_halves(): lax.ppermute(first, ('zt', 'c'), [(2 * a + b, 2 * b + a) for a, b in both])  8.56 us
  transfers between devices with their start and end apart: 31, of which 12 were waited for; matrix products, arithmetic and copies ran while one was open for 2% of the time, Pallas kernels for 2%

profile of v3, /device:TPU:1, one launch (start us, length us, event | category | flops | bytes accessed | tf_op | source)
XLA Modules:
  0.0 386.7 jit_solution(4129334486181211950)
XLA Ops:
  9.8 9.6 %collective-permute-start.3 = (bf16[128,384]{1,0:T(8,128)(2,1)S(1)}, bf16[128,384]{1,0:T(8,128)(2,1)S(1)}, u32[]{:S(2)}, u32[]{:S(2)}) collective-permute-start(bf16[128,384]{1,0:T(8,128)(2,1)S(1)} %get-tuple-element.44), channel_id=1, source_target_pairs={{0,1},{1,65},{64,0},{65,64},{2,3},{3,67},{66,2},{67,66},{4,5},{5,6... | collective-permute-start | bytes 294920 | tf_op jit(solution)/shard_map/ppermute | solution.py:34
  19.4 6.6 %collective-permute-start.2 = (bf16[128,384]{1,0:T(8,128)(2,1)S(1)}, bf16[128,384]{1,0:T(8,128)(2,1)S(1)}, u32[]{:S(2)}, u32[]{:S(2)}) collective-permute-start(bf16[128,384]{1,0:T(8,128)(2,1)S(1)} %get-tuple-element.43), channel_id=1, source_target_pairs={{0,0},{1,64},{64,1},{65,65},{2,2},{3,66},{66,3},{67,67},{4,4},{5,6... | collective-permute-start | bytes 294920 | tf_op jit(solution)/shard_map/ppermute | solution.py:33
  28.9 2.9 collective-permute-start
  31.9 6.7 %collective-permute-start.6 = (bf16[2,128,384]{2,1,0:T(8,128)(2,1)S(1)}, bf16[2,128,384]{2,1,0:T(8,128)(2,1)S(1)}, u32[]{:S(2)}, u32[]{:S(2)}) collective-permute-start(bf16[2,128,384]{2,1,0:T(8,128)(2,1)S(1)} %get-tuple-element.17), channel_id=1, source_target_pairs={{0,48},{16,32},{32,16},{48,0},{1,49},{17,33},{33,17},{49,1},{2,50}... | collective-permute-start | bytes 589832 | tf_op jit(solution)/shard_map/ppermute | solution.py:24
  40.6 8.6 %collective-permute-done = bf16[384,128]{1,0:T(8,128)(2,1)S(1)} collective-permute-done((bf16[384,128]{1,0:T(8,128)(2,1)S(1)}, bf16[384,128]{1,0:T(8,128)(2,1)S(1)}, u32[]{:S(2)}, u32[]{:S(2)}) %collective-permute-start) | collective-permute-done | bytes 98336 | tf_op jit(solution)/shard_map/ppermute | solution.py:33
  49.1 8.1 %collective-permute-start.4 = (bf16[2,128,384]{2,1,0:T(8,128)(2,1)S(1)}, bf16[2,128,384]{2,1,0:T(8,128)(2,1)S(1)}, u32[]{:S(2)}, u32[]{:S(2)}) collective-permute-start(bf16[2,128,384]{2,1,0:T(8,128)(2,1)S(1)} %get-tuple-element.17), channel_id=1, source_target_pairs={{0,16},{16,0},{32,48},{48,32},{1,17},{17,1},{33,49},{49,33},{2,18}... | collective-permute-start | bytes 589832 | tf_op jit(solution)/shard_map/ppermute | solution.py:24
  58.8 33.1 %collective-permute-done.5 = bf16[2,128,384]{2,1,0:T(8,128)(2,1)S(1)} collective-permute-done((bf16[2,128,384]{2,1,0:T(8,128)(2,1)S(1)}, bf16[2,128,384]{2,1,0:T(8,128)(2,1)S(1)}, u32[]{:S(2)}, u32[]{:S(2)}) %collective-permute-start.5) | collective-permute-done | bytes 196640 | tf_op jit(solution)/shard_map/ppermute | solution.py:24
  93.9 3.5 collective-permute-start.11
  101.3 5.4 %collective-permute-start.7 = (bf16[2,384,128]{2,1,0:T(8,128)(2,1)S(1)}, bf16[2,384,128]{2,1,0:T(8,128)(2,1)S(1)}, u32[]{:S(2)}, u32[]{:S(2)}) collective-permute-start(bf16[2,384,128]{2,1,0:T(8,128)(2,1)S(1)} %pad_maximum_fusion.2), channel_id=1, source_target_pairs={{0,16},{16,0},{32,48},{48,32},{1,17},{17,1},{33,49},{49,33},{2,18}... | collective-permute-start | bytes 589832 | tf_op jit(solution)/shard_map/ppermute | solution.py:24
  106.7 8.2 %collective-permute-done.9 = bf16[2,384,128]{2,1,0:T(8,128)(2,1)S(1)} collective-permute-done((bf16[2,384,128]{2,1,0:T(8,128)(2,1)S(1)}, bf16[2,384,128]{2,1,0:T(8,128)(2,1)S(1)}, u32[]{:S(2)}, u32[]{:S(2)}) %collective-permute-start.9) | collective-permute-done | bytes 196640 | tf_op jit(solution)/shard_map/ppermute | solution.py:24
  114.9 26.8 %collective-permute-done.8 = bf16[2,384,128]{2,1,0:T(8,128)(2,1)S(1)} collective-permute-done((bf16[2,384,128]{2,1,0:T(8,128)(2,1)S(1)}, bf16[2,384,128]{2,1,0:T(8,128)(2,1)S(1)}, u32[]{:S(2)}, u32[]{:S(2)}) %collective-permute-start.8) | collective-permute-done | bytes 196640 | tf_op jit(solution)/shard_map/ppermute | solution.py:24
  141.9 3.1 collective-permute-start.12
  145.0 4.6 %collective-permute-start.13 = (bf16[2,4,384,128]{3,2,1,0:T(8,128)(2,1)S(1)}, bf16[2,4,384,128]{3,2,1,0:T(8,128)(2,1)S(1)}, u32[]{:S(2)}, u32[]{:S(2)}) collective-permute-start(bf16[2,4,384,128]{3,2,1,0:T(8,128)(2,1)S(1)} %pad_maximum_fusion.1.w0), channel_id=1, source_target_pairs={{0,384},{128,256},{256,128},{384,0},{1,385},{129,257},{257,129},{3... | collective-permute-start | bytes 2359304 | tf_op jit(solution)/shard_map/ppermute | solution.py:24
  149.6 13.8 %collective-permute-done.12.w1 = bf16[2,4,384,128]{3,2,1,0:T(8,128)(2,1)S(1)} collective-permute-done((bf16[2,4,384,128]{3,2,1,0:T(8,128)(2,1)S(1)}, bf16[2,4,384,128]{3,2,1,0:T(8,128)(2,1)S(1)}, u32[]{:S(2)}, u32[]{:S(2)}) %collective-permute-start.12) | collective-permute-done | bytes 786464 | tf_op jit(solution)/shard_map/ppermute | solution.py:24
  163.4 4.2 %collective-permute-done.13.w3 = bf16[2,4,384,128]{3,2,1,0:T(8,128)(2,1)S(1)} collective-permute-done((bf16[2,4,384,128]{3,2,1,0:T(8,128)(2,1)S(1)}, bf16[2,4,384,128]{3,2,1,0:T(8,128)(2,1)S(1)}, u32[]{:S(2)}, u32[]{:S(2)}) %collective-permute-start.13) | collective-permute-done | bytes 786464 | tf_op jit(solution)/shard_map/ppermute | solution.py:24
  167.6 68.7 %all-gather.3.cloned.1.call-done = bf16[4352,256]{1,0:T(8,128)(2,1)} async-done(((bf16[272,256]{1,0:T(8,128)(2,1)}), bf16[4352,256]{1,0:T(8,128)(2,1)}) %all-gather.3.cloned.1.call-update) | async-done | bytes 2228240 | tf_op jit(solution)/shard_map/all_gather | solution.py:126
  236.3 3.3 collective-permute-start.14
  240.6 4.1 %collective-permute-start.15 = (bf16[1,4,128,384]{3,2,1,0:T(8,128)(2,1)S(1)}, bf16[1,4,128,384]{3,2,1,0:T(8,128)(2,1)S(1)}, u32[]{:S(2)}, u32[]{:S(2)}) collective-permute-start(bf16[1,4,128,384]{3,2,1,0:T(8,128)(2,1)S(1)} %slice.48), channel_id=1, source_target_pairs={{0,128},{128,0},{256,384},{384,256},{1,129},{129,1},{257,385},{385... | collective-permute-start | bytes 1179656 | tf_op jit(solution)/shard_map/ppermute | solution.py:24
  245.8 6.2 %collective-permute-start.16 = (bf16[1,4,128,384]{3,2,1,0:T(8,128)(2,1)S(1)}, bf16[1,4,128,384]{3,2,1,0:T(8,128)(2,1)S(1)}, u32[]{:S(2)}, u32[]{:S(2)}) collective-permute-start(bf16[1,4,128,384]{3,2,1,0:T(8,128)(2,1)S(1)} %slice.49), channel_id=1, source_target_pairs={{0,384},{128,256},{256,128},{384,0},{1,385},{129,257},{257,129},{3... | collective-permute-start | bytes 1179656 | tf_op jit(solution)/shard_map/ppermute | solution.py:24
  255.5 5.7 %collective-permute-done.16 = bf16[1,4,128,384]{3,2,1,0:T(8,128)(2,1)S(1)} collective-permute-done((bf16[1,4,128,384]{3,2,1,0:T(8,128)(2,1)S(1)}, bf16[1,4,128,384]{3,2,1,0:T(8,128)(2,1)S(1)}, u32[]{:S(2)}, u32[]{:S(2)}) %collective-permute-start.16) | collective-permute-done | bytes 393248 | tf_op jit(solution)/shard_map/ppermute | solution.py:24
  262.8 4.2 %collective-permute-start.18 = (bf16[1,4,384,128]{3,2,1,0:T(8,128)(2,1)}, bf16[1,4,384,128]{3,2,1,0:T(8,128)(2,1)}, u32[]{:S(2)}, u32[]{:S(2)}) collective-permute-start(bf16[1,4,384,128]{3,2,1,0:T(8,128)(2,1)} %slice.51), channel_id=1, source_target_pairs={{0,384},{128,256},{256,128},{384,0},{1,385},{129,257},{257,129},{3... | collective-permute-start | bytes 1179656 | tf_op jit(solution)/shard_map/ppermute | solution.py:24
  273.0 6.1 %shard_map.46.act = bf16[2,256,384]{2,1,0:T(8,128)(2,1)S(1)} custom-call(s32[6]{0:T(128)S(1)} %stack.75.place, bf16[16,272,256]{2,1,0:T(8,128)(2,1)S(1)} %bitcast.71, bf16[16,272,256]{2,1,0:T(8,128)(2,1)} %collective-permute-done.14.other, bf16[2,4,128,384]{3,2,1,0:T(8,128)(2,1)S(1)} %pad_maximum_fusion.w0, bf16[2,4,128,384]{3,2,1,0:T(8,128)(2,1)S(1)} %copy-done.2, ...), custom_call_target="tpu_custom_call" | custom-call | flops 1610612736 | bytes 7602200 | tf_op jit(solution)/shard_map/pallas_call | solution.py:104
  279.2 2.3 shard_map.47
  283.7 3.4 collective-permute-start.19
  289.8 22.7 %collective-permute-start.22 = (bf16[2,256,256]{2,1,0:T(8,128)(2,1)S(1)}, bf16[2,256,256]{2,1,0:T(8,128)(2,1)S(1)}, u32[]{:S(2)}, u32[]{:S(2)}) collective-permute-start(bf16[2,256,256]{2,1,0:T(8,128)(2,1)S(1)} %get-tuple-element.37), channel_id=1, source_target_pairs={{0,12},{4,8},{8,4},{12,0},{1,13},{5,9},{9,5},{13,1},{2,14},{6,10},... | collective-permute-start | bytes 786440 | tf_op jit(solution)/shard_map/ppermute | solution.py:24
  312.5 3.4 collective-permute-start.21
  318.2 3.6 collective-permute-start.26
  321.8 3.4 collective-permute-start.25
  327.4 29.5 %collective-permute-start.29 = (bf16[256,256]{1,0:T(8,128)(2,1)S(1)}, bf16[256,256]{1,0:T(8,128)(2,1)S(1)}, u32[]{:S(2)}, u32[]{:S(2)}) collective-permute-start(bf16[256,256]{1,0:T(8,128)(2,1)S(1)} %fusion.5), channel_id=1, source_target_pairs={{0,2},{2,0},{64,66},{66,64},{1,3},{3,1},{65,67},{67,65},{4,6},{6,4... | collective-permute-start | bytes 393224 | tf_op jit(solution)/shard_map/ppermute | solution.py:24
  359.0 11.4 %collective-permute-start.27 = (bf16[256,256]{1,0:T(8,128)(2,1)S(1)}, bf16[256,256]{1,0:T(8,128)(2,1)S(1)}, u32[]{:S(2)}, u32[]{:S(2)}) collective-permute-start(bf16[256,256]{1,0:T(8,128)(2,1)S(1)} %get-tuple-element.39), channel_id=1, source_target_pairs={{0,64},{2,66},{64,0},{66,2},{1,65},{3,67},{65,1},{67,3},{4,68},{6,... | collective-permute-start | bytes 393224 | tf_op jit(solution)/shard_map/ppermute | solution.py:24
  370.4 4.9 %collective-permute-done.28 = bf16[256,256]{1,0:T(8,128)(2,1)S(1)} collective-permute-done((bf16[256,256]{1,0:T(8,128)(2,1)S(1)}, bf16[256,256]{1,0:T(8,128)(2,1)S(1)}, u32[]{:S(2)}, u32[]{:S(2)}) %collective-permute-start.28) | collective-permute-done | bytes 131104 | tf_op jit(solution)/shard_map/ppermute | solution.py:24
  375.3 3.8 collective-permute-done.27
  (74 shorter events, 40.7 us)
Async XLA Ops:
  6.5 229.8 %all-gather.3.cloned.1.call-start = ((), (), s32[]{:S(2)}) async-start(), calls=%async_computation | async-start | bytes 2367488 | tf_op jit(solution)/shard_map/all_gather | solution.py:126
  9.8 22.0 %collective-permute-start.3 = (bf16[128,384]{1,0:T(8,128)(2,1)S(1)}, bf16[128,384]{1,0:T(8,128)(2,1)S(1)}, u32[]{:S(2)}, u32[]{:S(2)}) collective-permute-start(bf16[128,384]{1,0:T(8,128)(2,1)S(1)} %get-tuple-element.44), channel_id=1, source_target_pairs={{0,1},{1,65},{64,0},{65,64},{2,3},{3,67},{66,2},{67,66},{4,5},{5,6... | collective-permute-start | bytes 294920 | tf_op jit(solution)/shard_map/ppermute | solution.py:34
  19.4 12.4 %collective-permute-start.2 = (bf16[128,384]{1,0:T(8,128)(2,1)S(1)}, bf16[128,384]{1,0:T(8,128)(2,1)S(1)}, u32[]{:S(2)}, u32[]{:S(2)}) collective-permute-start(bf16[128,384]{1,0:T(8,128)(2,1)S(1)} %get-tuple-element.43), channel_id=1, source_target_pairs={{0,0},{1,64},{64,1},{65,65},{2,2},{3,66},{66,3},{67,67},{4,4},{5,6... | collective-permute-start | bytes 294920 | tf_op jit(solution)/shard_map/ppermute | solution.py:33
  27.0 13.6 %collective-permute-start.1 = (bf16[384,128]{1,0:T(8,128)(2,1)S(1)}, bf16[384,128]{1,0:T(8,128)(2,1)S(1)}, u32[]{:S(2)}, u32[]{:S(2)}) collective-permute-start(bf16[384,128]{1,0:T(8,128)(2,1)S(1)} %get-tuple-element.46), channel_id=1, source_target_pairs={{0,1},{1,65},{64,0},{65,64},{2,3},{3,67},{66,2},{67,66},{4,5},{5,6... | collective-permute-start | bytes 294920 | tf_op jit(solution)/shard_map/ppermute | solution.py:34
  28.9 20.2 %collective-permute-start = (bf16[384,128]{1,0:T(8,128)(2,1)S(1)}, bf16[384,128]{1,0:T(8,128)(2,1)S(1)}, u32[]{:S(2)}, u32[]{:S(2)}) collective-permute-start(bf16[384,128]{1,0:T(8,128)(2,1)S(1)} %get-tuple-element.45), channel_id=1, source_target_pairs={{0,0},{1,64},{64,1},{65,65},{2,2},{3,66},{66,3},{67,67},{4,4},{5,6... | collective-permute-start | bytes 294920 | tf_op jit(solution)/shard_map/ppermute | solution.py:33
  31.9 26.9 %collective-permute-start.6 = (bf16[2,128,384]{2,1,0:T(8,128)(2,1)S(1)}, bf16[2,128,384]{2,1,0:T(8,128)(2,1)S(1)}, u32[]{:S(2)}, u32[]{:S(2)}) collective-permute-start(bf16[2,128,384]{2,1,0:T(8,128)(2,1)S(1)} %get-tuple-element.17), channel_id=1, source_target_pairs={{0,48},{16,32},{32,16},{48,0},{1,49},{17,33},{33,17},{49,1},{2,50}... | collective-permute-start | bytes 589832 | tf_op jit(solution)/shard_map/ppermute | solution.py:24
  38.6 53.2 %collective-permute-start.5 = (bf16[2,128,384]{2,1,0:T(8,128)(2,1)S(1)}, bf16[2,128,384]{2,1,0:T(8,128)(2,1)S(1)}, u32[]{:S(2)}, u32[]{:S(2)}) collective-permute-start(bf16[2,128,384]{2,1,0:T(8,128)(2,1)S(1)} %get-tuple-element.17), channel_id=1, source_target_pairs={{0,32},{16,48},{32,0},{48,16},{1,33},{17,49},{33,1},{49,17},{2,34}... | collective-permute-start | bytes 589832 | tf_op jit(solution)/shard_map/ppermute | solution.py:24
  49.1 42.7 %collective-permute-start.4 = (bf16[2,128,384]{2,1,0:T(8,128)(2,1)S(1)}, bf16[2,128,384]{2,1,0:T(8,128)(2,1)S(1)}, u32[]{:S(2)}, u32[]{:S(2)}) collective-permute-start(bf16[2,128,384]{2,1,0:T(8,128)(2,1)S(1)} %get-tuple-element.17), channel_id=1, source_target_pairs={{0,16},{16,0},{32,48},{48,32},{1,17},{17,1},{33,49},{49,33},{2,18}... | collective-permute-start | bytes 589832 | tf_op jit(solution)/shard_map/ppermute | solution.py:24
  92.0 49.9 %collective-permute-start.10 = (bf16[2,4,128,384]{3,2,1,0:T(8,128)(2,1)S(1)}, bf16[2,4,128,384]{3,2,1,0:T(8,128)(2,1)S(1)}, u32[]{:S(2)}, u32[]{:S(2)}) collective-permute-start(bf16[2,4,128,384]{3,2,1,0:T(8,128)(2,1)S(1)} %pad_maximum_fusion.w0), channel_id=1, source_target_pairs={{0,128},{128,0},{256,384},{384,256},{1,129},{129,1},{257,385},{385... | collective-permute-start | bytes 2359304 | tf_op jit(solution)/shard_map/ppermute | solution.py:24
  93.9 48.0 %collective-permute-start.11 = (bf16[2,4,128,384]{3,2,1,0:T(8,128)(2,1)S(1)}, bf16[2,4,128,384]{3,2,1,0:T(8,128)(2,1)S(1)}, u32[]{:S(2)}, u32[]{:S(2)}) collective-permute-start(bf16[2,4,128,384]{3,2,1,0:T(8,128)(2,1)S(1)} %pad_maximum_fusion.w0), channel_id=1, source_target_pairs={{0,384},{128,256},{256,128},{384,0},{1,385},{129,257},{257,129},{3... | collective-permute-start | bytes 2359304 | tf_op jit(solution)/shard_map/ppermute | solution.py:24
  97.4 17.5 %collective-permute-start.9 = (bf16[2,384,128]{2,1,0:T(8,128)(2,1)S(1)}, bf16[2,384,128]{2,1,0:T(8,128)(2,1)S(1)}, u32[]{:S(2)}, u32[]{:S(2)}) collective-permute-start(bf16[2,384,128]{2,1,0:T(8,128)(2,1)S(1)} %pad_maximum_fusion.2), channel_id=1, source_target_pairs={{0,48},{16,32},{32,16},{48,0},{1,49},{17,33},{33,17},{49,1},{2,50}... | collective-permute-start | bytes 589832 | tf_op jit(solution)/shard_map/ppermute | solution.py:24
  99.3 42.4 %collective-permute-start.8 = (bf16[2,384,128]{2,1,0:T(8,128)(2,1)S(1)}, bf16[2,384,128]{2,1,0:T(8,128)(2,1)S(1)}, u32[]{:S(2)}, u32[]{:S(2)}) collective-permute-start(bf16[2,384,128]{2,1,0:T(8,128)(2,1)S(1)} %pad_maximum_fusion.2), channel_id=1, source_target_pairs={{0,32},{16,48},{32,0},{48,16},{1,33},{17,49},{33,1},{49,17},{2,34}... | collective-permute-start | bytes 589832 | tf_op jit(solution)/shard_map/ppermute | solution.py:24
  101.3 40.5 %collective-permute-start.7 = (bf16[2,384,128]{2,1,0:T(8,128)(2,1)S(1)}, bf16[2,384,128]{2,1,0:T(8,128)(2,1)S(1)}, u32[]{:S(2)}, u32[]{:S(2)}) collective-permute-start(bf16[2,384,128]{2,1,0:T(8,128)(2,1)S(1)} %pad_maximum_fusion.2), channel_id=1, source_target_pairs={{0,16},{16,0},{32,48},{48,32},{1,17},{17,1},{33,49},{49,33},{2,18}... | collective-permute-start | bytes 589832 | tf_op jit(solution)/shard_map/ppermute | solution.py:24
  141.9 21.5 %copy-start.1 = (bf16[2,4,128,384]{3,2,1,0:T(8,128)(2,1)}, bf16[2,4,128,384]{3,2,1,0:T(8,128)(2,1)S(1)}, u32[]{:S(2)}) copy-start(bf16[2,4,128,384]{3,2,1,0:T(8,128)(2,1)S(1)} %collective-permute-done.10.w1) | copy-start | bytes 2359300
  141.9 21.5 %collective-permute-start.12 = (bf16[2,4,384,128]{3,2,1,0:T(8,128)(2,1)S(1)}, bf16[2,4,384,128]{3,2,1,0:T(8,128)(2,1)S(1)}, u32[]{:S(2)}, u32[]{:S(2)}) collective-permute-start(bf16[2,4,384,128]{3,2,1,0:T(8,128)(2,1)S(1)} %pad_maximum_fusion.1.w0), channel_id=1, source_target_pairs={{0,128},{128,0},{256,384},{384,256},{1,129},{129,1},{257,385},{385... | collective-permute-start | bytes 2359304 | tf_op jit(solution)/shard_map/ppermute | solution.py:24
  145.0 22.6 %collective-permute-start.13 = (bf16[2,4,384,128]{3,2,1,0:T(8,128)(2,1)S(1)}, bf16[2,4,384,128]{3,2,1,0:T(8,128)(2,1)S(1)}, u32[]{:S(2)}, u32[]{:S(2)}) collective-permute-start(bf16[2,4,384,128]{3,2,1,0:T(8,128)(2,1)S(1)} %pad_maximum_fusion.1.w0), channel_id=1, source_target_pairs={{0,384},{128,256},{256,128},{384,0},{1,385},{129,257},{257,129},{3... | collective-permute-start | bytes 2359304 | tf_op jit(solution)/shard_map/ppermute | solution.py:24
  236.3 30.8 %collective-permute-start.14 = (bf16[16,272,256]{2,1,0:T(8,128)(2,1)}, bf16[16,272,256]{2,1,0:T(8,128)(2,1)}, u32[]{:S(2)}, u32[]{:S(2)}) collective-permute-start(bf16[16,272,256]{2,1,0:T(8,128)(2,1)} %bitcast.70), channel_id=1, source_target_pairs={{0,1},{1,0},{2,3},{3,2},{4,5},{5,4},{6,7},{7,6},{8,9},{9,8},{10,11... | collective-permute-start | bytes 6684680 | tf_op jit(solution)/shard_map/ppermute | solution.py:24
  240.6 14.1 %collective-permute-start.15 = (bf16[1,4,128,384]{3,2,1,0:T(8,128)(2,1)S(1)}, bf16[1,4,128,384]{3,2,1,0:T(8,128)(2,1)S(1)}, u32[]{:S(2)}, u32[]{:S(2)}) collective-permute-start(bf16[1,4,128,384]{3,2,1,0:T(8,128)(2,1)S(1)} %slice.48), channel_id=1, source_target_pairs={{0,128},{128,0},{256,384},{384,256},{1,129},{129,1},{257,385},{385... | collective-permute-start | bytes 1179656 | tf_op jit(solution)/shard_map/ppermute | solution.py:24
  245.8 15.4 %collective-permute-start.16 = (bf16[1,4,128,384]{3,2,1,0:T(8,128)(2,1)S(1)}, bf16[1,4,128,384]{3,2,1,0:T(8,128)(2,1)S(1)}, u32[]{:S(2)}, u32[]{:S(2)}) collective-permute-start(bf16[1,4,128,384]{3,2,1,0:T(8,128)(2,1)S(1)} %slice.49), channel_id=1, source_target_pairs={{0,384},{128,256},{256,128},{384,0},{1,385},{129,257},{257,129},{3... | collective-permute-start | bytes 1179656 | tf_op jit(solution)/shard_map/ppermute | solution.py:24
  252.8 26.4 %collective-permute-start.17 = (bf16[1,4,384,128]{3,2,1,0:T(8,128)(2,1)}, bf16[1,4,384,128]{3,2,1,0:T(8,128)(2,1)S(1)}, u32[]{:S(2)}, u32[]{:S(2)}) collective-permute-start(bf16[1,4,384,128]{3,2,1,0:T(8,128)(2,1)} %slice.64), channel_id=1, source_target_pairs={{0,128},{128,0},{256,384},{384,256},{1,129},{129,1},{257,385},{385... | collective-permute-start | bytes 1179656 | tf_op jit(solution)/shard_map/ppermute | solution.py:24
  262.8 16.4 %collective-permute-start.18 = (bf16[1,4,384,128]{3,2,1,0:T(8,128)(2,1)}, bf16[1,4,384,128]{3,2,1,0:T(8,128)(2,1)}, u32[]{:S(2)}, u32[]{:S(2)}) collective-permute-start(bf16[1,4,384,128]{3,2,1,0:T(8,128)(2,1)} %slice.51), channel_id=1, source_target_pairs={{0,384},{128,256},{256,128},{384,0},{1,385},{129,257},{257,129},{3... | collective-permute-start | bytes 1179656 | tf_op jit(solution)/shard_map/ppermute | solution.py:24
  283.7 5.7 %collective-permute-start.19 = (bf16[4,2,256,256]{3,2,1,0:T(8,128)(2,1)S(1)}, bf16[4,2,256,256]{3,2,1,0:T(8,128)(2,1)S(1)}, u32[]{:S(2)}, u32[]{:S(2)}) collective-permute-start(bf16[4,2,256,256]{3,2,1,0:T(8,128)(2,1)S(1)} %get-tuple-element.27), channel_id=1, source_target_pairs={{0,1},{1,0},{2,3},{3,2},{4,5},{5,4},{6,7},{7,6},{8,9},{9,8},{10,11... | collective-permute-start | bytes 3145736 | tf_op jit(solution)/shard_map/ppermute | solution.py:24
  287.1 30.7 %collective-permute-start.23 = (bf16[4,2,256,256]{3,2,1,0:T(8,128)(2,1)S(1)}, bf16[4,2,256,256]{3,2,1,0:T(8,128)(2,1)S(1)}, u32[]{:S(2)}, u32[]{:S(2)}) collective-permute-start(bf16[4,2,256,256]{3,2,1,0:T(8,128)(2,1)S(1)} %get-tuple-element.24), channel_id=1, source_target_pairs={{0,1},{1,0},{2,3},{3,2},{4,5},{5,4},{6,7},{7,6},{8,9},{9,8},{10,11... | collective-permute-start | bytes 3145736 | tf_op jit(solution)/shard_map/ppermute | solution.py:24
  289.8 35.5 %collective-permute-start.22 = (bf16[2,256,256]{2,1,0:T(8,128)(2,1)S(1)}, bf16[2,256,256]{2,1,0:T(8,128)(2,1)S(1)}, u32[]{:S(2)}, u32[]{:S(2)}) collective-permute-start(bf16[2,256,256]{2,1,0:T(8,128)(2,1)S(1)} %get-tuple-element.37), channel_id=1, source_target_pairs={{0,12},{4,8},{8,4},{12,0},{1,13},{5,9},{9,5},{13,1},{2,14},{6,10},... | collective-permute-start | bytes 786440 | tf_op jit(solution)/shard_map/ppermute | solution.py:24
  312.5 14.8 %collective-permute-start.21 = (bf16[2,256,256]{2,1,0:T(8,128)(2,1)S(1)}, bf16[2,256,256]{2,1,0:T(8,128)(2,1)S(1)}, u32[]{:S(2)}, u32[]{:S(2)}) collective-permute-start(bf16[2,256,256]{2,1,0:T(8,128)(2,1)S(1)} %get-tuple-element.38), channel_id=1, source_target_pairs={{0,8},{4,12},{8,0},{12,4},{1,9},{5,13},{9,1},{13,5},{2,10},{6,14},... | collective-permute-start | bytes 786440 | tf_op jit(solution)/shard_map/ppermute | solution.py:24
  315.9 11.3 %collective-permute-start.20 = (bf16[2,256,256]{2,1,0:T(8,128)(2,1)S(1)}, bf16[2,256,256]{2,1,0:T(8,128)(2,1)S(1)}, u32[]{:S(2)}, u32[]{:S(2)}) collective-permute-start(bf16[2,256,256]{2,1,0:T(8,128)(2,1)S(1)} %get-tuple-element.36), channel_id=1, source_target_pairs={{0,4},{4,0},{8,12},{12,8},{1,5},{5,1},{9,13},{13,9},{2,6},{6,2},{1... | collective-permute-start | bytes 786440 | tf_op jit(solution)/shard_map/ppermute | solution.py:24
  318.2 38.7 %collective-permute-start.26 = (bf16[2,256,256]{2,1,0:T(8,128)(2,1)S(1)}, bf16[2,256,256]{2,1,0:T(8,128)(2,1)S(1)}, u32[]{:S(2)}, u32[]{:S(2)}) collective-permute-start(bf16[2,256,256]{2,1,0:T(8,128)(2,1)S(1)} %get-tuple-element.34), channel_id=1, source_target_pairs={{0,12},{4,8},{8,4},{12,0},{1,13},{5,9},{9,5},{13,1},{2,14},{6,10},... | collective-permute-start | bytes 786440 | tf_op jit(solution)/shard_map/ppermute | solution.py:24
  321.8 35.1 %collective-permute-start.25 = (bf16[2,256,256]{2,1,0:T(8,128)(2,1)S(1)}, bf16[2,256,256]{2,1,0:T(8,128)(2,1)S(1)}, u32[]{:S(2)}, u32[]{:S(2)}) collective-permute-start(bf16[2,256,256]{2,1,0:T(8,128)(2,1)S(1)} %get-tuple-element.35), channel_id=1, source_target_pairs={{0,8},{4,12},{8,0},{12,4},{1,9},{5,13},{9,1},{13,5},{2,10},{6,14},... | collective-permute-start | bytes 786440 | tf_op jit(solution)/shard_map/ppermute | solution.py:24
  325.3 31.6 %collective-permute-start.24 = (bf16[2,256,256]{2,1,0:T(8,128)(2,1)S(1)}, bf16[2,256,256]{2,1,0:T(8,128)(2,1)S(1)}, u32[]{:S(2)}, u32[]{:S(2)}) collective-permute-start(bf16[2,256,256]{2,1,0:T(8,128)(2,1)S(1)} %get-tuple-element.33), channel_id=1, source_target_pairs={{0,4},{4,0},{8,12},{12,8},{1,5},{5,1},{9,13},{13,9},{2,6},{6,2},{1... | collective-permute-start | bytes 786440 | tf_op jit(solution)/shard_map/ppermute | solution.py:24
  327.4 43.0 %collective-permute-start.29 = (bf16[256,256]{1,0:T(8,128)(2,1)S(1)}, bf16[256,256]{1,0:T(8,128)(2,1)S(1)}, u32[]{:S(2)}, u32[]{:S(2)}) collective-permute-start(bf16[256,256]{1,0:T(8,128)(2,1)S(1)} %fusion.5), channel_id=1, source_target_pairs={{0,2},{2,0},{64,66},{66,64},{1,3},{3,1},{65,67},{67,65},{4,6},{6,4... | collective-permute-start | bytes 393224 | tf_op jit(solution)/shard_map/ppermute | solution.py:24
  357.0 18.3 %collective-permute-start.28 = (bf16[256,256]{1,0:T(8,128)(2,1)S(1)}, bf16[256,256]{1,0:T(8,128)(2,1)S(1)}, u32[]{:S(2)}, u32[]{:S(2)}) collective-permute-start(bf16[256,256]{1,0:T(8,128)(2,1)S(1)} %get-tuple-element.40), channel_id=1, source_target_pairs={{0,66},{2,64},{64,2},{66,0},{1,67},{3,65},{65,3},{67,1},{4,70},{6,... | collective-permute-start | bytes 393224 | tf_op jit(solution)/shard_map/ppermute | solution.py:24
  359.0 20.1 %collective-permute-start.27 = (bf16[256,256]{1,0:T(8,128)(2,1)S(1)}, bf16[256,256]{1,0:T(8,128)(2,1)S(1)}, u32[]{:S(2)}, u32[]{:S(2)}) collective-permute-start(bf16[256,256]{1,0:T(8,128)(2,1)S(1)} %get-tuple-element.39), channel_id=1, source_target_pairs={{0,64},{2,66},{64,0},{66,2},{1,65},{3,67},{65,1},{67,3},{4,68},{6,... | collective-permute-start | bytes 393224 | tf_op jit(solution)/shard_map/ppermute | solution.py:24
  (8 other events, 29.0 us)
Sparse Core Ops, SparseCore 0:
  9.4 226.8 all-gather.2

commit v4 on v2

--- a/solution.py
+++ b/solution.py
@@ -123,32 +123,26 @@
     def weight_half(which, axis, array):
         return lax.dynamic_slice_in_dim(array, which * half, half, axis)
 
+    both = jnp.concatenate([tokens, jnp.broadcast_to(norm_gain[None], (GAIN_ROWS, cols))], axis=0)
+    both = jnp.stack([both] + [send(both, ("zt", "zh"), k) for k in (1, 2, 3)])
     swapped = swap_halves(weight_half(zt, 1, w_inner), weight_half(1 - zt, 1, w_inner))
-    both = jnp.concatenate([tokens, jnp.broadcast_to(norm_gain[None], (GAIN_ROWS, cols))], axis=0)
-    near = [send(both, ("zt", "zh"), k) for k in (2, 3)]
 
-    inner = after(jnp.stack(swapped), *near)
+    inner = after(jnp.stack(swapped), both)
+    both = after(both, *swapped)
     inner = jnp.stack([inner] + [send(inner, ("zq",), k) for k in (1, 2, 3)], axis=1)
+    y1, y3 = from_neighbours(both, "y")
 
-    in1, in3 = from_neighbours(inner, "x")
-    far = send(after(both, inner), ("zt", "zh"), 1)
-    swapped = swap_halves(*(weight_half(h, 0, after(w_outer, inner)) for h in (zt, 1 - zt)))
+    in1, in3 = from_neighbours(after(inner, y1, y3), "x")
+    swapped = swap_halves(*(weight_half(h, 0, after(w_outer, inner, y1, y3)) for h in (zt, 1 - zt)))
+    y2 = send(after(both, inner, y1, y3), ("y",), 2)
+    both = jnp.stack([both, y1, y2, y3])
 
-    in2a, in2b = from_far(after(in1, far, *swapped), after(in3, far, *swapped), "x", 1)
-    both = after(jnp.stack([both, far] + near), in1, in3, *swapped)
-    y1, y3 = from_neighbours(both, "y")
-    outer = after(jnp.stack(swapped), in1, in3, far)
-    second = send(outer, ("zq",), 2)
+    in2a, in2b = from_far(after(in1, y2, *swapped), after(in3, y2, *swapped), "x", 1)
+    other = send(after(both, in1, in3, *swapped), ("c",), 1)
+    outer = after(jnp.stack(swapped), in1, in3, y2)
+    outer = jnp.stack([outer] + [send(outer, ("zq",), k) for k in (1, 2, 3)], axis=1)
 
-    y2a, y2b = from_far(after(y1, in2a, in2b, second), after(y3, in2a, in2b, second), "y", 2)
-    pair = send(after(jnp.stack([outer, second], axis=1), in2a, in2b, y1, y3), ("zq",), 1)
-    outer = jnp.stack([outer, pair[:, 0], second, pair[:, 1]], axis=1)
-
-    both = jnp.stack([both, y1, jnp.concatenate([y2a, y2b], axis=0), y3])
-    out1, out3 = from_neighbours(after(outer, y2a, y2b), "x")
-    other = send(after(both, pair), ("c",), 1)
-
-    out2a, out2b = from_far(after(out1, other), out3, "x", 1)
+    out1, out3 = from_neighbours(after(outer, in2a, in2b, other), "x")
 
     flops = 2 * 2 * rows * half * 16 * cols
     act = call(
@@ -156,10 +150,11 @@
         jax.ShapeDtypeStruct((2, rows, half), jnp.bfloat16),
         flops, place, both, other, inner, in1, in2a[0], in2b[0], in3,
     )
+    out2a, out2b = from_far(after(out1, act), after(out3, act), "x", 1)
     shape = jax.ShapeDtypeStruct((4, 2, rows, cols), jnp.bfloat16)
     outer_all = (outer, out1, out2a[0], out2b[0], out3)
     parts = []
-    for a in (1, 0):
+    for a in (0, 1):
         mine, other = call(
             functools.partial(out_kernel, a), (shape, shape), flops // 2, place, act, *outer_all
         )
@@ -167,7 +162,7 @@
         sent = total.astype(jnp.bfloat16)
         total = total[0] + sum(send(sent[k], ("y",), k).astype(jnp.float32) for k in (1, 2, 3))
         parts.append((total, total.astype(jnp.bfloat16)))
-    (_, away), (total, stay) = parts
+    (total, stay), (_, away) = parts
     total = total[0] + sum(
         send(piece, ("zt", "zh"), k).astype(jnp.float32)
         for k, piece in ((2, away[0]), (3, away[1]), (1, stay[1]))

time: 250 us -> 236 us (0.944)
  waiting for transfers between devices: 91.3 us -> 61.4 us
  starting transfers between devices: 131 us -> 145 us
    ppermute x32, waiting for transfers between devices: 84.8 us -> 55.1 us  [send(): return lax.ppermute(value, axes, [(i, i ^ k) for i in range(count)])]
    ppermute x32, starting transfers between devices: 108 us -> 122 us  [send(): return lax.ppermute(value, axes, [(i, i ^ k) for i in range(count)])]
    ppermute x2, starting transfers between devices: 11.9 us -> 8.95 us  [swap_halves(): lax.ppermute(first, ('zt', 'c'), [(2 * a + b, 2 * b + a) for a, b in both])]
    ppermute x2, starting transfers between devices: 11.6 us -> 14.3 us  [swap_halves(): lax.ppermute(second, ('zt', 'c'), [(2 * a + b, 2 * b + 1 - a) for a, b in...]
    unnamed x34 -> x22, local copies, waits for them, and re-layouts: 8.46 us -> 8.19 us
  transfers between devices with their start and end apart: 36 -> 36, of which waited for: 14 -> 13; matrix products, arithmetic and copies ran while one was open for 2% -> 2% of each run, Pallas kernels for 3% -> 3%
where the time goes in v4:
time: 236 us; the launch traced here: 233 us
  starting transfers between devices  145 us (61%)
  waiting for transfers between devices  61.4 us (26%)
  local copies, waits for them, and re-layouts  12.2 us (5%)
  Pallas kernels  10.6 us (4%)
  other arithmetic  3.1 us (1%)
    ppermute x32, starting transfers between devices, send(): return lax.ppermute(value, axes, [(i, i ^ k) for i in range(count)])  122 us
    ppermute x32, waiting for transfers between devices, send(): return lax.ppermute(value, axes, [(i, i ^ k) for i in range(count)])  55.1 us
    ppermute x2, starting transfers between devices, swap_halves(): lax.ppermute(second, ('zt', 'c'), [(2 * a + b, 2 * b + 1 - a) for a, b in...  14.3 us
    pallas_call x3, Pallas kernels, call(): pl.pallas_call(kernel, out_shape=out_shape, in_specs=[pl.BlockSpec(memory...  10.6 us
    ppermute x2, starting transfers between devices, swap_halves(): lax.ppermute(first, ('zt', 'c'), [(2 * a + b, 2 * b + a) for a, b in both])  8.95 us
    unnamed x22, local copies, waits for them, and re-layouts  8.19 us
    ppermute x2, waiting for transfers between devices, swap_halves(): lax.ppermute(first, ('zt', 'c'), [(2 * a + b, 2 * b + a) for a, b in both])  6.34 us
  transfers between devices with their start and end apart: 36, of which 13 were waited for; matrix products, arithmetic and copies ran while one was open for 2% of the time, Pallas kernels for 3%

profile of v4, /device:TPU:1, one launch (start us, length us, event | category | flops | bytes accessed | tf_op | source)
XLA Modules:
  0.0 233.0 jit_solution(12477507138612116548)
XLA Ops:
  1.6 9.6 %collective-permute-start.1 = (bf16[272,256]{1,0:T(8,128)(2,1)S(1)}, bf16[272,256]{1,0:T(8,128)(2,1)S(1)}, u32[]{:S(2)}, u32[]{:S(2)}) collective-permute-start(bf16[272,256]{1,0:T(8,128)(2,1)S(1)} %get-tuple-element.54), channel_id=1, source_target_pairs={{0,64},{2,66},{64,0},{66,2},{1,65},{3,67},{65,1},{67,3},{4,68},{6,... | collective-permute-start | bytes 417800 | tf_op jit(solution)/shard_map/ppermute | solution.py:24
  11.3 10.6 %collective-permute-start = (bf16[272,256]{1,0:T(8,128)(2,1)S(1)}, bf16[272,256]{1,0:T(8,128)(2,1)S(1)}, u32[]{:S(2)}, u32[]{:S(2)}) collective-permute-start(bf16[272,256]{1,0:T(8,128)(2,1)S(1)} %get-tuple-element.54), channel_id=1, source_target_pairs={{0,2},{2,0},{64,66},{66,64},{1,3},{3,1},{65,67},{67,65},{4,6},{6,4... | collective-permute-start | bytes 417800 | tf_op jit(solution)/shard_map/ppermute | solution.py:24
  24.8 5.2 %collective-permute-start.4 = (bf16[128,384]{1,0:T(8,128)(2,1)S(1)}, bf16[128,384]{1,0:T(8,128)(2,1)S(1)}, u32[]{:S(2)}, u32[]{:S(2)}) collective-permute-start(bf16[128,384]{1,0:T(8,128)(2,1)S(1)} %get-tuple-element.51), channel_id=1, source_target_pairs={{0,1},{1,65},{64,0},{65,64},{2,3},{3,67},{66,2},{67,66},{4,5},{5,6... | collective-permute-start | bytes 294920 | tf_op jit(solution)/shard_map/ppermute | solution.py:34
  30.0 5.9 %collective-permute-start.3 = (bf16[128,384]{1,0:T(8,128)(2,1)S(1)}, bf16[128,384]{1,0:T(8,128)(2,1)S(1)}, u32[]{:S(2)}, u32[]{:S(2)}) collective-permute-start(bf16[128,384]{1,0:T(8,128)(2,1)S(1)} %get-tuple-element.52), channel_id=1, source_target_pairs={{0,0},{1,64},{64,1},{65,65},{2,2},{3,66},{66,3},{67,67},{4,4},{5,6... | collective-permute-start | bytes 294920 | tf_op jit(solution)/shard_map/ppermute | solution.py:33
  35.9 12.3 %collective-permute-done.2 = bf16[272,256]{1,0:T(8,128)(2,1)S(1)} collective-permute-done((bf16[272,256]{1,0:T(8,128)(2,1)S(1)}, bf16[272,256]{1,0:T(8,128)(2,1)S(1)}, u32[]{:S(2)}, u32[]{:S(2)}) %collective-permute-start.2) | collective-permute-done | bytes 139296 | tf_op jit(solution)/shard_map/ppermute | solution.py:24
  48.4 3.4 %collective-permute-start.9 = (bf16[4,272,256]{2,1,0:T(8,128)(2,1)S(1)}, bf16[4,272,256]{2,1,0:T(8,128)(2,1)S(1)}, u32[]{:S(2)}, u32[]{:S(2)}) collective-permute-start(bf16[4,272,256]{2,1,0:T(8,128)(2,1)S(1)} %pad_maximum_fusion.3), channel_id=1, source_target_pairs={{0,12},{4,8},{8,4},{12,0},{1,13},{5,9},{9,5},{13,1},{2,14},{6,10},... | collective-permute-start | bytes 1671176 | tf_op jit(solution)/shard_map/ppermute | solution.py:24
  56.2 7.5 %collective-permute-start.7 = (bf16[2,128,384]{2,1,0:T(8,128)(2,1)S(1)}, bf16[2,128,384]{2,1,0:T(8,128)(2,1)S(1)}, u32[]{:S(2)}, u32[]{:S(2)}) collective-permute-start(bf16[2,128,384]{2,1,0:T(8,128)(2,1)S(1)} %pad_maximum_fusion.4), channel_id=1, source_target_pairs={{0,32},{16,48},{32,0},{48,16},{1,33},{17,49},{33,1},{49,17},{2,34}... | collective-permute-start | bytes 589832 | tf_op jit(solution)/shard_map/ppermute | solution.py:24
  65.7 11.2 %collective-permute-done.7 = bf16[2,128,384]{2,1,0:T(8,128)(2,1)S(1)} collective-permute-done((bf16[2,128,384]{2,1,0:T(8,128)(2,1)S(1)}, bf16[2,128,384]{2,1,0:T(8,128)(2,1)S(1)}, u32[]{:S(2)}, u32[]{:S(2)}) %collective-permute-start.7) | collective-permute-done | bytes 196640 | tf_op jit(solution)/shard_map/ppermute | solution.py:24
  77.1 4.4 %collective-permute-start.12 = (bf16[2,4,128,384]{3,2,1,0:T(8,128)(2,1)S(1)}, bf16[2,4,128,384]{3,2,1,0:T(8,128)(2,1)S(1)}, u32[]{:S(2)}, u32[]{:S(2)}) collective-permute-start(bf16[2,4,128,384]{3,2,1,0:T(8,128)(2,1)S(1)} %pad_maximum_fusion.1.w0), channel_id=1, source_target_pairs={{0,384},{128,256},{256,128},{384,0},{1,385},{129,257},{257,129},{3... | collective-permute-start | bytes 2359304 | tf_op jit(solution)/shard_map/ppermute | solution.py:24
  83.4 3.1 %collective-permute-start.10 = (bf16[4,272,256]{2,1,0:T(8,128)(2,1)S(1)}, bf16[4,272,256]{2,1,0:T(8,128)(2,1)S(1)}, u32[]{:S(2)}, u32[]{:S(2)}) collective-permute-start(bf16[4,272,256]{2,1,0:T(8,128)(2,1)S(1)} %pad_maximum_fusion.3), channel_id=1, source_target_pairs={{0,8},{4,12},{8,0},{12,4},{1,9},{5,13},{9,1},{13,5},{2,10},{6,14},... | collective-permute-start | bytes 1671176 | tf_op jit(solution)/shard_map/ppermute | solution.py:24
  86.5 9.1 %collective-permute-start.14 = (bf16[384,128]{1,0:T(8,128)(2,1)S(1)}, bf16[384,128]{1,0:T(8,128)(2,1)S(1)}, u32[]{:S(2)}, u32[]{:S(2)}) collective-permute-start(bf16[384,128]{1,0:T(8,128)(2,1)S(1)} %get-tuple-element.49), channel_id=1, source_target_pairs={{0,1},{1,65},{64,0},{65,64},{2,3},{3,67},{66,2},{67,66},{4,5},{5,6... | collective-permute-start | bytes 294920 | tf_op jit(solution)/shard_map/ppermute | solution.py:34
  95.7 3.1 %collective-permute-start.13 = (bf16[384,128]{1,0:T(8,128)(2,1)S(1)}, bf16[384,128]{1,0:T(8,128)(2,1)S(1)}, u32[]{:S(2)}, u32[]{:S(2)}) collective-permute-start(bf16[384,128]{1,0:T(8,128)(2,1)S(1)} %get-tuple-element.50), channel_id=1, source_target_pairs={{0,0},{1,64},{64,1},{65,65},{2,2},{3,66},{66,3},{67,67},{4,4},{5,6... | collective-permute-start | bytes 294920 | tf_op jit(solution)/shard_map/ppermute | solution.py:33
  100.3 6.3 %collective-permute-done.13 = bf16[384,128]{1,0:T(8,128)(2,1)S(1)} collective-permute-done((bf16[384,128]{1,0:T(8,128)(2,1)S(1)}, bf16[384,128]{1,0:T(8,128)(2,1)S(1)}, u32[]{:S(2)}, u32[]{:S(2)}) %collective-permute-start.13) | collective-permute-done | bytes 98336 | tf_op jit(solution)/shard_map/ppermute | solution.py:33
  108.6 3.9 %collective-permute-start.20 = (bf16[2,384,128]{2,1,0:T(8,128)(2,1)S(1)}, bf16[2,384,128]{2,1,0:T(8,128)(2,1)S(1)}, u32[]{:S(2)}, u32[]{:S(2)}) collective-permute-start(bf16[2,384,128]{2,1,0:T(8,128)(2,1)S(1)} %pad_maximum_fusion.5), channel_id=1, source_target_pairs={{0,48},{16,32},{32,16},{48,0},{1,49},{17,33},{33,17},{49,1},{2,50}... | collective-permute-start | bytes 589832 | tf_op jit(solution)/shard_map/ppermute | solution.py:24
  112.5 3.4 %collective-permute-start.16 = (bf16[1,4,128,384]{3,2,1,0:T(8,128)(2,1)S(1)}, bf16[1,4,128,384]{3,2,1,0:T(8,128)(2,1)S(1)}, u32[]{:S(2)}, u32[]{:S(2)}) collective-permute-start(bf16[1,4,128,384]{3,2,1,0:T(8,128)(2,1)S(1)} %slice.48), channel_id=1, source_target_pairs={{0,128},{128,0},{256,384},{384,256},{1,129},{129,1},{257,385},{385... | collective-permute-start | bytes 1179656 | tf_op jit(solution)/shard_map/ppermute | solution.py:24
  120.0 3.4 %collective-permute-start.18 = (bf16[2,384,128]{2,1,0:T(8,128)(2,1)S(1)}, bf16[2,384,128]{2,1,0:T(8,128)(2,1)S(1)}, u32[]{:S(2)}, u32[]{:S(2)}) collective-permute-start(bf16[2,384,128]{2,1,0:T(8,128)(2,1)S(1)} %pad_maximum_fusion.5), channel_id=1, source_target_pairs={{0,16},{16,0},{32,48},{48,32},{1,17},{17,1},{33,49},{49,33},{2,18}... | collective-permute-start | bytes 589832 | tf_op jit(solution)/shard_map/ppermute | solution.py:24
  123.5 7.4 %collective-permute-done.19 = bf16[2,384,128]{2,1,0:T(8,128)(2,1)S(1)} collective-permute-done((bf16[2,384,128]{2,1,0:T(8,128)(2,1)S(1)}, bf16[2,384,128]{2,1,0:T(8,128)(2,1)S(1)}, u32[]{:S(2)}, u32[]{:S(2)}) %collective-permute-start.19) | collective-permute-done | bytes 196640 | tf_op jit(solution)/shard_map/ppermute | solution.py:24
  133.4 4.4 %collective-permute-start.22 = (bf16[2,4,384,128]{3,2,1,0:T(8,128)(2,1)S(1)}, bf16[2,4,384,128]{3,2,1,0:T(8,128)(2,1)}, u32[]{:S(2)}, u32[]{:S(2)}) collective-permute-start(bf16[2,4,384,128]{3,2,1,0:T(8,128)(2,1)S(1)} %pad_maximum_fusion.2.w0), channel_id=1, source_target_pairs={{0,384},{128,256},{256,128},{384,0},{1,385},{129,257},{257,129},{3... | collective-permute-start | bytes 2359304 | tf_op jit(solution)/shard_map/ppermute | solution.py:24
  145.9 5.2 %shard_map.46.act = bf16[2,256,384]{2,1,0:T(8,128)(2,1)S(1)} custom-call(s32[5]{0:T(128)S(1)} %stack.101.place, bf16[4,4,272,256]{3,2,1,0:T(8,128)(2,1)S(1)} %pad_maximum_fusion.mine, bf16[4,4,272,256]{3,2,1,0:T(8,128)(2,1)S(1)} %copy-done.3, bf16[2,4,128,384]{3,2,1,0:T(8,128)(2,1)S(1)} %copy-done.1, bf16[2,4,128,384]{3,2,1,0:T(8,128)(2,1)S(1)} %copy-done.7, ...), custom_call_target="tpu_custom_call" | custom-call | flops 1610612736 | bytes 7602196 | tf_op jit(solution)/shard_map/pallas_call | solution.py:105
  157.4 4.4 %collective-permute-start.24 = (bf16[1,4,384,128]{3,2,1,0:T(8,128)(2,1)S(1)}, bf16[1,4,384,128]{3,2,1,0:T(8,128)(2,1)S(1)}, u32[]{:S(2)}, u32[]{:S(2)}) collective-permute-start(bf16[1,4,384,128]{3,2,1,0:T(8,128)(2,1)S(1)} %slice.51), channel_id=1, source_target_pairs={{0,384},{128,256},{256,128},{384,0},{1,385},{129,257},{257,129},{3... | collective-permute-start | bytes 1179656 | tf_op jit(solution)/shard_map/ppermute | solution.py:24
  164.3 3.3 %collective-permute-done.24 = bf16[1,4,384,128]{3,2,1,0:T(8,128)(2,1)S(1)} collective-permute-done((bf16[1,4,384,128]{3,2,1,0:T(8,128)(2,1)S(1)}, bf16[1,4,384,128]{3,2,1,0:T(8,128)(2,1)S(1)}, u32[]{:S(2)}, u32[]{:S(2)}) %collective-permute-start.24) | collective-permute-done | bytes 393248 | tf_op jit(solution)/shard_map/ppermute | solution.py:24
  167.5 2.7 %shard_map.48 = (bf16[4,2,256,256]{3,2,1,0:T(8,128)(2,1)S(1)}, bf16[4,2,256,256]{3,2,1,0:T(8,128)(2,1)S(1)}) custom-call(s32[5]{0:T(128)S(1)} %stack.101.place, bf16[2,256,384]{2,1,0:T(8,128)(2,1)S(1)} %shard_map.46.act, bf16[2,4,384,128]{3,2,1,0:T(8,128)(2,1)S(1)} %pad_maximum_fusion.2.w0, bf16[2,4,384,128]{3,2,1,0:T(8,128)(2,1)} %collective-permute-done.21.w1, ...), custom_call_target="tpu_custom_call" | custom-call | flops 805306368 | bytes 3538964 | tf_op jit(solution)/shard_map/pallas_call | solution.py:105
  170.2 6.4 %collective-permute-start.29 = (bf16[4,2,256,256]{3,2,1,0:T(8,128)(2,1)S(1)}, bf16[4,2,256,256]{3,2,1,0:T(8,128)(2,1)S(1)}, u32[]{:S(2)}, u32[]{:S(2)}) collective-permute-start(bf16[4,2,256,256]{3,2,1,0:T(8,128)(2,1)S(1)} %get-tuple-element.36), channel_id=1, source_target_pairs={{0,1},{1,0},{2,3},{3,2},{4,5},{5,4},{6,7},{7,6},{8,9},{9,8},{10,11... | collective-permute-start | bytes 3145736 | tf_op jit(solution)/shard_map/ppermute | solution.py:24
  176.6 2.7 %shard_map.47 = (bf16[4,2,256,256]{3,2,1,0:T(8,128)(2,1)S(1)}, bf16[4,2,256,256]{3,2,1,0:T(8,128)(2,1)S(1)}) custom-call(s32[5]{0:T(128)S(1)} %stack.101.place, bf16[2,256,384]{2,1,0:T(8,128)(2,1)S(1)} %shard_map.46.act, bf16[2,4,384,128]{3,2,1,0:T(8,128)(2,1)S(1)} %pad_maximum_fusion.2.w0, bf16[2,4,384,128]{3,2,1,0:T(8,128)(2,1)} %collective-permute-done.21.w1, ...), custom_call_target="tpu_custom_call" | custom-call | flops 805306368 | bytes 3538964 | tf_op jit(solution)/shard_map/pallas_call | solution.py:105
  183.8 4.3 %collective-permute-start.32 = (bf16[2,256,256]{2,1,0:T(8,128)(2,1)S(1)}, bf16[2,256,256]{2,1,0:T(8,128)(2,1)S(1)}, u32[]{:S(2)}, u32[]{:S(2)}) collective-permute-start(bf16[2,256,256]{2,1,0:T(8,128)(2,1)S(1)} %get-tuple-element.42), channel_id=1, source_target_pairs={{0,12},{4,8},{8,4},{12,0},{1,13},{5,9},{9,5},{13,1},{2,14},{6,10},... | collective-permute-start | bytes 786440 | tf_op jit(solution)/shard_map/ppermute | solution.py:24
  188.1 3.1 %collective-permute-start.31 = (bf16[2,256,256]{2,1,0:T(8,128)(2,1)S(1)}, bf16[2,256,256]{2,1,0:T(8,128)(2,1)S(1)}, u32[]{:S(2)}, u32[]{:S(2)}) collective-permute-start(bf16[2,256,256]{2,1,0:T(8,128)(2,1)S(1)} %get-tuple-element.43), channel_id=1, source_target_pairs={{0,8},{4,12},{8,0},{12,4},{1,9},{5,13},{9,1},{13,5},{2,10},{6,14},... | collective-permute-start | bytes 786440 | tf_op jit(solution)/shard_map/ppermute | solution.py:24
  193.5 4.0 %collective-permute-start.28 = (bf16[2,256,256]{2,1,0:T(8,128)(2,1)S(1)}, bf16[2,256,256]{2,1,0:T(8,128)(2,1)S(1)}, u32[]{:S(2)}, u32[]{:S(2)}) collective-permute-start(bf16[2,256,256]{2,1,0:T(8,128)(2,1)S(1)} %get-tuple-element.45), channel_id=1, source_target_pairs={{0,12},{4,8},{8,4},{12,0},{1,13},{5,9},{9,5},{13,1},{2,14},{6,10},... | collective-permute-start | bytes 786440 | tf_op jit(solution)/shard_map/ppermute | solution.py:24
  197.5 3.1 %collective-permute-start.27 = (bf16[2,256,256]{2,1,0:T(8,128)(2,1)S(1)}, bf16[2,256,256]{2,1,0:T(8,128)(2,1)S(1)}, u32[]{:S(2)}, u32[]{:S(2)}) collective-permute-start(bf16[2,256,256]{2,1,0:T(8,128)(2,1)S(1)} %get-tuple-element.46), channel_id=1, source_target_pairs={{0,8},{4,12},{8,0},{12,4},{1,9},{5,13},{9,1},{13,5},{2,10},{6,14},... | collective-permute-start | bytes 786440 | tf_op jit(solution)/shard_map/ppermute | solution.py:24
  200.8 7.3 %collective-permute-start.33 = (bf16[256,256]{1,0:T(8,128)(2,1)S(1)}, bf16[256,256]{1,0:T(8,128)(2,1)S(1)}, u32[]{:S(2)}, u32[]{:S(2)}) collective-permute-start(bf16[256,256]{1,0:T(8,128)(2,1)S(1)} %get-tuple-element.47), channel_id=1, source_target_pairs={{0,64},{2,66},{64,0},{66,2},{1,65},{3,67},{65,1},{67,3},{4,68},{6,... | collective-permute-start | bytes 393224 | tf_op jit(solution)/shard_map/ppermute | solution.py:24
  211.7 7.3 %collective-permute-start.35 = (bf16[256,256]{1,0:T(8,128)(2,1)S(1)}, bf16[256,256]{1,0:T(8,128)(2,1)S(1)}, u32[]{:S(2)}, u32[]{:S(2)}) collective-permute-start(bf16[256,256]{1,0:T(8,128)(2,1)S(1)} %fusion.5), channel_id=1, source_target_pairs={{0,2},{2,0},{64,66},{66,64},{1,3},{3,1},{65,67},{67,65},{4,6},{6,4... | collective-permute-start | bytes 393224 | tf_op jit(solution)/shard_map/ppermute | solution.py:24
  219.3 5.2 %collective-permute-done.34 = bf16[256,256]{1,0:T(8,128)(2,1)S(1)} collective-permute-done((bf16[256,256]{1,0:T(8,128)(2,1)S(1)}, bf16[256,256]{1,0:T(8,128)(2,1)S(1)}, u32[]{:S(2)}, u32[]{:S(2)}) %collective-permute-start.34) | collective-permute-done | bytes 131104 | tf_op jit(solution)/shard_map/ppermute | solution.py:24
  224.5 7.8 %collective-permute-done.35 = bf16[256,256]{1,0:T(8,128)(2,1)S(1)} collective-permute-done((bf16[256,256]{1,0:T(8,128)(2,1)S(1)}, bf16[256,256]{1,0:T(8,128)(2,1)S(1)}, u32[]{:S(2)}, u32[]{:S(2)}) %collective-permute-start.35) | collective-permute-done | bytes 131104 | tf_op jit(solution)/shard_map/ppermute | solution.py:24
  (89 shorter events, 51.2 us)
Async XLA Ops:
  1.6 34.3 %collective-permute-start.1 = (bf16[272,256]{1,0:T(8,128)(2,1)S(1)}, bf16[272,256]{1,0:T(8,128)(2,1)S(1)}, u32[]{:S(2)}, u32[]{:S(2)}) collective-permute-start(bf16[272,256]{1,0:T(8,128)(2,1)S(1)} %get-tuple-element.54), channel_id=1, source_target_pairs={{0,64},{2,66},{64,0},{66,2},{1,65},{3,67},{65,1},{67,3},{4,68},{6,... | collective-permute-start | bytes 417800 | tf_op jit(solution)/shard_map/ppermute | solution.py:24
  11.3 24.6 %collective-permute-start = (bf16[272,256]{1,0:T(8,128)(2,1)S(1)}, bf16[272,256]{1,0:T(8,128)(2,1)S(1)}, u32[]{:S(2)}, u32[]{:S(2)}) collective-permute-start(bf16[272,256]{1,0:T(8,128)(2,1)S(1)} %get-tuple-element.54), channel_id=1, source_target_pairs={{0,2},{2,0},{64,66},{66,64},{1,3},{3,1},{65,67},{67,65},{4,6},{6,4... | collective-permute-start | bytes 417800 | tf_op jit(solution)/shard_map/ppermute | solution.py:24
  21.9 26.3 %collective-permute-start.2 = (bf16[272,256]{1,0:T(8,128)(2,1)S(1)}, bf16[272,256]{1,0:T(8,128)(2,1)S(1)}, u32[]{:S(2)}, u32[]{:S(2)}) collective-permute-start(bf16[272,256]{1,0:T(8,128)(2,1)S(1)} %get-tuple-element.54), channel_id=1, source_target_pairs={{0,66},{2,64},{64,2},{66,0},{1,67},{3,65},{65,3},{67,1},{4,70},{6,... | collective-permute-start | bytes 417800 | tf_op jit(solution)/shard_map/ppermute | solution.py:24
  24.8 23.5 %collective-permute-start.4 = (bf16[128,384]{1,0:T(8,128)(2,1)S(1)}, bf16[128,384]{1,0:T(8,128)(2,1)S(1)}, u32[]{:S(2)}, u32[]{:S(2)}) collective-permute-start(bf16[128,384]{1,0:T(8,128)(2,1)S(1)} %get-tuple-element.51), channel_id=1, source_target_pairs={{0,1},{1,65},{64,0},{65,64},{2,3},{3,67},{66,2},{67,66},{4,5},{5,6... | collective-permute-start | bytes 294920 | tf_op jit(solution)/shard_map/ppermute | solution.py:34
  30.0 18.3 %collective-permute-start.3 = (bf16[128,384]{1,0:T(8,128)(2,1)S(1)}, bf16[128,384]{1,0:T(8,128)(2,1)S(1)}, u32[]{:S(2)}, u32[]{:S(2)}) collective-permute-start(bf16[128,384]{1,0:T(8,128)(2,1)S(1)} %get-tuple-element.52), channel_id=1, source_target_pairs={{0,0},{1,64},{64,1},{65,65},{2,2},{3,66},{66,3},{67,67},{4,4},{5,6... | collective-permute-start | bytes 294920 | tf_op jit(solution)/shard_map/ppermute | solution.py:33
  48.4 28.7 %collective-permute-start.9 = (bf16[4,272,256]{2,1,0:T(8,128)(2,1)S(1)}, bf16[4,272,256]{2,1,0:T(8,128)(2,1)S(1)}, u32[]{:S(2)}, u32[]{:S(2)}) collective-permute-start(bf16[4,272,256]{2,1,0:T(8,128)(2,1)S(1)} %pad_maximum_fusion.3), channel_id=1, source_target_pairs={{0,12},{4,8},{8,4},{12,0},{1,13},{5,9},{9,5},{13,1},{2,14},{6,10},... | collective-permute-start | bytes 1671176 | tf_op jit(solution)/shard_map/ppermute | solution.py:24
  51.8 25.3 %collective-permute-start.5 = (bf16[4,272,256]{2,1,0:T(8,128)(2,1)S(1)}, bf16[4,272,256]{2,1,0:T(8,128)(2,1)S(1)}, u32[]{:S(2)}, u32[]{:S(2)}) collective-permute-start(bf16[4,272,256]{2,1,0:T(8,128)(2,1)S(1)} %pad_maximum_fusion.3), channel_id=1, source_target_pairs={{0,4},{4,0},{8,12},{12,8},{1,5},{5,1},{9,13},{13,9},{2,6},{6,2},{1... | collective-permute-start | bytes 1671176 | tf_op jit(solution)/shard_map/ppermute | solution.py:24
  53.8 11.9 %collective-permute-start.8 = (bf16[2,128,384]{2,1,0:T(8,128)(2,1)S(1)}, bf16[2,128,384]{2,1,0:T(8,128)(2,1)S(1)}, u32[]{:S(2)}, u32[]{:S(2)}) collective-permute-start(bf16[2,128,384]{2,1,0:T(8,128)(2,1)S(1)} %pad_maximum_fusion.4), channel_id=1, source_target_pairs={{0,48},{16,32},{32,16},{48,0},{1,49},{17,33},{33,17},{49,1},{2,50}... | collective-permute-start | bytes 589832 | tf_op jit(solution)/shard_map/ppermute | solution.py:24
  56.2 20.7 %collective-permute-start.7 = (bf16[2,128,384]{2,1,0:T(8,128)(2,1)S(1)}, bf16[2,128,384]{2,1,0:T(8,128)(2,1)S(1)}, u32[]{:S(2)}, u32[]{:S(2)}) collective-permute-start(bf16[2,128,384]{2,1,0:T(8,128)(2,1)S(1)} %pad_maximum_fusion.4), channel_id=1, source_target_pairs={{0,32},{16,48},{32,0},{48,16},{1,33},{17,49},{33,1},{49,17},{2,34}... | collective-permute-start | bytes 589832 | tf_op jit(solution)/shard_map/ppermute | solution.py:24
  63.8 13.2 %collective-permute-start.6 = (bf16[2,128,384]{2,1,0:T(8,128)(2,1)S(1)}, bf16[2,128,384]{2,1,0:T(8,128)(2,1)S(1)}, u32[]{:S(2)}, u32[]{:S(2)}) collective-permute-start(bf16[2,128,384]{2,1,0:T(8,128)(2,1)S(1)} %pad_maximum_fusion.4), channel_id=1, source_target_pairs={{0,16},{16,0},{32,48},{48,32},{1,17},{17,1},{33,49},{49,33},{2,18}... | collective-permute-start | bytes 589832 | tf_op jit(solution)/shard_map/ppermute | solution.py:24
  77.1 29.5 %collective-permute-start.12 = (bf16[2,4,128,384]{3,2,1,0:T(8,128)(2,1)S(1)}, bf16[2,4,128,384]{3,2,1,0:T(8,128)(2,1)S(1)}, u32[]{:S(2)}, u32[]{:S(2)}) collective-permute-start(bf16[2,4,128,384]{3,2,1,0:T(8,128)(2,1)S(1)} %pad_maximum_fusion.1.w0), channel_id=1, source_target_pairs={{0,384},{128,256},{256,128},{384,0},{1,385},{129,257},{257,129},{3... | collective-permute-start | bytes 2359304 | tf_op jit(solution)/shard_map/ppermute | solution.py:24
  81.5 25.1 %collective-permute-start.11 = (bf16[2,4,128,384]{3,2,1,0:T(8,128)(2,1)S(1)}, bf16[2,4,128,384]{3,2,1,0:T(8,128)(2,1)S(1)}, u32[]{:S(2)}, u32[]{:S(2)}) collective-permute-start(bf16[2,4,128,384]{3,2,1,0:T(8,128)(2,1)S(1)} %pad_maximum_fusion.1.w0), channel_id=1, source_target_pairs={{0,128},{128,0},{256,384},{384,256},{1,129},{129,1},{257,385},{385... | collective-permute-start | bytes 2359304 | tf_op jit(solution)/shard_map/ppermute | solution.py:24
  83.4 16.5 %collective-permute-start.10 = (bf16[4,272,256]{2,1,0:T(8,128)(2,1)S(1)}, bf16[4,272,256]{2,1,0:T(8,128)(2,1)S(1)}, u32[]{:S(2)}, u32[]{:S(2)}) collective-permute-start(bf16[4,272,256]{2,1,0:T(8,128)(2,1)S(1)} %pad_maximum_fusion.3), channel_id=1, source_target_pairs={{0,8},{4,12},{8,0},{12,4},{1,9},{5,13},{9,1},{13,5},{2,10},{6,14},... | collective-permute-start | bytes 1671176 | tf_op jit(solution)/shard_map/ppermute | solution.py:24
  86.5 13.7 %collective-permute-start.14 = (bf16[384,128]{1,0:T(8,128)(2,1)S(1)}, bf16[384,128]{1,0:T(8,128)(2,1)S(1)}, u32[]{:S(2)}, u32[]{:S(2)}) collective-permute-start(bf16[384,128]{1,0:T(8,128)(2,1)S(1)} %get-tuple-element.49), channel_id=1, source_target_pairs={{0,1},{1,65},{64,0},{65,64},{2,3},{3,67},{66,2},{67,66},{4,5},{5,6... | collective-permute-start | bytes 294920 | tf_op jit(solution)/shard_map/ppermute | solution.py:34
  106.6 25.4 %collective-permute-start.15 = (bf16[4,4,272,256]{3,2,1,0:T(8,128)(2,1)S(1)}, bf16[4,4,272,256]{3,2,1,0:T(8,128)(2,1)S(1)}, u32[]{:S(2)}, u32[]{:S(2)}) collective-permute-start(bf16[4,4,272,256]{3,2,1,0:T(8,128)(2,1)S(1)} %pad_maximum_fusion.mine), channel_id=1, source_target_pairs={{0,1},{1,0},{2,3},{3,2},{4,5},{5,4},{6,7},{7,6},{8,9},{9,8},{10,11... | collective-permute-start | bytes 6684680 | tf_op jit(solution)/shard_map/ppermute | solution.py:24
  108.6 11.4 %collective-permute-start.20 = (bf16[2,384,128]{2,1,0:T(8,128)(2,1)S(1)}, bf16[2,384,128]{2,1,0:T(8,128)(2,1)S(1)}, u32[]{:S(2)}, u32[]{:S(2)}) collective-permute-start(bf16[2,384,128]{2,1,0:T(8,128)(2,1)S(1)} %pad_maximum_fusion.5), channel_id=1, source_target_pairs={{0,48},{16,32},{32,16},{48,0},{1,49},{17,33},{33,17},{49,1},{2,50}... | collective-permute-start | bytes 589832 | tf_op jit(solution)/shard_map/ppermute | solution.py:24
  112.5 18.7 %collective-permute-start.16 = (bf16[1,4,128,384]{3,2,1,0:T(8,128)(2,1)S(1)}, bf16[1,4,128,384]{3,2,1,0:T(8,128)(2,1)S(1)}, u32[]{:S(2)}, u32[]{:S(2)}) collective-permute-start(bf16[1,4,128,384]{3,2,1,0:T(8,128)(2,1)S(1)} %slice.48), channel_id=1, source_target_pairs={{0,128},{128,0},{256,384},{384,256},{1,129},{129,1},{257,385},{385... | collective-permute-start | bytes 1179656 | tf_op jit(solution)/shard_map/ppermute | solution.py:24
  116.0 15.3 %collective-permute-start.17 = (bf16[1,4,128,384]{3,2,1,0:T(8,128)(2,1)S(1)}, bf16[1,4,128,384]{3,2,1,0:T(8,128)(2,1)S(1)}, u32[]{:S(2)}, u32[]{:S(2)}) collective-permute-start(bf16[1,4,128,384]{3,2,1,0:T(8,128)(2,1)S(1)} %slice.49), channel_id=1, source_target_pairs={{0,384},{128,256},{256,128},{384,0},{1,385},{129,257},{257,129},{3... | collective-permute-start | bytes 1179656 | tf_op jit(solution)/shard_map/ppermute | solution.py:24
  118.1 12.8 %collective-permute-start.19 = (bf16[2,384,128]{2,1,0:T(8,128)(2,1)S(1)}, bf16[2,384,128]{2,1,0:T(8,128)(2,1)S(1)}, u32[]{:S(2)}, u32[]{:S(2)}) collective-permute-start(bf16[2,384,128]{2,1,0:T(8,128)(2,1)S(1)} %pad_maximum_fusion.5), channel_id=1, source_target_pairs={{0,32},{16,48},{32,0},{48,16},{1,33},{17,49},{33,1},{49,17},{2,34}... | collective-permute-start | bytes 589832 | tf_op jit(solution)/shard_map/ppermute | solution.py:24
  120.0 11.1 %collective-permute-start.18 = (bf16[2,384,128]{2,1,0:T(8,128)(2,1)S(1)}, bf16[2,384,128]{2,1,0:T(8,128)(2,1)S(1)}, u32[]{:S(2)}, u32[]{:S(2)}) collective-permute-start(bf16[2,384,128]{2,1,0:T(8,128)(2,1)S(1)} %pad_maximum_fusion.5), channel_id=1, source_target_pairs={{0,16},{16,0},{32,48},{48,32},{1,17},{17,1},{33,49},{49,33},{2,18}... | collective-permute-start | bytes 589832 | tf_op jit(solution)/shard_map/ppermute | solution.py:24
  133.4 20.0 %collective-permute-start.22 = (bf16[2,4,384,128]{3,2,1,0:T(8,128)(2,1)S(1)}, bf16[2,4,384,128]{3,2,1,0:T(8,128)(2,1)}, u32[]{:S(2)}, u32[]{:S(2)}) collective-permute-start(bf16[2,4,384,128]{3,2,1,0:T(8,128)(2,1)S(1)} %pad_maximum_fusion.2.w0), channel_id=1, source_target_pairs={{0,384},{128,256},{256,128},{384,0},{1,385},{129,257},{257,129},{3... | collective-permute-start | bytes 2359304 | tf_op jit(solution)/shard_map/ppermute | solution.py:24
  137.8 18.5 %collective-permute-start.21 = (bf16[2,4,384,128]{3,2,1,0:T(8,128)(2,1)S(1)}, bf16[2,4,384,128]{3,2,1,0:T(8,128)(2,1)}, u32[]{:S(2)}, u32[]{:S(2)}) collective-permute-start(bf16[2,4,384,128]{3,2,1,0:T(8,128)(2,1)S(1)} %pad_maximum_fusion.2.w0), channel_id=1, source_target_pairs={{0,128},{128,0},{256,384},{384,256},{1,129},{129,1},{257,385},{385... | collective-permute-start | bytes 2359304 | tf_op jit(solution)/shard_map/ppermute | solution.py:24
  179.3 11.9 %collective-permute-start.25 = (bf16[4,2,256,256]{3,2,1,0:T(8,128)(2,1)S(1)}, bf16[4,2,256,256]{3,2,1,0:T(8,128)(2,1)S(1)}, u32[]{:S(2)}, u32[]{:S(2)}) collective-permute-start(bf16[4,2,256,256]{3,2,1,0:T(8,128)(2,1)S(1)} %get-tuple-element.34), channel_id=1, source_target_pairs={{0,1},{1,0},{2,3},{3,2},{4,5},{5,4},{6,7},{7,6},{8,9},{9,8},{10,11... | collective-permute-start | bytes 3145736 | tf_op jit(solution)/shard_map/ppermute | solution.py:24
  181.6 15.9 %collective-permute-start.30 = (bf16[2,256,256]{2,1,0:T(8,128)(2,1)S(1)}, bf16[2,256,256]{2,1,0:T(8,128)(2,1)S(1)}, u32[]{:S(2)}, u32[]{:S(2)}) collective-permute-start(bf16[2,256,256]{2,1,0:T(8,128)(2,1)S(1)} %get-tuple-element.41), channel_id=1, source_target_pairs={{0,4},{4,0},{8,12},{12,8},{1,5},{5,1},{9,13},{13,9},{2,6},{6,2},{1... | collective-permute-start | bytes 786440 | tf_op jit(solution)/shard_map/ppermute | solution.py:24
  183.8 16.8 %collective-permute-start.32 = (bf16[2,256,256]{2,1,0:T(8,128)(2,1)S(1)}, bf16[2,256,256]{2,1,0:T(8,128)(2,1)S(1)}, u32[]{:S(2)}, u32[]{:S(2)}) collective-permute-start(bf16[2,256,256]{2,1,0:T(8,128)(2,1)S(1)} %get-tuple-element.42), channel_id=1, source_target_pairs={{0,12},{4,8},{8,4},{12,0},{1,13},{5,9},{9,5},{13,1},{2,14},{6,10},... | collective-permute-start | bytes 786440 | tf_op jit(solution)/shard_map/ppermute | solution.py:24
  188.1 12.5 %collective-permute-start.31 = (bf16[2,256,256]{2,1,0:T(8,128)(2,1)S(1)}, bf16[2,256,256]{2,1,0:T(8,128)(2,1)S(1)}, u32[]{:S(2)}, u32[]{:S(2)}) collective-permute-start(bf16[2,256,256]{2,1,0:T(8,128)(2,1)S(1)} %get-tuple-element.43), channel_id=1, source_target_pairs={{0,8},{4,12},{8,0},{12,4},{1,9},{5,13},{9,1},{13,5},{2,10},{6,14},... | collective-permute-start | bytes 786440 | tf_op jit(solution)/shard_map/ppermute | solution.py:24
  191.6 18.6 %collective-permute-start.26 = (bf16[2,256,256]{2,1,0:T(8,128)(2,1)S(1)}, bf16[2,256,256]{2,1,0:T(8,128)(2,1)S(1)}, u32[]{:S(2)}, u32[]{:S(2)}) collective-permute-start(bf16[2,256,256]{2,1,0:T(8,128)(2,1)S(1)} %get-tuple-element.44), channel_id=1, source_target_pairs={{0,4},{4,0},{8,12},{12,8},{1,5},{5,1},{9,13},{13,9},{2,6},{6,2},{1... | collective-permute-start | bytes 786440 | tf_op jit(solution)/shard_map/ppermute | solution.py:24
  193.5 18.0 %collective-permute-start.28 = (bf16[2,256,256]{2,1,0:T(8,128)(2,1)S(1)}, bf16[2,256,256]{2,1,0:T(8,128)(2,1)S(1)}, u32[]{:S(2)}, u32[]{:S(2)}) collective-permute-start(bf16[2,256,256]{2,1,0:T(8,128)(2,1)S(1)} %get-tuple-element.45), channel_id=1, source_target_pairs={{0,12},{4,8},{8,4},{12,0},{1,13},{5,9},{9,5},{13,1},{2,14},{6,10},... | collective-permute-start | bytes 786440 | tf_op jit(solution)/shard_map/ppermute | solution.py:24
  197.5 14.0 %collective-permute-start.27 = (bf16[2,256,256]{2,1,0:T(8,128)(2,1)S(1)}, bf16[2,256,256]{2,1,0:T(8,128)(2,1)S(1)}, u32[]{:S(2)}, u32[]{:S(2)}) collective-permute-start(bf16[2,256,256]{2,1,0:T(8,128)(2,1)S(1)} %get-tuple-element.46), channel_id=1, source_target_pairs={{0,8},{4,12},{8,0},{12,4},{1,9},{5,13},{9,1},{13,5},{2,10},{6,14},... | collective-permute-start | bytes 786440 | tf_op jit(solution)/shard_map/ppermute | solution.py:24
  200.8 18.5 %collective-permute-start.33 = (bf16[256,256]{1,0:T(8,128)(2,1)S(1)}, bf16[256,256]{1,0:T(8,128)(2,1)S(1)}, u32[]{:S(2)}, u32[]{:S(2)}) collective-permute-start(bf16[256,256]{1,0:T(8,128)(2,1)S(1)} %get-tuple-element.47), channel_id=1, source_target_pairs={{0,64},{2,66},{64,0},{66,2},{1,65},{3,67},{65,1},{67,3},{4,68},{6,... | collective-permute-start | bytes 393224 | tf_op jit(solution)/shard_map/ppermute | solution.py:24
  208.1 16.5 %collective-permute-start.34 = (bf16[256,256]{1,0:T(8,128)(2,1)S(1)}, bf16[256,256]{1,0:T(8,128)(2,1)S(1)}, u32[]{:S(2)}, u32[]{:S(2)}) collective-permute-start(bf16[256,256]{1,0:T(8,128)(2,1)S(1)} %get-tuple-element.48), channel_id=1, source_target_pairs={{0,66},{2,64},{64,2},{66,0},{1,67},{3,65},{65,3},{67,1},{4,70},{6,... | collective-permute-start | bytes 393224 | tf_op jit(solution)/shard_map/ppermute | solution.py:24
  211.7 20.6 %collective-permute-start.35 = (bf16[256,256]{1,0:T(8,128)(2,1)S(1)}, bf16[256,256]{1,0:T(8,128)(2,1)S(1)}, u32[]{:S(2)}, u32[]{:S(2)}) collective-permute-start(bf16[256,256]{1,0:T(8,128)(2,1)S(1)} %fusion.5), channel_id=1, source_target_pairs={{0,2},{2,0},{64,66},{66,64},{1,3},{3,1},{65,67},{67,65},{4,6},{6,4... | collective-permute-start | bytes 393224 | tf_op jit(solution)/shard_map/ppermute | solution.py:24
  (15 other events, 216.4 us)

commit v5 on v4

--- a/solution.py
+++ b/solution.py
@@ -47,15 +47,28 @@
     return {a: lax.axis_index(a) for a in AXES}
 
 
-def hidden_kernel(place, mine, other, w0, w1, w2a, w2b, w3, act):
+def hidden_kernel(place, *refs):
+    far, act, held, sems = refs[:7], refs[7], refs[8:15], refs[15]
     x, zq, y, zh, c = (place[i] for i in range(5))
+    copies = []
+    for i in range(far[0].shape[0]):
+        for ref, near in zip(far[:2], held[:2]):
+            copies.append(pltpu.make_async_copy(ref.at[i], near.at[i], sems.at[len(copies)]))
+    for ref, near in zip(far[2:], held[2:]):
+        copies.append(pltpu.make_async_copy(ref, near, sems.at[len(copies)]))
+    for copy in copies:
+        copy.start()
+    mine, other, w0, w1, w2a, w2b, w3 = held
     cores = (mine, other)
     rows = act.shape[1]
     width = mine.shape[3]
     count = 2 * mine.shape[0] * 2 * width
     slots = [[w.at[s] for s in range(2)] for w in (w0, w1)] + [[w2a, w2b]] + [[w3.at[s] for s in range(2)]]
+    for copy in copies[:8]:
+        copy.wait()
+    norms = []
     for a in range(2):
-        blocks = [(ref, i, 2 * a + j) for ref in cores for i in range(4) for j in range(2)]
+        blocks = [(ref, i, 2 * a + j) for i in range(4) for ref in cores for j in range(2)]
         total = jnp.zeros((rows, width), jnp.float32)
         for ref, i, j in blocks:
             total += ref[i, j, :rows, :].astype(jnp.float32)
@@ -64,7 +77,10 @@
         for ref, i, j in blocks:
             total += jnp.square(ref[i, j, :rows, :].astype(jnp.float32) - center)
         spread = jnp.sum(total, axis=1, keepdims=True) * (1.0 / count)
-        scale = lax.rsqrt(spread + epsilon)
+        norms.append((center, lax.rsqrt(spread + epsilon)))
+    for copy in copies[8:]:
+        copy.wait()
+    for a, (center, scale) in enumerate(norms):
         acc = jnp.zeros((rows, act.shape[2]), jnp.float32)
         for k in range(4):
             i = x ^ k ^ y
@@ -99,14 +115,17 @@
                 ).astype(ref.dtype)
 
 
-def call(kernel, out_shape, flops, *operands):
+def call(kernel, out_shape, flops, *operands, copied=False):
     vmem = pl.BlockSpec(memory_space=pltpu.VMEM)
+    given = pl.BlockSpec(memory_space=pltpu.HBM) if copied else vmem
     size = sum(o.size * o.dtype.itemsize for o in operands)
+    scratch = [pltpu.VMEM(o.shape, o.dtype) for o in operands[1:]]
     return pl.pallas_call(
         kernel,
         out_shape=out_shape,
-        in_specs=[pl.BlockSpec(memory_space=pltpu.SMEM)] + [vmem] * (len(operands) - 1),
+        in_specs=[pl.BlockSpec(memory_space=pltpu.SMEM)] + [given] * (len(operands) - 1),
         out_specs=jax.tree.map(lambda _: vmem, out_shape),
+        scratch_shapes=scratch + [pltpu.SemaphoreType.DMA((16,))] if copied else [],
         compiler_params=pltpu.CompilerParams(vmem_limit_bytes=40 * 1024 * 1024),
         cost_estimate=pl.CostEstimate(flops=flops, bytes_accessed=size, transcendentals=0),
     )(*operands)
@@ -128,29 +147,32 @@
     swapped = swap_halves(weight_half(zt, 1, w_inner), weight_half(1 - zt, 1, w_inner))
 
     inner = after(jnp.stack(swapped), both)
-    both = after(both, *swapped)
     inner = jnp.stack([inner] + [send(inner, ("zq",), k) for k in (1, 2, 3)], axis=1)
-    y1, y3 = from_neighbours(both, "y")
-
-    in1, in3 = from_neighbours(after(inner, y1, y3), "x")
-    swapped = swap_halves(*(weight_half(h, 0, after(w_outer, inner, y1, y3)) for h in (zt, 1 - zt)))
-    y2 = send(after(both, inner, y1, y3), ("y",), 2)
+
+    in1, in3 = from_neighbours(inner, "x")
+    swapped = swap_halves(*(weight_half(h, 0, after(w_outer, inner)) for h in (zt, 1 - zt)))
+    y1 = send(after(both, inner), ("y",), 1)
+    outer = jnp.stack(swapped)
+    second = send(outer, ("zq",), 2)
+    y3 = send(after(both, y1, *swapped), ("y",), 3)
+
+    in2a, in2b = from_far(after(in1, second, y1), after(in3, second, y1), "x", 1)
+    pair = send(after(jnp.stack([outer, second], axis=1), in1, in3), ("zq",), 1)
+    outer = jnp.stack([outer, pair[:, 0], second, pair[:, 1]], axis=1)
+    y2 = send(after(both, in1, in3, y3, second), ("y",), 2)
+
+    out1, out3 = from_neighbours(after(outer, in2a, in2b, y3), "x")
     both = jnp.stack([both, y1, y2, y3])
-
-    in2a, in2b = from_far(after(in1, y2, *swapped), after(in3, y2, *swapped), "x", 1)
-    other = send(after(both, in1, in3, *swapped), ("c",), 1)
-    outer = after(jnp.stack(swapped), in1, in3, y2)
-    outer = jnp.stack([outer] + [send(outer, ("zq",), k) for k in (1, 2, 3)], axis=1)
-
-    out1, out3 = from_neighbours(after(outer, in2a, in2b, other), "x")
+    other = send(after(both, outer, in2a, in2b), ("c",), 1)
+
+    out2a, out2b = from_far(after(out1, other), after(out3, other), "x", 1)
 
     flops = 2 * 2 * rows * half * 16 * cols
     act = call(
         hidden_kernel,
         jax.ShapeDtypeStruct((2, rows, half), jnp.bfloat16),
-        flops, place, both, other, inner, in1, in2a[0], in2b[0], in3,
+        flops, place, both, other, inner, in1, in2a[0], in2b[0], in3, copied=True,
     )
-    out2a, out2b = from_far(after(out1, act), after(out3, act), "x", 1)
     shape = jax.ShapeDtypeStruct((4, 2, rows, cols), jnp.bfloat16)
     outer_all = (outer, out1, out2a[0], out2b[0], out3)
     parts = []

time: 236 us -> 251 us (1.064)
  the two profiles are of different devices: /device:TPU:1 before, /device:TPU:40 now
where the time goes in v5:
time: 251 us; the launch traced here: 249 us
  starting transfers between devices  135 us (54%)
  waiting for transfers between devices  86.4 us (34%)
  local copies, waits for them, and re-layouts  13.8 us (5%)
  Pallas kernels  10.6 us (4%)
  other arithmetic  3.17 us (1%)
    ppermute x31, starting transfers between devices, send(): return lax.ppermute(value, axes, [(i, i ^ k) for i in range(count)])  126 us
    ppermute x31, waiting for transfers between devices, send(): return lax.ppermute(value, axes, [(i, i ^ k) for i in range(count)])  77.9 us
    pallas_call x3, Pallas kernels, call(): pl.pallas_call(kernel, out_shape=out_shape, in_specs=[pl.BlockSpec(memory...  10.6 us
    unnamed x34, local copies, waits for them, and re-layouts  10.1 us
    ppermute x2, waiting for transfers between devices, swap_halves(): lax.ppermute(second, ('zt', 'c'), [(2 * a + b, 2 * b + 1 - a) for a, b in...  8.54 us
    ppermute x2, starting transfers between devices, swap_halves(): lax.ppermute(second, ('zt', 'c'), [(2 * a + b, 2 * b + 1 - a) for a, b in...  7.11 us
  transfers between devices with their start and end apart: 35, of which 12 were waited for; matrix products, arithmetic and copies ran while one was open for 2% of the time, Pallas kernels for 3%

profile of v5, /device:TPU:40, one launch (start us, length us, event | category | flops | bytes accessed | tf_op | source)
XLA Modules:
  0.0 249.3 jit_solution(12332364667072070887)
XLA Ops:
  5.3 18.2 %collective-permute-start.2 = (bf16[272,256]{1,0:T(8,128)(2,1)S(1)}, bf16[272,256]{1,0:T(8,128)(2,1)S(1)}, u32[]{:S(2)}, u32[]{:S(2)}) collective-permute-start(bf16[272,256]{1,0:T(8,128)(2,1)S(1)} %get-tuple-element.60), channel_id=1, source_target_pairs={{0,66},{2,64},{64,2},{66,0},{1,67},{3,65},{65,3},{67,1},{4,70},{6,... | collective-permute-start | bytes 417800 | tf_op jit(solution)/shard_map/ppermute | solution.py:24
  25.4 7.3 %collective-permute-start = (bf16[272,256]{1,0:T(8,128)(2,1)S(1)}, bf16[272,256]{1,0:T(8,128)(2,1)S(1)}, u32[]{:S(2)}, u32[]{:S(2)}) collective-permute-start(bf16[272,256]{1,0:T(8,128)(2,1)S(1)} %get-tuple-element.60), channel_id=1, source_target_pairs={{0,2},{2,0},{64,66},{66,64},{1,3},{3,1},{65,67},{67,65},{4,6},{6,4... | collective-permute-start | bytes 417800 | tf_op jit(solution)/shard_map/ppermute | solution.py:24
  32.7 16.3 %collective-permute-done.1 = bf16[272,256]{1,0:T(8,128)(2,1)S(1)} collective-permute-done((bf16[272,256]{1,0:T(8,128)(2,1)S(1)}, bf16[272,256]{1,0:T(8,128)(2,1)S(1)}, u32[]{:S(2)}, u32[]{:S(2)}) %collective-permute-start.1) | collective-permute-done | bytes 139296 | tf_op jit(solution)/shard_map/ppermute | solution.py:24
  49.1 7.4 %collective-permute-start.7 = (bf16[2,128,384]{2,1,0:T(8,128)(2,1)S(1)}, bf16[2,128,384]{2,1,0:T(8,128)(2,1)S(1)}, u32[]{:S(2)}, u32[]{:S(2)}) collective-permute-start(bf16[2,128,384]{2,1,0:T(8,128)(2,1)S(1)} %pad_maximum_fusion.5), channel_id=1, source_target_pairs={{0,48},{16,32},{32,16},{48,0},{1,49},{17,33},{33,17},{49,1},{2,50}... | collective-permute-start | bytes 589832 | tf_op jit(solution)/shard_map/ppermute | solution.py:24
  56.6 5.1 %collective-permute-start.6 = (bf16[2,128,384]{2,1,0:T(8,128)(2,1)S(1)}, bf16[2,128,384]{2,1,0:T(8,128)(2,1)S(1)}, u32[]{:S(2)}, u32[]{:S(2)}) collective-permute-start(bf16[2,128,384]{2,1,0:T(8,128)(2,1)S(1)} %pad_maximum_fusion.5), channel_id=1, source_target_pairs={{0,32},{16,48},{32,0},{48,16},{1,33},{17,49},{33,1},{49,17},{2,34}... | collective-permute-start | bytes 589832 | tf_op jit(solution)/shard_map/ppermute | solution.py:24
  63.6 7.1 %collective-permute-done.7 = bf16[2,128,384]{2,1,0:T(8,128)(2,1)S(1)} collective-permute-done((bf16[2,128,384]{2,1,0:T(8,128)(2,1)S(1)}, bf16[2,128,384]{2,1,0:T(8,128)(2,1)S(1)}, u32[]{:S(2)}, u32[]{:S(2)}) %collective-permute-start.7) | collective-permute-done | bytes 196640 | tf_op jit(solution)/shard_map/ppermute | solution.py:24
  70.7 2.6 %collective-permute-done.6 = bf16[2,128,384]{2,1,0:T(8,128)(2,1)S(1)} collective-permute-done((bf16[2,128,384]{2,1,0:T(8,128)(2,1)S(1)}, bf16[2,128,384]{2,1,0:T(8,128)(2,1)S(1)}, u32[]{:S(2)}, u32[]{:S(2)}) %collective-permute-start.6) | collective-permute-done | bytes 196640 | tf_op jit(solution)/shard_map/ppermute | solution.py:24
  75.6 3.7 %collective-permute-start.9 = (bf16[2,4,128,384]{3,2,1,0:T(8,128)(2,1)S(1)}, bf16[2,4,128,384]{3,2,1,0:T(8,128)(2,1)S(1)}, u32[]{:S(2)}, u32[]{:S(2)}) collective-permute-start(bf16[2,4,128,384]{3,2,1,0:T(8,128)(2,1)S(1)} %pad_maximum_fusion.1.refs_2_), channel_id=1, source_target_pairs={{0,128},{128,0},{256,384},{384,256},{1,129},{129,1},{257,385},{385... | collective-permute-start | bytes 2359304 | tf_op jit(solution)/shard_map/ppermute | solution.py:24
  79.2 4.0 %collective-permute-start.10 = (bf16[2,4,128,384]{3,2,1,0:T(8,128)(2,1)S(1)}, bf16[2,4,128,384]{3,2,1,0:T(8,128)(2,1)S(1)}, u32[]{:S(2)}, u32[]{:S(2)}) collective-permute-start(bf16[2,4,128,384]{3,2,1,0:T(8,128)(2,1)S(1)} %pad_maximum_fusion.1.refs_2_), channel_id=1, source_target_pairs={{0,384},{128,256},{256,128},{384,0},{1,385},{129,257},{257,129},{3... | collective-permute-start | bytes 2359304 | tf_op jit(solution)/shard_map/ppermute | solution.py:24
  83.9 5.1 %collective-permute-start.12 = (bf16[384,128]{1,0:T(8,128)(2,1)S(1)}, bf16[384,128]{1,0:T(8,128)(2,1)S(1)}, u32[]{:S(2)}, u32[]{:S(2)}) collective-permute-start(bf16[384,128]{1,0:T(8,128)(2,1)S(1)} %get-tuple-element.55), channel_id=1, source_target_pairs={{0,1},{1,65},{64,0},{65,64},{2,3},{3,67},{66,2},{67,66},{4,5},{5,6... | collective-permute-start | bytes 294920 | tf_op jit(solution)/shard_map/ppermute | solution.py:34
  89.0 8.5 %collective-permute-done.12 = bf16[384,128]{1,0:T(8,128)(2,1)S(1)} collective-permute-done((bf16[384,128]{1,0:T(8,128)(2,1)S(1)}, bf16[384,128]{1,0:T(8,128)(2,1)S(1)}, u32[]{:S(2)}, u32[]{:S(2)}) %collective-permute-start.12) | collective-permute-done | bytes 98336 | tf_op jit(solution)/shard_map/ppermute | solution.py:34
  97.6 4.3 %collective-permute-start.13 = (bf16[4,272,256]{2,1,0:T(8,128)(2,1)S(1)}, bf16[4,272,256]{2,1,0:T(8,128)(2,1)S(1)}, u32[]{:S(2)}, u32[]{:S(2)}) collective-permute-start(bf16[4,272,256]{2,1,0:T(8,128)(2,1)S(1)} %get-tuple-element.25), channel_id=1, source_target_pairs={{0,12},{4,8},{8,4},{12,0},{1,13},{5,9},{9,5},{13,1},{2,14},{6,10},... | collective-permute-start | bytes 1671176 | tf_op jit(solution)/shard_map/ppermute | solution.py:24
  104.2 7.5 %collective-permute-done.14 = bf16[2,384,128]{2,1,0:T(8,128)(2,1)S(1)} collective-permute-done((bf16[2,384,128]{2,1,0:T(8,128)(2,1)S(1)}, bf16[2,384,128]{2,1,0:T(8,128)(2,1)S(1)}, u32[]{:S(2)}, u32[]{:S(2)}) %collective-permute-start.14) | collective-permute-done | bytes 196640 | tf_op jit(solution)/shard_map/ppermute | solution.py:24
  111.8 5.7 %collective-permute-start.16 = (bf16[2,2,384,128]{3,2,1,0:T(8,128)(2,1)S(1)}, bf16[2,2,384,128]{3,2,1,0:T(8,128)(2,1)S(1)}, u32[]{:S(2)}, u32[]{:S(2)}) collective-permute-start(bf16[2,2,384,128]{3,2,1,0:T(8,128)(2,1)S(1)} %pad_maximum_fusion.4), channel_id=1, source_target_pairs={{0,16},{16,0},{32,48},{48,32},{1,17},{17,1},{33,49},{49,33},{2,18}... | collective-permute-start | bytes 1179656 | tf_op jit(solution)/shard_map/ppermute | solution.py:24
  117.5 3.1 %collective-permute-start.15 = (bf16[4,272,256]{2,1,0:T(8,128)(2,1)S(1)}, bf16[4,272,256]{2,1,0:T(8,128)(2,1)S(1)}, u32[]{:S(2)}, u32[]{:S(2)}) collective-permute-start(bf16[4,272,256]{2,1,0:T(8,128)(2,1)S(1)} %get-tuple-element.25), channel_id=1, source_target_pairs={{0,8},{4,12},{8,0},{12,4},{1,9},{5,13},{9,1},{13,5},{2,10},{6,14},... | collective-permute-start | bytes 1671176 | tf_op jit(solution)/shard_map/ppermute | solution.py:24
  120.7 2.5 %collective-permute-start.17 = (bf16[1,4,128,384]{3,2,1,0:T(8,128)(2,1)S(1)}, bf16[1,4,128,384]{3,2,1,0:T(8,128)(2,1)S(1)}, u32[]{:S(2)}, u32[]{:S(2)}) collective-permute-start(bf16[1,4,128,384]{3,2,1,0:T(8,128)(2,1)S(1)} %slice.56), channel_id=1, source_target_pairs={{0,128},{128,0},{256,384},{384,256},{1,129},{129,1},{257,385},{385... | collective-permute-start | bytes 1179656 | tf_op jit(solution)/shard_map/ppermute | solution.py:24
  123.2 2.8 %collective-permute-start.18 = (bf16[1,4,128,384]{3,2,1,0:T(8,128)(2,1)S(1)}, bf16[1,4,128,384]{3,2,1,0:T(8,128)(2,1)S(1)}, u32[]{:S(2)}, u32[]{:S(2)}) collective-permute-start(bf16[1,4,128,384]{3,2,1,0:T(8,128)(2,1)S(1)} %slice.57), channel_id=1, source_target_pairs={{0,384},{128,256},{256,128},{384,0},{1,385},{129,257},{257,129},{3... | collective-permute-start | bytes 1179656 | tf_op jit(solution)/shard_map/ppermute | solution.py:24
  126.3 8.2 %collective-permute-done.15 = bf16[4,272,256]{2,1,0:T(8,128)(2,1)S(1)} collective-permute-done((bf16[4,272,256]{2,1,0:T(8,128)(2,1)S(1)}, bf16[4,272,256]{2,1,0:T(8,128)(2,1)S(1)}, u32[]{:S(2)}, u32[]{:S(2)}) %collective-permute-start.15) | collective-permute-done | bytes 557088 | tf_op jit(solution)/shard_map/ppermute | solution.py:24
  138.6 2.9 %collective-permute-start.21 = (bf16[2,4,384,128]{3,2,1,0:T(8,128)(2,1)S(1)}, bf16[2,4,384,128]{3,2,1,0:T(8,128)(2,1)S(1)}, u32[]{:S(2)}, u32[]{:S(2)}) collective-permute-start(bf16[2,4,384,128]{3,2,1,0:T(8,128)(2,1)S(1)} %pad_maximum_fusion.2.w0), channel_id=1, source_target_pairs={{0,384},{128,256},{256,128},{384,0},{1,385},{129,257},{257,129},{3... | collective-permute-start | bytes 2359304 | tf_op jit(solution)/shard_map/ppermute | solution.py:24
  143.4 18.2 %collective-permute-done.21.w3 = bf16[2,4,384,128]{3,2,1,0:T(8,128)(2,1)S(1)} collective-permute-done((bf16[2,4,384,128]{3,2,1,0:T(8,128)(2,1)S(1)}, bf16[2,4,384,128]{3,2,1,0:T(8,128)(2,1)S(1)}, u32[]{:S(2)}, u32[]{:S(2)}) %collective-permute-start.21) | collective-permute-done | bytes 786464 | tf_op jit(solution)/shard_map/ppermute | solution.py:24
  166.8 2.9 %collective-permute-start.23 = (bf16[1,4,384,128]{3,2,1,0:T(8,128)(2,1)}, bf16[1,4,384,128]{3,2,1,0:T(8,128)(2,1)}, u32[]{:S(2)}, u32[]{:S(2)}) collective-permute-start(bf16[1,4,384,128]{3,2,1,0:T(8,128)(2,1)} %slice.59), channel_id=1, source_target_pairs={{0,384},{128,256},{256,128},{384,0},{1,385},{129,257},{257,129},{3... | collective-permute-start | bytes 1179656 | tf_op jit(solution)/shard_map/ppermute | solution.py:24
  176.8 6.0 %shard_map.46.act = bf16[2,256,384]{2,1,0:T(8,128)(2,1)S(1)} custom-call(s32[5]{0:T(128)S(1)} %stack.100.place, bf16[4,4,272,256]{3,2,1,0:T(8,128)(2,1)S(1)} %pad_maximum_fusion.refs_0_, bf16[4,4,272,256]{3,2,1,0:T(8,128)(2,1)S(1)} %copy-done.7, bf16[2,4,128,384]{3,2,1,0:T(8,128)(2,1)S(1)} %copy-done.5, bf16[2,4,128,384]{3,2,1,0:T(8,128)(2,1)S(1)} %copy-done.9, ...), custom_call_target="tpu_custom_call" | custom-call | flops 1610612736 | bytes 7602196 | tf_op jit(solution)/shard_map/pallas_call | solution.py:123
  192.2 3.5 %collective-permute-start.27 = (bf16[2,256,256]{2,1,0:T(8,128)(2,1)S(1)}, bf16[2,256,256]{2,1,0:T(8,128)(2,1)S(1)}, u32[]{:S(2)}, u32[]{:S(2)}) collective-permute-start(bf16[2,256,256]{2,1,0:T(8,128)(2,1)S(1)} %get-tuple-element.45), channel_id=1, source_target_pairs={{0,12},{4,8},{8,4},{12,0},{1,13},{5,9},{9,5},{13,1},{2,14},{6,10},... | collective-permute-start | bytes 786440 | tf_op jit(solution)/shard_map/ppermute | solution.py:24
  195.7 3.9 %collective-permute-start.26 = (bf16[2,256,256]{2,1,0:T(8,128)(2,1)S(1)}, bf16[2,256,256]{2,1,0:T(8,128)(2,1)S(1)}, u32[]{:S(2)}, u32[]{:S(2)}) collective-permute-start(bf16[2,256,256]{2,1,0:T(8,128)(2,1)S(1)} %get-tuple-element.46), channel_id=1, source_target_pairs={{0,8},{4,12},{8,0},{12,4},{1,9},{5,13},{9,1},{13,5},{2,10},{6,14},... | collective-permute-start | bytes 786440 | tf_op jit(solution)/shard_map/ppermute | solution.py:24
  202.4 3.5 %collective-permute-start.31 = (bf16[2,256,256]{2,1,0:T(8,128)(2,1)S(1)}, bf16[2,256,256]{2,1,0:T(8,128)(2,1)S(1)}, u32[]{:S(2)}, u32[]{:S(2)}) collective-permute-start(bf16[2,256,256]{2,1,0:T(8,128)(2,1)S(1)} %get-tuple-element.42), channel_id=1, source_target_pairs={{0,12},{4,8},{8,4},{12,0},{1,13},{5,9},{9,5},{13,1},{2,14},{6,10},... | collective-permute-start | bytes 786440 | tf_op jit(solution)/shard_map/ppermute | solution.py:24
  205.9 3.9 %collective-permute-start.30 = (bf16[2,256,256]{2,1,0:T(8,128)(2,1)S(1)}, bf16[2,256,256]{2,1,0:T(8,128)(2,1)S(1)}, u32[]{:S(2)}, u32[]{:S(2)}) collective-permute-start(bf16[2,256,256]{2,1,0:T(8,128)(2,1)S(1)} %get-tuple-element.43), channel_id=1, source_target_pairs={{0,8},{4,12},{8,0},{12,4},{1,9},{5,13},{9,1},{13,5},{2,10},{6,14},... | collective-permute-start | bytes 786440 | tf_op jit(solution)/shard_map/ppermute | solution.py:24
  209.8 3.7 %collective-permute-start.29 = (bf16[2,256,256]{2,1,0:T(8,128)(2,1)S(1)}, bf16[2,256,256]{2,1,0:T(8,128)(2,1)S(1)}, u32[]{:S(2)}, u32[]{:S(2)}) collective-permute-start(bf16[2,256,256]{2,1,0:T(8,128)(2,1)S(1)} %get-tuple-element.41), channel_id=1, source_target_pairs={{0,4},{4,0},{8,12},{12,8},{1,5},{5,1},{9,13},{13,9},{2,6},{6,2},{1... | collective-permute-start | bytes 786440 | tf_op jit(solution)/shard_map/ppermute | solution.py:24
  213.7 7.3 %collective-permute-start.34 = (bf16[256,256]{1,0:T(8,128)(2,1)S(1)}, bf16[256,256]{1,0:T(8,128)(2,1)S(1)}, u32[]{:S(2)}, u32[]{:S(2)}) collective-permute-start(bf16[256,256]{1,0:T(8,128)(2,1)S(1)} %fusion.5), channel_id=1, source_target_pairs={{0,2},{2,0},{64,66},{66,64},{1,3},{3,1},{65,67},{67,65},{4,6},{6,4... | collective-permute-start | bytes 393224 | tf_op jit(solution)/shard_map/ppermute | solution.py:24
  223.2 5.4 %collective-permute-start.33 = (bf16[256,256]{1,0:T(8,128)(2,1)S(1)}, bf16[256,256]{1,0:T(8,128)(2,1)S(1)}, u32[]{:S(2)}, u32[]{:S(2)}) collective-permute-start(bf16[256,256]{1,0:T(8,128)(2,1)S(1)} %get-tuple-element.52), channel_id=1, source_target_pairs={{0,66},{2,64},{64,2},{66,0},{1,67},{3,65},{65,3},{67,1},{4,70},{6,... | collective-permute-start | bytes 393224 | tf_op jit(solution)/shard_map/ppermute | solution.py:24
  228.5 4.6 %collective-permute-start.32 = (bf16[256,256]{1,0:T(8,128)(2,1)S(1)}, bf16[256,256]{1,0:T(8,128)(2,1)S(1)}, u32[]{:S(2)}, u32[]{:S(2)}) collective-permute-start(bf16[256,256]{1,0:T(8,128)(2,1)S(1)} %get-tuple-element.51), channel_id=1, source_target_pairs={{0,64},{2,66},{64,0},{66,2},{1,65},{3,67},{65,1},{67,3},{4,68},{6,... | collective-permute-start | bytes 393224 | tf_op jit(solution)/shard_map/ppermute | solution.py:24
  233.1 7.5 %collective-permute-done.33 = bf16[256,256]{1,0:T(8,128)(2,1)S(1)} collective-permute-done((bf16[256,256]{1,0:T(8,128)(2,1)S(1)}, bf16[256,256]{1,0:T(8,128)(2,1)S(1)}, u32[]{:S(2)}, u32[]{:S(2)}) %collective-permute-start.33) | collective-permute-done | bytes 131104 | tf_op jit(solution)/shard_map/ppermute | solution.py:24
  240.7 8.0 %collective-permute-done.32 = bf16[256,256]{1,0:T(8,128)(2,1)S(1)} collective-permute-done((bf16[256,256]{1,0:T(8,128)(2,1)S(1)}, bf16[256,256]{1,0:T(8,128)(2,1)S(1)}, u32[]{:S(2)}, u32[]{:S(2)}) %collective-permute-start.32) | collective-permute-done | bytes 131104 | tf_op jit(solution)/shard_map/ppermute | solution.py:24
  (101 shorter events, 48.1 us)
Async XLA Ops:
  1.0 31.7 %collective-permute-start.4 = (bf16[128,384]{1,0:T(8,128)(2,1)S(1)}, bf16[128,384]{1,0:T(8,128)(2,1)S(1)}, u32[]{:S(2)}, u32[]{:S(2)}) collective-permute-start(bf16[128,384]{1,0:T(8,128)(2,1)S(1)} %get-tuple-element.58), channel_id=1, source_target_pairs={{0,1},{1,65},{64,0},{65,64},{2,3},{3,67},{66,2},{67,66},{4,5},{5,6... | collective-permute-start | bytes 294920 | tf_op jit(solution)/shard_map/ppermute | solution.py:34
  3.0 29.7 %collective-permute-start.3 = (bf16[128,384]{1,0:T(8,128)(2,1)S(1)}, bf16[128,384]{1,0:T(8,128)(2,1)S(1)}, u32[]{:S(2)}, u32[]{:S(2)}) collective-permute-start(bf16[128,384]{1,0:T(8,128)(2,1)S(1)} %get-tuple-element.57), channel_id=1, source_target_pairs={{0,0},{1,64},{64,1},{65,65},{2,2},{3,66},{66,3},{67,67},{4,4},{5,6... | collective-permute-start | bytes 294920 | tf_op jit(solution)/shard_map/ppermute | solution.py:33
  5.3 27.4 %collective-permute-start.2 = (bf16[272,256]{1,0:T(8,128)(2,1)S(1)}, bf16[272,256]{1,0:T(8,128)(2,1)S(1)}, u32[]{:S(2)}, u32[]{:S(2)}) collective-permute-start(bf16[272,256]{1,0:T(8,128)(2,1)S(1)} %get-tuple-element.60), channel_id=1, source_target_pairs={{0,66},{2,64},{64,2},{66,0},{1,67},{3,65},{65,3},{67,1},{4,70},{6,... | collective-permute-start | bytes 417800 | tf_op jit(solution)/shard_map/ppermute | solution.py:24
  23.5 25.5 %collective-permute-start.1 = (bf16[272,256]{1,0:T(8,128)(2,1)S(1)}, bf16[272,256]{1,0:T(8,128)(2,1)S(1)}, u32[]{:S(2)}, u32[]{:S(2)}) collective-permute-start(bf16[272,256]{1,0:T(8,128)(2,1)S(1)} %get-tuple-element.60), channel_id=1, source_target_pairs={{0,64},{2,66},{64,0},{66,2},{1,65},{3,67},{65,1},{67,3},{4,68},{6,... | collective-permute-start | bytes 417800 | tf_op jit(solution)/shard_map/ppermute | solution.py:24
  25.4 23.6 %collective-permute-start = (bf16[272,256]{1,0:T(8,128)(2,1)S(1)}, bf16[272,256]{1,0:T(8,128)(2,1)S(1)}, u32[]{:S(2)}, u32[]{:S(2)}) collective-permute-start(bf16[272,256]{1,0:T(8,128)(2,1)S(1)} %get-tuple-element.60), channel_id=1, source_target_pairs={{0,2},{2,0},{64,66},{66,64},{1,3},{3,1},{65,67},{67,65},{4,6},{6,4... | collective-permute-start | bytes 417800 | tf_op jit(solution)/shard_map/ppermute | solution.py:24
  49.1 21.6 %collective-permute-start.7 = (bf16[2,128,384]{2,1,0:T(8,128)(2,1)S(1)}, bf16[2,128,384]{2,1,0:T(8,128)(2,1)S(1)}, u32[]{:S(2)}, u32[]{:S(2)}) collective-permute-start(bf16[2,128,384]{2,1,0:T(8,128)(2,1)S(1)} %pad_maximum_fusion.5), channel_id=1, source_target_pairs={{0,48},{16,32},{32,16},{48,0},{1,49},{17,33},{33,17},{49,1},{2,50}... | collective-permute-start | bytes 589832 | tf_op jit(solution)/shard_map/ppermute | solution.py:24
  56.6 16.7 %collective-permute-start.6 = (bf16[2,128,384]{2,1,0:T(8,128)(2,1)S(1)}, bf16[2,128,384]{2,1,0:T(8,128)(2,1)S(1)}, u32[]{:S(2)}, u32[]{:S(2)}) collective-permute-start(bf16[2,128,384]{2,1,0:T(8,128)(2,1)S(1)} %pad_maximum_fusion.5), channel_id=1, source_target_pairs={{0,32},{16,48},{32,0},{48,16},{1,33},{17,49},{33,1},{49,17},{2,34}... | collective-permute-start | bytes 589832 | tf_op jit(solution)/shard_map/ppermute | solution.py:24
  61.7 11.6 %collective-permute-start.5 = (bf16[2,128,384]{2,1,0:T(8,128)(2,1)S(1)}, bf16[2,128,384]{2,1,0:T(8,128)(2,1)S(1)}, u32[]{:S(2)}, u32[]{:S(2)}) collective-permute-start(bf16[2,128,384]{2,1,0:T(8,128)(2,1)S(1)} %pad_maximum_fusion.5), channel_id=1, source_target_pairs={{0,16},{16,0},{32,48},{48,32},{1,17},{17,1},{33,49},{49,33},{2,18}... | collective-permute-start | bytes 589832 | tf_op jit(solution)/shard_map/ppermute | solution.py:24
  73.4 24.1 %collective-permute-start.8 = (bf16[4,272,256]{2,1,0:T(8,128)(2,1)S(1)}, bf16[4,272,256]{2,1,0:T(8,128)(2,1)S(1)}, u32[]{:S(2)}, u32[]{:S(2)}) collective-permute-start(bf16[4,272,256]{2,1,0:T(8,128)(2,1)S(1)} %get-tuple-element.25), channel_id=1, source_target_pairs={{0,4},{4,0},{8,12},{12,8},{1,5},{5,1},{9,13},{13,9},{2,6},{6,2},{1... | collective-permute-start | bytes 1671176 | tf_op jit(solution)/shard_map/ppermute | solution.py:24
  75.6 36.2 %collective-permute-start.9 = (bf16[2,4,128,384]{3,2,1,0:T(8,128)(2,1)S(1)}, bf16[2,4,128,384]{3,2,1,0:T(8,128)(2,1)S(1)}, u32[]{:S(2)}, u32[]{:S(2)}) collective-permute-start(bf16[2,4,128,384]{3,2,1,0:T(8,128)(2,1)S(1)} %pad_maximum_fusion.1.refs_2_), channel_id=1, source_target_pairs={{0,128},{128,0},{256,384},{384,256},{1,129},{129,1},{257,385},{385... | collective-permute-start | bytes 2359304 | tf_op jit(solution)/shard_map/ppermute | solution.py:24
  79.2 32.5 %collective-permute-start.10 = (bf16[2,4,128,384]{3,2,1,0:T(8,128)(2,1)S(1)}, bf16[2,4,128,384]{3,2,1,0:T(8,128)(2,1)S(1)}, u32[]{:S(2)}, u32[]{:S(2)}) collective-permute-start(bf16[2,4,128,384]{3,2,1,0:T(8,128)(2,1)S(1)} %pad_maximum_fusion.1.refs_2_), channel_id=1, source_target_pairs={{0,384},{128,256},{256,128},{384,0},{1,385},{129,257},{257,129},{3... | collective-permute-start | bytes 2359304 | tf_op jit(solution)/shard_map/ppermute | solution.py:24
  83.9 13.6 %collective-permute-start.12 = (bf16[384,128]{1,0:T(8,128)(2,1)S(1)}, bf16[384,128]{1,0:T(8,128)(2,1)S(1)}, u32[]{:S(2)}, u32[]{:S(2)}) collective-permute-start(bf16[384,128]{1,0:T(8,128)(2,1)S(1)} %get-tuple-element.55), channel_id=1, source_target_pairs={{0,1},{1,65},{64,0},{65,64},{2,3},{3,67},{66,2},{67,66},{4,5},{5,6... | collective-permute-start | bytes 294920 | tf_op jit(solution)/shard_map/ppermute | solution.py:34
  97.6 19.9 %collective-permute-start.13 = (bf16[4,272,256]{2,1,0:T(8,128)(2,1)S(1)}, bf16[4,272,256]{2,1,0:T(8,128)(2,1)S(1)}, u32[]{:S(2)}, u32[]{:S(2)}) collective-permute-start(bf16[4,272,256]{2,1,0:T(8,128)(2,1)S(1)} %get-tuple-element.25), channel_id=1, source_target_pairs={{0,12},{4,8},{8,4},{12,0},{1,13},{5,9},{9,5},{13,1},{2,14},{6,10},... | collective-permute-start | bytes 1671176 | tf_op jit(solution)/shard_map/ppermute | solution.py:24
  111.8 14.3 %collective-permute-start.16 = (bf16[2,2,384,128]{3,2,1,0:T(8,128)(2,1)S(1)}, bf16[2,2,384,128]{3,2,1,0:T(8,128)(2,1)S(1)}, u32[]{:S(2)}, u32[]{:S(2)}) collective-permute-start(bf16[2,2,384,128]{3,2,1,0:T(8,128)(2,1)S(1)} %pad_maximum_fusion.4), channel_id=1, source_target_pairs={{0,16},{16,0},{32,48},{48,32},{1,17},{17,1},{33,49},{49,33},{2,18}... | collective-permute-start | bytes 1179656 | tf_op jit(solution)/shard_map/ppermute | solution.py:24
  117.5 17.0 %collective-permute-start.15 = (bf16[4,272,256]{2,1,0:T(8,128)(2,1)S(1)}, bf16[4,272,256]{2,1,0:T(8,128)(2,1)S(1)}, u32[]{:S(2)}, u32[]{:S(2)}) collective-permute-start(bf16[4,272,256]{2,1,0:T(8,128)(2,1)S(1)} %get-tuple-element.25), channel_id=1, source_target_pairs={{0,8},{4,12},{8,0},{12,4},{1,9},{5,13},{9,1},{13,5},{2,10},{6,14},... | collective-permute-start | bytes 1671176 | tf_op jit(solution)/shard_map/ppermute | solution.py:24
  120.7 14.1 %collective-permute-start.17 = (bf16[1,4,128,384]{3,2,1,0:T(8,128)(2,1)S(1)}, bf16[1,4,128,384]{3,2,1,0:T(8,128)(2,1)S(1)}, u32[]{:S(2)}, u32[]{:S(2)}) collective-permute-start(bf16[1,4,128,384]{3,2,1,0:T(8,128)(2,1)S(1)} %slice.56), channel_id=1, source_target_pairs={{0,128},{128,0},{256,384},{384,256},{1,129},{129,1},{257,385},{385... | collective-permute-start | bytes 1179656 | tf_op jit(solution)/shard_map/ppermute | solution.py:24
  123.2 12.7 %collective-permute-start.18 = (bf16[1,4,128,384]{3,2,1,0:T(8,128)(2,1)S(1)}, bf16[1,4,128,384]{3,2,1,0:T(8,128)(2,1)S(1)}, u32[]{:S(2)}, u32[]{:S(2)}) collective-permute-start(bf16[1,4,128,384]{3,2,1,0:T(8,128)(2,1)S(1)} %slice.57), channel_id=1, source_target_pairs={{0,384},{128,256},{256,128},{384,0},{1,385},{129,257},{257,129},{3... | collective-permute-start | bytes 1179656 | tf_op jit(solution)/shard_map/ppermute | solution.py:24
  136.6 25.0 %collective-permute-start.19 = (bf16[4,4,272,256]{3,2,1,0:T(8,128)(2,1)S(1)}, bf16[4,4,272,256]{3,2,1,0:T(8,128)(2,1)S(1)}, u32[]{:S(2)}, u32[]{:S(2)}) collective-permute-start(bf16[4,4,272,256]{3,2,1,0:T(8,128)(2,1)S(1)} %pad_maximum_fusion.refs_0_), channel_id=1, source_target_pairs={{0,1},{1,0},{2,3},{3,2},{4,5},{5,4},{6,7},{7,6},{8,9},{9,8},{10,11... | collective-permute-start | bytes 6684680 | tf_op jit(solution)/shard_map/ppermute | solution.py:24
  138.6 23.0 %collective-permute-start.21 = (bf16[2,4,384,128]{3,2,1,0:T(8,128)(2,1)S(1)}, bf16[2,4,384,128]{3,2,1,0:T(8,128)(2,1)S(1)}, u32[]{:S(2)}, u32[]{:S(2)}) collective-permute-start(bf16[2,4,384,128]{3,2,1,0:T(8,128)(2,1)S(1)} %pad_maximum_fusion.2.w0), channel_id=1, source_target_pairs={{0,384},{128,256},{256,128},{384,0},{1,385},{129,257},{257,129},{3... | collective-permute-start | bytes 2359304 | tf_op jit(solution)/shard_map/ppermute | solution.py:24
  141.5 24.3 %collective-permute-start.20 = (bf16[2,4,384,128]{3,2,1,0:T(8,128)(2,1)S(1)}, bf16[2,4,384,128]{3,2,1,0:T(8,128)(2,1)S(1)}, u32[]{:S(2)}, u32[]{:S(2)}) collective-permute-start(bf16[2,4,384,128]{3,2,1,0:T(8,128)(2,1)S(1)} %pad_maximum_fusion.2.w0), channel_id=1, source_target_pairs={{0,128},{128,0},{256,384},{384,256},{1,129},{129,1},{257,385},{385... | collective-permute-start | bytes 2359304 | tf_op jit(solution)/shard_map/ppermute | solution.py:24
  163.8 19.0 %collective-permute-start.22 = (bf16[1,4,384,128]{3,2,1,0:T(8,128)(2,1)}, bf16[1,4,384,128]{3,2,1,0:T(8,128)(2,1)S(1)}, u32[]{:S(2)}, u32[]{:S(2)}) collective-permute-start(bf16[1,4,384,128]{3,2,1,0:T(8,128)(2,1)} %slice.58), channel_id=1, source_target_pairs={{0,128},{128,0},{256,384},{384,256},{1,129},{129,1},{257,385},{385... | collective-permute-start | bytes 1179656 | tf_op jit(solution)/shard_map/ppermute | solution.py:24
  166.8 16.1 %collective-permute-start.23 = (bf16[1,4,384,128]{3,2,1,0:T(8,128)(2,1)}, bf16[1,4,384,128]{3,2,1,0:T(8,128)(2,1)}, u32[]{:S(2)}, u32[]{:S(2)}) collective-permute-start(bf16[1,4,384,128]{3,2,1,0:T(8,128)(2,1)} %slice.59), channel_id=1, source_target_pairs={{0,384},{128,256},{256,128},{384,0},{1,385},{129,257},{257,129},{3... | collective-permute-start | bytes 1179656 | tf_op jit(solution)/shard_map/ppermute | solution.py:24
  189.4 12.6 %collective-permute-start.28 = (bf16[4,2,256,256]{3,2,1,0:T(8,128)(2,1)S(1)}, bf16[4,2,256,256]{3,2,1,0:T(8,128)(2,1)S(1)}, u32[]{:S(2)}, u32[]{:S(2)}) collective-permute-start(bf16[4,2,256,256]{3,2,1,0:T(8,128)(2,1)S(1)} %get-tuple-element.36), channel_id=1, source_target_pairs={{0,1},{1,0},{2,3},{3,2},{4,5},{5,4},{6,7},{7,6},{8,9},{9,8},{10,11... | collective-permute-start | bytes 3145736 | tf_op jit(solution)/shard_map/ppermute | solution.py:24
  192.2 17.6 %collective-permute-start.27 = (bf16[2,256,256]{2,1,0:T(8,128)(2,1)S(1)}, bf16[2,256,256]{2,1,0:T(8,128)(2,1)S(1)}, u32[]{:S(2)}, u32[]{:S(2)}) collective-permute-start(bf16[2,256,256]{2,1,0:T(8,128)(2,1)S(1)} %get-tuple-element.45), channel_id=1, source_target_pairs={{0,12},{4,8},{8,4},{12,0},{1,13},{5,9},{9,5},{13,1},{2,14},{6,10},... | collective-permute-start | bytes 786440 | tf_op jit(solution)/shard_map/ppermute | solution.py:24
  195.7 17.8 %collective-permute-start.26 = (bf16[2,256,256]{2,1,0:T(8,128)(2,1)S(1)}, bf16[2,256,256]{2,1,0:T(8,128)(2,1)S(1)}, u32[]{:S(2)}, u32[]{:S(2)}) collective-permute-start(bf16[2,256,256]{2,1,0:T(8,128)(2,1)S(1)} %get-tuple-element.46), channel_id=1, source_target_pairs={{0,8},{4,12},{8,0},{12,4},{1,9},{5,13},{9,1},{13,5},{2,10},{6,14},... | collective-permute-start | bytes 786440 | tf_op jit(solution)/shard_map/ppermute | solution.py:24
  199.6 13.9 %collective-permute-start.25 = (bf16[2,256,256]{2,1,0:T(8,128)(2,1)S(1)}, bf16[2,256,256]{2,1,0:T(8,128)(2,1)S(1)}, u32[]{:S(2)}, u32[]{:S(2)}) collective-permute-start(bf16[2,256,256]{2,1,0:T(8,128)(2,1)S(1)} %get-tuple-element.44), channel_id=1, source_target_pairs={{0,4},{4,0},{8,12},{12,8},{1,5},{5,1},{9,13},{13,9},{2,6},{6,2},{1... | collective-permute-start | bytes 786440 | tf_op jit(solution)/shard_map/ppermute | solution.py:24
  202.4 18.5 %collective-permute-start.31 = (bf16[2,256,256]{2,1,0:T(8,128)(2,1)S(1)}, bf16[2,256,256]{2,1,0:T(8,128)(2,1)S(1)}, u32[]{:S(2)}, u32[]{:S(2)}) collective-permute-start(bf16[2,256,256]{2,1,0:T(8,128)(2,1)S(1)} %get-tuple-element.42), channel_id=1, source_target_pairs={{0,12},{4,8},{8,4},{12,0},{1,13},{5,9},{9,5},{13,1},{2,14},{6,10},... | collective-permute-start | bytes 786440 | tf_op jit(solution)/shard_map/ppermute | solution.py:24
  205.9 15.1 %collective-permute-start.30 = (bf16[2,256,256]{2,1,0:T(8,128)(2,1)S(1)}, bf16[2,256,256]{2,1,0:T(8,128)(2,1)S(1)}, u32[]{:S(2)}, u32[]{:S(2)}) collective-permute-start(bf16[2,256,256]{2,1,0:T(8,128)(2,1)S(1)} %get-tuple-element.43), channel_id=1, source_target_pairs={{0,8},{4,12},{8,0},{12,4},{1,9},{5,13},{9,1},{13,5},{2,10},{6,14},... | collective-permute-start | bytes 786440 | tf_op jit(solution)/shard_map/ppermute | solution.py:24
  209.8 13.2 %collective-permute-start.29 = (bf16[2,256,256]{2,1,0:T(8,128)(2,1)S(1)}, bf16[2,256,256]{2,1,0:T(8,128)(2,1)S(1)}, u32[]{:S(2)}, u32[]{:S(2)}) collective-permute-start(bf16[2,256,256]{2,1,0:T(8,128)(2,1)S(1)} %get-tuple-element.41), channel_id=1, source_target_pairs={{0,4},{4,0},{8,12},{12,8},{1,5},{5,1},{9,13},{13,9},{2,6},{6,2},{1... | collective-permute-start | bytes 786440 | tf_op jit(solution)/shard_map/ppermute | solution.py:24
  213.7 19.5 %collective-permute-start.34 = (bf16[256,256]{1,0:T(8,128)(2,1)S(1)}, bf16[256,256]{1,0:T(8,128)(2,1)S(1)}, u32[]{:S(2)}, u32[]{:S(2)}) collective-permute-start(bf16[256,256]{1,0:T(8,128)(2,1)S(1)} %fusion.5), channel_id=1, source_target_pairs={{0,2},{2,0},{64,66},{66,64},{1,3},{3,1},{65,67},{67,65},{4,6},{6,4... | collective-permute-start | bytes 393224 | tf_op jit(solution)/shard_map/ppermute | solution.py:24
  223.2 17.5 %collective-permute-start.33 = (bf16[256,256]{1,0:T(8,128)(2,1)S(1)}, bf16[256,256]{1,0:T(8,128)(2,1)S(1)}, u32[]{:S(2)}, u32[]{:S(2)}) collective-permute-start(bf16[256,256]{1,0:T(8,128)(2,1)S(1)} %get-tuple-element.52), channel_id=1, source_target_pairs={{0,66},{2,64},{64,2},{66,0},{1,67},{3,65},{65,3},{67,1},{4,70},{6,... | collective-permute-start | bytes 393224 | tf_op jit(solution)/shard_map/ppermute | solution.py:24
  228.5 20.1 %collective-permute-start.32 = (bf16[256,256]{1,0:T(8,128)(2,1)S(1)}, bf16[256,256]{1,0:T(8,128)(2,1)S(1)}, u32[]{:S(2)}, u32[]{:S(2)}) collective-permute-start(bf16[256,256]{1,0:T(8,128)(2,1)S(1)} %get-tuple-element.51), channel_id=1, source_target_pairs={{0,64},{2,66},{64,0},{66,2},{1,65},{3,67},{65,1},{67,3},{4,68},{6,... | collective-permute-start | bytes 393224 | tf_op jit(solution)/shard_map/ppermute | solution.py:24
  (20 other events, 213.3 us)

commit v6 on v5

--- a/solution.py
+++ b/solution.py
@@ -41,6 +41,27 @@
 
 def from_far(one, three, axis, split):
     return send(three[:split], (axis,), 1), send(one[split:], (axis,), 3)
+
+
+def swap_blocks(block):
+    place = [(a, q) for a in range(2) for q in range(4)]
+    axes = ("zt", "zq", "c")
+    own = [(8 * a + 2 * q + a, 8 * a + 2 * q + q // 2) for a, q in place]
+    own += [(8 * a + 2 * q + 1 - a, 8 * a + 2 * q + 1 - q // 2) for a, q in place]
+    cross = [(8 * a + 2 * q + 1 - a, 8 * (1 - a) + 2 * q + q // 2) for a, q in place]
+    cross += [(8 * a + 2 * q + a, 8 * a + 2 * q + 1 - q // 2) for a, q in place]
+    return lax.ppermute(block, axes, own), lax.ppermute(block, axes, cross)
+
+
+def spread_blocks(blocks, at):
+    got = []
+    for k in (1, 2, 3):
+        pairs = [(2 * q + q // 2, 2 * (q ^ k) + q // 2) for q in range(4)]
+        pairs += [(2 * q + 1 - q // 2, 2 * q + (q // 2 + (k == 1)) % 2) for q in range(4)]
+        got.append(lax.ppermute(blocks, ("zq", "c"), pairs))
+    one, two, three = got
+    here = at["zq"] // 2 == at["c"]
+    return jnp.stack([jnp.where(here, blocks, two), jnp.where(here, one, three)], axis=1)
 
 
 def coordinates():
@@ -99,20 +120,21 @@
         act[a] = gelu_exact(acc).astype(act.dtype)
 
 
-def out_kernel(a, place, act, w0, w1, w2a, w2b, w3, mine, other):
-    x, zq, y, zh, c = (place[i] for i in range(5))
+def out_kernel(a, place, act, act_other, w0, w1, w2a, w2b, w3, out):
+    x, zq, y, zh, c, zt = (place[i] for i in range(6))
+    half = act.shape[2]
     slots = [[w.at[s] for s in range(2)] for w in (w0, w1)] + [[w2a, w2b]] + [[w3.at[s] for s in range(2)]]
-    for ck, ref in ((1, other), (0, mine)):
-        first = 2 * (c ^ ck)
-        for k in range(4):
-            for s in range(2):
-                weights = slots[k][s]
+    for k in range(4):
+        for s in range(2):
+            total = None
+            for core, part in ((c, act), (1 - c, act_other)):
+                units = pl.ds(pl.multiple_of(core * half, half), half)
                 block = jnp.concatenate(
-                    [weights[first ^ zq], weights[(first + 1) ^ zq]], axis=1
+                    [slots[k][s][zq & 1, units, :], slots[k][s][1 - (zq & 1), units, :]], axis=1
                 )
-                ref[x ^ k ^ y, zh ^ c ^ s] = jnp.dot(
-                    act[a], block, preferred_element_type=jnp.float32
-                ).astype(ref.dtype)
+                term = jnp.dot(part[a], block, preferred_element_type=jnp.float32)
+                total = term if total is None else total + term
+            out[x ^ k ^ y, zh ^ zt ^ s] = total.astype(out.dtype)
 
 
 def call(kernel, out_shape, flops, *operands, copied=False):
@@ -137,7 +159,7 @@
     rows, cols = tokens.shape
     d_dev, f_dev = w_inner.shape
     half = f_dev // 2
-    place = jnp.stack([at[a] for a in ("x", "zq", "y", "zh", "c")]).astype(jnp.int32)
+    place = jnp.stack([at[a] for a in ("x", "zq", "y", "zh", "c", "zt")]).astype(jnp.int32)
 
     def weight_half(which, axis, array):
         return lax.dynamic_slice_in_dim(array, which * half, half, axis)
@@ -147,21 +169,18 @@
     swapped = swap_halves(weight_half(zt, 1, w_inner), weight_half(1 - zt, 1, w_inner))
 
     inner = after(jnp.stack(swapped), both)
+    both = after(both, *swapped)
     inner = jnp.stack([inner] + [send(inner, ("zq",), k) for k in (1, 2, 3)], axis=1)
-
-    in1, in3 = from_neighbours(inner, "x")
-    swapped = swap_halves(*(weight_half(h, 0, after(w_outer, inner)) for h in (zt, 1 - zt)))
-    y1 = send(after(both, inner), ("y",), 1)
-    outer = jnp.stack(swapped)
-    second = send(outer, ("zq",), 2)
-    y3 = send(after(both, y1, *swapped), ("y",), 3)
-
-    in2a, in2b = from_far(after(in1, second, y1), after(in3, second, y1), "x", 1)
-    pair = send(after(jnp.stack([outer, second], axis=1), in1, in3), ("zq",), 1)
-    outer = jnp.stack([outer, pair[:, 0], second, pair[:, 1]], axis=1)
-    y2 = send(after(both, in1, in3, y3, second), ("y",), 2)
-
-    out1, out3 = from_neighbours(after(outer, in2a, in2b, y3), "x")
+    y1, y3 = from_neighbours(both, "y")
+
+    in1, in3 = from_neighbours(after(inner, y1, y3), "x")
+    swapped = swap_blocks(after(w_outer, inner, y1, y3))
+    y2 = send(after(both, inner, y1, y3), ("y",), 2)
+
+    in2a, in2b = from_far(after(in1, y2, *swapped), after(in3, y2, *swapped), "x", 1)
+    outer = spread_blocks(after(jnp.stack(swapped), in1, in3, y2), at)
+
+    out1, out3 = from_neighbours(after(outer, in2a, in2b), "x")
     both = jnp.stack([both, y1, y2, y3])
     other = send(after(both, outer, in2a, in2b), ("c",), 1)
 
@@ -173,16 +192,17 @@
         jax.ShapeDtypeStruct((2, rows, half), jnp.bfloat16),
         flops, place, both, other, inner, in1, in2a[0], in2b[0], in3, copied=True,
     )
+    act_other = send(act, ("c",), 1)
     shape = jax.ShapeDtypeStruct((4, 2, rows, cols), jnp.bfloat16)
-    outer_all = (outer, out1, out2a[0], out2b[0], out3)
     parts = []
     for a in (0, 1):
-        mine, other = call(
-            functools.partial(out_kernel, a), (shape, shape), flops // 2, place, act, *outer_all
+        sent = call(
+            functools.partial(out_kernel, a), shape, flops // 2,
+            place, act, act_other, outer, out1, out2a[0], out2b[0], out3,
         )
-        total = mine.astype(jnp.float32) + send(other, ("c",), 1).astype(jnp.float32)
-        sent = total.astype(jnp.bfloat16)
-        total = total[0] + sum(send(sent[k], ("y",), k).astype(jnp.float32) for k in (1, 2, 3))
+        total = sent[0].astype(jnp.float32) + sum(
+            send(sent[k], ("y",), k).astype(jnp.float32) for k in (1, 2, 3)
+        )
         parts.append((total, total.astype(jnp.bfloat16)))
     (total, stay), (_, away) = parts
     total = total[0] + sum(

time: 251 us -> 236 us (0.940)
  the two profiles are of different devices: /device:TPU:40 before, /device:TPU:1 now
where the time goes in v6:
time: 236 us; the launch traced here: 234 us
  starting transfers between devices  129 us (55%)
  waiting for transfers between devices  76.1 us (32%)
  Pallas kernels  11.8 us (5%)
  local copies, waits for them, and re-layouts  11 us (5%)
  other arithmetic  6.04 us (3%)
    ppermute x28, starting transfers between devices, send(): return lax.ppermute(value, axes, [(i, i ^ k) for i in range(count)])  102 us
    ppermute x28, waiting for transfers between devices, send(): return lax.ppermute(value, axes, [(i, i ^ k) for i in range(count)])  63.4 us
    pallas_call x3, Pallas kernels, call(): pl.pallas_call(kernel, out_shape=out_shape, in_specs=[pl.BlockSpec(memory...  11.8 us
    ppermute x3, starting transfers between devices, spread_blocks(): got.append(lax.ppermute(blocks, ('zq', 'c'), pairs))  11 us
    ppermute x1, waiting for transfers between devices, swap_halves(): lax.ppermute(first, ('zt', 'c'), [(2 * a + b, 2 * b + a) for a, b in both])  10.1 us
    ppermute x2, starting transfers between devices, swap_blocks(): return (lax.ppermute(block, axes, own), lax.ppermute(block, axes, cross))  7.43 us
    unnamed x22, local copies, waits for them, and re-layouts  6.93 us
    ppermute x1, starting transfers between devices, swap_halves(): lax.ppermute(first, ('zt', 'c'), [(2 * a + b, 2 * b + a) for a, b in both])  6.3 us
  transfers between devices with their start and end apart: 35, of which 15 were waited for; matrix products, arithmetic and copies ran while one was open for 3% of the time, Pallas kernels for 4%

profile of v6, /device:TPU:1, one launch (start us, length us, event | category | flops | bytes accessed | tf_op | source)
XLA Modules:
  0.0 234.1 jit_solution(1273093407560086794)
XLA Ops:
  1.6 13.3 %collective-permute-start.2 = (bf16[272,256]{1,0:T(8,128)(2,1)S(1)}, bf16[272,256]{1,0:T(8,128)(2,1)S(1)}, u32[]{:S(2)}, u32[]{:S(2)}) collective-permute-start(bf16[272,256]{1,0:T(8,128)(2,1)S(1)} %get-tuple-element.40), channel_id=1, source_target_pairs={{0,66},{2,64},{64,2},{66,0},{1,67},{3,65},{65,3},{67,1},{4,70},{6,... | collective-permute-start | bytes 417800 | tf_op jit(solution)/shard_map/ppermute | solution.py:24
  14.9 5.2 %collective-permute-start.1 = (bf16[272,256]{1,0:T(8,128)(2,1)S(1)}, bf16[272,256]{1,0:T(8,128)(2,1)S(1)}, u32[]{:S(2)}, u32[]{:S(2)}) collective-permute-start(bf16[272,256]{1,0:T(8,128)(2,1)S(1)} %get-tuple-element.40), channel_id=1, source_target_pairs={{0,64},{2,66},{64,0},{66,2},{1,65},{3,67},{65,1},{67,3},{4,68},{6,... | collective-permute-start | bytes 417800 | tf_op jit(solution)/shard_map/ppermute | solution.py:24
  20.1 3.7 %collective-permute-start = (bf16[272,256]{1,0:T(8,128)(2,1)S(1)}, bf16[272,256]{1,0:T(8,128)(2,1)S(1)}, u32[]{:S(2)}, u32[]{:S(2)}) collective-permute-start(bf16[272,256]{1,0:T(8,128)(2,1)S(1)} %get-tuple-element.40), channel_id=1, source_target_pairs={{0,2},{2,0},{64,66},{66,64},{1,3},{3,1},{65,67},{67,65},{4,6},{6,4... | collective-permute-start | bytes 417800 | tf_op jit(solution)/shard_map/ppermute | solution.py:24
  24.8 6.3 %collective-permute-start.3 = (bf16[128,384]{1,0:T(8,128)(2,1)S(1)}, bf16[128,384]{1,0:T(8,128)(2,1)S(1)}, u32[]{:S(2)}, u32[]{:S(2)}) collective-permute-start(bf16[128,384]{1,0:T(8,128)(2,1)S(1)} %get-tuple-element.38), channel_id=1, source_target_pairs={{0,0},{1,64},{64,1},{65,65},{2,2},{3,66},{66,3},{67,67},{4,4},{5,6... | collective-permute-start | bytes 294920 | tf_op jit(solution)/shard_map/ppermute | solution.py:33
  33.1 11.2 %collective-permute-done = bf16[272,256]{1,0:T(8,128)(2,1)S(1)} collective-permute-done((bf16[272,256]{1,0:T(8,128)(2,1)S(1)}, bf16[272,256]{1,0:T(8,128)(2,1)S(1)}, u32[]{:S(2)}, u32[]{:S(2)}) %collective-permute-start) | collective-permute-done | bytes 139296 | tf_op jit(solution)/shard_map/ppermute | solution.py:24
  44.3 10.1 %collective-permute-done.3 = bf16[128,384]{1,0:T(8,128)(2,1)S(1)} collective-permute-done((bf16[128,384]{1,0:T(8,128)(2,1)S(1)}, bf16[128,384]{1,0:T(8,128)(2,1)S(1)}, u32[]{:S(2)}, u32[]{:S(2)}) %collective-permute-start.3) | collective-permute-done | bytes 98336 | tf_op jit(solution)/shard_map/ppermute | solution.py:33
  54.4 4.6 %collective-permute-start.9 = (bf16[4,272,256]{2,1,0:T(8,128)(2,1)S(1)}, bf16[4,272,256]{2,1,0:T(8,128)(2,1)}, u32[]{:S(2)}, u32[]{:S(2)}) collective-permute-start(bf16[4,272,256]{2,1,0:T(8,128)(2,1)S(1)} %pad_maximum_fusion.3), channel_id=1, source_target_pairs={{0,12},{4,8},{8,4},{12,0},{1,13},{5,9},{9,5},{13,1},{2,14},{6,10},... | collective-permute-start | bytes 1671176 | tf_op jit(solution)/shard_map/ppermute | solution.py:24
  65.0 5.3 %collective-permute-start.6 = (bf16[2,128,384]{2,1,0:T(8,128)(2,1)S(1)}, bf16[2,128,384]{2,1,0:T(8,128)(2,1)S(1)}, u32[]{:S(2)}, u32[]{:S(2)}) collective-permute-start(bf16[2,128,384]{2,1,0:T(8,128)(2,1)S(1)} %pad_maximum_fusion.5), channel_id=1, source_target_pairs={{0,16},{16,0},{32,48},{48,32},{1,17},{17,1},{33,49},{49,33},{2,18}... | collective-permute-start | bytes 589832 | tf_op jit(solution)/shard_map/ppermute | solution.py:24
  70.3 9.9 %collective-permute-done.7 = bf16[2,128,384]{2,1,0:T(8,128)(2,1)S(1)} collective-permute-done((bf16[2,128,384]{2,1,0:T(8,128)(2,1)S(1)}, bf16[2,128,384]{2,1,0:T(8,128)(2,1)S(1)}, u32[]{:S(2)}, u32[]{:S(2)}) %collective-permute-start.7) | collective-permute-done | bytes 196640 | tf_op jit(solution)/shard_map/ppermute | solution.py:24
  80.4 3.1 %collective-permute-start.13 = (bf16[2,4,128,384]{3,2,1,0:T(8,128)(2,1)S(1)}, bf16[2,4,128,384]{3,2,1,0:T(8,128)(2,1)S(1)}, u32[]{:S(2)}, u32[]{:S(2)}) collective-permute-start(bf16[2,4,128,384]{3,2,1,0:T(8,128)(2,1)S(1)} %pad_maximum_fusion.1.refs_2_), channel_id=1, source_target_pairs={{0,128},{128,0},{256,384},{384,256},{1,129},{129,1},{257,385},{385... | collective-permute-start | bytes 2359304 | tf_op jit(solution)/shard_map/ppermute | solution.py:24
  83.6 3.7 %collective-permute-start.14 = (bf16[2,4,128,384]{3,2,1,0:T(8,128)(2,1)S(1)}, bf16[2,4,128,384]{3,2,1,0:T(8,128)(2,1)S(1)}, u32[]{:S(2)}, u32[]{:S(2)}) collective-permute-start(bf16[2,4,128,384]{3,2,1,0:T(8,128)(2,1)S(1)} %pad_maximum_fusion.1.refs_2_), channel_id=1, source_target_pairs={{0,384},{128,256},{256,128},{384,0},{1,385},{129,257},{257,129},{3... | collective-permute-start | bytes 2359304 | tf_op jit(solution)/shard_map/ppermute | solution.py:24
  88.2 3.1 %collective-permute-start.10 = (bf16[4,272,256]{2,1,0:T(8,128)(2,1)S(1)}, bf16[4,272,256]{2,1,0:T(8,128)(2,1)}, u32[]{:S(2)}, u32[]{:S(2)}) collective-permute-start(bf16[4,272,256]{2,1,0:T(8,128)(2,1)S(1)} %pad_maximum_fusion.3), channel_id=1, source_target_pairs={{0,8},{4,12},{8,0},{12,4},{1,9},{5,13},{9,1},{13,5},{2,10},{6,14},... | collective-permute-start | bytes 1671176 | tf_op jit(solution)/shard_map/ppermute | solution.py:24
  91.3 6.8 %collective-permute-start.12 = (bf16[768,128]{1,0:T(8,128)(2,1)S(1)}, bf16[768,128]{1,0:T(8,128)(2,1)S(1)}, u32[]{:S(2)}, u32[]{:S(2)}) collective-permute-start(bf16[768,128]{1,0:T(8,128)(2,1)S(1)} %copy-done.10), channel_id=1, source_target_pairs={{1,64},{17,80},{33,97},{49,113},{64,0},{80,16},{96,33},{112,49},{0... | collective-permute-start | bytes 589832 | tf_op jit(solution)/shard_map/ppermute | solution.py:53
  104.9 7.1 %collective-permute-start.15 = (bf16[2,768,128]{2,1,0:T(8,128)(2,1)}, bf16[2,768,128]{2,1,0:T(8,128)(2,1)}, u32[]{:S(2)}, u32[]{:S(2)}) collective-permute-start(bf16[2,768,128]{2,1,0:T(8,128)(2,1)} %pad_maximum_fusion.4), channel_id=1, source_target_pairs={{0,32},{16,48},{33,1},{49,17},{1,0},{17,16},{32,33},{48,49},{2,34}... | collective-permute-start | bytes 1179656 | tf_op jit(solution)/shard_map/ppermute | solution.py:61
  124.5 6.0 %collective-permute-done.18 = bf16[1,4,128,384]{3,2,1,0:T(8,128)(2,1)S(1)} collective-permute-done((bf16[1,4,128,384]{3,2,1,0:T(8,128)(2,1)S(1)}, bf16[1,4,128,384]{3,2,1,0:T(8,128)(2,1)S(1)}, u32[]{:S(2)}, u32[]{:S(2)}) %collective-permute-start.18) | collective-permute-done | bytes 393248 | tf_op jit(solution)/shard_map/ppermute | solution.py:24
  130.5 3.2 %collective-permute-done.19 = bf16[1,4,128,384]{3,2,1,0:T(8,128)(2,1)S(1)} collective-permute-done((bf16[1,4,128,384]{3,2,1,0:T(8,128)(2,1)S(1)}, bf16[1,4,128,384]{3,2,1,0:T(8,128)(2,1)S(1)}, u32[]{:S(2)}, u32[]{:S(2)}) %collective-permute-start.19) | collective-permute-done | bytes 393248 | tf_op jit(solution)/shard_map/ppermute | solution.py:24
  134.4 3.0 %collective-permute-start.20 = (bf16[4,4,272,256]{3,2,1,0:T(8,128)(2,1)S(1)}, bf16[4,4,272,256]{3,2,1,0:T(8,128)(2,1)}, u32[]{:S(2)}, u32[]{:S(2)}) collective-permute-start(bf16[4,4,272,256]{3,2,1,0:T(8,128)(2,1)S(1)} %pad_maximum_fusion.refs_0_), channel_id=1, source_target_pairs={{0,1},{1,0},{2,3},{3,2},{4,5},{5,4},{6,7},{7,6},{8,9},{9,8},{10,11... | collective-permute-start | bytes 6684680 | tf_op jit(solution)/shard_map/ppermute | solution.py:24
  146.4 6.5 %shard_map.46.act = bf16[2,256,384]{2,1,0:T(8,128)(2,1)S(1)} custom-call(s32[6]{0:T(128)S(1)} %stack.99.place, bf16[4,4,272,256]{3,2,1,0:T(8,128)(2,1)S(1)} %pad_maximum_fusion.refs_0_, bf16[4,4,272,256]{3,2,1,0:T(8,128)(2,1)} %collective-permute-done.20.refs_1_, bf16[2,4,128,384]{3,2,1,0:T(8,128)(2,1)S(1)} %copy-done.1, ...), custom_call_target="tpu_custom_call" | custom-call | flops 1610612736 | bytes 7602200 | tf_op jit(solution)/shard_map/pallas_call | solution.py:145
  155.1 4.7 %collective-permute-done.23.w3 = bf16[2,2,768,128]{3,2,1,0:T(8,128)(2,1)} collective-permute-done((bf16[2,2,768,128]{3,2,1,0:T(8,128)(2,1)S(1)}, bf16[2,2,768,128]{3,2,1,0:T(8,128)(2,1)}, u32[]{:S(2)}, u32[]{:S(2)}) %collective-permute-start.23) | collective-permute-done | bytes 786464 | tf_op jit(solution)/shard_map/ppermute | solution.py:24
  166.3 6.3 %collective-permute-done.24 = bf16[1,2,768,128]{3,2,1,0:T(8,128)(2,1)S(1)} collective-permute-done((bf16[1,2,768,128]{3,2,1,0:T(8,128)(2,1)S(1)}, bf16[1,2,768,128]{3,2,1,0:T(8,128)(2,1)S(1)}, u32[]{:S(2)}, u32[]{:S(2)}) %collective-permute-start.24) | collective-permute-done | bytes 393248 | tf_op jit(solution)/shard_map/ppermute | solution.py:24
  172.6 4.2 %collective-permute-done.25 = bf16[1,2,768,128]{3,2,1,0:T(8,128)(2,1)S(1)} collective-permute-done((bf16[1,2,768,128]{3,2,1,0:T(8,128)(2,1)S(1)}, bf16[1,2,768,128]{3,2,1,0:T(8,128)(2,1)S(1)}, u32[]{:S(2)}, u32[]{:S(2)}) %collective-permute-start.25) | collective-permute-done | bytes 393248 | tf_op jit(solution)/shard_map/ppermute | solution.py:24
  176.8 2.6 %shard_map.47 = bf16[4,2,256,256]{3,2,1,0:T(8,128)(2,1)S(1)} custom-call(s32[6]{0:T(128)S(1)} %stack.99.place, bf16[2,256,384]{2,1,0:T(8,128)(2,1)S(1)} %shard_map.46.act, bf16[2,256,384]{2,1,0:T(8,128)(2,1)S(1)} %collective-permute-done.21.act_other, bf16[2,2,768,128]{3,2,1,0:T(8,128)(2,1)S(1)} %pad_maximum_fusion.2.w0, ...), custom_call_target="tpu_custom_call" | custom-call | flops 805306368 | bytes 3932184 | tf_op jit(solution)/shard_map/pallas_call | solution.py:145
  179.5 4.6 %collective-permute-start.28 = (bf16[2,256,256]{2,1,0:T(8,128)(2,1)S(1)}, bf16[2,256,256]{2,1,0:T(8,128)(2,1)S(1)}, u32[]{:S(2)}, u32[]{:S(2)}) collective-permute-start(bf16[2,256,256]{2,1,0:T(8,128)(2,1)S(1)} %get-tuple-element.33), channel_id=1, source_target_pairs={{0,12},{4,8},{8,4},{12,0},{1,13},{5,9},{9,5},{13,1},{2,14},{6,10},... | collective-permute-start | bytes 786440 | tf_op jit(solution)/shard_map/ppermute | solution.py:24
  188.5 2.6 %shard_map.48 = bf16[4,2,256,256]{3,2,1,0:T(8,128)(2,1)S(1)} custom-call(s32[6]{0:T(128)S(1)} %stack.99.place, bf16[2,256,384]{2,1,0:T(8,128)(2,1)S(1)} %shard_map.46.act, bf16[2,256,384]{2,1,0:T(8,128)(2,1)S(1)} %collective-permute-done.21.act_other, bf16[2,2,768,128]{3,2,1,0:T(8,128)(2,1)S(1)} %pad_maximum_fusion.2.w0, ...), custom_call_target="tpu_custom_call" | custom-call | flops 805306368 | bytes 3932184 | tf_op jit(solution)/shard_map/pallas_call | solution.py:145
  191.2 4.6 %collective-permute-start.31 = (bf16[2,256,256]{2,1,0:T(8,128)(2,1)S(1)}, bf16[2,256,256]{2,1,0:T(8,128)(2,1)S(1)}, u32[]{:S(2)}, u32[]{:S(2)}) collective-permute-start(bf16[2,256,256]{2,1,0:T(8,128)(2,1)S(1)} %get-tuple-element.30), channel_id=1, source_target_pairs={{0,12},{4,8},{8,4},{12,0},{1,13},{5,9},{9,5},{13,1},{2,14},{6,10},... | collective-permute-start | bytes 786440 | tf_op jit(solution)/shard_map/ppermute | solution.py:24
  197.7 2.5 %collective-permute-start.29 = (bf16[2,256,256]{2,1,0:T(8,128)(2,1)S(1)}, bf16[2,256,256]{2,1,0:T(8,128)(2,1)S(1)}, u32[]{:S(2)}, u32[]{:S(2)}) collective-permute-start(bf16[2,256,256]{2,1,0:T(8,128)(2,1)S(1)} %get-tuple-element.29), channel_id=1, source_target_pairs={{0,4},{4,0},{8,12},{12,8},{1,5},{5,1},{9,13},{13,9},{2,6},{6,2},{1... | collective-permute-start | bytes 786440 | tf_op jit(solution)/shard_map/ppermute | solution.py:24
  200.4 7.4 %collective-permute-start.34 = (bf16[256,256]{1,0:T(8,128)(2,1)S(1)}, bf16[256,256]{1,0:T(8,128)(2,1)S(1)}, u32[]{:S(2)}, u32[]{:S(2)}) collective-permute-start(bf16[256,256]{1,0:T(8,128)(2,1)S(1)} %fusion.3), channel_id=1, source_target_pairs={{0,2},{2,0},{64,66},{66,64},{1,3},{3,1},{65,67},{67,65},{4,6},{6,4... | collective-permute-start | bytes 393224 | tf_op jit(solution)/shard_map/ppermute | solution.py:24
  208.0 5.8 %collective-permute-start.33 = (bf16[256,256]{1,0:T(8,128)(2,1)S(1)}, bf16[256,256]{1,0:T(8,128)(2,1)S(1)}, u32[]{:S(2)}, u32[]{:S(2)}) collective-permute-start(bf16[256,256]{1,0:T(8,128)(2,1)S(1)} %get-tuple-element.36), channel_id=1, source_target_pairs={{0,66},{2,64},{64,2},{66,0},{1,67},{3,65},{65,3},{67,1},{4,70},{6,... | collective-permute-start | bytes 393224 | tf_op jit(solution)/shard_map/ppermute | solution.py:24
  213.8 4.1 %collective-permute-start.32 = (bf16[256,256]{1,0:T(8,128)(2,1)S(1)}, bf16[256,256]{1,0:T(8,128)(2,1)S(1)}, u32[]{:S(2)}, u32[]{:S(2)}) collective-permute-start(bf16[256,256]{1,0:T(8,128)(2,1)S(1)} %get-tuple-element.35), channel_id=1, source_target_pairs={{0,64},{2,66},{64,0},{66,2},{1,65},{3,67},{65,1},{67,3},{4,68},{6,... | collective-permute-start | bytes 393224 | tf_op jit(solution)/shard_map/ppermute | solution.py:24
  217.9 6.2 %collective-permute-done.34 = bf16[256,256]{1,0:T(8,128)(2,1)S(1)} collective-permute-done((bf16[256,256]{1,0:T(8,128)(2,1)S(1)}, bf16[256,256]{1,0:T(8,128)(2,1)S(1)}, u32[]{:S(2)}, u32[]{:S(2)}) %collective-permute-start.34) | collective-permute-done | bytes 131104 | tf_op jit(solution)/shard_map/ppermute | solution.py:24
  224.2 5.7 %collective-permute-done.33 = bf16[256,256]{1,0:T(8,128)(2,1)S(1)} collective-permute-done((bf16[256,256]{1,0:T(8,128)(2,1)S(1)}, bf16[256,256]{1,0:T(8,128)(2,1)S(1)}, u32[]{:S(2)}, u32[]{:S(2)}) %collective-permute-start.33) | collective-permute-done | bytes 131104 | tf_op jit(solution)/shard_map/ppermute | solution.py:24
  229.8 3.5 %collective-permute-done.32 = bf16[256,256]{1,0:T(8,128)(2,1)S(1)} collective-permute-done((bf16[256,256]{1,0:T(8,128)(2,1)S(1)}, bf16[256,256]{1,0:T(8,128)(2,1)S(1)}, u32[]{:S(2)}, u32[]{:S(2)}) %collective-permute-start.32) | collective-permute-done | bytes 131104 | tf_op jit(solution)/shard_map/ppermute | solution.py:24
  (86 shorter events, 56.5 us)
Async XLA Ops:
  1.6 31.4 %collective-permute-start.2 = (bf16[272,256]{1,0:T(8,128)(2,1)S(1)}, bf16[272,256]{1,0:T(8,128)(2,1)S(1)}, u32[]{:S(2)}, u32[]{:S(2)}) collective-permute-start(bf16[272,256]{1,0:T(8,128)(2,1)S(1)} %get-tuple-element.40), channel_id=1, source_target_pairs={{0,66},{2,64},{64,2},{66,0},{1,67},{3,65},{65,3},{67,1},{4,70},{6,... | collective-permute-start | bytes 417800 | tf_op jit(solution)/shard_map/ppermute | solution.py:24
  14.9 18.2 %collective-permute-start.1 = (bf16[272,256]{1,0:T(8,128)(2,1)S(1)}, bf16[272,256]{1,0:T(8,128)(2,1)S(1)}, u32[]{:S(2)}, u32[]{:S(2)}) collective-permute-start(bf16[272,256]{1,0:T(8,128)(2,1)S(1)} %get-tuple-element.40), channel_id=1, source_target_pairs={{0,64},{2,66},{64,0},{66,2},{1,65},{3,67},{65,1},{67,3},{4,68},{6,... | collective-permute-start | bytes 417800 | tf_op jit(solution)/shard_map/ppermute | solution.py:24
  20.1 24.1 %collective-permute-start = (bf16[272,256]{1,0:T(8,128)(2,1)S(1)}, bf16[272,256]{1,0:T(8,128)(2,1)S(1)}, u32[]{:S(2)}, u32[]{:S(2)}) collective-permute-start(bf16[272,256]{1,0:T(8,128)(2,1)S(1)} %get-tuple-element.40), channel_id=1, source_target_pairs={{0,2},{2,0},{64,66},{66,64},{1,3},{3,1},{65,67},{67,65},{4,6},{6,4... | collective-permute-start | bytes 417800 | tf_op jit(solution)/shard_map/ppermute | solution.py:24
  24.8 29.6 %collective-permute-start.3 = (bf16[128,384]{1,0:T(8,128)(2,1)S(1)}, bf16[128,384]{1,0:T(8,128)(2,1)S(1)}, u32[]{:S(2)}, u32[]{:S(2)}) collective-permute-start(bf16[128,384]{1,0:T(8,128)(2,1)S(1)} %get-tuple-element.38), channel_id=1, source_target_pairs={{0,0},{1,64},{64,1},{65,65},{2,2},{3,66},{66,3},{67,67},{4,4},{5,6... | collective-permute-start | bytes 294920 | tf_op jit(solution)/shard_map/ppermute | solution.py:33
  31.1 23.3 %collective-permute-start.4 = (bf16[128,384]{1,0:T(8,128)(2,1)S(1)}, bf16[128,384]{1,0:T(8,128)(2,1)S(1)}, u32[]{:S(2)}, u32[]{:S(2)}) collective-permute-start(bf16[128,384]{1,0:T(8,128)(2,1)S(1)} %get-tuple-element.37), channel_id=1, source_target_pairs={{0,1},{1,65},{64,0},{65,64},{2,3},{3,67},{66,2},{67,66},{4,5},{5,6... | collective-permute-start | bytes 294920 | tf_op jit(solution)/shard_map/ppermute | solution.py:34
  54.4 26.0 %collective-permute-start.9 = (bf16[4,272,256]{2,1,0:T(8,128)(2,1)S(1)}, bf16[4,272,256]{2,1,0:T(8,128)(2,1)}, u32[]{:S(2)}, u32[]{:S(2)}) collective-permute-start(bf16[4,272,256]{2,1,0:T(8,128)(2,1)S(1)} %pad_maximum_fusion.3), channel_id=1, source_target_pairs={{0,12},{4,8},{8,4},{12,0},{1,13},{5,9},{9,5},{13,1},{2,14},{6,10},... | collective-permute-start | bytes 1671176 | tf_op jit(solution)/shard_map/ppermute | solution.py:24
  59.1 21.4 %collective-permute-start.5 = (bf16[4,272,256]{2,1,0:T(8,128)(2,1)S(1)}, bf16[4,272,256]{2,1,0:T(8,128)(2,1)}, u32[]{:S(2)}, u32[]{:S(2)}) collective-permute-start(bf16[4,272,256]{2,1,0:T(8,128)(2,1)S(1)} %pad_maximum_fusion.3), channel_id=1, source_target_pairs={{0,4},{4,0},{8,12},{12,8},{1,5},{5,1},{9,13},{13,9},{2,6},{6,2},{1... | collective-permute-start | bytes 1671176 | tf_op jit(solution)/shard_map/ppermute | solution.py:24
  63.1 17.2 %collective-permute-start.7 = (bf16[2,128,384]{2,1,0:T(8,128)(2,1)S(1)}, bf16[2,128,384]{2,1,0:T(8,128)(2,1)S(1)}, u32[]{:S(2)}, u32[]{:S(2)}) collective-permute-start(bf16[2,128,384]{2,1,0:T(8,128)(2,1)S(1)} %pad_maximum_fusion.5), channel_id=1, source_target_pairs={{0,32},{16,48},{32,0},{48,16},{1,33},{17,49},{33,1},{49,17},{2,34}... | collective-permute-start | bytes 589832 | tf_op jit(solution)/shard_map/ppermute | solution.py:24
  65.0 15.2 %collective-permute-start.6 = (bf16[2,128,384]{2,1,0:T(8,128)(2,1)S(1)}, bf16[2,128,384]{2,1,0:T(8,128)(2,1)S(1)}, u32[]{:S(2)}, u32[]{:S(2)}) collective-permute-start(bf16[2,128,384]{2,1,0:T(8,128)(2,1)S(1)} %pad_maximum_fusion.5), channel_id=1, source_target_pairs={{0,16},{16,0},{32,48},{48,32},{1,17},{17,1},{33,49},{49,33},{2,18}... | collective-permute-start | bytes 589832 | tf_op jit(solution)/shard_map/ppermute | solution.py:24
  80.4 23.3 %collective-permute-start.13 = (bf16[2,4,128,384]{3,2,1,0:T(8,128)(2,1)S(1)}, bf16[2,4,128,384]{3,2,1,0:T(8,128)(2,1)S(1)}, u32[]{:S(2)}, u32[]{:S(2)}) collective-permute-start(bf16[2,4,128,384]{3,2,1,0:T(8,128)(2,1)S(1)} %pad_maximum_fusion.1.refs_2_), channel_id=1, source_target_pairs={{0,128},{128,0},{256,384},{384,256},{1,129},{129,1},{257,385},{385... | collective-permute-start | bytes 2359304 | tf_op jit(solution)/shard_map/ppermute | solution.py:24
  83.6 20.5 %collective-permute-start.14 = (bf16[2,4,128,384]{3,2,1,0:T(8,128)(2,1)S(1)}, bf16[2,4,128,384]{3,2,1,0:T(8,128)(2,1)S(1)}, u32[]{:S(2)}, u32[]{:S(2)}) collective-permute-start(bf16[2,4,128,384]{3,2,1,0:T(8,128)(2,1)S(1)} %pad_maximum_fusion.1.refs_2_), channel_id=1, source_target_pairs={{0,384},{128,256},{256,128},{384,0},{1,385},{129,257},{257,129},{3... | collective-permute-start | bytes 2359304 | tf_op jit(solution)/shard_map/ppermute | solution.py:24
  88.2 15.5 %collective-permute-start.10 = (bf16[4,272,256]{2,1,0:T(8,128)(2,1)S(1)}, bf16[4,272,256]{2,1,0:T(8,128)(2,1)}, u32[]{:S(2)}, u32[]{:S(2)}) collective-permute-start(bf16[4,272,256]{2,1,0:T(8,128)(2,1)S(1)} %pad_maximum_fusion.3), channel_id=1, source_target_pairs={{0,8},{4,12},{8,0},{12,4},{1,9},{5,13},{9,1},{13,5},{2,10},{6,14},... | collective-permute-start | bytes 1671176 | tf_op jit(solution)/shard_map/ppermute | solution.py:24
  91.3 9.4 %collective-permute-start.12 = (bf16[768,128]{1,0:T(8,128)(2,1)S(1)}, bf16[768,128]{1,0:T(8,128)(2,1)S(1)}, u32[]{:S(2)}, u32[]{:S(2)}) collective-permute-start(bf16[768,128]{1,0:T(8,128)(2,1)S(1)} %copy-done.10), channel_id=1, source_target_pairs={{1,64},{17,80},{33,97},{49,113},{64,0},{80,16},{96,33},{112,49},{0... | collective-permute-start | bytes 589832 | tf_op jit(solution)/shard_map/ppermute | solution.py:53
  104.9 17.7 %collective-permute-start.15 = (bf16[2,768,128]{2,1,0:T(8,128)(2,1)}, bf16[2,768,128]{2,1,0:T(8,128)(2,1)}, u32[]{:S(2)}, u32[]{:S(2)}) collective-permute-start(bf16[2,768,128]{2,1,0:T(8,128)(2,1)} %pad_maximum_fusion.4), channel_id=1, source_target_pairs={{0,32},{16,48},{33,1},{49,17},{1,0},{17,16},{32,33},{48,49},{2,34}... | collective-permute-start | bytes 1179656 | tf_op jit(solution)/shard_map/ppermute | solution.py:61
  112.0 11.7 %collective-permute-start.16 = (bf16[2,768,128]{2,1,0:T(8,128)(2,1)}, bf16[2,768,128]{2,1,0:T(8,128)(2,1)S(1)}, u32[]{:S(2)}, u32[]{:S(2)}) collective-permute-start(bf16[2,768,128]{2,1,0:T(8,128)(2,1)} %pad_maximum_fusion.4), channel_id=1, source_target_pairs={{0,16},{16,0},{33,49},{49,33},{1,1},{17,17},{32,32},{48,48},{2,18}... | collective-permute-start | bytes 1179656 | tf_op jit(solution)/shard_map/ppermute | solution.py:61
  113.7 10.7 %collective-permute-start.17 = (bf16[2,768,128]{2,1,0:T(8,128)(2,1)}, bf16[2,768,128]{2,1,0:T(8,128)(2,1)S(1)}, u32[]{:S(2)}, u32[]{:S(2)}) collective-permute-start(bf16[2,768,128]{2,1,0:T(8,128)(2,1)} %pad_maximum_fusion.4), channel_id=1, source_target_pairs={{0,48},{16,32},{33,17},{49,1},{1,0},{17,16},{32,33},{48,49},{2,50}... | collective-permute-start | bytes 1179656 | tf_op jit(solution)/shard_map/ppermute | solution.py:61
  117.9 12.6 %collective-permute-start.18 = (bf16[1,4,128,384]{3,2,1,0:T(8,128)(2,1)S(1)}, bf16[1,4,128,384]{3,2,1,0:T(8,128)(2,1)S(1)}, u32[]{:S(2)}, u32[]{:S(2)}) collective-permute-start(bf16[1,4,128,384]{3,2,1,0:T(8,128)(2,1)S(1)} %slice.48), channel_id=1, source_target_pairs={{0,128},{128,0},{256,384},{384,256},{1,129},{129,1},{257,385},{385... | collective-permute-start | bytes 1179656 | tf_op jit(solution)/shard_map/ppermute | solution.py:24
  120.2 13.5 %collective-permute-start.19 = (bf16[1,4,128,384]{3,2,1,0:T(8,128)(2,1)S(1)}, bf16[1,4,128,384]{3,2,1,0:T(8,128)(2,1)S(1)}, u32[]{:S(2)}, u32[]{:S(2)}) collective-permute-start(bf16[1,4,128,384]{3,2,1,0:T(8,128)(2,1)S(1)} %slice.49), channel_id=1, source_target_pairs={{0,384},{128,256},{256,128},{384,0},{1,385},{129,257},{257,129},{3... | collective-permute-start | bytes 1179656 | tf_op jit(solution)/shard_map/ppermute | solution.py:24
  137.5 22.4 %collective-permute-start.23 = (bf16[2,2,768,128]{3,2,1,0:T(8,128)(2,1)S(1)}, bf16[2,2,768,128]{3,2,1,0:T(8,128)(2,1)}, u32[]{:S(2)}, u32[]{:S(2)}) collective-permute-start(bf16[2,2,768,128]{3,2,1,0:T(8,128)(2,1)S(1)} %pad_maximum_fusion.2.w0), channel_id=1, source_target_pairs={{0,384},{128,256},{256,128},{384,0},{1,385},{129,257},{257,129},{3... | collective-permute-start | bytes 2359304 | tf_op jit(solution)/shard_map/ppermute | solution.py:24
  139.9 22.9 %collective-permute-start.22 = (bf16[2,2,768,128]{3,2,1,0:T(8,128)(2,1)S(1)}, bf16[2,2,768,128]{3,2,1,0:T(8,128)(2,1)}, u32[]{:S(2)}, u32[]{:S(2)}) collective-permute-start(bf16[2,2,768,128]{3,2,1,0:T(8,128)(2,1)S(1)} %pad_maximum_fusion.2.w0), channel_id=1, source_target_pairs={{0,128},{128,0},{256,384},{384,256},{1,129},{129,1},{257,385},{385... | collective-permute-start | bytes 2359304 | tf_op jit(solution)/shard_map/ppermute | solution.py:24
  152.9 13.4 %collective-permute-start.21 = (bf16[2,256,384]{2,1,0:T(8,128)(2,1)S(1)}, bf16[2,256,384]{2,1,0:T(8,128)(2,1)S(1)}, u32[]{:S(2)}, u32[]{:S(2)}) collective-permute-start(bf16[2,256,384]{2,1,0:T(8,128)(2,1)S(1)} %shard_map.46.act), channel_id=1, source_target_pairs={{0,1},{1,0},{2,3},{3,2},{4,5},{5,4},{6,7},{7,6},{8,9},{9,8},{10,11... | collective-permute-start | bytes 1179656 | tf_op jit(solution)/shard_map/ppermute | solution.py:24
  160.9 11.7 %collective-permute-start.24 = (bf16[1,2,768,128]{3,2,1,0:T(8,128)(2,1)S(1)}, bf16[1,2,768,128]{3,2,1,0:T(8,128)(2,1)S(1)}, u32[]{:S(2)}, u32[]{:S(2)}) collective-permute-start(bf16[1,2,768,128]{3,2,1,0:T(8,128)(2,1)S(1)} %slice.50), channel_id=1, source_target_pairs={{0,128},{128,0},{256,384},{384,256},{1,129},{129,1},{257,385},{385... | collective-permute-start | bytes 1179656 | tf_op jit(solution)/shard_map/ppermute | solution.py:24
  163.8 12.9 %collective-permute-start.25 = (bf16[1,2,768,128]{3,2,1,0:T(8,128)(2,1)S(1)}, bf16[1,2,768,128]{3,2,1,0:T(8,128)(2,1)S(1)}, u32[]{:S(2)}, u32[]{:S(2)}) collective-permute-start(bf16[1,2,768,128]{3,2,1,0:T(8,128)(2,1)S(1)} %slice.51), channel_id=1, source_target_pairs={{0,384},{128,256},{256,128},{384,0},{1,385},{129,257},{257,129},{3... | collective-permute-start | bytes 1179656 | tf_op jit(solution)/shard_map/ppermute | solution.py:24
  179.5 18.2 %collective-permute-start.28 = (bf16[2,256,256]{2,1,0:T(8,128)(2,1)S(1)}, bf16[2,256,256]{2,1,0:T(8,128)(2,1)S(1)}, u32[]{:S(2)}, u32[]{:S(2)}) collective-permute-start(bf16[2,256,256]{2,1,0:T(8,128)(2,1)S(1)} %get-tuple-element.33), channel_id=1, source_target_pairs={{0,12},{4,8},{8,4},{12,0},{1,13},{5,9},{9,5},{13,1},{2,14},{6,10},... | collective-permute-start | bytes 786440 | tf_op jit(solution)/shard_map/ppermute | solution.py:24
  184.1 16.1 %collective-permute-start.27 = (bf16[2,256,256]{2,1,0:T(8,128)(2,1)S(1)}, bf16[2,256,256]{2,1,0:T(8,128)(2,1)S(1)}, u32[]{:S(2)}, u32[]{:S(2)}) collective-permute-start(bf16[2,256,256]{2,1,0:T(8,128)(2,1)S(1)} %get-tuple-element.34), channel_id=1, source_target_pairs={{0,8},{4,12},{8,0},{12,4},{1,9},{5,13},{9,1},{13,5},{2,10},{6,14},... | collective-permute-start | bytes 786440 | tf_op jit(solution)/shard_map/ppermute | solution.py:24
  186.0 14.2 %collective-permute-start.26 = (bf16[2,256,256]{2,1,0:T(8,128)(2,1)S(1)}, bf16[2,256,256]{2,1,0:T(8,128)(2,1)S(1)}, u32[]{:S(2)}, u32[]{:S(2)}) collective-permute-start(bf16[2,256,256]{2,1,0:T(8,128)(2,1)S(1)} %get-tuple-element.32), channel_id=1, source_target_pairs={{0,4},{4,0},{8,12},{12,8},{1,5},{5,1},{9,13},{13,9},{2,6},{6,2},{1... | collective-permute-start | bytes 786440 | tf_op jit(solution)/shard_map/ppermute | solution.py:24
  191.2 16.6 %collective-permute-start.31 = (bf16[2,256,256]{2,1,0:T(8,128)(2,1)S(1)}, bf16[2,256,256]{2,1,0:T(8,128)(2,1)S(1)}, u32[]{:S(2)}, u32[]{:S(2)}) collective-permute-start(bf16[2,256,256]{2,1,0:T(8,128)(2,1)S(1)} %get-tuple-element.30), channel_id=1, source_target_pairs={{0,12},{4,8},{8,4},{12,0},{1,13},{5,9},{9,5},{13,1},{2,14},{6,10},... | collective-permute-start | bytes 786440 | tf_op jit(solution)/shard_map/ppermute | solution.py:24
  195.8 12.0 %collective-permute-start.30 = (bf16[2,256,256]{2,1,0:T(8,128)(2,1)S(1)}, bf16[2,256,256]{2,1,0:T(8,128)(2,1)S(1)}, u32[]{:S(2)}, u32[]{:S(2)}) collective-permute-start(bf16[2,256,256]{2,1,0:T(8,128)(2,1)S(1)} %get-tuple-element.31), channel_id=1, source_target_pairs={{0,8},{4,12},{8,0},{12,4},{1,9},{5,13},{9,1},{13,5},{2,10},{6,14},... | collective-permute-start | bytes 786440 | tf_op jit(solution)/shard_map/ppermute | solution.py:24
  197.7 10.1 %collective-permute-start.29 = (bf16[2,256,256]{2,1,0:T(8,128)(2,1)S(1)}, bf16[2,256,256]{2,1,0:T(8,128)(2,1)S(1)}, u32[]{:S(2)}, u32[]{:S(2)}) collective-permute-start(bf16[2,256,256]{2,1,0:T(8,128)(2,1)S(1)} %get-tuple-element.29), channel_id=1, source_target_pairs={{0,4},{4,0},{8,12},{12,8},{1,5},{5,1},{9,13},{13,9},{2,6},{6,2},{1... | collective-permute-start | bytes 786440 | tf_op jit(solution)/shard_map/ppermute | solution.py:24
  200.4 23.8 %collective-permute-start.34 = (bf16[256,256]{1,0:T(8,128)(2,1)S(1)}, bf16[256,256]{1,0:T(8,128)(2,1)S(1)}, u32[]{:S(2)}, u32[]{:S(2)}) collective-permute-start(bf16[256,256]{1,0:T(8,128)(2,1)S(1)} %fusion.3), channel_id=1, source_target_pairs={{0,2},{2,0},{64,66},{66,64},{1,3},{3,1},{65,67},{67,65},{4,6},{6,4... | collective-permute-start | bytes 393224 | tf_op jit(solution)/shard_map/ppermute | solution.py:24
  208.0 21.9 %collective-permute-start.33 = (bf16[256,256]{1,0:T(8,128)(2,1)S(1)}, bf16[256,256]{1,0:T(8,128)(2,1)S(1)}, u32[]{:S(2)}, u32[]{:S(2)}) collective-permute-start(bf16[256,256]{1,0:T(8,128)(2,1)S(1)} %get-tuple-element.36), channel_id=1, source_target_pairs={{0,66},{2,64},{64,2},{66,0},{1,67},{3,65},{65,3},{67,1},{4,70},{6,... | collective-permute-start | bytes 393224 | tf_op jit(solution)/shard_map/ppermute | solution.py:24
  213.8 19.6 %collective-permute-start.32 = (bf16[256,256]{1,0:T(8,128)(2,1)S(1)}, bf16[256,256]{1,0:T(8,128)(2,1)S(1)}, u32[]{:S(2)}, u32[]{:S(2)}) collective-permute-start(bf16[256,256]{1,0:T(8,128)(2,1)S(1)} %get-tuple-element.35), channel_id=1, source_target_pairs={{0,64},{2,66},{64,0},{66,2},{1,65},{3,67},{65,1},{67,3},{4,68},{6,... | collective-permute-start | bytes 393224 | tf_op jit(solution)/shard_map/ppermute | solution.py:24
  (14 other events, 207.5 us)

commit v7 on v6

--- a/solution.py
+++ b/solution.py
@@ -50,7 +50,7 @@
     own += [(8 * a + 2 * q + 1 - a, 8 * a + 2 * q + 1 - q // 2) for a, q in place]
     cross = [(8 * a + 2 * q + 1 - a, 8 * (1 - a) + 2 * q + q // 2) for a, q in place]
     cross += [(8 * a + 2 * q + a, 8 * a + 2 * q + 1 - q // 2) for a, q in place]
-    return lax.ppermute(block, axes, own), lax.ppermute(block, axes, cross)
+    return lax.ppermute(block, axes, own), lambda block: lax.ppermute(block, axes, cross)
 
 
 def spread_blocks(blocks, at):
@@ -148,7 +148,7 @@
         in_specs=[pl.BlockSpec(memory_space=pltpu.SMEM)] + [given] * (len(operands) - 1),
         out_specs=jax.tree.map(lambda _: vmem, out_shape),
         scratch_shapes=scratch + [pltpu.SemaphoreType.DMA((16,))] if copied else [],
-        compiler_params=pltpu.CompilerParams(vmem_limit_bytes=40 * 1024 * 1024),
+        compiler_params=pltpu.CompilerParams(vmem_limit_bytes=(60 if copied else 40) * 1024 * 1024),
         cost_estimate=pl.CostEstimate(flops=flops, bytes_accessed=size, transcendentals=0),
     )(*operands)
 
@@ -165,26 +165,28 @@
         return lax.dynamic_slice_in_dim(array, which * half, half, axis)
 
     both = jnp.concatenate([tokens, jnp.broadcast_to(norm_gain[None], (GAIN_ROWS, cols))], axis=0)
-    both = jnp.stack([both] + [send(both, ("zt", "zh"), k) for k in (1, 2, 3)])
     swapped = swap_halves(weight_half(zt, 1, w_inner), weight_half(1 - zt, 1, w_inner))
-
-    inner = after(jnp.stack(swapped), both)
-    both = after(both, *swapped)
+    z1, z2 = (send(both, ("zt", "zh"), k) for k in (1, 2))
+    z3 = send(after(both, *swapped), ("zt", "zh"), 3)
+    own, swap_cross = swap_blocks(w_outer)
+    both = jnp.stack([both, z1, z2, z3])
+
+    inner = after(jnp.stack(swapped), both, own)
     inner = jnp.stack([inner] + [send(inner, ("zq",), k) for k in (1, 2, 3)], axis=1)
-    y1, y3 = from_neighbours(both, "y")
-
-    in1, in3 = from_neighbours(after(inner, y1, y3), "x")
-    swapped = swap_blocks(after(w_outer, inner, y1, y3))
-    y2 = send(after(both, inner, y1, y3), ("y",), 2)
-
-    in2a, in2b = from_far(after(in1, y2, *swapped), after(in3, y2, *swapped), "x", 1)
-    outer = spread_blocks(after(jnp.stack(swapped), in1, in3, y2), at)
-
-    out1, out3 = from_neighbours(after(outer, in2a, in2b), "x")
+    cross = swap_cross(after(w_outer, both, own))
+    y1 = send(after(both, own), ("y",), 1)
+
+    in1, in3 = from_neighbours(after(inner, y1, cross), "x")
+    outer = spread_blocks(after(jnp.stack([own, cross]), inner, y1), at)
+
+    in2a, in2b = from_far(after(in1, outer), after(in3, outer), "x", 1)
+    out1, out3 = from_neighbours(after(outer, in1, in3), "x")
+    y3 = send(after(both, outer), ("y",), 3)
+    y2 = send(after(both, in2a, in2b), ("y",), 2)
+
     both = jnp.stack([both, y1, y2, y3])
-    other = send(after(both, outer, in2a, in2b), ("c",), 1)
-
-    out2a, out2b = from_far(after(out1, other), after(out3, other), "x", 1)
+    other = send(after(both, out1, out3), ("c",), 1)
+    out2a, out2b = from_far(after(out1, y2, y3), after(out3, y2, y3), "x", 1)
 
     flops = 2 * 2 * rows * half * 16 * cols
     act = call(

time: 236 us -> 235 us (level)
  local copies, waits for them, and re-layouts: 11 us -> 3.56 us
  starting transfers between devices: 129 us -> 136 us
    ppermute x1, waiting for transfers between devices: 10.1 us -> 0.01 us  [swap_halves(): lax.ppermute(first, ('zt', 'c'), [(2 * a + b, 2 * b + a) for a, b in both])]
    ppermute x1, starting transfers between devices: 1.92 us -> 9.65 us  [swap_halves(): lax.ppermute(second, ('zt', 'c'), [(2 * a + b, 2 * b + 1 - a) for a, b in...]
    ppermute x3, waiting for transfers between devices: 0.64 us -> 6.55 us  [spread_blocks(): got.append(lax.ppermute(blocks, ('zq', 'c'), pairs))]
    unnamed x22 -> x28, local copies, waits for them, and re-layouts: 6.93 us -> 1.05 us
    ppermute x28, waiting for transfers between devices: 63.4 us -> 68.7 us  [send(): return lax.ppermute(value, axes, [(i, i ^ k) for i in range(count)])]
    ppermute x3, starting transfers between devices: 11 us -> 6.18 us  [spread_blocks(): got.append(lax.ppermute(blocks, ('zq', 'c'), pairs))]
  transfers between devices with their start and end apart: 35 -> 35, of which waited for: 15 -> 10; matrix products, arithmetic and copies ran while one was open for 3% -> 2% of each run, Pallas kernels for 4% -> 4%
where the time goes in v7:
time: 235 us; the launch traced here: 232 us
  starting transfers between devices  136 us (58%)
  waiting for transfers between devices  75.3 us (32%)
  Pallas kernels  11.7 us (5%)
  other arithmetic  4.85 us (2%)
  local copies, waits for them, and re-layouts  3.56 us (2%)
    ppermute x28, starting transfers between devices, send(): return lax.ppermute(value, axes, [(i, i ^ k) for i in range(count)])  104 us
    ppermute x28, waiting for transfers between devices, send(): return lax.ppermute(value, axes, [(i, i ^ k) for i in range(count)])  68.7 us
    pallas_call x3, Pallas kernels, call(): pl.pallas_call(kernel, out_shape=out_shape, in_specs=[pl.BlockSpec(memory...  11.7 us
    ppermute x1, starting transfers between devices, swap_halves(): lax.ppermute(second, ('zt', 'c'), [(2 * a + b, 2 * b + 1 - a) for a, b in...  9.65 us
    ppermute x1, starting transfers between devices, swap_blocks(): lax.ppermute(block, axes, cross)  7.62 us
    ppermute x1, starting transfers between devices, swap_halves(): lax.ppermute(first, ('zt', 'c'), [(2 * a + b, 2 * b + a) for a, b in both])  6.59 us
    ppermute x3, waiting for transfers between devices, spread_blocks(): got.append(lax.ppermute(blocks, ('zq', 'c'), pairs))  6.55 us
    ppermute x3, starting transfers between devices, spread_blocks(): got.append(lax.ppermute(blocks, ('zq', 'c'), pairs))  6.18 us
  transfers between devices with their start and end apart: 35, of which 10 were waited for; matrix products, arithmetic and copies ran while one was open for 2% of the time, Pallas kernels for 4%

profile of v7, /device:TPU:1, one launch (start us, length us, event | category | flops | bytes accessed | tf_op | source)
XLA Modules:
  0.0 231.7 jit_solution(2897155105426599115)
XLA Ops:
  1.0 9.6 %collective-permute-start.3 = (bf16[128,384]{1,0:T(8,128)(2,1)S(1)}, bf16[128,384]{1,0:T(8,128)(2,1)S(1)}, u32[]{:S(2)}, u32[]{:S(2)}) collective-permute-start(bf16[128,384]{1,0:T(8,128)(2,1)S(1)} %get-tuple-element.43), channel_id=1, source_target_pairs={{0,1},{1,65},{64,0},{65,64},{2,3},{3,67},{66,2},{67,66},{4,5},{5,6... | collective-permute-start | bytes 294920 | tf_op jit(solution)/shard_map/ppermute | solution.py:34
  10.7 6.6 %collective-permute-start.2 = (bf16[128,384]{1,0:T(8,128)(2,1)S(1)}, bf16[128,384]{1,0:T(8,128)(2,1)S(1)}, u32[]{:S(2)}, u32[]{:S(2)}) collective-permute-start(bf16[128,384]{1,0:T(8,128)(2,1)S(1)} %get-tuple-element.44), channel_id=1, source_target_pairs={{0,0},{1,64},{64,1},{65,65},{2,2},{3,66},{66,3},{67,67},{4,4},{5,6... | collective-permute-start | bytes 294920 | tf_op jit(solution)/shard_map/ppermute | solution.py:33
  20.8 10.1 %collective-permute-start = (bf16[272,256]{1,0:T(8,128)(2,1)S(1)}, bf16[272,256]{1,0:T(8,128)(2,1)S(1)}, u32[]{:S(2)}, u32[]{:S(2)}) collective-permute-start(bf16[272,256]{1,0:T(8,128)(2,1)S(1)} %get-tuple-element.19), channel_id=1, source_target_pairs={{0,2},{2,0},{64,66},{66,64},{1,3},{3,1},{65,67},{67,65},{4,6},{6,4... | collective-permute-start | bytes 417800 | tf_op jit(solution)/shard_map/ppermute | solution.py:24
  30.9 4.2 %collective-permute-start.4 = (bf16[272,256]{1,0:T(8,128)(2,1)S(1)}, bf16[272,256]{1,0:T(8,128)(2,1)S(1)}, u32[]{:S(2)}, u32[]{:S(2)}) collective-permute-start(bf16[272,256]{1,0:T(8,128)(2,1)S(1)} %get-tuple-element.19), channel_id=1, source_target_pairs={{0,66},{2,64},{64,2},{66,0},{1,67},{3,65},{65,3},{67,1},{4,70},{6,... | collective-permute-start | bytes 417800 | tf_op jit(solution)/shard_map/ppermute | solution.py:24
  36.7 11.5 %collective-permute-done.1 = bf16[272,256]{1,0:T(8,128)(2,1)S(1)} collective-permute-done((bf16[272,256]{1,0:T(8,128)(2,1)S(1)}, bf16[272,256]{1,0:T(8,128)(2,1)S(1)}, u32[]{:S(2)}, u32[]{:S(2)}) %collective-permute-start.1) | collective-permute-done | bytes 139296 | tf_op jit(solution)/shard_map/ppermute | solution.py:24
  48.2 6.2 %collective-permute-done.4 = bf16[272,256]{1,0:T(8,128)(2,1)S(1)} collective-permute-done((bf16[272,256]{1,0:T(8,128)(2,1)S(1)}, bf16[272,256]{1,0:T(8,128)(2,1)S(1)}, u32[]{:S(2)}, u32[]{:S(2)}) %collective-permute-start.4) | collective-permute-done | bytes 139296 | tf_op jit(solution)/shard_map/ppermute | solution.py:24
  57.2 7.6 %collective-permute-start.10 = (bf16[768,128]{1,0:T(8,128)(2,1)S(1)}, bf16[768,128]{1,0:T(8,128)(2,1)S(1)}, u32[]{:S(2)}, u32[]{:S(2)}) collective-permute-start(bf16[768,128]{1,0:T(8,128)(2,1)S(1)} %copy-done.13), channel_id=1, source_target_pairs={{1,64},{17,80},{33,97},{49,113},{64,0},{80,16},{96,33},{112,49},{0... | collective-permute-start | bytes 589832 | tf_op jit(solution)/shard_map/ppermute | solution.py:53
  64.8 6.7 %collective-permute-start.9 = (bf16[2,128,384]{2,1,0:T(8,128)(2,1)S(1)}, bf16[2,128,384]{2,1,0:T(8,128)(2,1)S(1)}, u32[]{:S(2)}, u32[]{:S(2)}) collective-permute-start(bf16[2,128,384]{2,1,0:T(8,128)(2,1)S(1)} %pad_maximum_fusion.5), channel_id=1, source_target_pairs={{0,48},{16,32},{32,16},{48,0},{1,49},{17,33},{33,17},{49,1},{2,50}... | collective-permute-start | bytes 589832 | tf_op jit(solution)/shard_map/ppermute | solution.py:24
  75.7 3.2 %collective-permute-done.9 = bf16[2,128,384]{2,1,0:T(8,128)(2,1)S(1)} collective-permute-done((bf16[2,128,384]{2,1,0:T(8,128)(2,1)S(1)}, bf16[2,128,384]{2,1,0:T(8,128)(2,1)S(1)}, u32[]{:S(2)}, u32[]{:S(2)}) %collective-permute-start.9) | collective-permute-done | bytes 196640 | tf_op jit(solution)/shard_map/ppermute | solution.py:24
  78.9 11.3 %collective-permute-done.8 = bf16[2,128,384]{2,1,0:T(8,128)(2,1)S(1)} collective-permute-done((bf16[2,128,384]{2,1,0:T(8,128)(2,1)S(1)}, bf16[2,128,384]{2,1,0:T(8,128)(2,1)S(1)}, u32[]{:S(2)}, u32[]{:S(2)}) %collective-permute-start.8) | collective-permute-done | bytes 196640 | tf_op jit(solution)/shard_map/ppermute | solution.py:24
  92.7 3.3 %collective-permute-start.16 = (bf16[2,4,128,384]{3,2,1,0:T(8,128)(2,1)S(1)}, bf16[2,4,128,384]{3,2,1,0:T(8,128)(2,1)S(1)}, u32[]{:S(2)}, u32[]{:S(2)}) collective-permute-start(bf16[2,4,128,384]{3,2,1,0:T(8,128)(2,1)S(1)} %pad_maximum_fusion.1.refs_2_), channel_id=1, source_target_pairs={{0,128},{128,0},{256,384},{384,256},{1,129},{129,1},{257,385},{385... | collective-permute-start | bytes 2359304 | tf_op jit(solution)/shard_map/ppermute | solution.py:24
  96.0 3.7 %collective-permute-start.11 = (bf16[2,4,128,384]{3,2,1,0:T(8,128)(2,1)S(1)}, bf16[2,4,128,384]{3,2,1,0:T(8,128)(2,1)S(1)}, u32[]{:S(2)}, u32[]{:S(2)}) collective-permute-start(bf16[2,4,128,384]{3,2,1,0:T(8,128)(2,1)S(1)} %pad_maximum_fusion.1.refs_2_), channel_id=1, source_target_pairs={{0,384},{128,256},{256,128},{384,0},{1,385},{129,257},{257,129},{3... | collective-permute-start | bytes 2359304 | tf_op jit(solution)/shard_map/ppermute | solution.py:24
  103.7 6.5 %collective-permute-done.14 = bf16[2,768,128]{2,1,0:T(8,128)(2,1)S(1)} collective-permute-done((bf16[2,768,128]{2,1,0:T(8,128)(2,1)S(1)}, bf16[2,768,128]{2,1,0:T(8,128)(2,1)S(1)}, u32[]{:S(2)}, u32[]{:S(2)}) %collective-permute-start.14) | collective-permute-done | bytes 393248 | tf_op jit(solution)/shard_map/ppermute | solution.py:61
  110.4 3.4 %collective-permute-done.16.refs_3_ = bf16[2,4,128,384]{3,2,1,0:T(8,128)(2,1)S(1)} collective-permute-done((bf16[2,4,128,384]{3,2,1,0:T(8,128)(2,1)S(1)}, bf16[2,4,128,384]{3,2,1,0:T(8,128)(2,1)S(1)}, u32[]{:S(2)}, u32[]{:S(2)}) %collective-permute-start.16) | collective-permute-done | bytes 786464 | tf_op jit(solution)/shard_map/ppermute | solution.py:24
  113.9 4.5 %collective-permute-start.17 = (bf16[1,4,128,384]{3,2,1,0:T(8,128)(2,1)S(1)}, bf16[1,4,128,384]{3,2,1,0:T(8,128)(2,1)S(1)}, u32[]{:S(2)}, u32[]{:S(2)}) collective-permute-start(bf16[1,4,128,384]{3,2,1,0:T(8,128)(2,1)S(1)} %slice.49), channel_id=1, source_target_pairs={{0,384},{128,256},{256,128},{384,0},{1,385},{129,257},{257,129},{3... | collective-permute-start | bytes 1179656 | tf_op jit(solution)/shard_map/ppermute | solution.py:24
  120.4 3.3 %collective-permute-start.21 = (bf16[2,2,768,128]{3,2,1,0:T(8,128)(2,1)S(1)}, bf16[2,2,768,128]{3,2,1,0:T(8,128)(2,1)S(1)}, u32[]{:S(2)}, u32[]{:S(2)}) collective-permute-start(bf16[2,2,768,128]{3,2,1,0:T(8,128)(2,1)S(1)} %pad_maximum_fusion.2.w0), channel_id=1, source_target_pairs={{0,384},{128,256},{256,128},{384,0},{1,385},{129,257},{257,129},{3... | collective-permute-start | bytes 2359304 | tf_op jit(solution)/shard_map/ppermute | solution.py:24
  123.7 2.8 %collective-permute-start.20 = (bf16[2,2,768,128]{3,2,1,0:T(8,128)(2,1)S(1)}, bf16[2,2,768,128]{3,2,1,0:T(8,128)(2,1)S(1)}, u32[]{:S(2)}, u32[]{:S(2)}) collective-permute-start(bf16[2,2,768,128]{3,2,1,0:T(8,128)(2,1)S(1)} %pad_maximum_fusion.2.w0), channel_id=1, source_target_pairs={{0,128},{128,0},{256,384},{384,256},{1,129},{129,1},{257,385},{385... | collective-permute-start | bytes 2359304 | tf_op jit(solution)/shard_map/ppermute | solution.py:24
  126.4 3.8 %collective-permute-start.19 = (bf16[4,272,256]{2,1,0:T(8,128)(2,1)S(1)}, bf16[4,272,256]{2,1,0:T(8,128)(2,1)S(1)}, u32[]{:S(2)}, u32[]{:S(2)}) collective-permute-start(bf16[4,272,256]{2,1,0:T(8,128)(2,1)S(1)} %copy-done.10), channel_id=1, source_target_pairs={{0,12},{4,8},{8,4},{12,0},{1,13},{5,9},{9,5},{13,1},{2,14},{6,10},... | collective-permute-start | bytes 1671176 | tf_op jit(solution)/shard_map/ppermute | solution.py:24
  130.3 4.1 %collective-permute-start.18 = (bf16[4,272,256]{2,1,0:T(8,128)(2,1)S(1)}, bf16[4,272,256]{2,1,0:T(8,128)(2,1)S(1)}, u32[]{:S(2)}, u32[]{:S(2)}) collective-permute-start(bf16[4,272,256]{2,1,0:T(8,128)(2,1)S(1)} %copy-done.10), channel_id=1, source_target_pairs={{0,8},{4,12},{8,0},{12,4},{1,9},{5,13},{9,1},{13,5},{2,10},{6,14},... | collective-permute-start | bytes 1671176 | tf_op jit(solution)/shard_map/ppermute | solution.py:24
  134.4 18.8 %collective-permute-done.19 = bf16[4,272,256]{2,1,0:T(8,128)(2,1)S(1)} collective-permute-done((bf16[4,272,256]{2,1,0:T(8,128)(2,1)S(1)}, bf16[4,272,256]{2,1,0:T(8,128)(2,1)S(1)}, u32[]{:S(2)}, u32[]{:S(2)}) %collective-permute-start.19) | collective-permute-done | bytes 557088 | tf_op jit(solution)/shard_map/ppermute | solution.py:24
  155.0 5.2 %collective-permute-start.22 = (bf16[4,4,272,256]{3,2,1,0:T(8,128)(2,1)}, bf16[4,4,272,256]{3,2,1,0:T(8,128)(2,1)}, u32[]{:S(2)}, u32[]{:S(2)}) collective-permute-start(bf16[4,4,272,256]{3,2,1,0:T(8,128)(2,1)} %pad_maximum_fusion.refs_0_), channel_id=1, source_target_pairs={{0,1},{1,0},{2,3},{3,2},{4,5},{5,4},{6,7},{7,6},{8,9},{9,8},{10,11... | collective-permute-start | bytes 6684680 | tf_op jit(solution)/shard_map/ppermute | solution.py:24
  160.8 2.5 %collective-permute-start.24 = (bf16[1,2,768,128]{3,2,1,0:T(8,128)(2,1)S(1)}, bf16[1,2,768,128]{3,2,1,0:T(8,128)(2,1)S(1)}, u32[]{:S(2)}, u32[]{:S(2)}) collective-permute-start(bf16[1,2,768,128]{3,2,1,0:T(8,128)(2,1)S(1)} %slice.50), channel_id=1, source_target_pairs={{0,128},{128,0},{256,384},{384,256},{1,129},{129,1},{257,385},{385... | collective-permute-start | bytes 1179656 | tf_op jit(solution)/shard_map/ppermute | solution.py:24
  163.3 3.2 %collective-permute-start.25 = (bf16[1,2,768,128]{3,2,1,0:T(8,128)(2,1)S(1)}, bf16[1,2,768,128]{3,2,1,0:T(8,128)(2,1)S(1)}, u32[]{:S(2)}, u32[]{:S(2)}) collective-permute-start(bf16[1,2,768,128]{3,2,1,0:T(8,128)(2,1)S(1)} %slice.51), channel_id=1, source_target_pairs={{0,384},{128,256},{256,128},{384,0},{1,385},{129,257},{257,129},{3... | collective-permute-start | bytes 1179656 | tf_op jit(solution)/shard_map/ppermute | solution.py:24
  166.6 8.1 %shard_map.46.act = bf16[2,256,384]{2,1,0:T(8,128)(2,1)} custom-call(s32[6]{0:T(128)} %stack.99.place, bf16[4,4,272,256]{3,2,1,0:T(8,128)(2,1)} %pad_maximum_fusion.refs_0_, bf16[4,4,272,256]{3,2,1,0:T(8,128)(2,1)} %collective-permute-done.22.refs_1_, bf16[2,4,128,384]{3,2,1,0:T(8,128)(2,1)} %copy-done.3, bf16[2,4,128,384]{3,2,1,0:T(8,128)(2,1)} %copy-done.5, ...), custom_call_target="tpu_custom_call" | custom-call | flops 1610612736 | bytes 7602200 | tf_op jit(solution)/shard_map/pallas_call | solution.py:145
  183.5 3.8 %collective-permute-start.28 = (bf16[2,256,256]{2,1,0:T(8,128)(2,1)S(1)}, bf16[2,256,256]{2,1,0:T(8,128)(2,1)S(1)}, u32[]{:S(2)}, u32[]{:S(2)}) collective-permute-start(bf16[2,256,256]{2,1,0:T(8,128)(2,1)S(1)} %get-tuple-element.37), channel_id=1, source_target_pairs={{0,12},{4,8},{8,4},{12,0},{1,13},{5,9},{9,5},{13,1},{2,14},{6,10},... | collective-permute-start | bytes 786440 | tf_op jit(solution)/shard_map/ppermute | solution.py:24
  187.3 3.2 %collective-permute-start.27 = (bf16[2,256,256]{2,1,0:T(8,128)(2,1)S(1)}, bf16[2,256,256]{2,1,0:T(8,128)(2,1)S(1)}, u32[]{:S(2)}, u32[]{:S(2)}) collective-permute-start(bf16[2,256,256]{2,1,0:T(8,128)(2,1)S(1)} %get-tuple-element.38), channel_id=1, source_target_pairs={{0,8},{4,12},{8,0},{12,4},{1,9},{5,13},{9,1},{13,5},{2,10},{6,14},... | collective-permute-start | bytes 786440 | tf_op jit(solution)/shard_map/ppermute | solution.py:24
  194.4 3.8 %collective-permute-start.31 = (bf16[2,256,256]{2,1,0:T(8,128)(2,1)S(1)}, bf16[2,256,256]{2,1,0:T(8,128)(2,1)S(1)}, u32[]{:S(2)}, u32[]{:S(2)}) collective-permute-start(bf16[2,256,256]{2,1,0:T(8,128)(2,1)S(1)} %get-tuple-element.34), channel_id=1, source_target_pairs={{0,12},{4,8},{8,4},{12,0},{1,13},{5,9},{9,5},{13,1},{2,14},{6,10},... | collective-permute-start | bytes 786440 | tf_op jit(solution)/shard_map/ppermute | solution.py:24
  198.2 3.2 %collective-permute-start.30 = (bf16[2,256,256]{2,1,0:T(8,128)(2,1)S(1)}, bf16[2,256,256]{2,1,0:T(8,128)(2,1)S(1)}, u32[]{:S(2)}, u32[]{:S(2)}) collective-permute-start(bf16[2,256,256]{2,1,0:T(8,128)(2,1)S(1)} %get-tuple-element.35), channel_id=1, source_target_pairs={{0,8},{4,12},{8,0},{12,4},{1,9},{5,13},{9,1},{13,5},{2,10},{6,14},... | collective-permute-start | bytes 786440 | tf_op jit(solution)/shard_map/ppermute | solution.py:24
  201.6 7.2 %collective-permute-start.34 = (bf16[256,256]{1,0:T(8,128)(2,1)S(1)}, bf16[256,256]{1,0:T(8,128)(2,1)S(1)}, u32[]{:S(2)}, u32[]{:S(2)}) collective-permute-start(bf16[256,256]{1,0:T(8,128)(2,1)S(1)} %fusion.3), channel_id=1, source_target_pairs={{0,2},{2,0},{64,66},{66,64},{1,3},{3,1},{65,67},{67,65},{4,6},{6,4... | collective-permute-start | bytes 393224 | tf_op jit(solution)/shard_map/ppermute | solution.py:24
  211.4 6.9 %collective-permute-start.33 = (bf16[256,256]{1,0:T(8,128)(2,1)S(1)}, bf16[256,256]{1,0:T(8,128)(2,1)S(1)}, u32[]{:S(2)}, u32[]{:S(2)}) collective-permute-start(bf16[256,256]{1,0:T(8,128)(2,1)S(1)} %get-tuple-element.42), channel_id=1, source_target_pairs={{0,66},{2,64},{64,2},{66,0},{1,67},{3,65},{65,3},{67,1},{4,70},{6,... | collective-permute-start | bytes 393224 | tf_op jit(solution)/shard_map/ppermute | solution.py:24
  218.3 7.1 %collective-permute-done.34 = bf16[256,256]{1,0:T(8,128)(2,1)S(1)} collective-permute-done((bf16[256,256]{1,0:T(8,128)(2,1)S(1)}, bf16[256,256]{1,0:T(8,128)(2,1)S(1)}, u32[]{:S(2)}, u32[]{:S(2)}) %collective-permute-start.34) | collective-permute-done | bytes 131104 | tf_op jit(solution)/shard_map/ppermute | solution.py:24
  225.4 5.6 %collective-permute-done.32 = bf16[256,256]{1,0:T(8,128)(2,1)S(1)} collective-permute-done((bf16[256,256]{1,0:T(8,128)(2,1)S(1)}, bf16[256,256]{1,0:T(8,128)(2,1)S(1)}, u32[]{:S(2)}, u32[]{:S(2)}) %collective-permute-start.32) | collective-permute-done | bytes 131104 | tf_op jit(solution)/shard_map/ppermute | solution.py:24
  (92 shorter events, 39.9 us)
Async XLA Ops:
  1.0 29.8 %collective-permute-start.3 = (bf16[128,384]{1,0:T(8,128)(2,1)S(1)}, bf16[128,384]{1,0:T(8,128)(2,1)S(1)}, u32[]{:S(2)}, u32[]{:S(2)}) collective-permute-start(bf16[128,384]{1,0:T(8,128)(2,1)S(1)} %get-tuple-element.43), channel_id=1, source_target_pairs={{0,1},{1,65},{64,0},{65,64},{2,3},{3,67},{66,2},{67,66},{4,5},{5,6... | collective-permute-start | bytes 294920 | tf_op jit(solution)/shard_map/ppermute | solution.py:34
  10.7 20.2 %collective-permute-start.2 = (bf16[128,384]{1,0:T(8,128)(2,1)S(1)}, bf16[128,384]{1,0:T(8,128)(2,1)S(1)}, u32[]{:S(2)}, u32[]{:S(2)}) collective-permute-start(bf16[128,384]{1,0:T(8,128)(2,1)S(1)} %get-tuple-element.44), channel_id=1, source_target_pairs={{0,0},{1,64},{64,1},{65,65},{2,2},{3,66},{66,3},{67,67},{4,4},{5,6... | collective-permute-start | bytes 294920 | tf_op jit(solution)/shard_map/ppermute | solution.py:33
  18.8 29.3 %collective-permute-start.1 = (bf16[272,256]{1,0:T(8,128)(2,1)S(1)}, bf16[272,256]{1,0:T(8,128)(2,1)S(1)}, u32[]{:S(2)}, u32[]{:S(2)}) collective-permute-start(bf16[272,256]{1,0:T(8,128)(2,1)S(1)} %get-tuple-element.19), channel_id=1, source_target_pairs={{0,64},{2,66},{64,0},{66,2},{1,65},{3,67},{65,1},{67,3},{4,68},{6,... | collective-permute-start | bytes 417800 | tf_op jit(solution)/shard_map/ppermute | solution.py:24
  20.8 27.4 %collective-permute-start = (bf16[272,256]{1,0:T(8,128)(2,1)S(1)}, bf16[272,256]{1,0:T(8,128)(2,1)S(1)}, u32[]{:S(2)}, u32[]{:S(2)}) collective-permute-start(bf16[272,256]{1,0:T(8,128)(2,1)S(1)} %get-tuple-element.19), channel_id=1, source_target_pairs={{0,2},{2,0},{64,66},{66,64},{1,3},{3,1},{65,67},{67,65},{4,6},{6,4... | collective-permute-start | bytes 417800 | tf_op jit(solution)/shard_map/ppermute | solution.py:24
  30.9 23.5 %collective-permute-start.4 = (bf16[272,256]{1,0:T(8,128)(2,1)S(1)}, bf16[272,256]{1,0:T(8,128)(2,1)S(1)}, u32[]{:S(2)}, u32[]{:S(2)}) collective-permute-start(bf16[272,256]{1,0:T(8,128)(2,1)S(1)} %get-tuple-element.19), channel_id=1, source_target_pairs={{0,66},{2,64},{64,2},{66,0},{1,67},{3,65},{65,3},{67,1},{4,70},{6,... | collective-permute-start | bytes 417800 | tf_op jit(solution)/shard_map/ppermute | solution.py:24
  35.1 20.2 %collective-permute-start.5 = (bf16[768,128]{1,0:T(8,128)(2,1)}, bf16[768,128]{1,0:T(8,128)(2,1)S(1)}, u32[]{:S(2)}, u32[]{:S(2)}) collective-permute-start(bf16[768,128]{1,0:T(8,128)(2,1)} %param.7), channel_id=1, source_target_pairs={{0,0},{16,16},{32,33},{48,49},{65,64},{81,80},{97,97},{113,113},{1... | collective-permute-start | bytes 589832 | tf_op jit(solution)/shard_map/ppermute | solution.py:53
  55.3 35.1 %collective-permute-start.6 = (bf16[4,272,256]{2,1,0:T(8,128)(2,1)S(1)}, bf16[4,272,256]{2,1,0:T(8,128)(2,1)S(1)}, u32[]{:S(2)}, u32[]{:S(2)}) collective-permute-start(bf16[4,272,256]{2,1,0:T(8,128)(2,1)S(1)} %get-tuple-element.27), channel_id=1, source_target_pairs={{0,4},{4,0},{8,12},{12,8},{1,5},{5,1},{9,13},{13,9},{2,6},{6,2},{1... | collective-permute-start | bytes 1671176 | tf_op jit(solution)/shard_map/ppermute | solution.py:24
  57.2 18.5 %collective-permute-start.10 = (bf16[768,128]{1,0:T(8,128)(2,1)S(1)}, bf16[768,128]{1,0:T(8,128)(2,1)S(1)}, u32[]{:S(2)}, u32[]{:S(2)}) collective-permute-start(bf16[768,128]{1,0:T(8,128)(2,1)S(1)} %copy-done.13), channel_id=1, source_target_pairs={{1,64},{17,80},{33,97},{49,113},{64,0},{80,16},{96,33},{112,49},{0... | collective-permute-start | bytes 589832 | tf_op jit(solution)/shard_map/ppermute | solution.py:53
  64.8 14.1 %collective-permute-start.9 = (bf16[2,128,384]{2,1,0:T(8,128)(2,1)S(1)}, bf16[2,128,384]{2,1,0:T(8,128)(2,1)S(1)}, u32[]{:S(2)}, u32[]{:S(2)}) collective-permute-start(bf16[2,128,384]{2,1,0:T(8,128)(2,1)S(1)} %pad_maximum_fusion.5), channel_id=1, source_target_pairs={{0,48},{16,32},{32,16},{48,0},{1,49},{17,33},{33,17},{49,1},{2,50}... | collective-permute-start | bytes 589832 | tf_op jit(solution)/shard_map/ppermute | solution.py:24
  71.5 18.7 %collective-permute-start.8 = (bf16[2,128,384]{2,1,0:T(8,128)(2,1)S(1)}, bf16[2,128,384]{2,1,0:T(8,128)(2,1)S(1)}, u32[]{:S(2)}, u32[]{:S(2)}) collective-permute-start(bf16[2,128,384]{2,1,0:T(8,128)(2,1)S(1)} %pad_maximum_fusion.5), channel_id=1, source_target_pairs={{0,32},{16,48},{32,0},{48,16},{1,33},{17,49},{33,1},{49,17},{2,34}... | collective-permute-start | bytes 589832 | tf_op jit(solution)/shard_map/ppermute | solution.py:24
  73.4 16.8 %collective-permute-start.7 = (bf16[2,128,384]{2,1,0:T(8,128)(2,1)S(1)}, bf16[2,128,384]{2,1,0:T(8,128)(2,1)S(1)}, u32[]{:S(2)}, u32[]{:S(2)}) collective-permute-start(bf16[2,128,384]{2,1,0:T(8,128)(2,1)S(1)} %pad_maximum_fusion.5), channel_id=1, source_target_pairs={{0,16},{16,0},{32,48},{48,32},{1,17},{17,1},{33,49},{49,33},{2,18}... | collective-permute-start | bytes 589832 | tf_op jit(solution)/shard_map/ppermute | solution.py:24
  90.4 13.3 %collective-permute-start.12 = (bf16[2,768,128]{2,1,0:T(8,128)(2,1)S(1)}, bf16[2,768,128]{2,1,0:T(8,128)(2,1)S(1)}, u32[]{:S(2)}, u32[]{:S(2)}) collective-permute-start(bf16[2,768,128]{2,1,0:T(8,128)(2,1)S(1)} %pad_maximum_fusion.4), channel_id=1, source_target_pairs={{0,32},{16,48},{33,1},{49,17},{1,0},{17,16},{32,33},{48,49},{2,34}... | collective-permute-start | bytes 1179656 | tf_op jit(solution)/shard_map/ppermute | solution.py:61
  92.7 21.2 %collective-permute-start.16 = (bf16[2,4,128,384]{3,2,1,0:T(8,128)(2,1)S(1)}, bf16[2,4,128,384]{3,2,1,0:T(8,128)(2,1)S(1)}, u32[]{:S(2)}, u32[]{:S(2)}) collective-permute-start(bf16[2,4,128,384]{3,2,1,0:T(8,128)(2,1)S(1)} %pad_maximum_fusion.1.refs_2_), channel_id=1, source_target_pairs={{0,128},{128,0},{256,384},{384,256},{1,129},{129,1},{257,385},{385... | collective-permute-start | bytes 2359304 | tf_op jit(solution)/shard_map/ppermute | solution.py:24
  96.0 22.4 %collective-permute-start.11 = (bf16[2,4,128,384]{3,2,1,0:T(8,128)(2,1)S(1)}, bf16[2,4,128,384]{3,2,1,0:T(8,128)(2,1)S(1)}, u32[]{:S(2)}, u32[]{:S(2)}) collective-permute-start(bf16[2,4,128,384]{3,2,1,0:T(8,128)(2,1)S(1)} %pad_maximum_fusion.1.refs_2_), channel_id=1, source_target_pairs={{0,384},{128,256},{256,128},{384,0},{1,385},{129,257},{257,129},{3... | collective-permute-start | bytes 2359304 | tf_op jit(solution)/shard_map/ppermute | solution.py:24
  113.9 16.4 %collective-permute-start.17 = (bf16[1,4,128,384]{3,2,1,0:T(8,128)(2,1)S(1)}, bf16[1,4,128,384]{3,2,1,0:T(8,128)(2,1)S(1)}, u32[]{:S(2)}, u32[]{:S(2)}) collective-permute-start(bf16[1,4,128,384]{3,2,1,0:T(8,128)(2,1)S(1)} %slice.49), channel_id=1, source_target_pairs={{0,384},{128,256},{256,128},{384,0},{1,385},{129,257},{257,129},{3... | collective-permute-start | bytes 1179656 | tf_op jit(solution)/shard_map/ppermute | solution.py:24
  118.4 11.8 %collective-permute-start.15 = (bf16[1,4,128,384]{3,2,1,0:T(8,128)(2,1)S(1)}, bf16[1,4,128,384]{3,2,1,0:T(8,128)(2,1)S(1)}, u32[]{:S(2)}, u32[]{:S(2)}) collective-permute-start(bf16[1,4,128,384]{3,2,1,0:T(8,128)(2,1)S(1)} %slice.48), channel_id=1, source_target_pairs={{0,128},{128,0},{256,384},{384,256},{1,129},{129,1},{257,385},{385... | collective-permute-start | bytes 1179656 | tf_op jit(solution)/shard_map/ppermute | solution.py:24
  120.4 34.6 %collective-permute-start.21 = (bf16[2,2,768,128]{3,2,1,0:T(8,128)(2,1)S(1)}, bf16[2,2,768,128]{3,2,1,0:T(8,128)(2,1)S(1)}, u32[]{:S(2)}, u32[]{:S(2)}) collective-permute-start(bf16[2,2,768,128]{3,2,1,0:T(8,128)(2,1)S(1)} %pad_maximum_fusion.2.w0), channel_id=1, source_target_pairs={{0,384},{128,256},{256,128},{384,0},{1,385},{129,257},{257,129},{3... | collective-permute-start | bytes 2359304 | tf_op jit(solution)/shard_map/ppermute | solution.py:24
  123.7 31.3 %collective-permute-start.20 = (bf16[2,2,768,128]{3,2,1,0:T(8,128)(2,1)S(1)}, bf16[2,2,768,128]{3,2,1,0:T(8,128)(2,1)S(1)}, u32[]{:S(2)}, u32[]{:S(2)}) collective-permute-start(bf16[2,2,768,128]{3,2,1,0:T(8,128)(2,1)S(1)} %pad_maximum_fusion.2.w0), channel_id=1, source_target_pairs={{0,128},{128,0},{256,384},{384,256},{1,129},{129,1},{257,385},{385... | collective-permute-start | bytes 2359304 | tf_op jit(solution)/shard_map/ppermute | solution.py:24
  126.4 26.8 %collective-permute-start.19 = (bf16[4,272,256]{2,1,0:T(8,128)(2,1)S(1)}, bf16[4,272,256]{2,1,0:T(8,128)(2,1)S(1)}, u32[]{:S(2)}, u32[]{:S(2)}) collective-permute-start(bf16[4,272,256]{2,1,0:T(8,128)(2,1)S(1)} %copy-done.10), channel_id=1, source_target_pairs={{0,12},{4,8},{8,4},{12,0},{1,13},{5,9},{9,5},{13,1},{2,14},{6,10},... | collective-permute-start | bytes 1671176 | tf_op jit(solution)/shard_map/ppermute | solution.py:24
  130.3 23.0 %collective-permute-start.18 = (bf16[4,272,256]{2,1,0:T(8,128)(2,1)S(1)}, bf16[4,272,256]{2,1,0:T(8,128)(2,1)S(1)}, u32[]{:S(2)}, u32[]{:S(2)}) collective-permute-start(bf16[4,272,256]{2,1,0:T(8,128)(2,1)S(1)} %copy-done.10), channel_id=1, source_target_pairs={{0,8},{4,12},{8,0},{12,4},{1,9},{5,13},{9,1},{13,5},{2,10},{6,14},... | collective-permute-start | bytes 1671176 | tf_op jit(solution)/shard_map/ppermute | solution.py:24
  155.0 11.6 %collective-permute-start.22 = (bf16[4,4,272,256]{3,2,1,0:T(8,128)(2,1)}, bf16[4,4,272,256]{3,2,1,0:T(8,128)(2,1)}, u32[]{:S(2)}, u32[]{:S(2)}) collective-permute-start(bf16[4,4,272,256]{3,2,1,0:T(8,128)(2,1)} %pad_maximum_fusion.refs_0_), channel_id=1, source_target_pairs={{0,1},{1,0},{2,3},{3,2},{4,5},{5,4},{6,7},{7,6},{8,9},{9,8},{10,11... | collective-permute-start | bytes 6684680 | tf_op jit(solution)/shard_map/ppermute | solution.py:24
  160.8 16.4 %collective-permute-start.24 = (bf16[1,2,768,128]{3,2,1,0:T(8,128)(2,1)S(1)}, bf16[1,2,768,128]{3,2,1,0:T(8,128)(2,1)S(1)}, u32[]{:S(2)}, u32[]{:S(2)}) collective-permute-start(bf16[1,2,768,128]{3,2,1,0:T(8,128)(2,1)S(1)} %slice.50), channel_id=1, source_target_pairs={{0,128},{128,0},{256,384},{384,256},{1,129},{129,1},{257,385},{385... | collective-permute-start | bytes 1179656 | tf_op jit(solution)/shard_map/ppermute | solution.py:24
  163.3 13.8 %collective-permute-start.25 = (bf16[1,2,768,128]{3,2,1,0:T(8,128)(2,1)S(1)}, bf16[1,2,768,128]{3,2,1,0:T(8,128)(2,1)S(1)}, u32[]{:S(2)}, u32[]{:S(2)}) collective-permute-start(bf16[1,2,768,128]{3,2,1,0:T(8,128)(2,1)S(1)} %slice.51), channel_id=1, source_target_pairs={{0,384},{128,256},{256,128},{384,0},{1,385},{129,257},{257,129},{3... | collective-permute-start | bytes 1179656 | tf_op jit(solution)/shard_map/ppermute | solution.py:24
  181.6 16.6 %collective-permute-start.26 = (bf16[2,256,256]{2,1,0:T(8,128)(2,1)S(1)}, bf16[2,256,256]{2,1,0:T(8,128)(2,1)S(1)}, u32[]{:S(2)}, u32[]{:S(2)}) collective-permute-start(bf16[2,256,256]{2,1,0:T(8,128)(2,1)S(1)} %get-tuple-element.36), channel_id=1, source_target_pairs={{0,4},{4,0},{8,12},{12,8},{1,5},{5,1},{9,13},{13,9},{2,6},{6,2},{1... | collective-permute-start | bytes 786440 | tf_op jit(solution)/shard_map/ppermute | solution.py:24
  183.5 18.0 %collective-permute-start.28 = (bf16[2,256,256]{2,1,0:T(8,128)(2,1)S(1)}, bf16[2,256,256]{2,1,0:T(8,128)(2,1)S(1)}, u32[]{:S(2)}, u32[]{:S(2)}) collective-permute-start(bf16[2,256,256]{2,1,0:T(8,128)(2,1)S(1)} %get-tuple-element.37), channel_id=1, source_target_pairs={{0,12},{4,8},{8,4},{12,0},{1,13},{5,9},{9,5},{13,1},{2,14},{6,10},... | collective-permute-start | bytes 786440 | tf_op jit(solution)/shard_map/ppermute | solution.py:24
  187.3 14.2 %collective-permute-start.27 = (bf16[2,256,256]{2,1,0:T(8,128)(2,1)S(1)}, bf16[2,256,256]{2,1,0:T(8,128)(2,1)S(1)}, u32[]{:S(2)}, u32[]{:S(2)}) collective-permute-start(bf16[2,256,256]{2,1,0:T(8,128)(2,1)S(1)} %get-tuple-element.38), channel_id=1, source_target_pairs={{0,8},{4,12},{8,0},{12,4},{1,9},{5,13},{9,1},{13,5},{2,10},{6,14},... | collective-permute-start | bytes 786440 | tf_op jit(solution)/shard_map/ppermute | solution.py:24
  192.4 16.4 %collective-permute-start.29 = (bf16[2,256,256]{2,1,0:T(8,128)(2,1)S(1)}, bf16[2,256,256]{2,1,0:T(8,128)(2,1)S(1)}, u32[]{:S(2)}, u32[]{:S(2)}) collective-permute-start(bf16[2,256,256]{2,1,0:T(8,128)(2,1)S(1)} %get-tuple-element.33), channel_id=1, source_target_pairs={{0,4},{4,0},{8,12},{12,8},{1,5},{5,1},{9,13},{13,9},{2,6},{6,2},{1... | collective-permute-start | bytes 786440 | tf_op jit(solution)/shard_map/ppermute | solution.py:24
  194.4 14.5 %collective-permute-start.31 = (bf16[2,256,256]{2,1,0:T(8,128)(2,1)S(1)}, bf16[2,256,256]{2,1,0:T(8,128)(2,1)S(1)}, u32[]{:S(2)}, u32[]{:S(2)}) collective-permute-start(bf16[2,256,256]{2,1,0:T(8,128)(2,1)S(1)} %get-tuple-element.34), channel_id=1, source_target_pairs={{0,12},{4,8},{8,4},{12,0},{1,13},{5,9},{9,5},{13,1},{2,14},{6,10},... | collective-permute-start | bytes 786440 | tf_op jit(solution)/shard_map/ppermute | solution.py:24
  198.2 10.7 %collective-permute-start.30 = (bf16[2,256,256]{2,1,0:T(8,128)(2,1)S(1)}, bf16[2,256,256]{2,1,0:T(8,128)(2,1)S(1)}, u32[]{:S(2)}, u32[]{:S(2)}) collective-permute-start(bf16[2,256,256]{2,1,0:T(8,128)(2,1)S(1)} %get-tuple-element.35), channel_id=1, source_target_pairs={{0,8},{4,12},{8,0},{12,4},{1,9},{5,13},{9,1},{13,5},{2,10},{6,14},... | collective-permute-start | bytes 786440 | tf_op jit(solution)/shard_map/ppermute | solution.py:24
  201.6 23.7 %collective-permute-start.34 = (bf16[256,256]{1,0:T(8,128)(2,1)S(1)}, bf16[256,256]{1,0:T(8,128)(2,1)S(1)}, u32[]{:S(2)}, u32[]{:S(2)}) collective-permute-start(bf16[256,256]{1,0:T(8,128)(2,1)S(1)} %fusion.3), channel_id=1, source_target_pairs={{0,2},{2,0},{64,66},{66,64},{1,3},{3,1},{65,67},{67,65},{4,6},{6,4... | collective-permute-start | bytes 393224 | tf_op jit(solution)/shard_map/ppermute | solution.py:24
  209.1 21.9 %collective-permute-start.32 = (bf16[256,256]{1,0:T(8,128)(2,1)S(1)}, bf16[256,256]{1,0:T(8,128)(2,1)S(1)}, u32[]{:S(2)}, u32[]{:S(2)}) collective-permute-start(bf16[256,256]{1,0:T(8,128)(2,1)S(1)} %get-tuple-element.41), channel_id=1, source_target_pairs={{0,64},{2,66},{64,0},{66,2},{1,65},{3,67},{65,1},{67,3},{4,68},{6,... | collective-permute-start | bytes 393224 | tf_op jit(solution)/shard_map/ppermute | solution.py:24
  211.4 19.6 %collective-permute-start.33 = (bf16[256,256]{1,0:T(8,128)(2,1)S(1)}, bf16[256,256]{1,0:T(8,128)(2,1)S(1)}, u32[]{:S(2)}, u32[]{:S(2)}) collective-permute-start(bf16[256,256]{1,0:T(8,128)(2,1)S(1)} %get-tuple-element.42), channel_id=1, source_target_pairs={{0,66},{2,64},{64,2},{66,0},{1,67},{3,65},{65,3},{67,1},{4,70},{6,... | collective-permute-start | bytes 393224 | tf_op jit(solution)/shard_map/ppermute | solution.py:24
  (17 other events, 361.5 us)

commit v8 on v7

--- a/solution.py
+++ b/solution.py
@@ -50,7 +50,7 @@
     own += [(8 * a + 2 * q + 1 - a, 8 * a + 2 * q + 1 - q // 2) for a, q in place]
     cross = [(8 * a + 2 * q + 1 - a, 8 * (1 - a) + 2 * q + q // 2) for a, q in place]
     cross += [(8 * a + 2 * q + a, 8 * a + 2 * q + 1 - q // 2) for a, q in place]
-    return lax.ppermute(block, axes, own), lambda block: lax.ppermute(block, axes, cross)
+    return lax.ppermute(block, axes, own), lax.ppermute(block, axes, cross)
 
 
 def spread_blocks(blocks, at):
@@ -165,28 +165,25 @@
         return lax.dynamic_slice_in_dim(array, which * half, half, axis)
 
     both = jnp.concatenate([tokens, jnp.broadcast_to(norm_gain[None], (GAIN_ROWS, cols))], axis=0)
+    z3, z2, z1 = (send(both, ("zt", "zh"), k) for k in (3, 2, 1))
     swapped = swap_halves(weight_half(zt, 1, w_inner), weight_half(1 - zt, 1, w_inner))
-    z1, z2 = (send(both, ("zt", "zh"), k) for k in (1, 2))
-    z3 = send(after(both, *swapped), ("zt", "zh"), 3)
-    own, swap_cross = swap_blocks(w_outer)
+    own, cross = swap_blocks(after(w_outer, *swapped))
     both = jnp.stack([both, z1, z2, z3])
 
-    inner = after(jnp.stack(swapped), both, own)
+    inner = after(jnp.stack(swapped), both, own, cross)
     inner = jnp.stack([inner] + [send(inner, ("zq",), k) for k in (1, 2, 3)], axis=1)
-    cross = swap_cross(after(w_outer, both, own))
-    y1 = send(after(both, own), ("y",), 1)
-
-    in1, in3 = from_neighbours(after(inner, y1, cross), "x")
-    outer = spread_blocks(after(jnp.stack([own, cross]), inner, y1), at)
+    y1, y3 = from_neighbours(after(both, own, cross), "y")
+
+    in1, in3 = from_neighbours(after(inner, y1, y3), "x")
+    outer = spread_blocks(after(jnp.stack([own, cross]), inner, y1, y3), at)
 
     in2a, in2b = from_far(after(in1, outer), after(in3, outer), "x", 1)
     out1, out3 = from_neighbours(after(outer, in1, in3), "x")
-    y3 = send(after(both, outer), ("y",), 3)
-    y2 = send(after(both, in2a, in2b), ("y",), 2)
+    y2 = send(after(both, outer), ("y",), 2)
 
     both = jnp.stack([both, y1, y2, y3])
-    other = send(after(both, out1, out3), ("c",), 1)
-    out2a, out2b = from_far(after(out1, y2, y3), after(out3, y2, y3), "x", 1)
+    other = send(after(both, out1, out3, in2a, in2b), ("c",), 1)
+    out2a, out2b = from_far(after(out1, y2), after(out3, y2), "x", 1)
 
     flops = 2 * 2 * rows * half * 16 * cols
     act = call(

time: 235 us -> 233 us (level)
  starting transfers between devices: 136 us -> 125 us
  local copies, waits for them, and re-layouts: 3.56 us -> 10.6 us
  waiting for transfers between devices: 75.3 us -> 77.9 us
    ppermute x1, starting transfers between devices: 9.65 us -> 1.92 us  [swap_halves(): lax.ppermute(second, ('zt', 'c'), [(2 * a + b, 2 * b + 1 - a) for a, b in...]
    ppermute x28, starting transfers between devices: 104 us -> 96.8 us  [send(): return lax.ppermute(value, axes, [(i, i ^ k) for i in range(count)])]
    ppermute x1, starting transfers between devices: 6.59 us -> 10.2 us  [swap_halves(): lax.ppermute(first, ('zt', 'c'), [(2 * a + b, 2 * b + a) for a, b in both])]
    slice x4, local copies, waits for them, and re-layouts: 0.14 us -> 3.68 us  [from_far(): return (send(three[:split], (axis,), 1), send(one[split:], (axis,), 3))]
    unnamed x28 -> x30, local copies, waits for them, and re-layouts: 1.05 us -> 4.46 us
    ppermute x3, starting transfers between devices: 6.18 us -> 9.28 us  [spread_blocks(): got.append(lax.ppermute(blocks, ('zq', 'c'), pairs))]
  transfers between devices with their start and end apart: 35 -> 35, of which waited for: 10 -> 14; matrix products, arithmetic and copies ran while one was open for 2% -> 4% of each run, Pallas kernels for 4% -> 4%
where the time goes in v8:
time: 233 us; the launch traced here: 232 us
  starting transfers between devices  125 us (54%)
  waiting for transfers between devices  77.9 us (33%)
  Pallas kernels  11.6 us (5%)
  local copies, waits for them, and re-layouts  10.6 us (5%)
  other arithmetic  5.83 us (3%)
    ppermute x28, starting transfers between devices, send(): return lax.ppermute(value, axes, [(i, i ^ k) for i in range(count)])  96.8 us
    ppermute x28, waiting for transfers between devices, send(): return lax.ppermute(value, axes, [(i, i ^ k) for i in range(count)])  70.3 us
    pallas_call x3, Pallas kernels, call(): pl.pallas_call(kernel, out_shape=out_shape, in_specs=[pl.BlockSpec(memory...  11.6 us
    ppermute x1, starting transfers between devices, swap_halves(): lax.ppermute(first, ('zt', 'c'), [(2 * a + b, 2 * b + a) for a, b in both])  10.2 us
    ppermute x3, starting transfers between devices, spread_blocks(): got.append(lax.ppermute(blocks, ('zq', 'c'), pairs))  9.28 us
    ppermute x3, waiting for transfers between devices, spread_blocks(): got.append(lax.ppermute(blocks, ('zq', 'c'), pairs))  7.56 us
    ppermute x2, starting transfers between devices, swap_blocks(): return (lax.ppermute(block, axes, own), lax.ppermute(block, axes, cross))  7.06 us
  transfers between devices with their start and end apart: 35, of which 14 were waited for; matrix products, arithmetic and copies ran while one was open for 4% of the time, Pallas kernels for 4%

profile of v8, /device:TPU:1, one launch (start us, length us, event | category | flops | bytes accessed | tf_op | source)
XLA Modules:
  0.0 231.9 jit_solution(18424350182804822060)
XLA Ops:
  1.0 10.2 %collective-permute-start.3 = (bf16[128,384]{1,0:T(8,128)(2,1)S(1)}, bf16[128,384]{1,0:T(8,128)(2,1)S(1)}, u32[]{:S(2)}, u32[]{:S(2)}) collective-permute-start(bf16[128,384]{1,0:T(8,128)(2,1)S(1)} %get-tuple-element.40), channel_id=1, source_target_pairs={{0,0},{1,64},{64,1},{65,65},{2,2},{3,66},{66,3},{67,67},{4,4},{5,6... | collective-permute-start | bytes 294920 | tf_op jit(solution)/shard_map/ppermute | solution.py:33
  14.7 8.6 %collective-permute-start.2 = (bf16[272,256]{1,0:T(8,128)(2,1)S(1)}, bf16[272,256]{1,0:T(8,128)(2,1)S(1)}, u32[]{:S(2)}, u32[]{:S(2)}) collective-permute-start(bf16[272,256]{1,0:T(8,128)(2,1)S(1)} %get-tuple-element.42), channel_id=1, source_target_pairs={{0,66},{2,64},{64,2},{66,0},{1,67},{3,65},{65,3},{67,1},{4,70},{6,... | collective-permute-start | bytes 417800 | tf_op jit(solution)/shard_map/ppermute | solution.py:24
  23.3 4.2 %collective-permute-start.1 = (bf16[272,256]{1,0:T(8,128)(2,1)S(1)}, bf16[272,256]{1,0:T(8,128)(2,1)S(1)}, u32[]{:S(2)}, u32[]{:S(2)}) collective-permute-start(bf16[272,256]{1,0:T(8,128)(2,1)S(1)} %get-tuple-element.42), channel_id=1, source_target_pairs={{0,64},{2,66},{64,0},{66,2},{1,65},{3,67},{65,1},{67,3},{4,68},{6,... | collective-permute-start | bytes 417800 | tf_op jit(solution)/shard_map/ppermute | solution.py:24
  27.5 4.7 %collective-permute-start = (bf16[272,256]{1,0:T(8,128)(2,1)S(1)}, bf16[272,256]{1,0:T(8,128)(2,1)S(1)}, u32[]{:S(2)}, u32[]{:S(2)}) collective-permute-start(bf16[272,256]{1,0:T(8,128)(2,1)S(1)} %get-tuple-element.42), channel_id=1, source_target_pairs={{0,2},{2,0},{64,66},{66,64},{1,3},{3,1},{65,67},{67,65},{4,6},{6,4... | collective-permute-start | bytes 417800 | tf_op jit(solution)/shard_map/ppermute | solution.py:24
  33.9 5.5 %collective-permute-start.6 = (bf16[768,128]{1,0:T(8,128)(2,1)}, bf16[768,128]{1,0:T(8,128)(2,1)S(1)}, u32[]{:S(2)}, u32[]{:S(2)}) collective-permute-start(bf16[768,128]{1,0:T(8,128)(2,1)} %param.7), channel_id=1, source_target_pairs={{1,64},{17,80},{33,97},{49,113},{64,0},{80,16},{96,33},{112,49},{0... | collective-permute-start | bytes 589832 | tf_op jit(solution)/shard_map/ppermute | solution.py:53
  39.4 22.0 %collective-permute-done.1 = bf16[272,256]{1,0:T(8,128)(2,1)S(1)} collective-permute-done((bf16[272,256]{1,0:T(8,128)(2,1)S(1)}, bf16[272,256]{1,0:T(8,128)(2,1)S(1)}, u32[]{:S(2)}, u32[]{:S(2)}) %collective-permute-start.1) | collective-permute-done | bytes 139296 | tf_op jit(solution)/shard_map/ppermute | solution.py:24
  62.3 4.6 %collective-permute-start.11 = (bf16[4,272,256]{2,1,0:T(8,128)(2,1)S(1)}, bf16[4,272,256]{2,1,0:T(8,128)(2,1)S(1)}, u32[]{:S(2)}, u32[]{:S(2)}) collective-permute-start(bf16[4,272,256]{2,1,0:T(8,128)(2,1)S(1)} %get-tuple-element.21), channel_id=1, source_target_pairs={{0,12},{4,8},{8,4},{12,0},{1,13},{5,9},{9,5},{13,1},{2,14},{6,10},... | collective-permute-start | bytes 1671176 | tf_op jit(solution)/shard_map/ppermute | solution.py:24
  72.7 5.4 %collective-permute-start.8 = (bf16[2,128,384]{2,1,0:T(8,128)(2,1)S(1)}, bf16[2,128,384]{2,1,0:T(8,128)(2,1)S(1)}, u32[]{:S(2)}, u32[]{:S(2)}) collective-permute-start(bf16[2,128,384]{2,1,0:T(8,128)(2,1)S(1)} %pad_maximum_fusion.5), channel_id=1, source_target_pairs={{0,16},{16,0},{32,48},{48,32},{1,17},{17,1},{33,49},{49,33},{2,18}... | collective-permute-start | bytes 589832 | tf_op jit(solution)/shard_map/ppermute | solution.py:24
  78.2 9.9 %collective-permute-done.9 = bf16[2,128,384]{2,1,0:T(8,128)(2,1)S(1)} collective-permute-done((bf16[2,128,384]{2,1,0:T(8,128)(2,1)S(1)}, bf16[2,128,384]{2,1,0:T(8,128)(2,1)S(1)}, u32[]{:S(2)}, u32[]{:S(2)}) %collective-permute-start.9) | collective-permute-done | bytes 196640 | tf_op jit(solution)/shard_map/ppermute | solution.py:24
  90.4 3.3 %collective-permute-start.12 = (bf16[2,768,128]{2,1,0:T(8,128)(2,1)S(1)}, bf16[2,768,128]{2,1,0:T(8,128)(2,1)S(1)}, u32[]{:S(2)}, u32[]{:S(2)}) collective-permute-start(bf16[2,768,128]{2,1,0:T(8,128)(2,1)S(1)} %pad_maximum_fusion.4), channel_id=1, source_target_pairs={{0,32},{16,48},{33,1},{49,17},{1,0},{17,16},{32,33},{48,49},{2,34}... | collective-permute-start | bytes 1179656 | tf_op jit(solution)/shard_map/ppermute | solution.py:61
  93.7 3.1 %collective-permute-start.16 = (bf16[2,4,128,384]{3,2,1,0:T(8,128)(2,1)S(1)}, bf16[2,4,128,384]{3,2,1,0:T(8,128)(2,1)S(1)}, u32[]{:S(2)}, u32[]{:S(2)}) collective-permute-start(bf16[2,4,128,384]{3,2,1,0:T(8,128)(2,1)S(1)} %pad_maximum_fusion.1.refs_2_), channel_id=1, source_target_pairs={{0,128},{128,0},{256,384},{384,256},{1,129},{129,1},{257,385},{385... | collective-permute-start | bytes 2359304 | tf_op jit(solution)/shard_map/ppermute | solution.py:24
  96.8 3.7 %collective-permute-start.17 = (bf16[2,4,128,384]{3,2,1,0:T(8,128)(2,1)S(1)}, bf16[2,4,128,384]{3,2,1,0:T(8,128)(2,1)S(1)}, u32[]{:S(2)}, u32[]{:S(2)}) collective-permute-start(bf16[2,4,128,384]{3,2,1,0:T(8,128)(2,1)S(1)} %pad_maximum_fusion.1.refs_2_), channel_id=1, source_target_pairs={{0,384},{128,256},{256,128},{384,0},{1,385},{129,257},{257,129},{3... | collective-permute-start | bytes 2359304 | tf_op jit(solution)/shard_map/ppermute | solution.py:24
  101.2 5.3 %collective-permute-start.14 = (bf16[2,768,128]{2,1,0:T(8,128)(2,1)S(1)}, bf16[2,768,128]{2,1,0:T(8,128)(2,1)}, u32[]{:S(2)}, u32[]{:S(2)}) collective-permute-start(bf16[2,768,128]{2,1,0:T(8,128)(2,1)S(1)} %pad_maximum_fusion.4), channel_id=1, source_target_pairs={{0,48},{16,32},{33,17},{49,1},{1,0},{17,16},{32,33},{48,49},{2,50}... | collective-permute-start | bytes 1179656 | tf_op jit(solution)/shard_map/ppermute | solution.py:61
  106.7 7.6 %collective-permute-done.14 = bf16[2,768,128]{2,1,0:T(8,128)(2,1)} collective-permute-done((bf16[2,768,128]{2,1,0:T(8,128)(2,1)S(1)}, bf16[2,768,128]{2,1,0:T(8,128)(2,1)}, u32[]{:S(2)}, u32[]{:S(2)}) %collective-permute-start.14) | collective-permute-done | bytes 393248 | tf_op jit(solution)/shard_map/ppermute | solution.py:61
  121.5 3.7 %collective-permute-start.19 = (bf16[2,2,768,128]{3,2,1,0:T(8,128)(2,1)S(1)}, bf16[2,2,768,128]{3,2,1,0:T(8,128)(2,1)S(1)}, u32[]{:S(2)}, u32[]{:S(2)}) collective-permute-start(bf16[2,2,768,128]{3,2,1,0:T(8,128)(2,1)S(1)} %pad_maximum_fusion.2.w0), channel_id=1, source_target_pairs={{0,384},{128,256},{256,128},{384,0},{1,385},{129,257},{257,129},{3... | collective-permute-start | bytes 2359304 | tf_op jit(solution)/shard_map/ppermute | solution.py:24
  125.3 3.1 %collective-permute-start.15 = (bf16[4,272,256]{2,1,0:T(8,128)(2,1)S(1)}, bf16[4,272,256]{2,1,0:T(8,128)(2,1)S(1)}, u32[]{:S(2)}, u32[]{:S(2)}) collective-permute-start(bf16[4,272,256]{2,1,0:T(8,128)(2,1)S(1)} %copy-done.12), channel_id=1, source_target_pairs={{0,8},{4,12},{8,0},{12,4},{1,9},{5,13},{9,1},{13,5},{2,10},{6,14},... | collective-permute-start | bytes 1671176 | tf_op jit(solution)/shard_map/ppermute | solution.py:24
  129.4 2.8 %collective-permute-start.20 = (bf16[1,4,128,384]{3,2,1,0:T(8,128)(2,1)S(1)}, bf16[1,4,128,384]{3,2,1,0:T(8,128)(2,1)S(1)}, u32[]{:S(2)}, u32[]{:S(2)}) collective-permute-start(bf16[1,4,128,384]{3,2,1,0:T(8,128)(2,1)S(1)} %slice.48), channel_id=1, source_target_pairs={{0,128},{128,0},{256,384},{384,256},{1,129},{129,1},{257,385},{385... | collective-permute-start | bytes 1179656 | tf_op jit(solution)/shard_map/ppermute | solution.py:24
  133.3 2.8 %collective-permute-start.21 = (bf16[1,4,128,384]{3,2,1,0:T(8,128)(2,1)S(1)}, bf16[1,4,128,384]{3,2,1,0:T(8,128)(2,1)S(1)}, u32[]{:S(2)}, u32[]{:S(2)}) collective-permute-start(bf16[1,4,128,384]{3,2,1,0:T(8,128)(2,1)S(1)} %slice.49), channel_id=1, source_target_pairs={{0,384},{128,256},{256,128},{384,0},{1,385},{129,257},{257,129},{3... | collective-permute-start | bytes 1179656 | tf_op jit(solution)/shard_map/ppermute | solution.py:24
  136.0 5.4 %collective-permute-done.15 = bf16[4,272,256]{2,1,0:T(8,128)(2,1)S(1)} collective-permute-done((bf16[4,272,256]{2,1,0:T(8,128)(2,1)S(1)}, bf16[4,272,256]{2,1,0:T(8,128)(2,1)S(1)}, u32[]{:S(2)}, u32[]{:S(2)}) %collective-permute-start.15) | collective-permute-done | bytes 557088 | tf_op jit(solution)/shard_map/ppermute | solution.py:24
  143.1 4.8 %collective-permute-done.20 = bf16[1,4,128,384]{3,2,1,0:T(8,128)(2,1)S(1)} collective-permute-done((bf16[1,4,128,384]{3,2,1,0:T(8,128)(2,1)S(1)}, bf16[1,4,128,384]{3,2,1,0:T(8,128)(2,1)S(1)}, u32[]{:S(2)}, u32[]{:S(2)}) %collective-permute-start.20) | collective-permute-done | bytes 393248 | tf_op jit(solution)/shard_map/ppermute | solution.py:24
  147.8 3.1 %collective-permute-done.21 = bf16[1,4,128,384]{3,2,1,0:T(8,128)(2,1)S(1)} collective-permute-done((bf16[1,4,128,384]{3,2,1,0:T(8,128)(2,1)S(1)}, bf16[1,4,128,384]{3,2,1,0:T(8,128)(2,1)S(1)}, u32[]{:S(2)}, u32[]{:S(2)}) %collective-permute-start.21) | collective-permute-done | bytes 393248 | tf_op jit(solution)/shard_map/ppermute | solution.py:24
  151.0 3.9 %collective-permute-start.22 = (bf16[4,4,272,256]{3,2,1,0:T(8,128)(2,1)}, bf16[4,4,272,256]{3,2,1,0:T(8,128)(2,1)}, u32[]{:S(2)}, u32[]{:S(2)}) collective-permute-start(bf16[4,4,272,256]{3,2,1,0:T(8,128)(2,1)} %pad_maximum_fusion.refs_0_), channel_id=1, source_target_pairs={{0,1},{1,0},{2,3},{3,2},{4,5},{5,4},{6,7},{7,6},{8,9},{9,8},{10,11... | collective-permute-start | bytes 6684680 | tf_op jit(solution)/shard_map/ppermute | solution.py:24
  159.4 3.7 %collective-permute-start.25 = (bf16[1,2,768,128]{3,2,1,0:T(8,128)(2,1)}, bf16[1,2,768,128]{3,2,1,0:T(8,128)(2,1)S(1)}, u32[]{:S(2)}, u32[]{:S(2)}) collective-permute-start(bf16[1,2,768,128]{3,2,1,0:T(8,128)(2,1)} %slice.51), channel_id=1, source_target_pairs={{0,384},{128,256},{256,128},{384,0},{1,385},{129,257},{257,129},{3... | collective-permute-start | bytes 1179656 | tf_op jit(solution)/shard_map/ppermute | solution.py:24
  163.1 8.0 %shard_map.46.act = bf16[2,256,384]{2,1,0:T(8,128)(2,1)} custom-call(s32[6]{0:T(128)} %stack.99.place, bf16[4,4,272,256]{3,2,1,0:T(8,128)(2,1)} %pad_maximum_fusion.refs_0_, bf16[4,4,272,256]{3,2,1,0:T(8,128)(2,1)} %collective-permute-done.22.refs_1_, bf16[2,4,128,384]{3,2,1,0:T(8,128)(2,1)} %copy-done.3, bf16[2,4,128,384]{3,2,1,0:T(8,128)(2,1)} %copy-done.5, ...), custom_call_target="tpu_custom_call" | custom-call | flops 1610612736 | bytes 7602200 | tf_op jit(solution)/shard_map/pallas_call | solution.py:145
  178.1 2.6 %collective-permute-start.28 = (bf16[2,256,256]{2,1,0:T(8,128)(2,1)S(1)}, bf16[2,256,256]{2,1,0:T(8,128)(2,1)S(1)}, u32[]{:S(2)}, u32[]{:S(2)}) collective-permute-start(bf16[2,256,256]{2,1,0:T(8,128)(2,1)S(1)} %get-tuple-element.33), channel_id=1, source_target_pairs={{0,12},{4,8},{8,4},{12,0},{1,13},{5,9},{9,5},{13,1},{2,14},{6,10},... | collective-permute-start | bytes 786440 | tf_op jit(solution)/shard_map/ppermute | solution.py:24
  180.7 4.5 %collective-permute-start.27 = (bf16[2,256,256]{2,1,0:T(8,128)(2,1)S(1)}, bf16[2,256,256]{2,1,0:T(8,128)(2,1)S(1)}, u32[]{:S(2)}, u32[]{:S(2)}) collective-permute-start(bf16[2,256,256]{2,1,0:T(8,128)(2,1)S(1)} %get-tuple-element.34), channel_id=1, source_target_pairs={{0,8},{4,12},{8,0},{12,4},{1,9},{5,13},{9,1},{13,5},{2,10},{6,14},... | collective-permute-start | bytes 786440 | tf_op jit(solution)/shard_map/ppermute | solution.py:24
  191.6 4.5 %collective-permute-start.30 = (bf16[2,256,256]{2,1,0:T(8,128)(2,1)S(1)}, bf16[2,256,256]{2,1,0:T(8,128)(2,1)S(1)}, u32[]{:S(2)}, u32[]{:S(2)}) collective-permute-start(bf16[2,256,256]{2,1,0:T(8,128)(2,1)S(1)} %get-tuple-element.31), channel_id=1, source_target_pairs={{0,8},{4,12},{8,0},{12,4},{1,9},{5,13},{9,1},{13,5},{2,10},{6,14},... | collective-permute-start | bytes 786440 | tf_op jit(solution)/shard_map/ppermute | solution.py:24
  198.3 4.7 %collective-permute-start.34 = (bf16[256,256]{1,0:T(8,128)(2,1)S(1)}, bf16[256,256]{1,0:T(8,128)(2,1)S(1)}, u32[]{:S(2)}, u32[]{:S(2)}) collective-permute-start(bf16[256,256]{1,0:T(8,128)(2,1)S(1)} %fusion.3), channel_id=1, source_target_pairs={{0,2},{2,0},{64,66},{66,64},{1,3},{3,1},{65,67},{67,65},{4,6},{6,4... | collective-permute-start | bytes 393224 | tf_op jit(solution)/shard_map/ppermute | solution.py:24
  204.6 2.7 %collective-permute-done.29 = bf16[2,256,256]{2,1,0:T(8,128)(2,1)S(1)} collective-permute-done((bf16[2,256,256]{2,1,0:T(8,128)(2,1)S(1)}, bf16[2,256,256]{2,1,0:T(8,128)(2,1)S(1)}, u32[]{:S(2)}, u32[]{:S(2)}) %collective-permute-start.29) | collective-permute-done | bytes 262176 | tf_op jit(solution)/shard_map/ppermute | solution.py:24
  207.6 5.3 %collective-permute-start.33 = (bf16[256,256]{1,0:T(8,128)(2,1)S(1)}, bf16[256,256]{1,0:T(8,128)(2,1)S(1)}, u32[]{:S(2)}, u32[]{:S(2)}) collective-permute-start(bf16[256,256]{1,0:T(8,128)(2,1)S(1)} %get-tuple-element.38), channel_id=1, source_target_pairs={{0,66},{2,64},{64,2},{66,0},{1,67},{3,65},{65,3},{67,1},{4,70},{6,... | collective-permute-start | bytes 393224 | tf_op jit(solution)/shard_map/ppermute | solution.py:24
  215.0 10.9 %collective-permute-done.33 = bf16[256,256]{1,0:T(8,128)(2,1)S(1)} collective-permute-done((bf16[256,256]{1,0:T(8,128)(2,1)S(1)}, bf16[256,256]{1,0:T(8,128)(2,1)S(1)}, u32[]{:S(2)}, u32[]{:S(2)}) %collective-permute-start.33) | collective-permute-done | bytes 131104 | tf_op jit(solution)/shard_map/ppermute | solution.py:24
  225.9 5.3 %collective-permute-done.32 = bf16[256,256]{1,0:T(8,128)(2,1)S(1)} collective-permute-done((bf16[256,256]{1,0:T(8,128)(2,1)S(1)}, bf16[256,256]{1,0:T(8,128)(2,1)S(1)}, u32[]{:S(2)}, u32[]{:S(2)}) %collective-permute-start.32) | collective-permute-done | bytes 131104 | tf_op jit(solution)/shard_map/ppermute | solution.py:24
  (94 shorter events, 51.1 us)
Async XLA Ops:
  1.0 31.3 %collective-permute-start.3 = (bf16[128,384]{1,0:T(8,128)(2,1)S(1)}, bf16[128,384]{1,0:T(8,128)(2,1)S(1)}, u32[]{:S(2)}, u32[]{:S(2)}) collective-permute-start(bf16[128,384]{1,0:T(8,128)(2,1)S(1)} %get-tuple-element.40), channel_id=1, source_target_pairs={{0,0},{1,64},{64,1},{65,65},{2,2},{3,66},{66,3},{67,67},{4,4},{5,6... | collective-permute-start | bytes 294920 | tf_op jit(solution)/shard_map/ppermute | solution.py:33
  11.2 21.1 %collective-permute-start.4 = (bf16[128,384]{1,0:T(8,128)(2,1)S(1)}, bf16[128,384]{1,0:T(8,128)(2,1)S(1)}, u32[]{:S(2)}, u32[]{:S(2)}) collective-permute-start(bf16[128,384]{1,0:T(8,128)(2,1)S(1)} %get-tuple-element.39), channel_id=1, source_target_pairs={{0,1},{1,65},{64,0},{65,64},{2,3},{3,67},{66,2},{67,66},{4,5},{5,6... | collective-permute-start | bytes 294920 | tf_op jit(solution)/shard_map/ppermute | solution.py:34
  14.7 24.7 %collective-permute-start.2 = (bf16[272,256]{1,0:T(8,128)(2,1)S(1)}, bf16[272,256]{1,0:T(8,128)(2,1)S(1)}, u32[]{:S(2)}, u32[]{:S(2)}) collective-permute-start(bf16[272,256]{1,0:T(8,128)(2,1)S(1)} %get-tuple-element.42), channel_id=1, source_target_pairs={{0,66},{2,64},{64,2},{66,0},{1,67},{3,65},{65,3},{67,1},{4,70},{6,... | collective-permute-start | bytes 417800 | tf_op jit(solution)/shard_map/ppermute | solution.py:24
  23.3 38.0 %collective-permute-start.1 = (bf16[272,256]{1,0:T(8,128)(2,1)S(1)}, bf16[272,256]{1,0:T(8,128)(2,1)S(1)}, u32[]{:S(2)}, u32[]{:S(2)}) collective-permute-start(bf16[272,256]{1,0:T(8,128)(2,1)S(1)} %get-tuple-element.42), channel_id=1, source_target_pairs={{0,64},{2,66},{64,0},{66,2},{1,65},{3,67},{65,1},{67,3},{4,68},{6,... | collective-permute-start | bytes 417800 | tf_op jit(solution)/shard_map/ppermute | solution.py:24
  27.5 33.8 %collective-permute-start = (bf16[272,256]{1,0:T(8,128)(2,1)S(1)}, bf16[272,256]{1,0:T(8,128)(2,1)S(1)}, u32[]{:S(2)}, u32[]{:S(2)}) collective-permute-start(bf16[272,256]{1,0:T(8,128)(2,1)S(1)} %get-tuple-element.42), channel_id=1, source_target_pairs={{0,2},{2,0},{64,66},{66,64},{1,3},{3,1},{65,67},{67,65},{4,6},{6,4... | collective-permute-start | bytes 417800 | tf_op jit(solution)/shard_map/ppermute | solution.py:24
  32.3 30.0 %collective-permute-start.5 = (bf16[768,128]{1,0:T(8,128)(2,1)}, bf16[768,128]{1,0:T(8,128)(2,1)S(1)}, u32[]{:S(2)}, u32[]{:S(2)}) collective-permute-start(bf16[768,128]{1,0:T(8,128)(2,1)} %param.7), channel_id=1, source_target_pairs={{0,0},{16,16},{32,33},{48,49},{65,64},{81,80},{97,97},{113,113},{1... | collective-permute-start | bytes 589832 | tf_op jit(solution)/shard_map/ppermute | solution.py:53
  33.9 28.4 %collective-permute-start.6 = (bf16[768,128]{1,0:T(8,128)(2,1)}, bf16[768,128]{1,0:T(8,128)(2,1)S(1)}, u32[]{:S(2)}, u32[]{:S(2)}) collective-permute-start(bf16[768,128]{1,0:T(8,128)(2,1)} %param.7), channel_id=1, source_target_pairs={{1,64},{17,80},{33,97},{49,113},{64,0},{80,16},{96,33},{112,49},{0... | collective-permute-start | bytes 589832 | tf_op jit(solution)/shard_map/ppermute | solution.py:53
  62.3 26.4 %collective-permute-start.11 = (bf16[4,272,256]{2,1,0:T(8,128)(2,1)S(1)}, bf16[4,272,256]{2,1,0:T(8,128)(2,1)S(1)}, u32[]{:S(2)}, u32[]{:S(2)}) collective-permute-start(bf16[4,272,256]{2,1,0:T(8,128)(2,1)S(1)} %get-tuple-element.21), channel_id=1, source_target_pairs={{0,12},{4,8},{8,4},{12,0},{1,13},{5,9},{9,5},{13,1},{2,14},{6,10},... | collective-permute-start | bytes 1671176 | tf_op jit(solution)/shard_map/ppermute | solution.py:24
  66.9 21.8 %collective-permute-start.7 = (bf16[4,272,256]{2,1,0:T(8,128)(2,1)S(1)}, bf16[4,272,256]{2,1,0:T(8,128)(2,1)S(1)}, u32[]{:S(2)}, u32[]{:S(2)}) collective-permute-start(bf16[4,272,256]{2,1,0:T(8,128)(2,1)S(1)} %get-tuple-element.21), channel_id=1, source_target_pairs={{0,4},{4,0},{8,12},{12,8},{1,5},{5,1},{9,13},{13,9},{2,6},{6,2},{1... | collective-permute-start | bytes 1671176 | tf_op jit(solution)/shard_map/ppermute | solution.py:24
  70.8 17.3 %collective-permute-start.9 = (bf16[2,128,384]{2,1,0:T(8,128)(2,1)S(1)}, bf16[2,128,384]{2,1,0:T(8,128)(2,1)S(1)}, u32[]{:S(2)}, u32[]{:S(2)}) collective-permute-start(bf16[2,128,384]{2,1,0:T(8,128)(2,1)S(1)} %pad_maximum_fusion.5), channel_id=1, source_target_pairs={{0,32},{16,48},{32,0},{48,16},{1,33},{17,49},{33,1},{49,17},{2,34}... | collective-permute-start | bytes 589832 | tf_op jit(solution)/shard_map/ppermute | solution.py:24
  72.7 15.8 %collective-permute-start.8 = (bf16[2,128,384]{2,1,0:T(8,128)(2,1)S(1)}, bf16[2,128,384]{2,1,0:T(8,128)(2,1)S(1)}, u32[]{:S(2)}, u32[]{:S(2)}) collective-permute-start(bf16[2,128,384]{2,1,0:T(8,128)(2,1)S(1)} %pad_maximum_fusion.5), channel_id=1, source_target_pairs={{0,16},{16,0},{32,48},{48,32},{1,17},{17,1},{33,49},{49,33},{2,18}... | collective-permute-start | bytes 589832 | tf_op jit(solution)/shard_map/ppermute | solution.py:24
  90.4 16.2 %collective-permute-start.12 = (bf16[2,768,128]{2,1,0:T(8,128)(2,1)S(1)}, bf16[2,768,128]{2,1,0:T(8,128)(2,1)S(1)}, u32[]{:S(2)}, u32[]{:S(2)}) collective-permute-start(bf16[2,768,128]{2,1,0:T(8,128)(2,1)S(1)} %pad_maximum_fusion.4), channel_id=1, source_target_pairs={{0,32},{16,48},{33,1},{49,17},{1,0},{17,16},{32,33},{48,49},{2,34}... | collective-permute-start | bytes 1179656 | tf_op jit(solution)/shard_map/ppermute | solution.py:61
  93.7 21.7 %collective-permute-start.16 = (bf16[2,4,128,384]{3,2,1,0:T(8,128)(2,1)S(1)}, bf16[2,4,128,384]{3,2,1,0:T(8,128)(2,1)S(1)}, u32[]{:S(2)}, u32[]{:S(2)}) collective-permute-start(bf16[2,4,128,384]{3,2,1,0:T(8,128)(2,1)S(1)} %pad_maximum_fusion.1.refs_2_), channel_id=1, source_target_pairs={{0,128},{128,0},{256,384},{384,256},{1,129},{129,1},{257,385},{385... | collective-permute-start | bytes 2359304 | tf_op jit(solution)/shard_map/ppermute | solution.py:24
  96.8 21.9 %collective-permute-start.17 = (bf16[2,4,128,384]{3,2,1,0:T(8,128)(2,1)S(1)}, bf16[2,4,128,384]{3,2,1,0:T(8,128)(2,1)S(1)}, u32[]{:S(2)}, u32[]{:S(2)}) collective-permute-start(bf16[2,4,128,384]{3,2,1,0:T(8,128)(2,1)S(1)} %pad_maximum_fusion.1.refs_2_), channel_id=1, source_target_pairs={{0,384},{128,256},{256,128},{384,0},{1,385},{129,257},{257,129},{3... | collective-permute-start | bytes 2359304 | tf_op jit(solution)/shard_map/ppermute | solution.py:24
  101.2 13.0 %collective-permute-start.14 = (bf16[2,768,128]{2,1,0:T(8,128)(2,1)S(1)}, bf16[2,768,128]{2,1,0:T(8,128)(2,1)}, u32[]{:S(2)}, u32[]{:S(2)}) collective-permute-start(bf16[2,768,128]{2,1,0:T(8,128)(2,1)S(1)} %pad_maximum_fusion.4), channel_id=1, source_target_pairs={{0,48},{16,32},{33,17},{49,1},{1,0},{17,16},{32,33},{48,49},{2,50}... | collective-permute-start | bytes 1179656 | tf_op jit(solution)/shard_map/ppermute | solution.py:61
  119.6 31.4 %collective-permute-start.18 = (bf16[2,2,768,128]{3,2,1,0:T(8,128)(2,1)S(1)}, bf16[2,2,768,128]{3,2,1,0:T(8,128)(2,1)S(1)}, u32[]{:S(2)}, u32[]{:S(2)}) collective-permute-start(bf16[2,2,768,128]{3,2,1,0:T(8,128)(2,1)S(1)} %pad_maximum_fusion.2.w0), channel_id=1, source_target_pairs={{0,128},{128,0},{256,384},{384,256},{1,129},{129,1},{257,385},{385... | collective-permute-start | bytes 2359304 | tf_op jit(solution)/shard_map/ppermute | solution.py:24
  121.5 29.5 %collective-permute-start.19 = (bf16[2,2,768,128]{3,2,1,0:T(8,128)(2,1)S(1)}, bf16[2,2,768,128]{3,2,1,0:T(8,128)(2,1)S(1)}, u32[]{:S(2)}, u32[]{:S(2)}) collective-permute-start(bf16[2,2,768,128]{3,2,1,0:T(8,128)(2,1)S(1)} %pad_maximum_fusion.2.w0), channel_id=1, source_target_pairs={{0,384},{128,256},{256,128},{384,0},{1,385},{129,257},{257,129},{3... | collective-permute-start | bytes 2359304 | tf_op jit(solution)/shard_map/ppermute | solution.py:24
  125.3 16.1 %collective-permute-start.15 = (bf16[4,272,256]{2,1,0:T(8,128)(2,1)S(1)}, bf16[4,272,256]{2,1,0:T(8,128)(2,1)S(1)}, u32[]{:S(2)}, u32[]{:S(2)}) collective-permute-start(bf16[4,272,256]{2,1,0:T(8,128)(2,1)S(1)} %copy-done.12), channel_id=1, source_target_pairs={{0,8},{4,12},{8,0},{12,4},{1,9},{5,13},{9,1},{13,5},{2,10},{6,14},... | collective-permute-start | bytes 1671176 | tf_op jit(solution)/shard_map/ppermute | solution.py:24
  129.4 18.4 %collective-permute-start.20 = (bf16[1,4,128,384]{3,2,1,0:T(8,128)(2,1)S(1)}, bf16[1,4,128,384]{3,2,1,0:T(8,128)(2,1)S(1)}, u32[]{:S(2)}, u32[]{:S(2)}) collective-permute-start(bf16[1,4,128,384]{3,2,1,0:T(8,128)(2,1)S(1)} %slice.48), channel_id=1, source_target_pairs={{0,128},{128,0},{256,384},{384,256},{1,129},{129,1},{257,385},{385... | collective-permute-start | bytes 1179656 | tf_op jit(solution)/shard_map/ppermute | solution.py:24
  133.3 17.7 %collective-permute-start.21 = (bf16[1,4,128,384]{3,2,1,0:T(8,128)(2,1)S(1)}, bf16[1,4,128,384]{3,2,1,0:T(8,128)(2,1)S(1)}, u32[]{:S(2)}, u32[]{:S(2)}) collective-permute-start(bf16[1,4,128,384]{3,2,1,0:T(8,128)(2,1)S(1)} %slice.49), channel_id=1, source_target_pairs={{0,384},{128,256},{256,128},{384,0},{1,385},{129,257},{257,129},{3... | collective-permute-start | bytes 1179656 | tf_op jit(solution)/shard_map/ppermute | solution.py:24
  151.0 12.1 %collective-permute-start.22 = (bf16[4,4,272,256]{3,2,1,0:T(8,128)(2,1)}, bf16[4,4,272,256]{3,2,1,0:T(8,128)(2,1)}, u32[]{:S(2)}, u32[]{:S(2)}) collective-permute-start(bf16[4,4,272,256]{3,2,1,0:T(8,128)(2,1)} %pad_maximum_fusion.refs_0_), channel_id=1, source_target_pairs={{0,1},{1,0},{2,3},{3,2},{4,5},{5,4},{6,7},{7,6},{8,9},{9,8},{10,11... | collective-permute-start | bytes 6684680 | tf_op jit(solution)/shard_map/ppermute | solution.py:24
  156.4 17.3 %collective-permute-start.24 = (bf16[1,2,768,128]{3,2,1,0:T(8,128)(2,1)}, bf16[1,2,768,128]{3,2,1,0:T(8,128)(2,1)S(1)}, u32[]{:S(2)}, u32[]{:S(2)}) collective-permute-start(bf16[1,2,768,128]{3,2,1,0:T(8,128)(2,1)} %slice.50), channel_id=1, source_target_pairs={{0,128},{128,0},{256,384},{384,256},{1,129},{129,1},{257,385},{385... | collective-permute-start | bytes 1179656 | tf_op jit(solution)/shard_map/ppermute | solution.py:24
  159.4 14.3 %collective-permute-start.25 = (bf16[1,2,768,128]{3,2,1,0:T(8,128)(2,1)}, bf16[1,2,768,128]{3,2,1,0:T(8,128)(2,1)S(1)}, u32[]{:S(2)}, u32[]{:S(2)}) collective-permute-start(bf16[1,2,768,128]{3,2,1,0:T(8,128)(2,1)} %slice.51), channel_id=1, source_target_pairs={{0,384},{128,256},{256,128},{384,0},{1,385},{129,257},{257,129},{3... | collective-permute-start | bytes 1179656 | tf_op jit(solution)/shard_map/ppermute | solution.py:24
  178.1 18.0 %collective-permute-start.28 = (bf16[2,256,256]{2,1,0:T(8,128)(2,1)S(1)}, bf16[2,256,256]{2,1,0:T(8,128)(2,1)S(1)}, u32[]{:S(2)}, u32[]{:S(2)}) collective-permute-start(bf16[2,256,256]{2,1,0:T(8,128)(2,1)S(1)} %get-tuple-element.33), channel_id=1, source_target_pairs={{0,12},{4,8},{8,4},{12,0},{1,13},{5,9},{9,5},{13,1},{2,14},{6,10},... | collective-permute-start | bytes 786440 | tf_op jit(solution)/shard_map/ppermute | solution.py:24
  180.7 17.4 %collective-permute-start.27 = (bf16[2,256,256]{2,1,0:T(8,128)(2,1)S(1)}, bf16[2,256,256]{2,1,0:T(8,128)(2,1)S(1)}, u32[]{:S(2)}, u32[]{:S(2)}) collective-permute-start(bf16[2,256,256]{2,1,0:T(8,128)(2,1)S(1)} %get-tuple-element.34), channel_id=1, source_target_pairs={{0,8},{4,12},{8,0},{12,4},{1,9},{5,13},{9,1},{13,5},{2,10},{6,14},... | collective-permute-start | bytes 786440 | tf_op jit(solution)/shard_map/ppermute | solution.py:24
  185.3 12.8 %collective-permute-start.26 = (bf16[2,256,256]{2,1,0:T(8,128)(2,1)S(1)}, bf16[2,256,256]{2,1,0:T(8,128)(2,1)S(1)}, u32[]{:S(2)}, u32[]{:S(2)}) collective-permute-start(bf16[2,256,256]{2,1,0:T(8,128)(2,1)S(1)} %get-tuple-element.32), channel_id=1, source_target_pairs={{0,4},{4,0},{8,12},{12,8},{1,5},{5,1},{9,13},{13,9},{2,6},{6,2},{1... | collective-permute-start | bytes 786440 | tf_op jit(solution)/shard_map/ppermute | solution.py:24
  189.1 15.6 %collective-permute-start.31 = (bf16[2,256,256]{2,1,0:T(8,128)(2,1)S(1)}, bf16[2,256,256]{2,1,0:T(8,128)(2,1)S(1)}, u32[]{:S(2)}, u32[]{:S(2)}) collective-permute-start(bf16[2,256,256]{2,1,0:T(8,128)(2,1)S(1)} %get-tuple-element.30), channel_id=1, source_target_pairs={{0,12},{4,8},{8,4},{12,0},{1,13},{5,9},{9,5},{13,1},{2,14},{6,10},... | collective-permute-start | bytes 786440 | tf_op jit(solution)/shard_map/ppermute | solution.py:24
  191.6 13.0 %collective-permute-start.30 = (bf16[2,256,256]{2,1,0:T(8,128)(2,1)S(1)}, bf16[2,256,256]{2,1,0:T(8,128)(2,1)S(1)}, u32[]{:S(2)}, u32[]{:S(2)}) collective-permute-start(bf16[2,256,256]{2,1,0:T(8,128)(2,1)S(1)} %get-tuple-element.31), channel_id=1, source_target_pairs={{0,8},{4,12},{8,0},{12,4},{1,9},{5,13},{9,1},{13,5},{2,10},{6,14},... | collective-permute-start | bytes 786440 | tf_op jit(solution)/shard_map/ppermute | solution.py:24
  196.1 11.2 %collective-permute-start.29 = (bf16[2,256,256]{2,1,0:T(8,128)(2,1)S(1)}, bf16[2,256,256]{2,1,0:T(8,128)(2,1)S(1)}, u32[]{:S(2)}, u32[]{:S(2)}) collective-permute-start(bf16[2,256,256]{2,1,0:T(8,128)(2,1)S(1)} %get-tuple-element.29), channel_id=1, source_target_pairs={{0,4},{4,0},{8,12},{12,8},{1,5},{5,1},{9,13},{13,9},{2,6},{6,2},{1... | collective-permute-start | bytes 786440 | tf_op jit(solution)/shard_map/ppermute | solution.py:24
  198.3 16.8 %collective-permute-start.34 = (bf16[256,256]{1,0:T(8,128)(2,1)S(1)}, bf16[256,256]{1,0:T(8,128)(2,1)S(1)}, u32[]{:S(2)}, u32[]{:S(2)}) collective-permute-start(bf16[256,256]{1,0:T(8,128)(2,1)S(1)} %fusion.3), channel_id=1, source_target_pairs={{0,2},{2,0},{64,66},{66,64},{1,3},{3,1},{65,67},{67,65},{4,6},{6,4... | collective-permute-start | bytes 393224 | tf_op jit(solution)/shard_map/ppermute | solution.py:24
  207.6 18.3 %collective-permute-start.33 = (bf16[256,256]{1,0:T(8,128)(2,1)S(1)}, bf16[256,256]{1,0:T(8,128)(2,1)S(1)}, u32[]{:S(2)}, u32[]{:S(2)}) collective-permute-start(bf16[256,256]{1,0:T(8,128)(2,1)S(1)} %get-tuple-element.38), channel_id=1, source_target_pairs={{0,66},{2,64},{64,2},{66,0},{1,67},{3,65},{65,3},{67,1},{4,70},{6,... | collective-permute-start | bytes 393224 | tf_op jit(solution)/shard_map/ppermute | solution.py:24
  212.9 18.3 %collective-permute-start.32 = (bf16[256,256]{1,0:T(8,128)(2,1)S(1)}, bf16[256,256]{1,0:T(8,128)(2,1)S(1)}, u32[]{:S(2)}, u32[]{:S(2)}) collective-permute-start(bf16[256,256]{1,0:T(8,128)(2,1)S(1)} %get-tuple-element.37), channel_id=1, source_target_pairs={{0,64},{2,66},{64,0},{66,2},{1,65},{3,67},{65,1},{67,3},{4,68},{6,... | collective-permute-start | bytes 393224 | tf_op jit(solution)/shard_map/ppermute | solution.py:24
  (18 other events, 269.6 us)

commit v9 on v8

--- a/solution.py
+++ b/solution.py
@@ -179,10 +179,10 @@
 
     in2a, in2b = from_far(after(in1, outer), after(in3, outer), "x", 1)
     out1, out3 = from_neighbours(after(outer, in1, in3), "x")
-    y2 = send(after(both, outer), ("y",), 2)
+    y2 = send(after(both, in2a, in2b), ("y",), 2)
 
     both = jnp.stack([both, y1, y2, y3])
-    other = send(after(both, out1, out3, in2a, in2b), ("c",), 1)
+    other = send(after(both, out1, out3), ("c",), 1)
     out2a, out2b = from_far(after(out1, y2), after(out3, y2), "x", 1)
 
     flops = 2 * 2 * rows * half * 16 * cols

time: 233 us -> 227 us (0.974)
  the two profiles are of different devices: /device:TPU:1 before, /device:TPU:50 now
where the time goes in v9:
time: 227 us; the launch traced here: 226 us
  starting transfers between devices  129 us (57%)
  waiting for transfers between devices  76.1 us (34%)
  Pallas kernels  11.7 us (5%)
  other arithmetic  4.84 us (2%)
  local copies, waits for them, and re-layouts  3.58 us (2%)
    ppermute x28, starting transfers between devices, send(): return lax.ppermute(value, axes, [(i, i ^ k) for i in range(count)])  106 us
    ppermute x28, waiting for transfers between devices, send(): return lax.ppermute(value, axes, [(i, i ^ k) for i in range(count)])  62.6 us
    pallas_call x3, Pallas kernels, call(): pl.pallas_call(kernel, out_shape=out_shape, in_specs=[pl.BlockSpec(memory...  11.7 us
    ppermute x1, starting transfers between devices, swap_halves(): lax.ppermute(second, ('zt', 'c'), [(2 * a + b, 2 * b + 1 - a) for a, b in...  10.5 us
    ppermute x3, waiting for transfers between devices, spread_blocks(): got.append(lax.ppermute(blocks, ('zq', 'c'), pairs))  9.37 us
    ppermute x3, starting transfers between devices, spread_blocks(): got.append(lax.ppermute(blocks, ('zq', 'c'), pairs))  8.23 us
  transfers between devices with their start and end apart: 35, of which 16 were waited for; matrix products, arithmetic and copies ran while one was open for 2% of the time, Pallas kernels for 4%

profile of v9, /device:TPU:50, one launch (start us, length us, event | category | flops | bytes accessed | tf_op | source)
XLA Modules:
  0.0 225.9 jit_solution(14191185803657190494)
XLA Ops:
  1.6 10.5 %collective-permute-start.4 = (bf16[128,384]{1,0:T(8,128)(2,1)S(1)}, bf16[128,384]{1,0:T(8,128)(2,1)S(1)}, u32[]{:S(2)}, u32[]{:S(2)}) collective-permute-start(bf16[128,384]{1,0:T(8,128)(2,1)S(1)} %get-tuple-element.39), channel_id=1, source_target_pairs={{0,1},{1,65},{64,0},{65,64},{2,3},{3,67},{66,2},{67,66},{4,5},{5,6... | collective-permute-start | bytes 294920 | tf_op jit(solution)/shard_map/ppermute | solution.py:34
  13.7 7.5 %collective-permute-start.2 = (bf16[272,256]{1,0:T(8,128)(2,1)S(1)}, bf16[272,256]{1,0:T(8,128)(2,1)S(1)}, u32[]{:S(2)}, u32[]{:S(2)}) collective-permute-start(bf16[272,256]{1,0:T(8,128)(2,1)S(1)} %get-tuple-element.42), channel_id=1, source_target_pairs={{0,66},{2,64},{64,2},{66,0},{1,67},{3,65},{65,3},{67,1},{4,70},{6,... | collective-permute-start | bytes 417800 | tf_op jit(solution)/shard_map/ppermute | solution.py:24
  21.2 5.0 %collective-permute-start.1 = (bf16[272,256]{1,0:T(8,128)(2,1)S(1)}, bf16[272,256]{1,0:T(8,128)(2,1)S(1)}, u32[]{:S(2)}, u32[]{:S(2)}) collective-permute-start(bf16[272,256]{1,0:T(8,128)(2,1)S(1)} %get-tuple-element.42), channel_id=1, source_target_pairs={{0,64},{2,66},{64,0},{66,2},{1,65},{3,67},{65,1},{67,3},{4,68},{6,... | collective-permute-start | bytes 417800 | tf_op jit(solution)/shard_map/ppermute | solution.py:24
  26.2 4.5 %collective-permute-start = (bf16[272,256]{1,0:T(8,128)(2,1)S(1)}, bf16[272,256]{1,0:T(8,128)(2,1)S(1)}, u32[]{:S(2)}, u32[]{:S(2)}) collective-permute-start(bf16[272,256]{1,0:T(8,128)(2,1)S(1)} %get-tuple-element.42), channel_id=1, source_target_pairs={{0,2},{2,0},{64,66},{66,64},{1,3},{3,1},{65,67},{67,65},{4,6},{6,4... | collective-permute-start | bytes 417800 | tf_op jit(solution)/shard_map/ppermute | solution.py:24
  34.3 19.3 %collective-permute-done.1 = bf16[272,256]{1,0:T(8,128)(2,1)S(1)} collective-permute-done((bf16[272,256]{1,0:T(8,128)(2,1)S(1)}, bf16[272,256]{1,0:T(8,128)(2,1)S(1)}, u32[]{:S(2)}, u32[]{:S(2)}) %collective-permute-start.1) | collective-permute-done | bytes 139296 | tf_op jit(solution)/shard_map/ppermute | solution.py:24
  54.5 4.1 %collective-permute-done.6 = bf16[768,128]{1,0:T(8,128)(2,1)S(1)} collective-permute-done((bf16[768,128]{1,0:T(8,128)(2,1)}, bf16[768,128]{1,0:T(8,128)(2,1)S(1)}, u32[]{:S(2)}, u32[]{:S(2)}) %collective-permute-start.6) | collective-permute-done | bytes 196640 | tf_op jit(solution)/shard_map/ppermute | solution.py:53
  60.9 3.0 %collective-permute-start.7 = (bf16[4,272,256]{2,1,0:T(8,128)(2,1)S(1)}, bf16[4,272,256]{2,1,0:T(8,128)(2,1)S(1)}, u32[]{:S(2)}, u32[]{:S(2)}) collective-permute-start(bf16[4,272,256]{2,1,0:T(8,128)(2,1)S(1)} %get-tuple-element.24), channel_id=1, source_target_pairs={{0,4},{4,0},{8,12},{12,8},{1,5},{5,1},{9,13},{13,9},{2,6},{6,2},{1... | collective-permute-start | bytes 1671176 | tf_op jit(solution)/shard_map/ppermute | solution.py:24
  63.9 3.4 %collective-permute-start.10 = (bf16[2,128,384]{2,1,0:T(8,128)(2,1)S(1)}, bf16[2,128,384]{2,1,0:T(8,128)(2,1)S(1)}, u32[]{:S(2)}, u32[]{:S(2)}) collective-permute-start(bf16[2,128,384]{2,1,0:T(8,128)(2,1)S(1)} %pad_maximum_fusion.5), channel_id=1, source_target_pairs={{0,48},{16,32},{32,16},{48,0},{1,49},{17,33},{33,17},{49,1},{2,50}... | collective-permute-start | bytes 589832 | tf_op jit(solution)/shard_map/ppermute | solution.py:24
  67.3 7.4 %collective-permute-start.9 = (bf16[2,128,384]{2,1,0:T(8,128)(2,1)S(1)}, bf16[2,128,384]{2,1,0:T(8,128)(2,1)S(1)}, u32[]{:S(2)}, u32[]{:S(2)}) collective-permute-start(bf16[2,128,384]{2,1,0:T(8,128)(2,1)S(1)} %pad_maximum_fusion.5), channel_id=1, source_target_pairs={{0,32},{16,48},{32,0},{48,16},{1,33},{17,49},{33,1},{49,17},{2,34}... | collective-permute-start | bytes 589832 | tf_op jit(solution)/shard_map/ppermute | solution.py:24
  76.7 4.1 %collective-permute-done.10 = bf16[2,128,384]{2,1,0:T(8,128)(2,1)S(1)} collective-permute-done((bf16[2,128,384]{2,1,0:T(8,128)(2,1)S(1)}, bf16[2,128,384]{2,1,0:T(8,128)(2,1)S(1)}, u32[]{:S(2)}, u32[]{:S(2)}) %collective-permute-start.10) | collective-permute-done | bytes 196640 | tf_op jit(solution)/shard_map/ppermute | solution.py:24
  84.5 4.0 %collective-permute-start.13 = (bf16[2,768,128]{2,1,0:T(8,128)(2,1)S(1)}, bf16[2,768,128]{2,1,0:T(8,128)(2,1)S(1)}, u32[]{:S(2)}, u32[]{:S(2)}) collective-permute-start(bf16[2,768,128]{2,1,0:T(8,128)(2,1)S(1)} %pad_maximum_fusion.4), channel_id=1, source_target_pairs={{0,32},{16,48},{33,1},{49,17},{1,0},{17,16},{32,33},{48,49},{2,34}... | collective-permute-start | bytes 1179656 | tf_op jit(solution)/shard_map/ppermute | solution.py:61
  88.5 3.4 %collective-permute-start.12 = (bf16[2,4,128,384]{3,2,1,0:T(8,128)(2,1)S(1)}, bf16[2,4,128,384]{3,2,1,0:T(8,128)(2,1)S(1)}, u32[]{:S(2)}, u32[]{:S(2)}) collective-permute-start(bf16[2,4,128,384]{3,2,1,0:T(8,128)(2,1)S(1)} %pad_maximum_fusion.1.refs_2_), channel_id=1, source_target_pairs={{0,384},{128,256},{256,128},{384,0},{1,385},{129,257},{257,129},{3... | collective-permute-start | bytes 2359304 | tf_op jit(solution)/shard_map/ppermute | solution.py:24
  91.9 3.7 %collective-permute-start.17 = (bf16[2,4,128,384]{3,2,1,0:T(8,128)(2,1)S(1)}, bf16[2,4,128,384]{3,2,1,0:T(8,128)(2,1)S(1)}, u32[]{:S(2)}, u32[]{:S(2)}) collective-permute-start(bf16[2,4,128,384]{3,2,1,0:T(8,128)(2,1)S(1)} %pad_maximum_fusion.1.refs_2_), channel_id=1, source_target_pairs={{0,128},{128,0},{256,384},{384,256},{1,129},{129,1},{257,385},{385... | collective-permute-start | bytes 2359304 | tf_op jit(solution)/shard_map/ppermute | solution.py:24
  100.0 7.5 %collective-permute-done.14 = bf16[2,768,128]{2,1,0:T(8,128)(2,1)S(1)} collective-permute-done((bf16[2,768,128]{2,1,0:T(8,128)(2,1)S(1)}, bf16[2,768,128]{2,1,0:T(8,128)(2,1)S(1)}, u32[]{:S(2)}, u32[]{:S(2)}) %collective-permute-start.14) | collective-permute-done | bytes 393248 | tf_op jit(solution)/shard_map/ppermute | solution.py:61
  112.1 4.1 %collective-permute-start.18 = (bf16[1,4,128,384]{3,2,1,0:T(8,128)(2,1)S(1)}, bf16[1,4,128,384]{3,2,1,0:T(8,128)(2,1)S(1)}, u32[]{:S(2)}, u32[]{:S(2)}) collective-permute-start(bf16[1,4,128,384]{3,2,1,0:T(8,128)(2,1)S(1)} %slice.49), channel_id=1, source_target_pairs={{0,384},{128,256},{256,128},{384,0},{1,385},{129,257},{257,129},{3... | collective-permute-start | bytes 1179656 | tf_op jit(solution)/shard_map/ppermute | solution.py:24
  118.7 3.3 %collective-permute-start.21 = (bf16[2,2,768,128]{3,2,1,0:T(8,128)(2,1)S(1)}, bf16[2,2,768,128]{3,2,1,0:T(8,128)(2,1)S(1)}, u32[]{:S(2)}, u32[]{:S(2)}) collective-permute-start(bf16[2,2,768,128]{3,2,1,0:T(8,128)(2,1)S(1)} %pad_maximum_fusion.2.w0), channel_id=1, source_target_pairs={{0,384},{128,256},{256,128},{384,0},{1,385},{129,257},{257,129},{3... | collective-permute-start | bytes 2359304 | tf_op jit(solution)/shard_map/ppermute | solution.py:24
  123.4 2.7 %collective-permute-done.18 = bf16[1,4,128,384]{3,2,1,0:T(8,128)(2,1)S(1)} collective-permute-done((bf16[1,4,128,384]{3,2,1,0:T(8,128)(2,1)S(1)}, bf16[1,4,128,384]{3,2,1,0:T(8,128)(2,1)S(1)}, u32[]{:S(2)}, u32[]{:S(2)}) %collective-permute-start.18) | collective-permute-done | bytes 393248 | tf_op jit(solution)/shard_map/ppermute | solution.py:24
  126.1 3.9 %collective-permute-start.19 = (bf16[4,272,256]{2,1,0:T(8,128)(2,1)S(1)}, bf16[4,272,256]{2,1,0:T(8,128)(2,1)S(1)}, u32[]{:S(2)}, u32[]{:S(2)}) collective-permute-start(bf16[4,272,256]{2,1,0:T(8,128)(2,1)S(1)} %copy-done.12), channel_id=1, source_target_pairs={{0,8},{4,12},{8,0},{12,4},{1,9},{5,13},{9,1},{13,5},{2,10},{6,14},... | collective-permute-start | bytes 1671176 | tf_op jit(solution)/shard_map/ppermute | solution.py:24
  130.0 12.2 %collective-permute-done.19 = bf16[4,272,256]{2,1,0:T(8,128)(2,1)S(1)} collective-permute-done((bf16[4,272,256]{2,1,0:T(8,128)(2,1)S(1)}, bf16[4,272,256]{2,1,0:T(8,128)(2,1)S(1)}, u32[]{:S(2)}, u32[]{:S(2)}) %collective-permute-start.19) | collective-permute-done | bytes 557088 | tf_op jit(solution)/shard_map/ppermute | solution.py:24
  146.5 5.2 %collective-permute-start.24 = (bf16[1,2,768,128]{3,2,1,0:T(8,128)(2,1)S(1)}, bf16[1,2,768,128]{3,2,1,0:T(8,128)(2,1)S(1)}, u32[]{:S(2)}, u32[]{:S(2)}) collective-permute-start(bf16[1,2,768,128]{3,2,1,0:T(8,128)(2,1)S(1)} %slice.50), channel_id=1, source_target_pairs={{0,128},{128,0},{256,384},{384,256},{1,129},{129,1},{257,385},{385... | collective-permute-start | bytes 1179656 | tf_op jit(solution)/shard_map/ppermute | solution.py:24
  153.7 8.1 %shard_map.46.act = bf16[2,256,384]{2,1,0:T(8,128)(2,1)} custom-call(s32[6]{0:T(128)} %stack.99.place, bf16[4,4,272,256]{3,2,1,0:T(8,128)(2,1)} %pad_maximum_fusion.refs_0_, bf16[4,4,272,256]{3,2,1,0:T(8,128)(2,1)} %collective-permute-done.22.refs_1_, bf16[2,4,128,384]{3,2,1,0:T(8,128)(2,1)} %copy-done.3, bf16[2,4,128,384]{3,2,1,0:T(8,128)(2,1)} %copy-done.6, ...), custom_call_target="tpu_custom_call" | custom-call | flops 1610612736 | bytes 7602200 | tf_op jit(solution)/shard_map/pallas_call | solution.py:145
  168.5 4.2 %collective-permute-start.28 = (bf16[2,256,256]{2,1,0:T(8,128)(2,1)S(1)}, bf16[2,256,256]{2,1,0:T(8,128)(2,1)S(1)}, u32[]{:S(2)}, u32[]{:S(2)}) collective-permute-start(bf16[2,256,256]{2,1,0:T(8,128)(2,1)S(1)} %get-tuple-element.33), channel_id=1, source_target_pairs={{0,12},{4,8},{8,4},{12,0},{1,13},{5,9},{9,5},{13,1},{2,14},{6,10},... | collective-permute-start | bytes 786440 | tf_op jit(solution)/shard_map/ppermute | solution.py:24
  172.7 2.8 %collective-permute-start.27 = (bf16[2,256,256]{2,1,0:T(8,128)(2,1)S(1)}, bf16[2,256,256]{2,1,0:T(8,128)(2,1)S(1)}, u32[]{:S(2)}, u32[]{:S(2)}) collective-permute-start(bf16[2,256,256]{2,1,0:T(8,128)(2,1)S(1)} %get-tuple-element.34), channel_id=1, source_target_pairs={{0,8},{4,12},{8,0},{12,4},{1,9},{5,13},{9,1},{13,5},{2,10},{6,14},... | collective-permute-start | bytes 786440 | tf_op jit(solution)/shard_map/ppermute | solution.py:24
  175.5 3.1 %collective-permute-start.26 = (bf16[2,256,256]{2,1,0:T(8,128)(2,1)S(1)}, bf16[2,256,256]{2,1,0:T(8,128)(2,1)S(1)}, u32[]{:S(2)}, u32[]{:S(2)}) collective-permute-start(bf16[2,256,256]{2,1,0:T(8,128)(2,1)S(1)} %get-tuple-element.32), channel_id=1, source_target_pairs={{0,4},{4,0},{8,12},{12,8},{1,5},{5,1},{9,13},{13,9},{2,6},{6,2},{1... | collective-permute-start | bytes 786440 | tf_op jit(solution)/shard_map/ppermute | solution.py:24
  180.5 3.9 %collective-permute-start.31 = (bf16[2,256,256]{2,1,0:T(8,128)(2,1)S(1)}, bf16[2,256,256]{2,1,0:T(8,128)(2,1)S(1)}, u32[]{:S(2)}, u32[]{:S(2)}) collective-permute-start(bf16[2,256,256]{2,1,0:T(8,128)(2,1)S(1)} %get-tuple-element.30), channel_id=1, source_target_pairs={{0,12},{4,8},{8,4},{12,0},{1,13},{5,9},{9,5},{13,1},{2,14},{6,10},... | collective-permute-start | bytes 786440 | tf_op jit(solution)/shard_map/ppermute | solution.py:24
  184.4 2.8 %collective-permute-start.30 = (bf16[2,256,256]{2,1,0:T(8,128)(2,1)S(1)}, bf16[2,256,256]{2,1,0:T(8,128)(2,1)S(1)}, u32[]{:S(2)}, u32[]{:S(2)}) collective-permute-start(bf16[2,256,256]{2,1,0:T(8,128)(2,1)S(1)} %get-tuple-element.31), channel_id=1, source_target_pairs={{0,8},{4,12},{8,0},{12,4},{1,9},{5,13},{9,1},{13,5},{2,10},{6,14},... | collective-permute-start | bytes 786440 | tf_op jit(solution)/shard_map/ppermute | solution.py:24
  187.2 3.1 %collective-permute-start.29 = (bf16[2,256,256]{2,1,0:T(8,128)(2,1)S(1)}, bf16[2,256,256]{2,1,0:T(8,128)(2,1)S(1)}, u32[]{:S(2)}, u32[]{:S(2)}) collective-permute-start(bf16[2,256,256]{2,1,0:T(8,128)(2,1)S(1)} %get-tuple-element.29), channel_id=1, source_target_pairs={{0,4},{4,0},{8,12},{12,8},{1,5},{5,1},{9,13},{13,9},{2,6},{6,2},{1... | collective-permute-start | bytes 786440 | tf_op jit(solution)/shard_map/ppermute | solution.py:24
  190.5 7.1 %collective-permute-start.34 = (bf16[256,256]{1,0:T(8,128)(2,1)S(1)}, bf16[256,256]{1,0:T(8,128)(2,1)S(1)}, u32[]{:S(2)}, u32[]{:S(2)}) collective-permute-start(bf16[256,256]{1,0:T(8,128)(2,1)S(1)} %fusion.3), channel_id=1, source_target_pairs={{0,2},{2,0},{64,66},{66,64},{1,3},{3,1},{65,67},{67,65},{4,6},{6,4... | collective-permute-start | bytes 393224 | tf_op jit(solution)/shard_map/ppermute | solution.py:24
  200.2 7.1 %collective-permute-start.33 = (bf16[256,256]{1,0:T(8,128)(2,1)S(1)}, bf16[256,256]{1,0:T(8,128)(2,1)S(1)}, u32[]{:S(2)}, u32[]{:S(2)}) collective-permute-start(bf16[256,256]{1,0:T(8,128)(2,1)S(1)} %get-tuple-element.38), channel_id=1, source_target_pairs={{0,66},{2,64},{64,2},{66,0},{1,67},{3,65},{65,3},{67,1},{4,70},{6,... | collective-permute-start | bytes 393224 | tf_op jit(solution)/shard_map/ppermute | solution.py:24
  209.8 3.4 %collective-permute-done.34 = bf16[256,256]{1,0:T(8,128)(2,1)S(1)} collective-permute-done((bf16[256,256]{1,0:T(8,128)(2,1)S(1)}, bf16[256,256]{1,0:T(8,128)(2,1)S(1)}, u32[]{:S(2)}, u32[]{:S(2)}) %collective-permute-start.34) | collective-permute-done | bytes 131104 | tf_op jit(solution)/shard_map/ppermute | solution.py:24
  213.2 4.2 %collective-permute-done.33 = bf16[256,256]{1,0:T(8,128)(2,1)S(1)} collective-permute-done((bf16[256,256]{1,0:T(8,128)(2,1)S(1)}, bf16[256,256]{1,0:T(8,128)(2,1)S(1)}, u32[]{:S(2)}, u32[]{:S(2)}) %collective-permute-start.33) | collective-permute-done | bytes 131104 | tf_op jit(solution)/shard_map/ppermute | solution.py:24
  217.4 7.8 %collective-permute-done.32 = bf16[256,256]{1,0:T(8,128)(2,1)S(1)} collective-permute-done((bf16[256,256]{1,0:T(8,128)(2,1)S(1)}, bf16[256,256]{1,0:T(8,128)(2,1)S(1)}, u32[]{:S(2)}, u32[]{:S(2)}) %collective-permute-start.32) | collective-permute-done | bytes 131104 | tf_op jit(solution)/shard_map/ppermute | solution.py:24
  (94 shorter events, 49.0 us)
Async XLA Ops:
  1.0 29.8 %collective-permute-start.3 = (bf16[128,384]{1,0:T(8,128)(2,1)S(1)}, bf16[128,384]{1,0:T(8,128)(2,1)S(1)}, u32[]{:S(2)}, u32[]{:S(2)}) collective-permute-start(bf16[128,384]{1,0:T(8,128)(2,1)S(1)} %get-tuple-element.40), channel_id=1, source_target_pairs={{0,0},{1,64},{64,1},{65,65},{2,2},{3,66},{66,3},{67,67},{4,4},{5,6... | collective-permute-start | bytes 294920 | tf_op jit(solution)/shard_map/ppermute | solution.py:33
  1.6 29.1 %collective-permute-start.4 = (bf16[128,384]{1,0:T(8,128)(2,1)S(1)}, bf16[128,384]{1,0:T(8,128)(2,1)S(1)}, u32[]{:S(2)}, u32[]{:S(2)}) collective-permute-start(bf16[128,384]{1,0:T(8,128)(2,1)S(1)} %get-tuple-element.39), channel_id=1, source_target_pairs={{0,1},{1,65},{64,0},{65,64},{2,3},{3,67},{66,2},{67,66},{4,5},{5,6... | collective-permute-start | bytes 294920 | tf_op jit(solution)/shard_map/ppermute | solution.py:34
  13.7 20.6 %collective-permute-start.2 = (bf16[272,256]{1,0:T(8,128)(2,1)S(1)}, bf16[272,256]{1,0:T(8,128)(2,1)S(1)}, u32[]{:S(2)}, u32[]{:S(2)}) collective-permute-start(bf16[272,256]{1,0:T(8,128)(2,1)S(1)} %get-tuple-element.42), channel_id=1, source_target_pairs={{0,66},{2,64},{64,2},{66,0},{1,67},{3,65},{65,3},{67,1},{4,70},{6,... | collective-permute-start | bytes 417800 | tf_op jit(solution)/shard_map/ppermute | solution.py:24
  21.2 32.3 %collective-permute-start.1 = (bf16[272,256]{1,0:T(8,128)(2,1)S(1)}, bf16[272,256]{1,0:T(8,128)(2,1)S(1)}, u32[]{:S(2)}, u32[]{:S(2)}) collective-permute-start(bf16[272,256]{1,0:T(8,128)(2,1)S(1)} %get-tuple-element.42), channel_id=1, source_target_pairs={{0,64},{2,66},{64,0},{66,2},{1,65},{3,67},{65,1},{67,3},{4,68},{6,... | collective-permute-start | bytes 417800 | tf_op jit(solution)/shard_map/ppermute | solution.py:24
  26.2 27.4 %collective-permute-start = (bf16[272,256]{1,0:T(8,128)(2,1)S(1)}, bf16[272,256]{1,0:T(8,128)(2,1)S(1)}, u32[]{:S(2)}, u32[]{:S(2)}) collective-permute-start(bf16[272,256]{1,0:T(8,128)(2,1)S(1)} %get-tuple-element.42), channel_id=1, source_target_pairs={{0,2},{2,0},{64,66},{66,64},{1,3},{3,1},{65,67},{67,65},{4,6},{6,4... | collective-permute-start | bytes 417800 | tf_op jit(solution)/shard_map/ppermute | solution.py:24
  30.8 23.7 %collective-permute-start.5 = (bf16[768,128]{1,0:T(8,128)(2,1)}, bf16[768,128]{1,0:T(8,128)(2,1)S(1)}, u32[]{:S(2)}, u32[]{:S(2)}) collective-permute-start(bf16[768,128]{1,0:T(8,128)(2,1)} %param.7), channel_id=1, source_target_pairs={{0,0},{16,16},{32,33},{48,49},{65,64},{81,80},{97,97},{113,113},{1... | collective-permute-start | bytes 589832 | tf_op jit(solution)/shard_map/ppermute | solution.py:53
  32.3 26.2 %collective-permute-start.6 = (bf16[768,128]{1,0:T(8,128)(2,1)}, bf16[768,128]{1,0:T(8,128)(2,1)S(1)}, u32[]{:S(2)}, u32[]{:S(2)}) collective-permute-start(bf16[768,128]{1,0:T(8,128)(2,1)} %param.7), channel_id=1, source_target_pairs={{1,64},{17,80},{33,97},{49,113},{64,0},{80,16},{96,33},{112,49},{0... | collective-permute-start | bytes 589832 | tf_op jit(solution)/shard_map/ppermute | solution.py:53
  58.6 25.9 %collective-permute-start.11 = (bf16[4,272,256]{2,1,0:T(8,128)(2,1)S(1)}, bf16[4,272,256]{2,1,0:T(8,128)(2,1)S(1)}, u32[]{:S(2)}, u32[]{:S(2)}) collective-permute-start(bf16[4,272,256]{2,1,0:T(8,128)(2,1)S(1)} %get-tuple-element.24), channel_id=1, source_target_pairs={{0,12},{4,8},{8,4},{12,0},{1,13},{5,9},{9,5},{13,1},{2,14},{6,10},... | collective-permute-start | bytes 1671176 | tf_op jit(solution)/shard_map/ppermute | solution.py:24
  60.9 23.6 %collective-permute-start.7 = (bf16[4,272,256]{2,1,0:T(8,128)(2,1)S(1)}, bf16[4,272,256]{2,1,0:T(8,128)(2,1)S(1)}, u32[]{:S(2)}, u32[]{:S(2)}) collective-permute-start(bf16[4,272,256]{2,1,0:T(8,128)(2,1)S(1)} %get-tuple-element.24), channel_id=1, source_target_pairs={{0,4},{4,0},{8,12},{12,8},{1,5},{5,1},{9,13},{13,9},{2,6},{6,2},{1... | collective-permute-start | bytes 1671176 | tf_op jit(solution)/shard_map/ppermute | solution.py:24
  63.9 16.9 %collective-permute-start.10 = (bf16[2,128,384]{2,1,0:T(8,128)(2,1)S(1)}, bf16[2,128,384]{2,1,0:T(8,128)(2,1)S(1)}, u32[]{:S(2)}, u32[]{:S(2)}) collective-permute-start(bf16[2,128,384]{2,1,0:T(8,128)(2,1)S(1)} %pad_maximum_fusion.5), channel_id=1, source_target_pairs={{0,48},{16,32},{32,16},{48,0},{1,49},{17,33},{33,17},{49,1},{2,50}... | collective-permute-start | bytes 589832 | tf_op jit(solution)/shard_map/ppermute | solution.py:24
  67.3 15.7 %collective-permute-start.9 = (bf16[2,128,384]{2,1,0:T(8,128)(2,1)S(1)}, bf16[2,128,384]{2,1,0:T(8,128)(2,1)S(1)}, u32[]{:S(2)}, u32[]{:S(2)}) collective-permute-start(bf16[2,128,384]{2,1,0:T(8,128)(2,1)S(1)} %pad_maximum_fusion.5), channel_id=1, source_target_pairs={{0,32},{16,48},{32,0},{48,16},{1,33},{17,49},{33,1},{49,17},{2,34}... | collective-permute-start | bytes 589832 | tf_op jit(solution)/shard_map/ppermute | solution.py:24
  84.5 15.4 %collective-permute-start.13 = (bf16[2,768,128]{2,1,0:T(8,128)(2,1)S(1)}, bf16[2,768,128]{2,1,0:T(8,128)(2,1)S(1)}, u32[]{:S(2)}, u32[]{:S(2)}) collective-permute-start(bf16[2,768,128]{2,1,0:T(8,128)(2,1)S(1)} %pad_maximum_fusion.4), channel_id=1, source_target_pairs={{0,32},{16,48},{33,1},{49,17},{1,0},{17,16},{32,33},{48,49},{2,34}... | collective-permute-start | bytes 1179656 | tf_op jit(solution)/shard_map/ppermute | solution.py:61
  88.5 21.1 %collective-permute-start.12 = (bf16[2,4,128,384]{3,2,1,0:T(8,128)(2,1)S(1)}, bf16[2,4,128,384]{3,2,1,0:T(8,128)(2,1)S(1)}, u32[]{:S(2)}, u32[]{:S(2)}) collective-permute-start(bf16[2,4,128,384]{3,2,1,0:T(8,128)(2,1)S(1)} %pad_maximum_fusion.1.refs_2_), channel_id=1, source_target_pairs={{0,384},{128,256},{256,128},{384,0},{1,385},{129,257},{257,129},{3... | collective-permute-start | bytes 2359304 | tf_op jit(solution)/shard_map/ppermute | solution.py:24
  91.9 20.1 %collective-permute-start.17 = (bf16[2,4,128,384]{3,2,1,0:T(8,128)(2,1)S(1)}, bf16[2,4,128,384]{3,2,1,0:T(8,128)(2,1)S(1)}, u32[]{:S(2)}, u32[]{:S(2)}) collective-permute-start(bf16[2,4,128,384]{3,2,1,0:T(8,128)(2,1)S(1)} %pad_maximum_fusion.1.refs_2_), channel_id=1, source_target_pairs={{0,128},{128,0},{256,384},{384,256},{1,129},{129,1},{257,385},{385... | collective-permute-start | bytes 2359304 | tf_op jit(solution)/shard_map/ppermute | solution.py:24
  95.6 11.9 %collective-permute-start.14 = (bf16[2,768,128]{2,1,0:T(8,128)(2,1)S(1)}, bf16[2,768,128]{2,1,0:T(8,128)(2,1)S(1)}, u32[]{:S(2)}, u32[]{:S(2)}) collective-permute-start(bf16[2,768,128]{2,1,0:T(8,128)(2,1)S(1)} %pad_maximum_fusion.4), channel_id=1, source_target_pairs={{0,16},{16,0},{33,49},{49,33},{1,1},{17,17},{32,32},{48,48},{2,18}... | collective-permute-start | bytes 1179656 | tf_op jit(solution)/shard_map/ppermute | solution.py:61
  98.0 11.4 %collective-permute-start.15 = (bf16[2,768,128]{2,1,0:T(8,128)(2,1)S(1)}, bf16[2,768,128]{2,1,0:T(8,128)(2,1)}, u32[]{:S(2)}, u32[]{:S(2)}) collective-permute-start(bf16[2,768,128]{2,1,0:T(8,128)(2,1)S(1)} %pad_maximum_fusion.4), channel_id=1, source_target_pairs={{0,48},{16,32},{33,17},{49,1},{1,0},{17,16},{32,33},{48,49},{2,50}... | collective-permute-start | bytes 1179656 | tf_op jit(solution)/shard_map/ppermute | solution.py:61
  109.6 13.8 %collective-permute-start.16 = (bf16[1,4,128,384]{3,2,1,0:T(8,128)(2,1)S(1)}, bf16[1,4,128,384]{3,2,1,0:T(8,128)(2,1)S(1)}, u32[]{:S(2)}, u32[]{:S(2)}) collective-permute-start(bf16[1,4,128,384]{3,2,1,0:T(8,128)(2,1)S(1)} %slice.48), channel_id=1, source_target_pairs={{0,128},{128,0},{256,384},{384,256},{1,129},{129,1},{257,385},{385... | collective-permute-start | bytes 1179656 | tf_op jit(solution)/shard_map/ppermute | solution.py:24
  112.1 14.0 %collective-permute-start.18 = (bf16[1,4,128,384]{3,2,1,0:T(8,128)(2,1)S(1)}, bf16[1,4,128,384]{3,2,1,0:T(8,128)(2,1)S(1)}, u32[]{:S(2)}, u32[]{:S(2)}) collective-permute-start(bf16[1,4,128,384]{3,2,1,0:T(8,128)(2,1)S(1)} %slice.49), channel_id=1, source_target_pairs={{0,384},{128,256},{256,128},{384,0},{1,385},{129,257},{257,129},{3... | collective-permute-start | bytes 1179656 | tf_op jit(solution)/shard_map/ppermute | solution.py:24
  116.2 27.8 %collective-permute-start.20 = (bf16[2,2,768,128]{3,2,1,0:T(8,128)(2,1)S(1)}, bf16[2,2,768,128]{3,2,1,0:T(8,128)(2,1)S(1)}, u32[]{:S(2)}, u32[]{:S(2)}) collective-permute-start(bf16[2,2,768,128]{3,2,1,0:T(8,128)(2,1)S(1)} %pad_maximum_fusion.2.w0), channel_id=1, source_target_pairs={{0,128},{128,0},{256,384},{384,256},{1,129},{129,1},{257,385},{385... | collective-permute-start | bytes 2359304 | tf_op jit(solution)/shard_map/ppermute | solution.py:24
  118.7 25.3 %collective-permute-start.21 = (bf16[2,2,768,128]{3,2,1,0:T(8,128)(2,1)S(1)}, bf16[2,2,768,128]{3,2,1,0:T(8,128)(2,1)S(1)}, u32[]{:S(2)}, u32[]{:S(2)}) collective-permute-start(bf16[2,2,768,128]{3,2,1,0:T(8,128)(2,1)S(1)} %pad_maximum_fusion.2.w0), channel_id=1, source_target_pairs={{0,384},{128,256},{256,128},{384,0},{1,385},{129,257},{257,129},{3... | collective-permute-start | bytes 2359304 | tf_op jit(solution)/shard_map/ppermute | solution.py:24
  126.1 16.2 %collective-permute-start.19 = (bf16[4,272,256]{2,1,0:T(8,128)(2,1)S(1)}, bf16[4,272,256]{2,1,0:T(8,128)(2,1)S(1)}, u32[]{:S(2)}, u32[]{:S(2)}) collective-permute-start(bf16[4,272,256]{2,1,0:T(8,128)(2,1)S(1)} %copy-done.12), channel_id=1, source_target_pairs={{0,8},{4,12},{8,0},{12,4},{1,9},{5,13},{9,1},{13,5},{2,10},{6,14},... | collective-permute-start | bytes 1671176 | tf_op jit(solution)/shard_map/ppermute | solution.py:24
  146.5 17.3 %collective-permute-start.24 = (bf16[1,2,768,128]{3,2,1,0:T(8,128)(2,1)S(1)}, bf16[1,2,768,128]{3,2,1,0:T(8,128)(2,1)S(1)}, u32[]{:S(2)}, u32[]{:S(2)}) collective-permute-start(bf16[1,2,768,128]{3,2,1,0:T(8,128)(2,1)S(1)} %slice.50), channel_id=1, source_target_pairs={{0,128},{128,0},{256,384},{384,256},{1,129},{129,1},{257,385},{385... | collective-permute-start | bytes 1179656 | tf_op jit(solution)/shard_map/ppermute | solution.py:24
  151.8 13.1 %collective-permute-start.25 = (bf16[1,2,768,128]{3,2,1,0:T(8,128)(2,1)S(1)}, bf16[1,2,768,128]{3,2,1,0:T(8,128)(2,1)S(1)}, u32[]{:S(2)}, u32[]{:S(2)}) collective-permute-start(bf16[1,2,768,128]{3,2,1,0:T(8,128)(2,1)S(1)} %slice.51), channel_id=1, source_target_pairs={{0,384},{128,256},{256,128},{384,0},{1,385},{129,257},{257,129},{3... | collective-permute-start | bytes 1179656 | tf_op jit(solution)/shard_map/ppermute | solution.py:24
  168.5 18.8 %collective-permute-start.28 = (bf16[2,256,256]{2,1,0:T(8,128)(2,1)S(1)}, bf16[2,256,256]{2,1,0:T(8,128)(2,1)S(1)}, u32[]{:S(2)}, u32[]{:S(2)}) collective-permute-start(bf16[2,256,256]{2,1,0:T(8,128)(2,1)S(1)} %get-tuple-element.33), channel_id=1, source_target_pairs={{0,12},{4,8},{8,4},{12,0},{1,13},{5,9},{9,5},{13,1},{2,14},{6,10},... | collective-permute-start | bytes 786440 | tf_op jit(solution)/shard_map/ppermute | solution.py:24
  172.7 17.7 %collective-permute-start.27 = (bf16[2,256,256]{2,1,0:T(8,128)(2,1)S(1)}, bf16[2,256,256]{2,1,0:T(8,128)(2,1)S(1)}, u32[]{:S(2)}, u32[]{:S(2)}) collective-permute-start(bf16[2,256,256]{2,1,0:T(8,128)(2,1)S(1)} %get-tuple-element.34), channel_id=1, source_target_pairs={{0,8},{4,12},{8,0},{12,4},{1,9},{5,13},{9,1},{13,5},{2,10},{6,14},... | collective-permute-start | bytes 786440 | tf_op jit(solution)/shard_map/ppermute | solution.py:24
  175.5 14.9 %collective-permute-start.26 = (bf16[2,256,256]{2,1,0:T(8,128)(2,1)S(1)}, bf16[2,256,256]{2,1,0:T(8,128)(2,1)S(1)}, u32[]{:S(2)}, u32[]{:S(2)}) collective-permute-start(bf16[2,256,256]{2,1,0:T(8,128)(2,1)S(1)} %get-tuple-element.32), channel_id=1, source_target_pairs={{0,4},{4,0},{8,12},{12,8},{1,5},{5,1},{9,13},{13,9},{2,6},{6,2},{1... | collective-permute-start | bytes 786440 | tf_op jit(solution)/shard_map/ppermute | solution.py:24
  180.5 17.2 %collective-permute-start.31 = (bf16[2,256,256]{2,1,0:T(8,128)(2,1)S(1)}, bf16[2,256,256]{2,1,0:T(8,128)(2,1)S(1)}, u32[]{:S(2)}, u32[]{:S(2)}) collective-permute-start(bf16[2,256,256]{2,1,0:T(8,128)(2,1)S(1)} %get-tuple-element.30), channel_id=1, source_target_pairs={{0,12},{4,8},{8,4},{12,0},{1,13},{5,9},{9,5},{13,1},{2,14},{6,10},... | collective-permute-start | bytes 786440 | tf_op jit(solution)/shard_map/ppermute | solution.py:24
  184.4 13.2 %collective-permute-start.30 = (bf16[2,256,256]{2,1,0:T(8,128)(2,1)S(1)}, bf16[2,256,256]{2,1,0:T(8,128)(2,1)S(1)}, u32[]{:S(2)}, u32[]{:S(2)}) collective-permute-start(bf16[2,256,256]{2,1,0:T(8,128)(2,1)S(1)} %get-tuple-element.31), channel_id=1, source_target_pairs={{0,8},{4,12},{8,0},{12,4},{1,9},{5,13},{9,1},{13,5},{2,10},{6,14},... | collective-permute-start | bytes 786440 | tf_op jit(solution)/shard_map/ppermute | solution.py:24
  187.2 12.7 %collective-permute-start.29 = (bf16[2,256,256]{2,1,0:T(8,128)(2,1)S(1)}, bf16[2,256,256]{2,1,0:T(8,128)(2,1)S(1)}, u32[]{:S(2)}, u32[]{:S(2)}) collective-permute-start(bf16[2,256,256]{2,1,0:T(8,128)(2,1)S(1)} %get-tuple-element.29), channel_id=1, source_target_pairs={{0,4},{4,0},{8,12},{12,8},{1,5},{5,1},{9,13},{13,9},{2,6},{6,2},{1... | collective-permute-start | bytes 786440 | tf_op jit(solution)/shard_map/ppermute | solution.py:24
  190.5 22.7 %collective-permute-start.34 = (bf16[256,256]{1,0:T(8,128)(2,1)S(1)}, bf16[256,256]{1,0:T(8,128)(2,1)S(1)}, u32[]{:S(2)}, u32[]{:S(2)}) collective-permute-start(bf16[256,256]{1,0:T(8,128)(2,1)S(1)} %fusion.3), channel_id=1, source_target_pairs={{0,2},{2,0},{64,66},{66,64},{1,3},{3,1},{65,67},{67,65},{4,6},{6,4... | collective-permute-start | bytes 393224 | tf_op jit(solution)/shard_map/ppermute | solution.py:24
  200.2 17.2 %collective-permute-start.33 = (bf16[256,256]{1,0:T(8,128)(2,1)S(1)}, bf16[256,256]{1,0:T(8,128)(2,1)S(1)}, u32[]{:S(2)}, u32[]{:S(2)}) collective-permute-start(bf16[256,256]{1,0:T(8,128)(2,1)S(1)} %get-tuple-element.38), channel_id=1, source_target_pairs={{0,66},{2,64},{64,2},{66,0},{1,67},{3,65},{65,3},{67,1},{4,70},{6,... | collective-permute-start | bytes 393224 | tf_op jit(solution)/shard_map/ppermute | solution.py:24
  207.3 17.9 %collective-permute-start.32 = (bf16[256,256]{1,0:T(8,128)(2,1)S(1)}, bf16[256,256]{1,0:T(8,128)(2,1)S(1)}, u32[]{:S(2)}, u32[]{:S(2)}) collective-permute-start(bf16[256,256]{1,0:T(8,128)(2,1)S(1)} %get-tuple-element.37), channel_id=1, source_target_pairs={{0,64},{2,66},{64,0},{66,2},{1,65},{3,67},{65,1},{67,3},{4,68},{6,... | collective-permute-start | bytes 393224 | tf_op jit(solution)/shard_map/ppermute | solution.py:24
  (18 other events, 339.2 us)

commit v10 on v9

--- a/solution.py
+++ b/solution.py
@@ -206,7 +206,7 @@
     (total, stay), (_, away) = parts
     total = total[0] + sum(
         send(piece, ("zt", "zh"), k).astype(jnp.float32)
-        for k, piece in ((2, away[0]), (3, away[1]), (1, stay[1]))
+        for k, piece in ((1, stay[1]), (3, away[1]), (2, away[0]))
     )
     return total.astype(jnp.bfloat16)
 

time: 227 us -> 229 us (level)
  the two profiles are of different devices: /device:TPU:50 before, /device:TPU:45 now
where the time goes in v10:
time: 229 us; the launch traced here: 228 us
  starting transfers between devices  137 us (60%)
  waiting for transfers between devices  68.9 us (30%)
  Pallas kernels  11.6 us (5%)
  other arithmetic  5.82 us (3%)
  local copies, waits for them, and re-layouts  3.58 us (2%)
    ppermute x28, starting transfers between devices, send(): return lax.ppermute(value, axes, [(i, i ^ k) for i in range(count)])  106 us
    ppermute x28, waiting for transfers between devices, send(): return lax.ppermute(value, axes, [(i, i ^ k) for i in range(count)])  60.5 us
    ppermute x3, starting transfers between devices, spread_blocks(): got.append(lax.ppermute(blocks, ('zq', 'c'), pairs))  12.6 us
    pallas_call x3, Pallas kernels, call(): pl.pallas_call(kernel, out_shape=out_shape, in_specs=[pl.BlockSpec(memory...  11.6 us
    ppermute x1, starting transfers between devices, swap_halves(): lax.ppermute(first, ('zt', 'c'), [(2 * a + b, 2 * b + a) for a, b in both])  9.38 us
    ppermute x3, waiting for transfers between devices, spread_blocks(): got.append(lax.ppermute(blocks, ('zq', 'c'), pairs))  8.43 us
    ppermute x2, starting transfers between devices, swap_blocks(): return (lax.ppermute(block, axes, own), lax.ppermute(block, axes, cross))  7.06 us
  transfers between devices with their start and end apart: 35, of which 11 were waited for; matrix products, arithmetic and copies ran while one was open for 3% of the time, Pallas kernels for 4%

profile of v10, /device:TPU:45, one launch (start us, length us, event | category | flops | bytes accessed | tf_op | source)
XLA Modules:
  0.0 228.0 jit_solution(1443981286223932879)
XLA Ops:
  1.0 9.4 %collective-permute-start.3 = (bf16[128,384]{1,0:T(8,128)(2,1)S(1)}, bf16[128,384]{1,0:T(8,128)(2,1)S(1)}, u32[]{:S(2)}, u32[]{:S(2)}) collective-permute-start(bf16[128,384]{1,0:T(8,128)(2,1)S(1)} %get-tuple-element.40), channel_id=1, source_target_pairs={{0,0},{1,64},{64,1},{65,65},{2,2},{3,66},{66,3},{67,67},{4,4},{5,6... | collective-permute-start | bytes 294920 | tf_op jit(solution)/shard_map/ppermute | solution.py:33
  13.9 7.7 %collective-permute-start.2 = (bf16[272,256]{1,0:T(8,128)(2,1)S(1)}, bf16[272,256]{1,0:T(8,128)(2,1)S(1)}, u32[]{:S(2)}, u32[]{:S(2)}) collective-permute-start(bf16[272,256]{1,0:T(8,128)(2,1)S(1)} %get-tuple-element.42), channel_id=1, source_target_pairs={{0,66},{2,64},{64,2},{66,0},{1,67},{3,65},{65,3},{67,1},{4,70},{6,... | collective-permute-start | bytes 417800 | tf_op jit(solution)/shard_map/ppermute | solution.py:24
  21.6 4.2 %collective-permute-start.1 = (bf16[272,256]{1,0:T(8,128)(2,1)S(1)}, bf16[272,256]{1,0:T(8,128)(2,1)S(1)}, u32[]{:S(2)}, u32[]{:S(2)}) collective-permute-start(bf16[272,256]{1,0:T(8,128)(2,1)S(1)} %get-tuple-element.42), channel_id=1, source_target_pairs={{0,64},{2,66},{64,0},{66,2},{1,65},{3,67},{65,1},{67,3},{4,68},{6,... | collective-permute-start | bytes 417800 | tf_op jit(solution)/shard_map/ppermute | solution.py:24
  25.8 4.7 %collective-permute-start = (bf16[272,256]{1,0:T(8,128)(2,1)S(1)}, bf16[272,256]{1,0:T(8,128)(2,1)S(1)}, u32[]{:S(2)}, u32[]{:S(2)}) collective-permute-start(bf16[272,256]{1,0:T(8,128)(2,1)S(1)} %get-tuple-element.42), channel_id=1, source_target_pairs={{0,2},{2,0},{64,66},{66,64},{1,3},{3,1},{65,67},{67,65},{4,6},{6,4... | collective-permute-start | bytes 417800 | tf_op jit(solution)/shard_map/ppermute | solution.py:24
  32.2 5.5 %collective-permute-start.6 = (bf16[768,128]{1,0:T(8,128)(2,1)}, bf16[768,128]{1,0:T(8,128)(2,1)S(1)}, u32[]{:S(2)}, u32[]{:S(2)}) collective-permute-start(bf16[768,128]{1,0:T(8,128)(2,1)} %param.7), channel_id=1, source_target_pairs={{1,64},{17,80},{33,97},{49,113},{64,0},{80,16},{96,33},{112,49},{0... | collective-permute-start | bytes 589832 | tf_op jit(solution)/shard_map/ppermute | solution.py:53
  37.7 16.0 %collective-permute-done.1 = bf16[272,256]{1,0:T(8,128)(2,1)S(1)} collective-permute-done((bf16[272,256]{1,0:T(8,128)(2,1)S(1)}, bf16[272,256]{1,0:T(8,128)(2,1)S(1)}, u32[]{:S(2)}, u32[]{:S(2)}) %collective-permute-start.1) | collective-permute-done | bytes 139296 | tf_op jit(solution)/shard_map/ppermute | solution.py:24
  54.6 3.2 %collective-permute-start.11 = (bf16[4,272,256]{2,1,0:T(8,128)(2,1)S(1)}, bf16[4,272,256]{2,1,0:T(8,128)(2,1)S(1)}, u32[]{:S(2)}, u32[]{:S(2)}) collective-permute-start(bf16[4,272,256]{2,1,0:T(8,128)(2,1)S(1)} %get-tuple-element.24), channel_id=1, source_target_pairs={{0,12},{4,8},{8,4},{12,0},{1,13},{5,9},{9,5},{13,1},{2,14},{6,10},... | collective-permute-start | bytes 1671176 | tf_op jit(solution)/shard_map/ppermute | solution.py:24
  57.8 3.5 %collective-permute-start.7 = (bf16[4,272,256]{2,1,0:T(8,128)(2,1)S(1)}, bf16[4,272,256]{2,1,0:T(8,128)(2,1)S(1)}, u32[]{:S(2)}, u32[]{:S(2)}) collective-permute-start(bf16[4,272,256]{2,1,0:T(8,128)(2,1)S(1)} %get-tuple-element.24), channel_id=1, source_target_pairs={{0,4},{4,0},{8,12},{12,8},{1,5},{5,1},{9,13},{13,9},{2,6},{6,2},{1... | collective-permute-start | bytes 1671176 | tf_op jit(solution)/shard_map/ppermute | solution.py:24
  61.4 6.4 %collective-permute-start.10 = (bf16[2,128,384]{2,1,0:T(8,128)(2,1)S(1)}, bf16[2,128,384]{2,1,0:T(8,128)(2,1)S(1)}, u32[]{:S(2)}, u32[]{:S(2)}) collective-permute-start(bf16[2,128,384]{2,1,0:T(8,128)(2,1)S(1)} %pad_maximum_fusion.5), channel_id=1, source_target_pairs={{0,48},{16,32},{32,16},{48,0},{1,49},{17,33},{33,17},{49,1},{2,50}... | collective-permute-start | bytes 589832 | tf_op jit(solution)/shard_map/ppermute | solution.py:24
  67.8 6.1 %collective-permute-start.9 = (bf16[2,128,384]{2,1,0:T(8,128)(2,1)S(1)}, bf16[2,128,384]{2,1,0:T(8,128)(2,1)S(1)}, u32[]{:S(2)}, u32[]{:S(2)}) collective-permute-start(bf16[2,128,384]{2,1,0:T(8,128)(2,1)S(1)} %pad_maximum_fusion.5), channel_id=1, source_target_pairs={{0,32},{16,48},{32,0},{48,16},{1,33},{17,49},{33,1},{49,17},{2,34}... | collective-permute-start | bytes 589832 | tf_op jit(solution)/shard_map/ppermute | solution.py:24
  75.9 7.2 %collective-permute-done.9 = bf16[2,128,384]{2,1,0:T(8,128)(2,1)S(1)} collective-permute-done((bf16[2,128,384]{2,1,0:T(8,128)(2,1)S(1)}, bf16[2,128,384]{2,1,0:T(8,128)(2,1)S(1)}, u32[]{:S(2)}, u32[]{:S(2)}) %collective-permute-start.9) | collective-permute-done | bytes 196640 | tf_op jit(solution)/shard_map/ppermute | solution.py:24
  83.3 5.7 %collective-permute-start.13 = (bf16[2,768,128]{2,1,0:T(8,128)(2,1)S(1)}, bf16[2,768,128]{2,1,0:T(8,128)(2,1)S(1)}, u32[]{:S(2)}, u32[]{:S(2)}) collective-permute-start(bf16[2,768,128]{2,1,0:T(8,128)(2,1)S(1)} %pad_maximum_fusion.4), channel_id=1, source_target_pairs={{0,32},{16,48},{33,1},{49,17},{1,0},{17,16},{32,33},{48,49},{2,34}... | collective-permute-start | bytes 1179656 | tf_op jit(solution)/shard_map/ppermute | solution.py:61
  91.2 2.8 %collective-permute-start.17 = (bf16[2,4,128,384]{3,2,1,0:T(8,128)(2,1)S(1)}, bf16[2,4,128,384]{3,2,1,0:T(8,128)(2,1)S(1)}, u32[]{:S(2)}, u32[]{:S(2)}) collective-permute-start(bf16[2,4,128,384]{3,2,1,0:T(8,128)(2,1)S(1)} %pad_maximum_fusion.1.refs_2_), channel_id=1, source_target_pairs={{0,128},{128,0},{256,384},{384,256},{1,129},{129,1},{257,385},{385... | collective-permute-start | bytes 2359304 | tf_op jit(solution)/shard_map/ppermute | solution.py:24
  94.7 6.2 %collective-permute-start.15 = (bf16[2,768,128]{2,1,0:T(8,128)(2,1)S(1)}, bf16[2,768,128]{2,1,0:T(8,128)(2,1)}, u32[]{:S(2)}, u32[]{:S(2)}) collective-permute-start(bf16[2,768,128]{2,1,0:T(8,128)(2,1)S(1)} %pad_maximum_fusion.4), channel_id=1, source_target_pairs={{0,48},{16,32},{33,17},{49,1},{1,0},{17,16},{32,33},{48,49},{2,50}... | collective-permute-start | bytes 1179656 | tf_op jit(solution)/shard_map/ppermute | solution.py:61
  101.0 8.4 %collective-permute-done.15 = bf16[2,768,128]{2,1,0:T(8,128)(2,1)} collective-permute-done((bf16[2,768,128]{2,1,0:T(8,128)(2,1)S(1)}, bf16[2,768,128]{2,1,0:T(8,128)(2,1)}, u32[]{:S(2)}, u32[]{:S(2)}) %collective-permute-start.15) | collective-permute-done | bytes 393248 | tf_op jit(solution)/shard_map/ppermute | solution.py:61
  110.7 2.5 %collective-permute-start.16 = (bf16[1,4,128,384]{3,2,1,0:T(8,128)(2,1)S(1)}, bf16[1,4,128,384]{3,2,1,0:T(8,128)(2,1)S(1)}, u32[]{:S(2)}, u32[]{:S(2)}) collective-permute-start(bf16[1,4,128,384]{3,2,1,0:T(8,128)(2,1)S(1)} %slice.48), channel_id=1, source_target_pairs={{0,128},{128,0},{256,384},{384,256},{1,129},{129,1},{257,385},{385... | collective-permute-start | bytes 1179656 | tf_op jit(solution)/shard_map/ppermute | solution.py:24
  113.3 3.2 %collective-permute-start.18 = (bf16[1,4,128,384]{3,2,1,0:T(8,128)(2,1)S(1)}, bf16[1,4,128,384]{3,2,1,0:T(8,128)(2,1)S(1)}, u32[]{:S(2)}, u32[]{:S(2)}) collective-permute-start(bf16[1,4,128,384]{3,2,1,0:T(8,128)(2,1)S(1)} %slice.49), channel_id=1, source_target_pairs={{0,384},{128,256},{256,128},{384,0},{1,385},{129,257},{257,129},{3... | collective-permute-start | bytes 1179656 | tf_op jit(solution)/shard_map/ppermute | solution.py:24
  116.5 4.0 %collective-permute-start.20 = (bf16[2,2,768,128]{3,2,1,0:T(8,128)(2,1)S(1)}, bf16[2,2,768,128]{3,2,1,0:T(8,128)(2,1)S(1)}, u32[]{:S(2)}, u32[]{:S(2)}) collective-permute-start(bf16[2,2,768,128]{3,2,1,0:T(8,128)(2,1)S(1)} %pad_maximum_fusion.2.w0), channel_id=1, source_target_pairs={{0,128},{128,0},{256,384},{384,256},{1,129},{129,1},{257,385},{385... | collective-permute-start | bytes 2359304 | tf_op jit(solution)/shard_map/ppermute | solution.py:24
  126.3 12.1 %collective-permute-done.19 = bf16[4,272,256]{2,1,0:T(8,128)(2,1)S(1)} collective-permute-done((bf16[4,272,256]{2,1,0:T(8,128)(2,1)S(1)}, bf16[4,272,256]{2,1,0:T(8,128)(2,1)S(1)}, u32[]{:S(2)}, u32[]{:S(2)}) %collective-permute-start.19) | collective-permute-done | bytes 557088 | tf_op jit(solution)/shard_map/ppermute | solution.py:24
  142.0 4.5 %collective-permute-start.22 = (bf16[4,4,272,256]{3,2,1,0:T(8,128)(2,1)}, bf16[4,4,272,256]{3,2,1,0:T(8,128)(2,1)}, u32[]{:S(2)}, u32[]{:S(2)}) collective-permute-start(bf16[4,4,272,256]{3,2,1,0:T(8,128)(2,1)} %pad_maximum_fusion.refs_0_), channel_id=1, source_target_pairs={{0,1},{1,0},{2,3},{3,2},{4,5},{5,4},{6,7},{7,6},{8,9},{9,8},{10,11... | collective-permute-start | bytes 6684680 | tf_op jit(solution)/shard_map/ppermute | solution.py:24
  147.1 4.4 %collective-permute-start.24 = (bf16[1,2,768,128]{3,2,1,0:T(8,128)(2,1)S(1)}, bf16[1,2,768,128]{3,2,1,0:T(8,128)(2,1)S(1)}, u32[]{:S(2)}, u32[]{:S(2)}) collective-permute-start(bf16[1,2,768,128]{3,2,1,0:T(8,128)(2,1)S(1)} %slice.50), channel_id=1, source_target_pairs={{0,128},{128,0},{256,384},{384,256},{1,129},{129,1},{257,385},{385... | collective-permute-start | bytes 1179656 | tf_op jit(solution)/shard_map/ppermute | solution.py:24
  151.6 4.6 %collective-permute-start.25 = (bf16[1,2,768,128]{3,2,1,0:T(8,128)(2,1)S(1)}, bf16[1,2,768,128]{3,2,1,0:T(8,128)(2,1)S(1)}, u32[]{:S(2)}, u32[]{:S(2)}) collective-permute-start(bf16[1,2,768,128]{3,2,1,0:T(8,128)(2,1)S(1)} %slice.51), channel_id=1, source_target_pairs={{0,384},{128,256},{256,128},{384,0},{1,385},{129,257},{257,129},{3... | collective-permute-start | bytes 1179656 | tf_op jit(solution)/shard_map/ppermute | solution.py:24
  156.2 8.0 %shard_map.46.act = bf16[2,256,384]{2,1,0:T(8,128)(2,1)} custom-call(s32[6]{0:T(128)} %stack.99.place, bf16[4,4,272,256]{3,2,1,0:T(8,128)(2,1)} %pad_maximum_fusion.refs_0_, bf16[4,4,272,256]{3,2,1,0:T(8,128)(2,1)} %collective-permute-done.22.refs_1_, bf16[2,4,128,384]{3,2,1,0:T(8,128)(2,1)} %copy-done.3, bf16[2,4,128,384]{3,2,1,0:T(8,128)(2,1)} %copy-done.6, ...), custom_call_target="tpu_custom_call" | custom-call | flops 1610612736 | bytes 7602200 | tf_op jit(solution)/shard_map/pallas_call | solution.py:145
  164.2 2.5 %collective-permute-start.23 = (bf16[2,256,384]{2,1,0:T(8,128)(2,1)}, bf16[2,256,384]{2,1,0:T(8,128)(2,1)S(1)}, u32[]{:S(2)}, u32[]{:S(2)}) collective-permute-start(bf16[2,256,384]{2,1,0:T(8,128)(2,1)} %shard_map.46.act), channel_id=1, source_target_pairs={{0,1},{1,0},{2,3},{3,2},{4,5},{5,4},{6,7},{7,6},{8,9},{9,8},{10,11... | collective-permute-start | bytes 1179656 | tf_op jit(solution)/shard_map/ppermute | solution.py:24
  173.1 3.8 %collective-permute-start.31 = (bf16[2,256,256]{2,1,0:T(8,128)(2,1)S(1)}, bf16[2,256,256]{2,1,0:T(8,128)(2,1)S(1)}, u32[]{:S(2)}, u32[]{:S(2)}) collective-permute-start(bf16[2,256,256]{2,1,0:T(8,128)(2,1)S(1)} %get-tuple-element.31), channel_id=1, source_target_pairs={{0,8},{4,12},{8,0},{12,4},{1,9},{5,13},{9,1},{13,5},{2,10},{6,14},... | collective-permute-start | bytes 786440 | tf_op jit(solution)/shard_map/ppermute | solution.py:24
  176.9 3.3 %collective-permute-start.30 = (bf16[2,256,256]{2,1,0:T(8,128)(2,1)S(1)}, bf16[2,256,256]{2,1,0:T(8,128)(2,1)S(1)}, u32[]{:S(2)}, u32[]{:S(2)}) collective-permute-start(bf16[2,256,256]{2,1,0:T(8,128)(2,1)S(1)} %get-tuple-element.29), channel_id=1, source_target_pairs={{0,4},{4,0},{8,12},{12,8},{1,5},{5,1},{9,13},{13,9},{2,6},{6,2},{1... | collective-permute-start | bytes 786440 | tf_op jit(solution)/shard_map/ppermute | solution.py:24
  184.0 3.8 %collective-permute-start.27 = (bf16[2,256,256]{2,1,0:T(8,128)(2,1)S(1)}, bf16[2,256,256]{2,1,0:T(8,128)(2,1)S(1)}, u32[]{:S(2)}, u32[]{:S(2)}) collective-permute-start(bf16[2,256,256]{2,1,0:T(8,128)(2,1)S(1)} %get-tuple-element.34), channel_id=1, source_target_pairs={{0,8},{4,12},{8,0},{12,4},{1,9},{5,13},{9,1},{13,5},{2,10},{6,14},... | collective-permute-start | bytes 786440 | tf_op jit(solution)/shard_map/ppermute | solution.py:24
  187.8 3.3 %collective-permute-start.26 = (bf16[2,256,256]{2,1,0:T(8,128)(2,1)S(1)}, bf16[2,256,256]{2,1,0:T(8,128)(2,1)S(1)}, u32[]{:S(2)}, u32[]{:S(2)}) collective-permute-start(bf16[2,256,256]{2,1,0:T(8,128)(2,1)S(1)} %get-tuple-element.32), channel_id=1, source_target_pairs={{0,4},{4,0},{8,12},{12,8},{1,5},{5,1},{9,13},{13,9},{2,6},{6,2},{1... | collective-permute-start | bytes 786440 | tf_op jit(solution)/shard_map/ppermute | solution.py:24
  191.2 4.2 %collective-permute-start.34 = (bf16[256,256]{1,0:T(8,128)(2,1)S(1)}, bf16[256,256]{1,0:T(8,128)(2,1)S(1)}, u32[]{:S(2)}, u32[]{:S(2)}) collective-permute-start(bf16[256,256]{1,0:T(8,128)(2,1)S(1)} %get-tuple-element.38), channel_id=1, source_target_pairs={{0,64},{2,66},{64,0},{66,2},{1,65},{3,67},{65,1},{67,3},{4,68},{6,... | collective-permute-start | bytes 393224 | tf_op jit(solution)/shard_map/ppermute | solution.py:24
  195.5 4.8 %collective-permute-start.33 = (bf16[256,256]{1,0:T(8,128)(2,1)S(1)}, bf16[256,256]{1,0:T(8,128)(2,1)S(1)}, u32[]{:S(2)}, u32[]{:S(2)}) collective-permute-start(bf16[256,256]{1,0:T(8,128)(2,1)S(1)} %get-tuple-element.37), channel_id=1, source_target_pairs={{0,66},{2,64},{64,2},{66,0},{1,67},{3,65},{65,3},{67,1},{4,70},{6,... | collective-permute-start | bytes 393224 | tf_op jit(solution)/shard_map/ppermute | solution.py:24
  200.6 7.0 %collective-permute-start.29 = (bf16[256,256]{1,0:T(8,128)(2,1)S(1)}, bf16[256,256]{1,0:T(8,128)(2,1)S(1)}, u32[]{:S(2)}, u32[]{:S(2)}) collective-permute-start(bf16[256,256]{1,0:T(8,128)(2,1)S(1)} %fusion.3), channel_id=1, source_target_pairs={{0,2},{2,0},{64,66},{66,64},{1,3},{3,1},{65,67},{67,65},{4,6},{6,4... | collective-permute-start | bytes 393224 | tf_op jit(solution)/shard_map/ppermute | solution.py:24
  210.0 17.3 %collective-permute-done.29 = bf16[256,256]{1,0:T(8,128)(2,1)S(1)} collective-permute-done((bf16[256,256]{1,0:T(8,128)(2,1)S(1)}, bf16[256,256]{1,0:T(8,128)(2,1)S(1)}, u32[]{:S(2)}, u32[]{:S(2)}) %collective-permute-start.29) | collective-permute-done | bytes 131104 | tf_op jit(solution)/shard_map/ppermute | solution.py:24
  (94 shorter events, 36.9 us)
Async XLA Ops:
  1.0 29.6 %collective-permute-start.3 = (bf16[128,384]{1,0:T(8,128)(2,1)S(1)}, bf16[128,384]{1,0:T(8,128)(2,1)S(1)}, u32[]{:S(2)}, u32[]{:S(2)}) collective-permute-start(bf16[128,384]{1,0:T(8,128)(2,1)S(1)} %get-tuple-element.40), channel_id=1, source_target_pairs={{0,0},{1,64},{64,1},{65,65},{2,2},{3,66},{66,3},{67,67},{4,4},{5,6... | collective-permute-start | bytes 294920 | tf_op jit(solution)/shard_map/ppermute | solution.py:33
  10.3 20.2 %collective-permute-start.4 = (bf16[128,384]{1,0:T(8,128)(2,1)S(1)}, bf16[128,384]{1,0:T(8,128)(2,1)S(1)}, u32[]{:S(2)}, u32[]{:S(2)}) collective-permute-start(bf16[128,384]{1,0:T(8,128)(2,1)S(1)} %get-tuple-element.39), channel_id=1, source_target_pairs={{0,1},{1,65},{64,0},{65,64},{2,3},{3,67},{66,2},{67,66},{4,5},{5,6... | collective-permute-start | bytes 294920 | tf_op jit(solution)/shard_map/ppermute | solution.py:34
  13.9 23.8 %collective-permute-start.2 = (bf16[272,256]{1,0:T(8,128)(2,1)S(1)}, bf16[272,256]{1,0:T(8,128)(2,1)S(1)}, u32[]{:S(2)}, u32[]{:S(2)}) collective-permute-start(bf16[272,256]{1,0:T(8,128)(2,1)S(1)} %get-tuple-element.42), channel_id=1, source_target_pairs={{0,66},{2,64},{64,2},{66,0},{1,67},{3,65},{65,3},{67,1},{4,70},{6,... | collective-permute-start | bytes 417800 | tf_op jit(solution)/shard_map/ppermute | solution.py:24
  21.6 32.1 %collective-permute-start.1 = (bf16[272,256]{1,0:T(8,128)(2,1)S(1)}, bf16[272,256]{1,0:T(8,128)(2,1)S(1)}, u32[]{:S(2)}, u32[]{:S(2)}) collective-permute-start(bf16[272,256]{1,0:T(8,128)(2,1)S(1)} %get-tuple-element.42), channel_id=1, source_target_pairs={{0,64},{2,66},{64,0},{66,2},{1,65},{3,67},{65,1},{67,3},{4,68},{6,... | collective-permute-start | bytes 417800 | tf_op jit(solution)/shard_map/ppermute | solution.py:24
  25.8 27.9 %collective-permute-start = (bf16[272,256]{1,0:T(8,128)(2,1)S(1)}, bf16[272,256]{1,0:T(8,128)(2,1)S(1)}, u32[]{:S(2)}, u32[]{:S(2)}) collective-permute-start(bf16[272,256]{1,0:T(8,128)(2,1)S(1)} %get-tuple-element.42), channel_id=1, source_target_pairs={{0,2},{2,0},{64,66},{66,64},{1,3},{3,1},{65,67},{67,65},{4,6},{6,4... | collective-permute-start | bytes 417800 | tf_op jit(solution)/shard_map/ppermute | solution.py:24
  30.6 24.0 %collective-permute-start.5 = (bf16[768,128]{1,0:T(8,128)(2,1)}, bf16[768,128]{1,0:T(8,128)(2,1)S(1)}, u32[]{:S(2)}, u32[]{:S(2)}) collective-permute-start(bf16[768,128]{1,0:T(8,128)(2,1)} %param.7), channel_id=1, source_target_pairs={{0,0},{16,16},{32,33},{48,49},{65,64},{81,80},{97,97},{113,113},{1... | collective-permute-start | bytes 589832 | tf_op jit(solution)/shard_map/ppermute | solution.py:53
  32.2 22.5 %collective-permute-start.6 = (bf16[768,128]{1,0:T(8,128)(2,1)}, bf16[768,128]{1,0:T(8,128)(2,1)S(1)}, u32[]{:S(2)}, u32[]{:S(2)}) collective-permute-start(bf16[768,128]{1,0:T(8,128)(2,1)} %param.7), channel_id=1, source_target_pairs={{1,64},{17,80},{33,97},{49,113},{64,0},{80,16},{96,33},{112,49},{0... | collective-permute-start | bytes 589832 | tf_op jit(solution)/shard_map/ppermute | solution.py:53
  54.6 28.7 %collective-permute-start.11 = (bf16[4,272,256]{2,1,0:T(8,128)(2,1)S(1)}, bf16[4,272,256]{2,1,0:T(8,128)(2,1)S(1)}, u32[]{:S(2)}, u32[]{:S(2)}) collective-permute-start(bf16[4,272,256]{2,1,0:T(8,128)(2,1)S(1)} %get-tuple-element.24), channel_id=1, source_target_pairs={{0,12},{4,8},{8,4},{12,0},{1,13},{5,9},{9,5},{13,1},{2,14},{6,10},... | collective-permute-start | bytes 1671176 | tf_op jit(solution)/shard_map/ppermute | solution.py:24
  57.8 25.5 %collective-permute-start.7 = (bf16[4,272,256]{2,1,0:T(8,128)(2,1)S(1)}, bf16[4,272,256]{2,1,0:T(8,128)(2,1)S(1)}, u32[]{:S(2)}, u32[]{:S(2)}) collective-permute-start(bf16[4,272,256]{2,1,0:T(8,128)(2,1)S(1)} %get-tuple-element.24), channel_id=1, source_target_pairs={{0,4},{4,0},{8,12},{12,8},{1,5},{5,1},{9,13},{13,9},{2,6},{6,2},{1... | collective-permute-start | bytes 1671176 | tf_op jit(solution)/shard_map/ppermute | solution.py:24
  61.4 14.6 %collective-permute-start.10 = (bf16[2,128,384]{2,1,0:T(8,128)(2,1)S(1)}, bf16[2,128,384]{2,1,0:T(8,128)(2,1)S(1)}, u32[]{:S(2)}, u32[]{:S(2)}) collective-permute-start(bf16[2,128,384]{2,1,0:T(8,128)(2,1)S(1)} %pad_maximum_fusion.5), channel_id=1, source_target_pairs={{0,48},{16,32},{32,16},{48,0},{1,49},{17,33},{33,17},{49,1},{2,50}... | collective-permute-start | bytes 589832 | tf_op jit(solution)/shard_map/ppermute | solution.py:24
  67.8 15.3 %collective-permute-start.9 = (bf16[2,128,384]{2,1,0:T(8,128)(2,1)S(1)}, bf16[2,128,384]{2,1,0:T(8,128)(2,1)S(1)}, u32[]{:S(2)}, u32[]{:S(2)}) collective-permute-start(bf16[2,128,384]{2,1,0:T(8,128)(2,1)S(1)} %pad_maximum_fusion.5), channel_id=1, source_target_pairs={{0,32},{16,48},{32,0},{48,16},{1,33},{17,49},{33,1},{49,17},{2,34}... | collective-permute-start | bytes 589832 | tf_op jit(solution)/shard_map/ppermute | solution.py:24
  83.3 17.6 %collective-permute-start.13 = (bf16[2,768,128]{2,1,0:T(8,128)(2,1)S(1)}, bf16[2,768,128]{2,1,0:T(8,128)(2,1)S(1)}, u32[]{:S(2)}, u32[]{:S(2)}) collective-permute-start(bf16[2,768,128]{2,1,0:T(8,128)(2,1)S(1)} %pad_maximum_fusion.4), channel_id=1, source_target_pairs={{0,32},{16,48},{33,1},{49,17},{1,0},{17,16},{32,33},{48,49},{2,34}... | collective-permute-start | bytes 1179656 | tf_op jit(solution)/shard_map/ppermute | solution.py:61
  89.0 21.5 %collective-permute-start.12 = (bf16[2,4,128,384]{3,2,1,0:T(8,128)(2,1)S(1)}, bf16[2,4,128,384]{3,2,1,0:T(8,128)(2,1)S(1)}, u32[]{:S(2)}, u32[]{:S(2)}) collective-permute-start(bf16[2,4,128,384]{3,2,1,0:T(8,128)(2,1)S(1)} %pad_maximum_fusion.1.refs_2_), channel_id=1, source_target_pairs={{0,384},{128,256},{256,128},{384,0},{1,385},{129,257},{257,129},{3... | collective-permute-start | bytes 2359304 | tf_op jit(solution)/shard_map/ppermute | solution.py:24
  91.2 22.0 %collective-permute-start.17 = (bf16[2,4,128,384]{3,2,1,0:T(8,128)(2,1)S(1)}, bf16[2,4,128,384]{3,2,1,0:T(8,128)(2,1)S(1)}, u32[]{:S(2)}, u32[]{:S(2)}) collective-permute-start(bf16[2,4,128,384]{3,2,1,0:T(8,128)(2,1)S(1)} %pad_maximum_fusion.1.refs_2_), channel_id=1, source_target_pairs={{0,128},{128,0},{256,384},{384,256},{1,129},{129,1},{257,385},{385... | collective-permute-start | bytes 2359304 | tf_op jit(solution)/shard_map/ppermute | solution.py:24
  94.7 14.7 %collective-permute-start.15 = (bf16[2,768,128]{2,1,0:T(8,128)(2,1)S(1)}, bf16[2,768,128]{2,1,0:T(8,128)(2,1)}, u32[]{:S(2)}, u32[]{:S(2)}) collective-permute-start(bf16[2,768,128]{2,1,0:T(8,128)(2,1)S(1)} %pad_maximum_fusion.4), channel_id=1, source_target_pairs={{0,48},{16,32},{33,17},{49,1},{1,0},{17,16},{32,33},{48,49},{2,50}... | collective-permute-start | bytes 1179656 | tf_op jit(solution)/shard_map/ppermute | solution.py:61
  110.7 11.9 %collective-permute-start.16 = (bf16[1,4,128,384]{3,2,1,0:T(8,128)(2,1)S(1)}, bf16[1,4,128,384]{3,2,1,0:T(8,128)(2,1)S(1)}, u32[]{:S(2)}, u32[]{:S(2)}) collective-permute-start(bf16[1,4,128,384]{3,2,1,0:T(8,128)(2,1)S(1)} %slice.48), channel_id=1, source_target_pairs={{0,128},{128,0},{256,384},{384,256},{1,129},{129,1},{257,385},{385... | collective-permute-start | bytes 1179656 | tf_op jit(solution)/shard_map/ppermute | solution.py:24
  113.3 11.1 %collective-permute-start.18 = (bf16[1,4,128,384]{3,2,1,0:T(8,128)(2,1)S(1)}, bf16[1,4,128,384]{3,2,1,0:T(8,128)(2,1)S(1)}, u32[]{:S(2)}, u32[]{:S(2)}) collective-permute-start(bf16[1,4,128,384]{3,2,1,0:T(8,128)(2,1)S(1)} %slice.49), channel_id=1, source_target_pairs={{0,384},{128,256},{256,128},{384,0},{1,385},{129,257},{257,129},{3... | collective-permute-start | bytes 1179656 | tf_op jit(solution)/shard_map/ppermute | solution.py:24
  116.5 23.6 %collective-permute-start.20 = (bf16[2,2,768,128]{3,2,1,0:T(8,128)(2,1)S(1)}, bf16[2,2,768,128]{3,2,1,0:T(8,128)(2,1)S(1)}, u32[]{:S(2)}, u32[]{:S(2)}) collective-permute-start(bf16[2,2,768,128]{3,2,1,0:T(8,128)(2,1)S(1)} %pad_maximum_fusion.2.w0), channel_id=1, source_target_pairs={{0,128},{128,0},{256,384},{384,256},{1,129},{129,1},{257,385},{385... | collective-permute-start | bytes 2359304 | tf_op jit(solution)/shard_map/ppermute | solution.py:24
  120.4 21.5 %collective-permute-start.21 = (bf16[2,2,768,128]{3,2,1,0:T(8,128)(2,1)S(1)}, bf16[2,2,768,128]{3,2,1,0:T(8,128)(2,1)S(1)}, u32[]{:S(2)}, u32[]{:S(2)}) collective-permute-start(bf16[2,2,768,128]{3,2,1,0:T(8,128)(2,1)S(1)} %pad_maximum_fusion.2.w0), channel_id=1, source_target_pairs={{0,384},{128,256},{256,128},{384,0},{1,385},{129,257},{257,129},{3... | collective-permute-start | bytes 2359304 | tf_op jit(solution)/shard_map/ppermute | solution.py:24
  124.4 14.0 %collective-permute-start.19 = (bf16[4,272,256]{2,1,0:T(8,128)(2,1)S(1)}, bf16[4,272,256]{2,1,0:T(8,128)(2,1)S(1)}, u32[]{:S(2)}, u32[]{:S(2)}) collective-permute-start(bf16[4,272,256]{2,1,0:T(8,128)(2,1)S(1)} %copy-done.12), channel_id=1, source_target_pairs={{0,8},{4,12},{8,0},{12,4},{1,9},{5,13},{9,1},{13,5},{2,10},{6,14},... | collective-permute-start | bytes 1671176 | tf_op jit(solution)/shard_map/ppermute | solution.py:24
  142.0 14.2 %collective-permute-start.22 = (bf16[4,4,272,256]{3,2,1,0:T(8,128)(2,1)}, bf16[4,4,272,256]{3,2,1,0:T(8,128)(2,1)}, u32[]{:S(2)}, u32[]{:S(2)}) collective-permute-start(bf16[4,4,272,256]{3,2,1,0:T(8,128)(2,1)} %pad_maximum_fusion.refs_0_), channel_id=1, source_target_pairs={{0,1},{1,0},{2,3},{3,2},{4,5},{5,4},{6,7},{7,6},{8,9},{9,8},{10,11... | collective-permute-start | bytes 6684680 | tf_op jit(solution)/shard_map/ppermute | solution.py:24
  147.1 19.7 %collective-permute-start.24 = (bf16[1,2,768,128]{3,2,1,0:T(8,128)(2,1)S(1)}, bf16[1,2,768,128]{3,2,1,0:T(8,128)(2,1)S(1)}, u32[]{:S(2)}, u32[]{:S(2)}) collective-permute-start(bf16[1,2,768,128]{3,2,1,0:T(8,128)(2,1)S(1)} %slice.50), channel_id=1, source_target_pairs={{0,128},{128,0},{256,384},{384,256},{1,129},{129,1},{257,385},{385... | collective-permute-start | bytes 1179656 | tf_op jit(solution)/shard_map/ppermute | solution.py:24
  151.6 15.2 %collective-permute-start.25 = (bf16[1,2,768,128]{3,2,1,0:T(8,128)(2,1)S(1)}, bf16[1,2,768,128]{3,2,1,0:T(8,128)(2,1)S(1)}, u32[]{:S(2)}, u32[]{:S(2)}) collective-permute-start(bf16[1,2,768,128]{3,2,1,0:T(8,128)(2,1)S(1)} %slice.51), channel_id=1, source_target_pairs={{0,384},{128,256},{256,128},{384,0},{1,385},{129,257},{257,129},{3... | collective-permute-start | bytes 1179656 | tf_op jit(solution)/shard_map/ppermute | solution.py:24
  171.1 16.6 %collective-permute-start.32 = (bf16[2,256,256]{2,1,0:T(8,128)(2,1)S(1)}, bf16[2,256,256]{2,1,0:T(8,128)(2,1)S(1)}, u32[]{:S(2)}, u32[]{:S(2)}) collective-permute-start(bf16[2,256,256]{2,1,0:T(8,128)(2,1)S(1)} %get-tuple-element.30), channel_id=1, source_target_pairs={{0,12},{4,8},{8,4},{12,0},{1,13},{5,9},{9,5},{13,1},{2,14},{6,10},... | collective-permute-start | bytes 786440 | tf_op jit(solution)/shard_map/ppermute | solution.py:24
  173.1 18.0 %collective-permute-start.31 = (bf16[2,256,256]{2,1,0:T(8,128)(2,1)S(1)}, bf16[2,256,256]{2,1,0:T(8,128)(2,1)S(1)}, u32[]{:S(2)}, u32[]{:S(2)}) collective-permute-start(bf16[2,256,256]{2,1,0:T(8,128)(2,1)S(1)} %get-tuple-element.31), channel_id=1, source_target_pairs={{0,8},{4,12},{8,0},{12,4},{1,9},{5,13},{9,1},{13,5},{2,10},{6,14},... | collective-permute-start | bytes 786440 | tf_op jit(solution)/shard_map/ppermute | solution.py:24
  176.9 14.2 %collective-permute-start.30 = (bf16[2,256,256]{2,1,0:T(8,128)(2,1)S(1)}, bf16[2,256,256]{2,1,0:T(8,128)(2,1)S(1)}, u32[]{:S(2)}, u32[]{:S(2)}) collective-permute-start(bf16[2,256,256]{2,1,0:T(8,128)(2,1)S(1)} %get-tuple-element.29), channel_id=1, source_target_pairs={{0,4},{4,0},{8,12},{12,8},{1,5},{5,1},{9,13},{13,9},{2,6},{6,2},{1... | collective-permute-start | bytes 786440 | tf_op jit(solution)/shard_map/ppermute | solution.py:24
  182.0 18.3 %collective-permute-start.28 = (bf16[2,256,256]{2,1,0:T(8,128)(2,1)S(1)}, bf16[2,256,256]{2,1,0:T(8,128)(2,1)S(1)}, u32[]{:S(2)}, u32[]{:S(2)}) collective-permute-start(bf16[2,256,256]{2,1,0:T(8,128)(2,1)S(1)} %get-tuple-element.33), channel_id=1, source_target_pairs={{0,12},{4,8},{8,4},{12,0},{1,13},{5,9},{9,5},{13,1},{2,14},{6,10},... | collective-permute-start | bytes 786440 | tf_op jit(solution)/shard_map/ppermute | solution.py:24
  184.0 16.3 %collective-permute-start.27 = (bf16[2,256,256]{2,1,0:T(8,128)(2,1)S(1)}, bf16[2,256,256]{2,1,0:T(8,128)(2,1)S(1)}, u32[]{:S(2)}, u32[]{:S(2)}) collective-permute-start(bf16[2,256,256]{2,1,0:T(8,128)(2,1)S(1)} %get-tuple-element.34), channel_id=1, source_target_pairs={{0,8},{4,12},{8,0},{12,4},{1,9},{5,13},{9,1},{13,5},{2,10},{6,14},... | collective-permute-start | bytes 786440 | tf_op jit(solution)/shard_map/ppermute | solution.py:24
  187.8 12.7 %collective-permute-start.26 = (bf16[2,256,256]{2,1,0:T(8,128)(2,1)S(1)}, bf16[2,256,256]{2,1,0:T(8,128)(2,1)S(1)}, u32[]{:S(2)}, u32[]{:S(2)}) collective-permute-start(bf16[2,256,256]{2,1,0:T(8,128)(2,1)S(1)} %get-tuple-element.32), channel_id=1, source_target_pairs={{0,4},{4,0},{8,12},{12,8},{1,5},{5,1},{9,13},{13,9},{2,6},{6,2},{1... | collective-permute-start | bytes 786440 | tf_op jit(solution)/shard_map/ppermute | solution.py:24
  191.2 16.4 %collective-permute-start.34 = (bf16[256,256]{1,0:T(8,128)(2,1)S(1)}, bf16[256,256]{1,0:T(8,128)(2,1)S(1)}, u32[]{:S(2)}, u32[]{:S(2)}) collective-permute-start(bf16[256,256]{1,0:T(8,128)(2,1)S(1)} %get-tuple-element.38), channel_id=1, source_target_pairs={{0,64},{2,66},{64,0},{66,2},{1,65},{3,67},{65,1},{67,3},{4,68},{6,... | collective-permute-start | bytes 393224 | tf_op jit(solution)/shard_map/ppermute | solution.py:24
  195.5 14.5 %collective-permute-start.33 = (bf16[256,256]{1,0:T(8,128)(2,1)S(1)}, bf16[256,256]{1,0:T(8,128)(2,1)S(1)}, u32[]{:S(2)}, u32[]{:S(2)}) collective-permute-start(bf16[256,256]{1,0:T(8,128)(2,1)S(1)} %get-tuple-element.37), channel_id=1, source_target_pairs={{0,66},{2,64},{64,2},{66,0},{1,67},{3,65},{65,3},{67,1},{4,70},{6,... | collective-permute-start | bytes 393224 | tf_op jit(solution)/shard_map/ppermute | solution.py:24
  200.6 26.7 %collective-permute-start.29 = (bf16[256,256]{1,0:T(8,128)(2,1)S(1)}, bf16[256,256]{1,0:T(8,128)(2,1)S(1)}, u32[]{:S(2)}, u32[]{:S(2)}) collective-permute-start(bf16[256,256]{1,0:T(8,128)(2,1)S(1)} %fusion.3), channel_id=1, source_target_pairs={{0,2},{2,0},{64,66},{66,64},{1,3},{3,1},{65,67},{67,65},{4,6},{6,4... | collective-permute-start | bytes 393224 | tf_op jit(solution)/shard_map/ppermute | solution.py:24
  (18 other events, 308.5 us)
